TPU v7x, 32 devices: a whole 2x2x4 slice. The times are simulated.
32 devices in a mesh: parts: 2 (over y), ap: 16 (over z, x, core).
Axes of the slice: x: 2, y: 2, z: 4, core: 2. Of those that a mesh axis runs over, the one named last changes fastest.
Arguments:
- channel: bfloat16 [32, 12, 2, 32, 512], P(('parts', 'ap')), parts along dimension 0, may hold values from -6 to 6
- precoder: bfloat16 [2, 16384, 512], P(None, ('parts', 'ap')), parts along dimension 1
- visible: int32 [32, 12], P(('parts', 'ap')), parts along dimension 0, may hold values from 0 to 15, all different within a row
- cluster: int32 [1024, 4], P('parts'), parts along dimension 0, may hold values from 0 to 15, all different within a row; in each aligned block of 512 rows (0 to 511, 512 to 1023, ...) at most 256 rows name the same one
Outputs:
- effective: float32 [1024, 2, 512], P(('parts', 'ap')), parts along dimension 0
There are 2 independent parts, one for each index of `parts`. A program takes and returns all parts, laid end to end along the dimension named above; each array names one. Nothing has to cross between parts.
Inputs may be any that keep to these rules, and one draw needn't show every extreme that they name: `visible`: each row names 12 different user groups, and every user group is named by some AP group. `cluster`: each row names 4 different AP groups; every AP group serves some planned user, at most 256 of them, and some AP group serves exactly 256.
All inputs are finite; a program needn't handle non-finite values.
Results may differ from a plain program's by a relative error of at most 0.0029.
Values sent between devices are 32-bit elements; how exact they have to be, the bound alone decides.
No kernel may reach another device: no remote copies, remote signals or barrier semaphores. Data moves between devices by JAX's collectives and lax.ppermute only.
A program may use at most 128 MiB of HBM per device.

v0:
```python
import jax
import jax.numpy as jnp
from jax import lax
from jax.sharding import PartitionSpec as P

epsilon = 1e-06


def place_slots(groups, partial_value, device_count):
    empty = jnp.zeros((device_count,) + partial_value.shape[1:], jnp.float32)
    return empty.at[groups].set(partial_value)


def on_device(channel, precoder, visible, cluster):
    myself = lax.axis_index("ap")
    device_count = lax.axis_size("ap")
    served_flag = jnp.any(cluster == myself, axis=1)
    served_mask = served_flag.astype(jnp.float32)
    masked_channel = precoder.astype(jnp.float32) * served_mask[None, None, :]
    local_power = jnp.sum(masked_channel * masked_channel, axis=(0, 1))
    power = lax.psum(local_power, "ap")
    scaled = (masked_channel * lax.rsqrt(power + epsilon)).astype(jnp.bfloat16)
    chan_real = channel[0, :, 0]
    chan_imag = channel[0, :, 1]
    groups = visible[0]
    group_rows = chan_real.shape[1]
    column_count = cluster.shape[0]
    first = jnp.concatenate([scaled[0], scaled[1]], axis=-1)
    second = jnp.concatenate([scaled[1], -scaled[0]], axis=-1)
    partial_value = jnp.einsum("vua,ar->vur", chan_real, first, preferred_element_type=jnp.float32)
    partial_value = partial_value + jnp.einsum(
        "vua,ar->vur", chan_imag, second, preferred_element_type=jnp.float32
    )
    width = partial_value.shape[2]
    slots = place_slots(groups, partial_value, device_count)
    flat = slots.reshape(device_count * group_rows, width)
    result = lax.psum_scatter(flat, "ap", scatter_dimension=0, tiled=True)
    return result.reshape(group_rows, 2, column_count)


def solution(mesh):
    in_specs = (
        P(("parts", "ap"), None, None, None, None),
        P(None, ("parts", "ap"), None),
        P(("parts", "ap"), None),
        P("parts", None),
    )
    out_specs = P(("parts", "ap"), None, None)
    return jax.shard_map(
        on_device, mesh=mesh, in_specs=in_specs, out_specs=out_specs, check_vma=False
    )
```

profile of v0, /device:TPU:0, one launch (start us, length us, event | category | flops | bytes accessed | tf_op | source)
XLA Modules:
  0.0 120.3 jit_solution(17885114760625687215)
XLA Ops:
  6.5 0.0 reduce-scatter.2.cloned.1.call-start
  6.5 0.7 compare_reduce_fusion
  7.3 1.6 %multiply_reduce_fusion = f32[512]{0:T(512)S(1)} fusion(bf16[2,512,512]{2,1,0:T(8,128)(2,1)} %param.5, f32[512]{0:T(512)S(1)} %convert_element_type.14), kind=kLoop, calls=%fused_computation.2 | loop fusion | flops 2096640 | bytes 1052672 | tf_op jit(solution)/shard_map/reduce_sum | solution.py:20
  8.8 34.9 %psum.7 = f32[512]{0:T(512)S(1)} all-reduce(f32[512]{0:T(512)S(1)} %multiply_reduce_fusion), channel_id=1, replica_groups=mesh['parts'=2,'ap'=16] {'ap'}, use_global_device_ids=true, to_apply=%region_2.0 | all-reduce | flops 512 | bytes 4096 | tf_op jit(solution)/shard_map/psum | solution.py:21
  43.7 1.5 %multiply_convert_fusion = bf16[2,512,512]{2,1,0:T(8,128)(2,1)S(1)} fusion(bf16[2,512,512]{2,1,0:T(8,128)(2,1)} %param.5, f32[512]{0:T(512)S(1)} %add_rsqrt_fusion, f32[512]{0:T(512)S(1)} %convert_element_type.14), kind=kLoop, calls=%fused_computation.1 | loop fusion | flops 2097152 | bytes 2101248 | tf_op jit(solution)/shard_map/convert_element_type | solution.py:22
  45.2 0.0 copy-start.2
  45.2 0.0 copy-start.1
  45.3 0.1 slice_bitcast_fusion.1
  45.4 0.5 copy-done.2
  45.9 0.5 copy-done.1
  46.4 0.6 fusion
  47.0 1.7 %add_bitcast_fusion = f32[12,32,1024]{2,1,0:T(8,128)} fusion(f32[1024,12,32]{0,2,1:T(8,128)S(1)} %fusion, bf16[512,512]{1,0:T(8,128)(2,1)S(1)} %fusion.12, bf16[512,512]{1,0:T(8,128)(2,1)S(1)} %get-tuple-element.6, bf16[1,12,2,32,512]{4,3,2,1,0:T(8,128)(2,1)S(1)} %copy-done.1), kind=kOutput, calls=%fused_computation.4 | convolution fusion | flops 405143552 | bytes 4587520 | tf_op jit(solution)/shard_map/vua,ar->vur/dot_general | solution.py:31
  48.7 0.2 broadcast_in_dim.2
  48.9 2.4 %scatter_fusion = f32[16,32,1024]{2,1,0:T(8,128)S(1)} fusion(f32[16,32,1024]{2,1,0:T(8,128)S(1)} %broadcast_in_dim.2, s32[12]{0:T(128)S(1)} %fusion.9, f32[12,32,1024]{2,1,0:T(8,128)} %add_bitcast_fusion), kind=kCustom, calls=%fused_computation | custom fusion | bytes 4718640 | tf_op jit(solution)/shard_map/scatter | solution.py:11
  51.4 0.0 copy-start
  51.4 1.3 %copy-done = f32[16,32,1024]{2,1,0:T(8,128)} copy-done((f32[16,32,1024]{2,1,0:T(8,128)}, f32[16,32,1024]{2,1,0:T(8,128)S(1)}, u32[]{:S(2)}) %copy-start) | copy-done | bytes 2097176
  52.7 0.0 reduce-scatter.2.cloned.1.call-update
  52.8 59.0 %reduce-scatter.2.cloned.1.call-done = f32[32,1024]{1,0:T(8,128)} async-done(((f32[512,1024]{1,0:T(8,128)}), f32[32,1024]{1,0:T(8,128)}) %reduce-scatter.2.cloned.1.call-update) | async-done | bytes 131088 | tf_op jit(solution)/shard_map/reduce_scatter | solution.py:37
  111.7 1.7 %reshape.39 = f32[32,2,512]{2,1,0:T(2,128)} reshape(f32[32,1024]{1,0:T(8,128)} %reduce-scatter.2.cloned.1.call-done) | data formatting | bytes 262144 | tf_op jit(solution)/shard_map/reshape | solution.py:38
  (4 shorter events, 0.1 us)
Async XLA Ops:
  6.5 105.2 %reduce-scatter.2.cloned.1.call-start = ((), (), s32[]{:S(2)}) async-start(), calls=%async_computation.1 | async-start | bytes 2228224 | tf_op jit(solution)/shard_map/reduce_scatter | solution.py:37
  45.2 0.7 copy-start.2
  45.2 1.1 copy-start.1
  51.4 1.4 %copy-start = (f32[16,32,1024]{2,1,0:T(8,128)}, f32[16,32,1024]{2,1,0:T(8,128)S(1)}, u32[]{:S(2)}) copy-start(f32[16,32,1024]{2,1,0:T(8,128)S(1)} %scatter_fusion) | copy-start | bytes 6291460
Sparse Core Ops, SparseCore 0:
  52.9 58.8 reduce-scatter.1
where the time goes:
time: 121 us; the launch traced here: 120 us
  waiting for transfers between devices  59 us (49%)
  blocking collectives  34.9 us (29%)
  between operations  13.5 us (11%)
  local copies, waits for them, and re-layouts  6.76 us (6%)
  other arithmetic  3.82 us (3%)
  matrix products  2.32 us (2%)
    reduce_scatter x1, waiting for transfers between devices, on_device(): result = lax.psum_scatter(flat, 'ap', scatter_dimension=0, tiled=True)  59 us
    psum x1, blocking collectives, on_device(): power = lax.psum(local_power, 'ap')  34.9 us
    scatter x1, local copies, waits for them, and re-layouts, place_slots(): return empty.at[groups].set(partial_value)  2.43 us
  transfers between devices with their start and end apart: 1, of which 1 were waited for; matrix products, arithmetic and copies ran while one was open for 0% of the time, Pallas kernels for 0%

commit v1 on v0

v1 whole, which is shorter than its diff:
```python
import functools

import jax
import jax.numpy as jnp
from jax import lax
from jax.experimental import pallas as pl
from jax.experimental.pallas import tpu as pltpu
from jax.sharding import PartitionSpec as P

epsilon = 1e-06
MIB = 1 << 20


def bit_orders(bits):
    first = list(range(bits))
    second = list(first)
    if bits > 2:
        second[1], second[2] = second[2], second[1]
    return first, second


def second_place(place, bits):
    first, second = bit_orders(bits)
    tail = bits - 1
    value = {bit: (place >> (tail - 1 - at)) & 1 for at, bit in enumerate(first[1:])}
    out = 0
    for bit in second[1:]:
        out = out * 2 + value[bit]
    return out


def local_kernel(which, bits, visible, cluster, channel, precoder, out, rows):
    me = lax.axis_index("ap")
    held, users = channel.shape[1], channel.shape[3]
    columns = precoder.shape[2]
    slots = out.shape[0] // (2 * (users // 8) * (columns // 128))
    tiles = (users // 8) * (columns // 128)
    first, _ = bit_orders(bits)
    rows[...] = jnp.zeros_like(rows)

    def place_one(v):
        relative = visible[0, v] ^ me
        place = 0
        for bit in first[1:]:
            place = place * 2 + (1 - ((relative >> bit) & 1))

        @pl.when((relative & 1) == which)
        def _():
            at = pl.ds(pl.multiple_of(place * users, users), users)
            rows[0, at, :] = channel[0, v, 0]
            rows[1, at, :] = channel[0, v, 1]

    for v in range(held):
        place_one(v)

    served = jnp.max((cluster[...] == me).astype(jnp.float32), axis=0, keepdims=True) > 0.0
    real, imag = precoder[0], precoder[1]
    chunk = min(slots, 8)

    def dot(a, b):
        return jnp.dot(a, b, preferred_element_type=jnp.float32)

    for base in range(0, slots, chunk):
        at = slice(base * users, (base + chunk) * users)
        left, right = rows[0, at, :], rows[1, at, :]
        parts = (
            dot(left, real) + dot(right, imag),
            dot(left, imag) - dot(right, real),
        )
        for half, value in enumerate(parts):
            value = jnp.where(served, value, 0.0)
            for slot in range(chunk):
                place = base + slot
                if half == 1:
                    place = slots + second_place(place, bits)
                for block in range(columns // 128):
                    piece = value[slot * users:(slot + 1) * users, block * 128:(block + 1) * 128]
                    start = place * tiles + block * (users // 8)
                    out[start:start + users // 8] = piece.reshape(users // 8, 8, 128)
    power = jnp.zeros((1, columns), jnp.float32)
    for plane in range(2):
        wide = precoder[plane].astype(jnp.float32)
        power = power + jnp.sum(wide * wide, axis=0, keepdims=True)
    power = jnp.where(served, power, 0.0)
    tile = jnp.concatenate(
        [power[:, block * 128:(block + 1) * 128] for block in range(columns // 128)]
        + [jnp.zeros((8 - columns // 128, 128), jnp.float32)],
        axis=0,
    )
    out[2 * slots * tiles] = tile


def local_products(which, bits, visible, cluster, channel, precoder):
    held, users, antennas = channel.shape[1], channel.shape[3], channel.shape[4]
    columns = precoder.shape[2]
    tiles = (users // 8) * (columns // 128)
    slots = 1 << (bits - 1)
    vmem = pl.BlockSpec(memory_space=pltpu.VMEM)
    flops = 8 * slots * users * antennas * columns
    size = channel.size * 2 + precoder.size * 2 + 2 * slots * tiles * 4096
    return pl.pallas_call(
        functools.partial(local_kernel, which, bits),
        out_shape=jax.ShapeDtypeStruct((2 * slots * tiles + 1, 8, 128), jnp.float32),
        in_specs=[pl.BlockSpec(memory_space=pltpu.SMEM), vmem, vmem, vmem],
        out_specs=vmem,
        scratch_shapes=[pltpu.VMEM((2, slots * users, antennas), jnp.bfloat16)],
        compiler_params=pltpu.CompilerParams(vmem_limit_bytes=48 * MIB if slots > 8 else 24 * MIB),
        cost_estimate=pl.CostEstimate(flops=flops, bytes_accessed=size, transcendentals=0),
        name="local_products",
    )(visible, cluster, channel, precoder)


def part_spec(start, count):
    return pl.BlockSpec((count, 8, 128), lambda i: (start // count, 0, 0))


def sum_kernel(halves, terms, with_power, count, *refs):
    out = refs[-1]
    at = 0
    for half in range(halves):
        total = refs[at][...]
        for term in range(1, terms):
            total = total + refs[at + term][...]
        at += terms
        out[half * count:(half + 1) * count] = total
    if with_power:
        total = refs[at][...]
        for term in range(1, terms):
            total = total + refs[at + term][...]
        out[halves * count:] = total


def summed(held, halves, left, tiles, with_power):
    count = left * tiles
    arrays, specs = [], []
    for half in halves:
        for pieces in held:
            array, base, slots = pieces[half]
            arrays.append(array)
            specs.append(part_spec((base + slots - 2 * left) * tiles, count))
    if with_power:
        for pieces in held:
            array = pieces[0][0]
            arrays.append(array)
            specs.append(part_spec(array.shape[0] - 1, 1))
    size = len(halves) * count + int(with_power)
    return pl.pallas_call(
        functools.partial(sum_kernel, len(halves), len(held), with_power, count),
        grid=(1,),
        out_shape=jax.ShapeDtypeStruct((size, 8, 128), jnp.float32),
        in_specs=specs,
        out_specs=pl.BlockSpec((size, 8, 128), lambda i: (0, 0, 0)),
        compiler_params=pltpu.CompilerParams(vmem_limit_bytes=48 * MIB if left > 4 else 24 * MIB),
        cost_estimate=pl.CostEstimate(
            flops=size * 1024 * len(held), bytes_accessed=size * 4096 * (len(held) + 1), transcendentals=0
        ),
        name="summed",
    )(*arrays)


def final_kernel(terms, users, *refs):
    out = refs[-1]
    power = refs[2 * terms][0]
    for term in range(1, terms):
        power = power + refs[2 * terms + term][0]
    scale = lax.rsqrt(power + epsilon)
    blocks = out.shape[2] // 128
    for half in range(2):
        for block in range(blocks):
            at = slice(block * (users // 8), (block + 1) * (users // 8))
            total = refs[half * terms][at]
            for term in range(1, terms):
                total = total + refs[half * terms + term][at]
            factor = scale[block:block + 1, :]
            total = total.reshape(users, 128)
            value = jnp.where(factor > 0.0, total * factor, 0.0)
            out[:, half, block * 128:(block + 1) * 128] = value


def finish(held, tiles, users, columns):
    arrays, specs = [], []
    for half in range(2):
        for pieces in held:
            array, base, slots = pieces[half]
            arrays.append(array)
            specs.append(part_spec((base + slots - 1) * tiles, tiles))
    for pieces in held:
        array = pieces[0][0]
        arrays.append(array)
        specs.append(part_spec(array.shape[0] - 1, 1))
    return pl.pallas_call(
        functools.partial(final_kernel, len(held), users),
        grid=(1,),
        out_shape=jax.ShapeDtypeStruct((users, 2, columns), jnp.float32),
        in_specs=specs,
        out_specs=pl.BlockSpec((users, 2, columns), lambda i: (0, 0, 0)),
        name="finish",
    )(*arrays)


def on_device(channel, precoder, visible, cluster):
    devices = lax.axis_size("ap")
    bits = devices.bit_length() - 1
    users, columns = channel.shape[3], precoder.shape[2]
    tiles = (users // 8) * (columns // 128)
    orders = bit_orders(bits)
    turned = cluster.T

    def swap(value, bit):
        return lax.ppermute(value, "ap", [(i, i ^ (1 << bit)) for i in range(devices)])

    slots = devices // 2
    sent = local_products(1, bits, visible, turned, channel, precoder)
    got = swap(sent, 0)
    kept = local_products(0, bits, visible, turned, channel, precoder)
    held = [
        ((kept, 0, slots), (kept, slots, slots)),
        ((got, 0, slots), (got, slots, slots)),
    ]
    for step in range(1, bits):
        slots //= 2
        if orders[0][step] == orders[1][step]:
            sent = summed(held, (0, 1), slots, tiles, True)
            got = swap(sent, orders[0][step])
            held.append(((got, 0, slots), (got, slots, slots)))
        else:
            sent = [summed(held, (half,), slots, tiles, half == 0) for half in range(2)]
            got = [swap(sent[half], orders[half][step]) for half in range(2)]
            held.append(((got[0], 0, slots), (got[1], 0, slots)))
    return finish(held, tiles, users, columns)


def solution(mesh):
    in_specs = (
        P(("parts", "ap"), None, None, None, None),
        P(None, ("parts", "ap"), None),
        P(("parts", "ap"), None),
        P("parts", None),
    )
    out_specs = P(("parts", "ap"), None, None)
    return jax.shard_map(
        on_device, mesh=mesh, in_specs=in_specs, out_specs=out_specs, check_vma=False
    )
```

time: 121 us -> 35.6 us (0.29)
  waiting for transfers between devices: 59 us -> 14.2 us
  blocking collectives: 34.9 us -> 0 us
  between operations: 13.5 us -> 0.08 us
  starting transfers between devices: 0.01 us -> 11.1 us
  Pallas kernels: 0 us -> 4.96 us
  other arithmetic: 3.82 us -> 0 us
  matrix products: 2.32 us -> 0 us
  local copies, waits for them, and re-layouts: 6.76 us -> 4.99 us
    reduce_scatter x1 -> x0, waiting for transfers between devices: 59 us -> none  [on_device(): result = lax.psum_scatter(flat, 'ap', scatter_dimension=0, tiled=True)]
    psum x1 -> x0, blocking collectives: 34.9 us -> none  [on_device(): power = lax.psum(local_power, 'ap')]
    ppermute x0 -> x6, waiting for transfers between devices: none -> 14.2 us  [swap(): lax.ppermute(value, 'ap', [(i, i ^ 1 << bit) for i in range(devices)])]
    ppermute x0 -> x6, starting transfers between devices: none -> 11.1 us  [swap(): lax.ppermute(value, 'ap', [(i, i ^ 1 << bit) for i in range(devices)])]
    pallas_call x0 -> x8, Pallas kernels: none -> 4.96 us  [the longest x2 2.88 us: local_products(): pl.pallas_call(functools.partial(local_kernel, which, bits), out_shape=ja...]
    unnamed x6 -> x22, local copies, waits for them, and re-layouts: 2.35 us -> 4.99 us
    scatter x1 -> x0, local copies, waits for them, and re-layouts: 2.43 us -> none  [place_slots(): return empty.at[groups].set(partial_value)]
    dot_general x2 -> x0, matrix products: 2.32 us -> none  [the longest x1 1.74 us: on_device(): jnp.einsum('vua,ar->vur', chan_imag, second, preferred_element_type=jnp.f...]
  transfers between devices with their start and end apart: 1 -> 6, of which waited for: 1 -> 4; matrix products, arithmetic and copies ran while one was open for 0% -> 0% of each run, Pallas kernels for 0% -> 4%
where the time goes in v1:
time: 35.6 us; the launch traced here: 35.3 us
  waiting for transfers between devices  14.2 us (40%)
  starting transfers between devices  11.1 us (31%)
  local copies, waits for them, and re-layouts  4.99 us (14%)
  Pallas kernels  4.96 us (14%)
    ppermute x6, waiting for transfers between devices, swap(): lax.ppermute(value, 'ap', [(i, i ^ 1 << bit) for i in range(devices)])  14.2 us
    ppermute x6, starting transfers between devices, swap(): lax.ppermute(value, 'ap', [(i, i ^ 1 << bit) for i in range(devices)])  11.1 us
    unnamed x22, local copies, waits for them, and re-layouts  4.99 us
    pallas_call x2, Pallas kernels, local_products(): pl.pallas_call(functools.partial(local_kernel, which, bits), out_shape=ja...  2.88 us
    pallas_call x1, Pallas kernels, finish(): pl.pallas_call(functools.partial(final_kernel, len(held), users), grid=(1...  1.89 us
  transfers between devices with their start and end apart: 6, of which 4 were waited for; matrix products, arithmetic and copies ran while one was open for 0% of the time, Pallas kernels for 4%

profile of v1, /device:TPU:0, one launch (start us, length us, event | category | flops | bytes accessed | tf_op | source)
XLA Modules:
  0.0 35.3 jit_solution(14935099516675838859)
XLA Ops:
  0.0 0.0 copy-start.3
  0.0 1.2 %copy-done.3 = bf16[2,512,512]{2,1,0:T(8,128)(2,1)S(1)} copy-done((bf16[2,512,512]{2,1,0:T(8,128)(2,1)S(1)}, bf16[2,512,512]{2,1,0:T(8,128)(2,1)}, u32[]{:S(2)}) %copy-start.3) | copy-done | bytes 1048600
  1.2 0.0 copy-start.4
  1.2 1.1 %copy-done.4 = bf16[1,12,2,32,512]{4,3,2,1,0:T(8,128)(2,1)S(1)} copy-done((bf16[1,12,2,32,512]{4,3,2,1,0:T(8,128)(2,1)S(1)}, bf16[1,12,2,32,512]{4,3,2,1,0:T(8,128)(2,1)}, u32[]{:S(2)}) %copy-start.4) | copy-done | bytes 786456
  2.4 0.0 copy-start.8
  2.4 0.7 %copy-done.8 = s32[512,4]{0,1:T(4,128)S(1)} copy-done((s32[512,4]{0,1:T(4,128)S(1)}, s32[512,4]{0,1:T(4,128)}, u32[]{:S(2)}) %copy-start.8) | copy-done | bytes 8216
  3.1 0.0 copy-start.9
  3.1 0.7 %copy-done.9 = s32[1,12]{1,0:T(1,128)S(1)} copy-done((s32[1,12]{1,0:T(1,128)S(1)}, s32[1,12]{1,0:T(1,128)}, u32[]{:S(2)}) %copy-start.9) | copy-done | bytes 72
  3.7 1.4 %local_products.3 = f32[257,8,128]{2,1,0:T(8,128)S(1)} custom-call(s32[1,12]{1,0:T(1,128)S(1)} %copy-done.9, s32[4,512]{1,0:T(4,128)S(1)} %bitcast.1, bf16[1,12,2,32,512]{4,3,2,1,0:T(8,128)(2,1)S(1)} %copy-done.4, bf16[2,512,512]{2,1,0:T(8,128)(2,1)S(1)} %copy-done.3), custom_call_target="tpu_custom_call" | custom-call | flops 536870912 | bytes 2883584 | tf_op jit(solution)/shard_map/local_products/pallas_call | solution.py:101
  5.2 0.5 %collective-permute-start = (f32[257,8,128]{2,1,0:T(8,128)S(1)}, f32[257,8,128]{2,1,0:T(8,128)S(1)}, u32[]{:S(2)}, u32[]{:S(2)}) collective-permute-start(f32[257,8,128]{2,1,0:T(8,128)S(1)} %local_products.3), channel_id=1, source_target_pairs={{0,1},{1,0},{2,3},{3,2},{4,5},{5,4},{6,7},{7,6},{8,9},{9,8},{10,11... | collective-permute-start | bytes 3158024 | tf_op jit(solution)/shard_map/ppermute | solution.py:210
  5.7 1.4 %local_products.2.refs_0_.refs_2_.refs_3_.refs_4_.refs_8_.refs_5_.refs_10_ = f32[257,8,128]{2,1,0:T(8,128)S(1)} custom-call(s32[1,12]{1,0:T(1,128)S(1)} %copy-done.9, s32[4,512]{1,0:T(4,128)S(1)} %bitcast.2, bf16[1,12,2,32,512]{4,3,2,1,0:T(8,128)(2,1)S(1)} %copy-done.4, bf16[2,512,512]{2,1,0:T(8,128)(2,1)S(1)} %copy-done.3), custom_call_target="tpu_custom_call" | custom-call | flops 536870912 | bytes 2883584 | tf_op jit(solution)/shard_map/local_products/pallas_call | solution.py:101
  7.1 0.0 copy-start
  7.1 0.8 %collective-permute-done.refs_1_.refs_3_.refs_4_.refs_5_.refs_9_.refs_6_.refs_11_ = f32[257,8,128]{2,1,0:T(8,128)S(1)} collective-permute-done((f32[257,8,128]{2,1,0:T(8,128)S(1)}, f32[257,8,128]{2,1,0:T(8,128)S(1)}, u32[]{:S(2)}, u32[]{:S(2)}) %collective-permute-start) | collective-permute-done | bytes 1052704 | tf_op jit(solution)/shard_map/ppermute | solution.py:210
  8.0 0.0 copy-start.1
  8.0 2.9 %collective-permute-start.1 = (f32[65,8,128]{2,1,0:T(8,128)S(1)}, f32[65,8,128]{2,1,0:T(8,128)S(1)}, u32[]{:S(2)}, u32[]{:S(2)}) collective-permute-start(f32[65,8,128]{2,1,0:T(8,128)S(1)} %summed.5), channel_id=1, source_target_pairs={{0,2},{1,3},{2,0},{3,1},{4,6},{5,7},{6,4},{7,5},{8,10},{9,11},{10,... | collective-permute-start | bytes 798728 | tf_op jit(solution)/shard_map/ppermute | solution.py:210
  11.0 1.6 %collective-permute-start.3 = (f32[64,8,128]{2,1,0:T(8,128)S(1)}, f32[64,8,128]{2,1,0:T(8,128)S(1)}, u32[]{:S(2)}, u32[]{:S(2)}) collective-permute-start(f32[64,8,128]{2,1,0:T(8,128)S(1)} %summed.7), channel_id=1, source_target_pairs={{0,4},{1,5},{2,6},{3,7},{4,0},{5,1},{6,2},{7,3},{8,12},{9,13},{10,... | collective-permute-start | bytes 786440 | tf_op jit(solution)/shard_map/ppermute | solution.py:210
  12.6 5.0 %collective-permute-done.1.refs_2_.refs_5_.refs_10_.refs_12_ = f32[65,8,128]{2,1,0:T(8,128)S(1)} collective-permute-done((f32[65,8,128]{2,1,0:T(8,128)S(1)}, f32[65,8,128]{2,1,0:T(8,128)S(1)}, u32[]{:S(2)}, u32[]{:S(2)}) %collective-permute-start.1) | collective-permute-done | bytes 266272 | tf_op jit(solution)/shard_map/ppermute | solution.py:210
  17.6 0.0 copy-start.2
  17.7 1.9 %collective-permute-start.2 = (f32[33,8,128]{2,1,0:T(8,128)S(1)}, f32[33,8,128]{2,1,0:T(8,128)S(1)}, u32[]{:S(2)}, u32[]{:S(2)}) collective-permute-start(f32[33,8,128]{2,1,0:T(8,128)S(1)} %summed.6), channel_id=1, source_target_pairs={{0,4},{1,5},{2,6},{3,7},{4,0},{5,1},{6,2},{7,3},{8,12},{9,13},{10,... | collective-permute-start | bytes 405512 | tf_op jit(solution)/shard_map/ppermute | solution.py:210
  19.6 0.0 collective-permute-done.3.refs_2_.refs_6_.refs_7_
  19.6 0.0 copy-start.5
  19.6 1.6 %collective-permute-start.4 = (f32[32,8,128]{2,1,0:T(8,128)S(1)}, f32[32,8,128]{2,1,0:T(8,128)S(1)}, u32[]{:S(2)}, u32[]{:S(2)}) collective-permute-start(f32[32,8,128]{2,1,0:T(8,128)S(1)} %summed.8), channel_id=1, source_target_pairs={{0,2},{1,3},{2,0},{3,1},{4,6},{5,7},{6,4},{7,5},{8,10},{9,11},{10,... | collective-permute-start | bytes 393224 | tf_op jit(solution)/shard_map/ppermute | solution.py:210
  21.1 3.5 %collective-permute-done.4.refs_7_.refs_8_ = f32[32,8,128]{2,1,0:T(8,128)S(1)} collective-permute-done((f32[32,8,128]{2,1,0:T(8,128)S(1)}, f32[32,8,128]{2,1,0:T(8,128)S(1)}, u32[]{:S(2)}, u32[]{:S(2)}) %collective-permute-start.4) | collective-permute-done | bytes 131104 | tf_op jit(solution)/shard_map/ppermute | solution.py:210
  24.6 0.0 copy-start.7
  24.6 0.0 collective-permute-done.2.refs_3_.refs_11_.refs_13_
  24.6 0.0 copy-done
  24.6 0.0 copy-done.1
  24.6 0.0 copy-done.2
  24.7 0.0 copy-done.5
  24.7 0.0 copy-start.6
  24.7 0.1 summed.9
  24.7 0.5 %copy-done.7 = f32[32,8,128]{2,1,0:T(8,128)} copy-done((f32[32,8,128]{2,1,0:T(8,128)}, f32[32,8,128]{2,1,0:T(8,128)S(1)}, u32[]{:S(2)}) %copy-start.7) | copy-done | bytes 131096
  25.3 0.1 copy-done.6
  25.3 2.6 %collective-permute-start.5 = (f32[33,8,128]{2,1,0:T(8,128)S(1)}, f32[33,8,128]{2,1,0:T(8,128)S(1)}, u32[]{:S(2)}, u32[]{:S(2)}) collective-permute-start(f32[33,8,128]{2,1,0:T(8,128)S(1)} %summed.9), channel_id=1, source_target_pairs={{0,8},{1,9},{2,10},{3,11},{4,12},{5,13},{6,14},{7,15},{8,0},{9,1},... | collective-permute-start | bytes 405512 | tf_op jit(solution)/shard_map/ppermute | solution.py:210
  27.9 4.9 %collective-permute-done.5.refs_4_.refs_9_.refs_14_ = f32[33,8,128]{2,1,0:T(8,128)S(1)} collective-permute-done((f32[33,8,128]{2,1,0:T(8,128)S(1)}, f32[33,8,128]{2,1,0:T(8,128)S(1)}, u32[]{:S(2)}, u32[]{:S(2)}) %collective-permute-start.5) | collective-permute-done | bytes 135200 | tf_op jit(solution)/shard_map/ppermute | solution.py:210
  32.8 0.0 copy-start.10
  32.8 0.7 %copy-done.10 = f32[33,8,128]{2,1,0:T(8,128)} copy-done((f32[33,8,128]{2,1,0:T(8,128)}, f32[33,8,128]{2,1,0:T(8,128)S(1)}, u32[]{:S(2)}) %copy-start.10) | copy-done | bytes 135192
  33.5 1.9 %finish.1 = f32[32,2,512]{2,1,0:T(2,128)} custom-call(f32[257,8,128]{2,1,0:T(8,128)} %copy-done, f32[257,8,128]{2,1,0:T(8,128)} %copy-done.1, f32[65,8,128]{2,1,0:T(8,128)} %copy-done.2, f32[33,8,128]{2,1,0:T(8,128)} %copy-done.6, f32[33,8,128]{2,1,0:T(8,128)} %copy-done.10, f32[257,8,128]{2,1,0:T(8,128)} %copy-done, f32[257,8,128]{2,1,0:T(8,128)} %copy-done.1, ...), custom_call_target="tpu_custom_call" | custom-call | tf_op jit(solution)/shard_map/finish/pallas_call | solution.py:191
  (4 shorter events, 0.1 us)
Async XLA Ops:
  0.0 1.2 %copy-start.3 = (bf16[2,512,512]{2,1,0:T(8,128)(2,1)S(1)}, bf16[2,512,512]{2,1,0:T(8,128)(2,1)}, u32[]{:S(2)}) copy-start(bf16[2,512,512]{2,1,0:T(8,128)(2,1)} %precoder.3) | copy-start | bytes 3145732
  1.2 1.1 %copy-start.4 = (bf16[1,12,2,32,512]{4,3,2,1,0:T(8,128)(2,1)S(1)}, bf16[1,12,2,32,512]{4,3,2,1,0:T(8,128)(2,1)}, u32[]{:S(2)}) copy-start(bf16[1,12,2,32,512]{4,3,2,1,0:T(8,128)(2,1)} %channel.3) | copy-start | bytes 2359300
  2.4 0.7 %copy-start.8 = (s32[512,4]{0,1:T(4,128)S(1)}, s32[512,4]{0,1:T(4,128)}, u32[]{:S(2)}) copy-start(s32[512,4]{0,1:T(4,128)} %param.7) | copy-start | bytes 24580
  3.1 0.7 %copy-start.9 = (s32[1,12]{1,0:T(1,128)S(1)}, s32[1,12]{1,0:T(1,128)}, u32[]{:S(2)}) copy-start(s32[1,12]{1,0:T(1,128)} %visible.3) | copy-start | bytes 148
  5.2 2.8 %collective-permute-start = (f32[257,8,128]{2,1,0:T(8,128)S(1)}, f32[257,8,128]{2,1,0:T(8,128)S(1)}, u32[]{:S(2)}, u32[]{:S(2)}) collective-permute-start(f32[257,8,128]{2,1,0:T(8,128)S(1)} %local_products.3), channel_id=1, source_target_pairs={{0,1},{1,0},{2,3},{3,2},{4,5},{5,4},{6,7},{7,6},{8,9},{9,8},{10,11... | collective-permute-start | bytes 3158024 | tf_op jit(solution)/shard_map/ppermute | solution.py:210
  7.1 17.5 %copy-start = (f32[257,8,128]{2,1,0:T(8,128)}, f32[257,8,128]{2,1,0:T(8,128)S(1)}, u32[]{:S(2)}) copy-start(f32[257,8,128]{2,1,0:T(8,128)S(1)} %local_products.2.refs_0_.refs_2_.refs_3_.refs_4_.refs_8_.refs_5_.refs_10_) | copy-start | bytes 3158020
  8.0 16.7 %copy-start.1 = (f32[257,8,128]{2,1,0:T(8,128)}, f32[257,8,128]{2,1,0:T(8,128)S(1)}, u32[]{:S(2)}) copy-start(f32[257,8,128]{2,1,0:T(8,128)S(1)} %collective-permute-done.refs_1_.refs_3_.refs_4_.refs_5_.refs_9_.refs_6_.refs_11_) | copy-start | bytes 3158020
  8.0 9.6 %collective-permute-start.1 = (f32[65,8,128]{2,1,0:T(8,128)S(1)}, f32[65,8,128]{2,1,0:T(8,128)S(1)}, u32[]{:S(2)}, u32[]{:S(2)}) collective-permute-start(f32[65,8,128]{2,1,0:T(8,128)S(1)} %summed.5), channel_id=1, source_target_pairs={{0,2},{1,3},{2,0},{3,1},{4,6},{5,7},{6,4},{7,5},{8,10},{9,11},{10,... | collective-permute-start | bytes 798728 | tf_op jit(solution)/shard_map/ppermute | solution.py:210
  11.0 8.6 %collective-permute-start.3 = (f32[64,8,128]{2,1,0:T(8,128)S(1)}, f32[64,8,128]{2,1,0:T(8,128)S(1)}, u32[]{:S(2)}, u32[]{:S(2)}) collective-permute-start(f32[64,8,128]{2,1,0:T(8,128)S(1)} %summed.7), channel_id=1, source_target_pairs={{0,4},{1,5},{2,6},{3,7},{4,0},{5,1},{6,2},{7,3},{8,12},{9,13},{10,... | collective-permute-start | bytes 786440 | tf_op jit(solution)/shard_map/ppermute | solution.py:210
  17.6 7.0 %copy-start.2 = (f32[65,8,128]{2,1,0:T(8,128)}, f32[65,8,128]{2,1,0:T(8,128)S(1)}, u32[]{:S(2)}) copy-start(f32[65,8,128]{2,1,0:T(8,128)S(1)} %collective-permute-done.1.refs_2_.refs_5_.refs_10_.refs_12_) | copy-start | bytes 798724
  17.7 7.0 %collective-permute-start.2 = (f32[33,8,128]{2,1,0:T(8,128)S(1)}, f32[33,8,128]{2,1,0:T(8,128)S(1)}, u32[]{:S(2)}, u32[]{:S(2)}) collective-permute-start(f32[33,8,128]{2,1,0:T(8,128)S(1)} %summed.6), channel_id=1, source_target_pairs={{0,4},{1,5},{2,6},{3,7},{4,0},{5,1},{6,2},{7,3},{8,12},{9,13},{10,... | collective-permute-start | bytes 405512 | tf_op jit(solution)/shard_map/ppermute | solution.py:210
  19.6 5.1 %copy-start.5 = (f32[64,8,128]{2,1,0:T(8,128)}, f32[64,8,128]{2,1,0:T(8,128)S(1)}, u32[]{:S(2)}) copy-start(f32[64,8,128]{2,1,0:T(8,128)S(1)} %collective-permute-done.3.refs_2_.refs_6_.refs_7_) | copy-start | bytes 786436
  19.6 5.0 %collective-permute-start.4 = (f32[32,8,128]{2,1,0:T(8,128)S(1)}, f32[32,8,128]{2,1,0:T(8,128)S(1)}, u32[]{:S(2)}, u32[]{:S(2)}) collective-permute-start(f32[32,8,128]{2,1,0:T(8,128)S(1)} %summed.8), channel_id=1, source_target_pairs={{0,2},{1,3},{2,0},{3,1},{4,6},{5,7},{6,4},{7,5},{8,10},{9,11},{10,... | collective-permute-start | bytes 393224 | tf_op jit(solution)/shard_map/ppermute | solution.py:210
  24.6 0.7 %copy-start.7 = (f32[32,8,128]{2,1,0:T(8,128)}, f32[32,8,128]{2,1,0:T(8,128)S(1)}, u32[]{:S(2)}) copy-start(f32[32,8,128]{2,1,0:T(8,128)S(1)} %collective-permute-done.4.refs_7_.refs_8_) | copy-start | bytes 393220
  24.7 0.7 %copy-start.6 = (f32[33,8,128]{2,1,0:T(8,128)}, f32[33,8,128]{2,1,0:T(8,128)S(1)}, u32[]{:S(2)}) copy-start(f32[33,8,128]{2,1,0:T(8,128)S(1)} %collective-permute-done.2.refs_3_.refs_11_.refs_13_) | copy-start | bytes 405508
  25.3 7.5 %collective-permute-start.5 = (f32[33,8,128]{2,1,0:T(8,128)S(1)}, f32[33,8,128]{2,1,0:T(8,128)S(1)}, u32[]{:S(2)}, u32[]{:S(2)}) collective-permute-start(f32[33,8,128]{2,1,0:T(8,128)S(1)} %summed.9), channel_id=1, source_target_pairs={{0,8},{1,9},{2,10},{3,11},{4,12},{5,13},{6,14},{7,15},{8,0},{9,1},... | collective-permute-start | bytes 405512 | tf_op jit(solution)/shard_map/ppermute | solution.py:210
  32.8 0.7 %copy-start.10 = (f32[33,8,128]{2,1,0:T(8,128)}, f32[33,8,128]{2,1,0:T(8,128)S(1)}, u32[]{:S(2)}) copy-start(f32[33,8,128]{2,1,0:T(8,128)S(1)} %collective-permute-done.5.refs_4_.refs_9_.refs_14_) | copy-start | bytes 405508

commit v2 on v1

v2 whole, which is shorter than its diff:
```python
import functools

import jax
import jax.numpy as jnp
from jax import lax
from jax.experimental import pallas as pl
from jax.experimental.pallas import tpu as pltpu
from jax.sharding import PartitionSpec as P

epsilon = 1e-06
MIB = 1 << 20
CHUNKS = 2


def bit_orders(bits):
    first = list(range(bits))
    second = list(first)
    if bits > 2:
        second[1], second[2] = second[2], second[1]
    return first, second


def second_place(place, bits):
    first, second = bit_orders(bits)
    tail = bits - 1
    value = {bit: (place >> (tail - 1 - at)) & 1 for at, bit in enumerate(first[1:])}
    out = 0
    for bit in second[1:]:
        out = out * 2 + value[bit]
    return out


def write_products(bits, slots, rows, weights, served, out):
    users = rows.shape[0] // slots
    antennas = rows.shape[1] // 2
    width = weights.shape[1]
    blocks, steps = width // 128, users // 8
    tiles = blocks * steps
    group = min(slots, 8)
    for base in range(0, slots, group):
        plain = rows[base * users:(base + group) * users, :]
        turned = jnp.concatenate([-plain[:, antennas:], plain[:, :antennas]], axis=1)
        both = jnp.concatenate([plain, turned], axis=0)
        value = jnp.dot(both, weights, preferred_element_type=jnp.float32)
        value = jnp.where(served, value, 0.0)
        for half in range(2):
            for slot in range(group):
                place = base + slot
                if half == 1:
                    place = slots + second_place(place, bits)
                top = (half * group + slot) * users
                for block in range(blocks):
                    piece = value[top:top + users, block * 128:(block + 1) * 128]
                    start = place * tiles + block * steps
                    out[start:start + steps] = piece.reshape(steps, 8, 128)


def power_tile(weights, served):
    wide = weights.astype(jnp.float32)
    power = jnp.sum(wide * wide, axis=0, keepdims=True)
    power = jnp.where(served, power, 0.0)
    blocks = power.shape[1] // 128
    pieces = [power[:, block * 128:(block + 1) * 128] for block in range(blocks)]
    return jnp.concatenate(pieces + [jnp.zeros((8 - blocks, 128), jnp.float32)], axis=0)


def first_kernel(
    bits, visible, cluster, channel, precoder,
    out, rows, weights, served,
    seen, names, raw, sems,
):
    me = lax.axis_index("ap")
    held, users, antennas = raw.shape[1], raw.shape[3], raw.shape[4]
    columns = weights.shape[1]
    width = columns // CHUNKS
    slots = rows.shape[1] // users
    first, _ = bit_orders(bits)
    loads = [
        pltpu.make_async_copy(visible, seen, sems.at[0]),
        pltpu.make_async_copy(cluster, names, sems.at[1]),
        pltpu.make_async_copy(channel, raw, sems.at[2]),
    ]
    for chunk in range(CHUNKS):
        at = pl.ds(chunk * width, width)
        loads.append(
            pltpu.make_async_copy(precoder.at[:, at], weights.at[:, at], sems.at[3 + chunk])
        )
    for load in loads:
        load.start()
    rows[...] = jnp.zeros_like(rows)
    loads[0].wait()
    loads[1].wait()
    mask = jnp.max((names[...] == me).astype(jnp.float32), axis=0, keepdims=True)
    served[...] = mask
    loads[2].wait()
    for v in range(held):
        relative = seen[0, v] ^ me
        place = 0
        for bit in first[1:]:
            place = place * 2 + (1 - ((relative >> bit) & 1))
        which = 1 - (relative & 1)
        at = pl.ds(pl.multiple_of(place * users, users), users)
        rows[which, at, 0:antennas] = raw[0, v, 0]
        rows[which, at, antennas:2 * antennas] = raw[0, v, 1]
    loads[3].wait()
    mine = mask[:, 0:width] > 0.0
    chosen = weights[:, 0:width]
    write_products(bits, slots, rows.at[0], chosen, mine, out)
    out[out.shape[0] - 1] = power_tile(chosen, mine)
    for load in loads[4:]:
        load.wait()


def next_kernel(bits, which, chunk, rows, weights, served, out):
    width = weights.shape[1] // CHUNKS
    at = slice(chunk * width, (chunk + 1) * width)
    mine = served[:, at] > 0.0
    chosen = weights[:, at]
    slots = 1 << (bits - 1)
    write_products(bits, slots, rows.at[which], chosen, mine, out)
    out[out.shape[0] - 1] = power_tile(chosen, mine)


def message(tiles):
    return jax.ShapeDtypeStruct((tiles, 8, 128), jnp.float32)


def estimate(slots, users, antennas, columns):
    return pl.CostEstimate(
        flops=8 * slots * users * antennas * columns,
        bytes_accessed=slots * users * (antennas * 4 + columns * 8) + antennas * columns * 4,
        transcendentals=0,
    )


def first_products(bits, visible, cluster, channel, precoder):
    held, users, antennas = channel.shape[1], channel.shape[3], channel.shape[4]
    columns = precoder.shape[1]
    slots = 1 << (bits - 1)
    tiles = (users // 8) * (columns // CHUNKS // 128)
    hbm = pl.BlockSpec(memory_space=pltpu.HBM)
    vmem = pl.BlockSpec(memory_space=pltpu.VMEM)
    return pl.pallas_call(
        functools.partial(first_kernel, bits),
        out_shape=(
            message(2 * slots * tiles + 1),
            jax.ShapeDtypeStruct((2, slots * users, 2 * antennas), jnp.bfloat16),
            jax.ShapeDtypeStruct(precoder.shape, jnp.bfloat16),
            jax.ShapeDtypeStruct((1, columns), jnp.float32),
        ),
        in_specs=[hbm] * 4,
        out_specs=(vmem,) * 4,
        scratch_shapes=[
            pltpu.SMEM(visible.shape, jnp.int32),
            pltpu.VMEM(cluster.shape, jnp.int32),
            pltpu.VMEM(channel.shape, jnp.bfloat16),
            pltpu.SemaphoreType.DMA((3 + CHUNKS,)),
        ],
        compiler_params=pltpu.CompilerParams(vmem_limit_bytes=48 * MIB if slots > 8 else 24 * MIB),
        cost_estimate=estimate(slots, users, antennas, columns // CHUNKS),
        name="first_products",
    )(*[pltpu.with_memory_space_constraint(a, pltpu.HBM) for a in (visible, cluster, channel, precoder)])


def next_products(bits, which, chunk, rows, weights, served, users):
    slots = 1 << (bits - 1)
    antennas, columns = weights.shape[0] // 2, weights.shape[1]
    tiles = (users // 8) * (columns // CHUNKS // 128)
    vmem = pl.BlockSpec(memory_space=pltpu.VMEM)
    return pl.pallas_call(
        functools.partial(next_kernel, bits, which, chunk),
        out_shape=message(2 * slots * tiles + 1),
        in_specs=[vmem] * 3,
        out_specs=vmem,
        compiler_params=pltpu.CompilerParams(vmem_limit_bytes=48 * MIB if slots > 8 else 16 * MIB),
        cost_estimate=estimate(slots, users, antennas, columns // CHUNKS),
        name="next_products",
    )(rows, weights, served)


def part_spec(start, count):
    return pl.BlockSpec((count, 8, 128), lambda i: (start // count, 0, 0))


def sum_kernel(halves, terms, with_power, count, *refs):
    out = refs[-1]
    at = 0
    for half in range(halves):
        total = refs[at][...]
        for term in range(1, terms):
            total = total + refs[at + term][...]
        at += terms
        out[half * count:(half + 1) * count] = total
    if with_power:
        total = refs[at][...]
        for term in range(1, terms):
            total = total + refs[at + term][...]
        out[halves * count:] = total


def summed(held, halves, left, tiles, with_power):
    count = left * tiles
    arrays, specs = [], []
    for half in halves:
        for pieces in held:
            array, base, slots = pieces[half]
            arrays.append(array)
            specs.append(part_spec((base + slots - 2 * left) * tiles, count))
    if with_power:
        for pieces in held:
            array = pieces[0][0]
            arrays.append(array)
            specs.append(part_spec(array.shape[0] - 1, 1))
    size = len(halves) * count + int(with_power)
    return pl.pallas_call(
        functools.partial(sum_kernel, len(halves), len(held), with_power, count),
        grid=(1,),
        out_shape=message(size),
        in_specs=specs,
        out_specs=pl.BlockSpec((size, 8, 128), lambda i: (0, 0, 0)),
        compiler_params=pltpu.CompilerParams(vmem_limit_bytes=48 * MIB if left > 4 else 8 * MIB),
        cost_estimate=pl.CostEstimate(
            flops=size * 1024 * len(held), bytes_accessed=size * 4096 * (len(held) + 1), transcendentals=0
        ),
        name="summed",
    )(*arrays)


def final_kernel(terms, users, *refs):
    out = refs[-1]
    blocks = out.shape[2] // 128 // CHUNKS
    steps = users // 8
    for chunk in range(CHUNKS):
        mine = refs[chunk * 3 * terms:(chunk + 1) * 3 * terms]
        power = mine[2 * terms][0]
        for term in range(1, terms):
            power = power + mine[2 * terms + term][0]
        scale = lax.rsqrt(power + epsilon)
        for half in range(2):
            for block in range(blocks):
                at = slice(block * steps, (block + 1) * steps)
                total = mine[half * terms][at]
                for term in range(1, terms):
                    total = total + mine[half * terms + term][at]
                factor = scale[block:block + 1, :]
                total = total.reshape(users, 128)
                value = jnp.where(factor > 0.0, total * factor, 0.0)
                left = (chunk * blocks + block) * 128
                out[:, half, left:left + 128] = value


def finish(helds, tiles, users, columns):
    arrays, specs = [], []
    for held in helds:
        for half in range(2):
            for pieces in held:
                array, base, slots = pieces[half]
                arrays.append(array)
                specs.append(part_spec((base + slots - 1) * tiles, tiles))
        for pieces in held:
            array = pieces[0][0]
            arrays.append(array)
            specs.append(part_spec(array.shape[0] - 1, 1))
    return pl.pallas_call(
        functools.partial(final_kernel, len(helds[0]), users),
        grid=(1,),
        out_shape=jax.ShapeDtypeStruct((users, 2, columns), jnp.float32),
        in_specs=specs,
        out_specs=pl.BlockSpec((users, 2, columns), lambda i: (0, 0, 0)),
        compiler_params=pltpu.CompilerParams(vmem_limit_bytes=8 * MIB),
        name="finish",
    )(*arrays)


def on_device(channel, precoder, visible, cluster):
    devices = lax.axis_size("ap")
    bits = devices.bit_length() - 1
    users, columns = channel.shape[3], precoder.shape[2]
    tiles = (users // 8) * (columns // CHUNKS // 128)
    orders = bit_orders(bits)
    flat = precoder.reshape(-1, columns)

    def swap(value, bit):
        return lax.ppermute(value, "ap", [(i, i ^ (1 << bit)) for i in range(devices)])

    slots = devices // 2
    sent, rows, weights, served = first_products(bits, visible, cluster.T, channel, flat)
    got = [swap(sent, 0)]
    for chunk in range(1, CHUNKS):
        got.append(swap(next_products(bits, 0, chunk, rows, weights, served, users), 0))
    helds = []
    for chunk in range(CHUNKS):
        kept = next_products(bits, 1, chunk, rows, weights, served, users)
        helds.append([
            ((kept, 0, slots), (kept, slots, slots)),
            ((got[chunk], 0, slots), (got[chunk], slots, slots)),
        ])
    for step in range(1, bits):
        slots //= 2
        for held in helds:
            if orders[0][step] == orders[1][step]:
                sent = summed(held, (0, 1), slots, tiles, True)
                got = swap(sent, orders[0][step])
                held.append(((got, 0, slots), (got, slots, slots)))
            else:
                sent = [summed(held, (half,), slots, tiles, half == 0) for half in range(2)]
                got = [swap(sent[half], orders[half][step]) for half in range(2)]
                held.append(((got[0], 0, slots), (got[1], 0, slots)))
    return finish(helds, tiles, users, columns)


def solution(mesh):
    in_specs = (
        P(("parts", "ap"), None, None, None, None),
        P(None, ("parts", "ap"), None),
        P(("parts", "ap"), None),
        P("parts", None),
    )
    out_specs = P(("parts", "ap"), None, None)
    return jax.shard_map(
        on_device, mesh=mesh, in_specs=in_specs, out_specs=out_specs, check_vma=False
    )
```

time: 35.6 us -> 29.9 us (0.84)
  starting transfers between devices: 11.1 us -> 17.4 us
  waiting for transfers between devices: 14.2 us -> 8.22 us
  local copies, waits for them, and re-layouts: 4.99 us -> 0 us
  Pallas kernels: 4.96 us -> 4.07 us
    ppermute x6 -> x12, starting transfers between devices: 11.1 us -> 17.4 us  [swap(): lax.ppermute(value, 'ap', [(i, i ^ 1 << bit) for i in range(devices)])]
    ppermute x6 -> x12, waiting for transfers between devices: 14.2 us -> 8.22 us  [swap(): lax.ppermute(value, 'ap', [(i, i ^ 1 << bit) for i in range(devices)])]
    unnamed x22 -> x0, local copies, waits for them, and re-layouts: 4.99 us -> none
    pallas_call x3 -> x5, Pallas kernels: 4.77 us -> 3.89 us  [the longest x1 1.79 us: first_products(): pl.pallas_call(functools.partial(first_kernel, bits), out_shape=(message(...]
  transfers between devices with their start and end apart: 6 -> 12, of which waited for: 4 -> 6; matrix products, arithmetic and copies ran while one was open for 0% -> 0% of each run, Pallas kernels for 4% -> 4%
where the time goes in v2:
time: 29.9 us; the launch traced here: 29.8 us
  starting transfers between devices  17.4 us (58%)
  waiting for transfers between devices  8.22 us (27%)
  Pallas kernels  4.07 us (14%)
    ppermute x12, starting transfers between devices, swap(): lax.ppermute(value, 'ap', [(i, i ^ 1 << bit) for i in range(devices)])  17.4 us
    ppermute x12, waiting for transfers between devices, swap(): lax.ppermute(value, 'ap', [(i, i ^ 1 << bit) for i in range(devices)])  8.22 us
    pallas_call x1, Pallas kernels, first_products(): pl.pallas_call(functools.partial(first_kernel, bits), out_shape=(message(...  1.79 us
    pallas_call x3, Pallas kernels, next_products(): pl.pallas_call(functools.partial(next_kernel, bits, which, chunk), out_sh...  1.32 us
    pallas_call x1, Pallas kernels, finish(): pl.pallas_call(functools.partial(final_kernel, len(helds[0]), users), gri...  0.78 us
  transfers between devices with their start and end apart: 12, of which 6 were waited for; matrix products, arithmetic and copies ran while one was open for 0% of the time, Pallas kernels for 4%

profile of v2, /device:TPU:0, one launch (start us, length us, event | category | flops | bytes accessed | tf_op | source)
XLA Modules:
  0.0 29.8 jit_solution(1698333011487808470)
XLA Ops:
  0.0 1.8 %first_products.1 = (f32[129,8,128]{2,1,0:T(8,128)S(1)}, bf16[2,256,1024]{2,1,0:T(8,128)(2,1)S(1)}, bf16[1024,512]{1,0:T(8,128)(2,1)S(1)}, f32[1,512]{1,0:T(1,128)S(1)}) custom-call(s32[1,12]{1,0:T(1,128)} %visible.1, s32[4,512]{1,0:T(4,128)} %bitcast.3, bf16[1,12,2,32,512]{4,3,2,1,0:T(8,128)(2,1)} %channel.1, bf16[1024,512]{1,0:T(8,128)(2,1)} %bitcast.2), custom_call_target="tpu_custom_call" | custom-call | flops 268435456 | bytes 1572864 | tf_op jit(solution)/shard_map/first_products/pallas_call | solution.py:143
  1.8 0.4 %next_products.5 = f32[129,8,128]{2,1,0:T(8,128)S(1)} custom-call(bf16[2,256,1024]{2,1,0:T(8,128)(2,1)S(1)} %get-tuple-element.9.rows, bf16[1024,512]{1,0:T(8,128)(2,1)S(1)} %get-tuple-element.10.weights, f32[1,512]{1,0:T(1,128)S(1)} %get-tuple-element.11.served), custom_call_target="tpu_custom_call" | custom-call | flops 268435456 | bytes 1572864 | tf_op jit(solution)/shard_map/next_products/pallas_call | solution.py:170
  2.2 0.5 %collective-permute-start.6 = (f32[129,8,128]{2,1,0:T(8,128)S(1)}, f32[129,8,128]{2,1,0:T(8,128)S(1)}, u32[]{:S(2)}, u32[]{:S(2)}) collective-permute-start(f32[129,8,128]{2,1,0:T(8,128)S(1)} %next_products.5), channel_id=1, source_target_pairs={{0,1},{1,0},{2,3},{3,2},{4,5},{5,4},{6,7},{7,6},{8,9},{9,8},{10,11... | collective-permute-start | bytes 1585160 | tf_op jit(solution)/shard_map/ppermute | solution.py:284
  2.8 0.1 collective-permute-start
  2.8 0.4 %next_products.4.refs_0_.refs_2_.refs_3_.refs_4_.refs_8_.refs_15_.refs_20_.refs_25_ = f32[129,8,128]{2,1,0:T(8,128)S(1)} custom-call(bf16[2,256,1024]{2,1,0:T(8,128)(2,1)S(1)} %get-tuple-element.9.rows, bf16[1024,512]{1,0:T(8,128)(2,1)S(1)} %get-tuple-element.10.weights, f32[1,512]{1,0:T(1,128)S(1)} %get-tuple-element.11.served), custom_call_target="tpu_custom_call" | custom-call | flops 268435456 | bytes 1572864 | tf_op jit(solution)/shard_map/next_products/pallas_call | solution.py:170
  3.3 1.0 %collective-permute-done.6.refs_1_.refs_3_.refs_4_.refs_5_.refs_9_.refs_16_.refs_21_.refs_26_ = f32[129,8,128]{2,1,0:T(8,128)S(1)} collective-permute-done((f32[129,8,128]{2,1,0:T(8,128)S(1)}, f32[129,8,128]{2,1,0:T(8,128)S(1)}, u32[]{:S(2)}, u32[]{:S(2)}) %collective-permute-start.6) | collective-permute-done | bytes 528416 | tf_op jit(solution)/shard_map/ppermute | solution.py:284
  4.3 2.9 %collective-permute-start.7 = (f32[33,8,128]{2,1,0:T(8,128)S(1)}, f32[33,8,128]{2,1,0:T(8,128)S(1)}, u32[]{:S(2)}, u32[]{:S(2)}) collective-permute-start(f32[33,8,128]{2,1,0:T(8,128)S(1)} %summed.15), channel_id=1, source_target_pairs={{0,2},{1,3},{2,0},{3,1},{4,6},{5,7},{6,4},{7,5},{8,10},{9,11},{10,... | collective-permute-start | bytes 405512 | tf_op jit(solution)/shard_map/ppermute | solution.py:284
  7.3 0.4 %next_products.3.refs_0_.refs_2_.refs_3_.refs_4_.refs_8_.refs_5_.refs_10_ = f32[129,8,128]{2,1,0:T(8,128)S(1)} custom-call(bf16[2,256,1024]{2,1,0:T(8,128)(2,1)S(1)} %get-tuple-element.9.rows, bf16[1024,512]{1,0:T(8,128)(2,1)S(1)} %get-tuple-element.10.weights, f32[1,512]{1,0:T(1,128)S(1)} %get-tuple-element.11.served), custom_call_target="tpu_custom_call" | custom-call | flops 268435456 | bytes 1572864 | tf_op jit(solution)/shard_map/next_products/pallas_call | solution.py:170
  7.7 0.0 collective-permute-done.refs_1_.refs_3_.refs_4_.refs_5_.refs_9_.refs_6_.refs_11_
  7.7 0.3 collective-permute-start.1
  8.0 2.0 %collective-permute-start.9 = (f32[32,8,128]{2,1,0:T(8,128)S(1)}, f32[32,8,128]{2,1,0:T(8,128)S(1)}, u32[]{:S(2)}, u32[]{:S(2)}) collective-permute-start(f32[32,8,128]{2,1,0:T(8,128)S(1)} %summed.17), channel_id=1, source_target_pairs={{0,4},{1,5},{2,6},{3,7},{4,0},{5,1},{6,2},{7,3},{8,12},{9,13},{10,... | collective-permute-start | bytes 393224 | tf_op jit(solution)/shard_map/ppermute | solution.py:284
  10.0 0.2 collective-permute-start.3
  10.2 1.4 %collective-permute-done.7.refs_2_.refs_5_.refs_10_.refs_17_.refs_27_ = f32[33,8,128]{2,1,0:T(8,128)S(1)} collective-permute-done((f32[33,8,128]{2,1,0:T(8,128)S(1)}, f32[33,8,128]{2,1,0:T(8,128)S(1)}, u32[]{:S(2)}, u32[]{:S(2)}) %collective-permute-start.7) | collective-permute-done | bytes 135200 | tf_op jit(solution)/shard_map/ppermute | solution.py:284
  11.6 2.2 %collective-permute-start.8 = (f32[17,8,128]{2,1,0:T(8,128)S(1)}, f32[17,8,128]{2,1,0:T(8,128)S(1)}, u32[]{:S(2)}, u32[]{:S(2)}) collective-permute-start(f32[17,8,128]{2,1,0:T(8,128)S(1)} %summed.16), channel_id=1, source_target_pairs={{0,4},{1,5},{2,6},{3,7},{4,0},{5,1},{6,2},{7,3},{8,12},{9,13},{10,... | collective-permute-start | bytes 208904 | tf_op jit(solution)/shard_map/ppermute | solution.py:284
  13.9 0.2 collective-permute-done.1.refs_2_.refs_5_.refs_10_.refs_12_
  14.1 1.9 %collective-permute-start.2 = (f32[17,8,128]{2,1,0:T(8,128)S(1)}, f32[17,8,128]{2,1,0:T(8,128)S(1)}, u32[]{:S(2)}, u32[]{:S(2)}) collective-permute-start(f32[17,8,128]{2,1,0:T(8,128)S(1)} %summed.11), channel_id=1, source_target_pairs={{0,4},{1,5},{2,6},{3,7},{4,0},{5,1},{6,2},{7,3},{8,12},{9,13},{10,... | collective-permute-start | bytes 208904 | tf_op jit(solution)/shard_map/ppermute | solution.py:284
  16.0 0.0 collective-permute-done.9.refs_2_.refs_6_.refs_22_
  16.0 1.6 %collective-permute-start.10 = (f32[16,8,128]{2,1,0:T(8,128)S(1)}, f32[16,8,128]{2,1,0:T(8,128)S(1)}, u32[]{:S(2)}, u32[]{:S(2)}) collective-permute-start(f32[16,8,128]{2,1,0:T(8,128)S(1)} %summed.18), channel_id=1, source_target_pairs={{0,2},{1,3},{2,0},{3,1},{4,6},{5,7},{6,4},{7,5},{8,10},{9,11},{10,... | collective-permute-start | bytes 196616 | tf_op jit(solution)/shard_map/ppermute | solution.py:284
  17.5 0.0 collective-permute-done.3.refs_2_.refs_6_.refs_7_
  17.5 1.6 %collective-permute-start.4 = (f32[16,8,128]{2,1,0:T(8,128)S(1)}, f32[16,8,128]{2,1,0:T(8,128)S(1)}, u32[]{:S(2)}, u32[]{:S(2)}) collective-permute-start(f32[16,8,128]{2,1,0:T(8,128)S(1)} %summed.13), channel_id=1, source_target_pairs={{0,2},{1,3},{2,0},{3,1},{4,6},{5,7},{6,4},{7,5},{8,10},{9,11},{10,... | collective-permute-start | bytes 196616 | tf_op jit(solution)/shard_map/ppermute | solution.py:284
  19.2 1.2 %collective-permute-done.10.refs_7_.refs_23_ = f32[16,8,128]{2,1,0:T(8,128)S(1)} collective-permute-done((f32[16,8,128]{2,1,0:T(8,128)S(1)}, f32[16,8,128]{2,1,0:T(8,128)S(1)}, u32[]{:S(2)}, u32[]{:S(2)}) %collective-permute-start.10) | collective-permute-done | bytes 65568 | tf_op jit(solution)/shard_map/ppermute | solution.py:284
  20.4 0.0 collective-permute-done.8.refs_3_.refs_11_.refs_18_.refs_28_
  20.4 2.7 %collective-permute-start.11 = (f32[17,8,128]{2,1,0:T(8,128)S(1)}, f32[17,8,128]{2,1,0:T(8,128)S(1)}, u32[]{:S(2)}, u32[]{:S(2)}) collective-permute-start(f32[17,8,128]{2,1,0:T(8,128)S(1)} %summed.19), channel_id=1, source_target_pairs={{0,8},{1,9},{2,10},{3,11},{4,12},{5,13},{6,14},{7,15},{8,0},{9,1},... | collective-permute-start | bytes 208904 | tf_op jit(solution)/shard_map/ppermute | solution.py:284
  23.0 0.0 collective-permute-done.4.refs_7_.refs_8_
  23.0 0.0 collective-permute-done.2.refs_3_.refs_11_.refs_13_
  23.1 1.5 %collective-permute-start.5 = (f32[17,8,128]{2,1,0:T(8,128)S(1)}, f32[17,8,128]{2,1,0:T(8,128)S(1)}, u32[]{:S(2)}, u32[]{:S(2)}) collective-permute-start(f32[17,8,128]{2,1,0:T(8,128)S(1)} %summed.14), channel_id=1, source_target_pairs={{0,8},{1,9},{2,10},{3,11},{4,12},{5,13},{6,14},{7,15},{8,0},{9,1},... | collective-permute-start | bytes 208904 | tf_op jit(solution)/shard_map/ppermute | solution.py:284
  24.6 2.7 %collective-permute-done.11.refs_19_.refs_24_.refs_29_ = f32[17,8,128]{2,1,0:T(8,128)S(1)} collective-permute-done((f32[17,8,128]{2,1,0:T(8,128)S(1)}, f32[17,8,128]{2,1,0:T(8,128)S(1)}, u32[]{:S(2)}, u32[]{:S(2)}) %collective-permute-start.11) | collective-permute-done | bytes 69664 | tf_op jit(solution)/shard_map/ppermute | solution.py:284
  27.3 1.7 %collective-permute-done.5.refs_4_.refs_9_.refs_14_ = f32[17,8,128]{2,1,0:T(8,128)S(1)} collective-permute-done((f32[17,8,128]{2,1,0:T(8,128)S(1)}, f32[17,8,128]{2,1,0:T(8,128)S(1)}, u32[]{:S(2)}, u32[]{:S(2)}) %collective-permute-start.5) | collective-permute-done | bytes 69664 | tf_op jit(solution)/shard_map/ppermute | solution.py:284
  29.0 0.8 %finish.1 = f32[32,2,512]{2,1,0:T(2,128)} custom-call(f32[129,8,128]{2,1,0:T(8,128)S(1)} %next_products.3.refs_0_.refs_2_.refs_3_.refs_4_.refs_8_.refs_5_.refs_10_, f32[129,8,128]{2,1,0:T(8,128)S(1)} %collective-permute-done.refs_1_.refs_3_.refs_4_.refs_5_.refs_9_.refs_6_.refs_11_, ...), custom_call_target="tpu_custom_call" | custom-call | tf_op jit(solution)/shard_map/finish/pallas_call | solution.py:264
  (10 shorter events, 0.2 us)
Async XLA Ops:
  2.2 2.1 %collective-permute-start.6 = (f32[129,8,128]{2,1,0:T(8,128)S(1)}, f32[129,8,128]{2,1,0:T(8,128)S(1)}, u32[]{:S(2)}, u32[]{:S(2)}) collective-permute-start(f32[129,8,128]{2,1,0:T(8,128)S(1)} %next_products.5), channel_id=1, source_target_pairs={{0,1},{1,0},{2,3},{3,2},{4,5},{5,4},{6,7},{7,6},{8,9},{9,8},{10,11... | collective-permute-start | bytes 1585160 | tf_op jit(solution)/shard_map/ppermute | solution.py:284
  2.8 4.9 %collective-permute-start = (f32[129,8,128]{2,1,0:T(8,128)S(1)}, f32[129,8,128]{2,1,0:T(8,128)S(1)}, u32[]{:S(2)}, u32[]{:S(2)}) collective-permute-start(f32[129,8,128]{2,1,0:T(8,128)S(1)} %get-tuple-element.12), channel_id=1, source_target_pairs={{0,1},{1,0},{2,3},{3,2},{4,5},{5,4},{6,7},{7,6},{8,9},{9,8},{10,11... | collective-permute-start | bytes 1585160 | tf_op jit(solution)/shard_map/ppermute | solution.py:284
  4.3 7.3 %collective-permute-start.7 = (f32[33,8,128]{2,1,0:T(8,128)S(1)}, f32[33,8,128]{2,1,0:T(8,128)S(1)}, u32[]{:S(2)}, u32[]{:S(2)}) collective-permute-start(f32[33,8,128]{2,1,0:T(8,128)S(1)} %summed.15), channel_id=1, source_target_pairs={{0,2},{1,3},{2,0},{3,1},{4,6},{5,7},{6,4},{7,5},{8,10},{9,11},{10,... | collective-permute-start | bytes 405512 | tf_op jit(solution)/shard_map/ppermute | solution.py:284
  7.7 6.3 %collective-permute-start.1 = (f32[33,8,128]{2,1,0:T(8,128)S(1)}, f32[33,8,128]{2,1,0:T(8,128)S(1)}, u32[]{:S(2)}, u32[]{:S(2)}) collective-permute-start(f32[33,8,128]{2,1,0:T(8,128)S(1)} %summed.10), channel_id=1, source_target_pairs={{0,2},{1,3},{2,0},{3,1},{4,6},{5,7},{6,4},{7,5},{8,10},{9,11},{10,... | collective-permute-start | bytes 405512 | tf_op jit(solution)/shard_map/ppermute | solution.py:284
  8.0 7.9 %collective-permute-start.9 = (f32[32,8,128]{2,1,0:T(8,128)S(1)}, f32[32,8,128]{2,1,0:T(8,128)S(1)}, u32[]{:S(2)}, u32[]{:S(2)}) collective-permute-start(f32[32,8,128]{2,1,0:T(8,128)S(1)} %summed.17), channel_id=1, source_target_pairs={{0,4},{1,5},{2,6},{3,7},{4,0},{5,1},{6,2},{7,3},{8,12},{9,13},{10,... | collective-permute-start | bytes 393224 | tf_op jit(solution)/shard_map/ppermute | solution.py:284
  10.0 7.5 %collective-permute-start.3 = (f32[32,8,128]{2,1,0:T(8,128)S(1)}, f32[32,8,128]{2,1,0:T(8,128)S(1)}, u32[]{:S(2)}, u32[]{:S(2)}) collective-permute-start(f32[32,8,128]{2,1,0:T(8,128)S(1)} %summed.12), channel_id=1, source_target_pairs={{0,4},{1,5},{2,6},{3,7},{4,0},{5,1},{6,2},{7,3},{8,12},{9,13},{10,... | collective-permute-start | bytes 393224 | tf_op jit(solution)/shard_map/ppermute | solution.py:284
  11.6 8.7 %collective-permute-start.8 = (f32[17,8,128]{2,1,0:T(8,128)S(1)}, f32[17,8,128]{2,1,0:T(8,128)S(1)}, u32[]{:S(2)}, u32[]{:S(2)}) collective-permute-start(f32[17,8,128]{2,1,0:T(8,128)S(1)} %summed.16), channel_id=1, source_target_pairs={{0,4},{1,5},{2,6},{3,7},{4,0},{5,1},{6,2},{7,3},{8,12},{9,13},{10,... | collective-permute-start | bytes 208904 | tf_op jit(solution)/shard_map/ppermute | solution.py:284
  14.1 9.0 %collective-permute-start.2 = (f32[17,8,128]{2,1,0:T(8,128)S(1)}, f32[17,8,128]{2,1,0:T(8,128)S(1)}, u32[]{:S(2)}, u32[]{:S(2)}) collective-permute-start(f32[17,8,128]{2,1,0:T(8,128)S(1)} %summed.11), channel_id=1, source_target_pairs={{0,4},{1,5},{2,6},{3,7},{4,0},{5,1},{6,2},{7,3},{8,12},{9,13},{10,... | collective-permute-start | bytes 208904 | tf_op jit(solution)/shard_map/ppermute | solution.py:284
  16.0 4.4 %collective-permute-start.10 = (f32[16,8,128]{2,1,0:T(8,128)S(1)}, f32[16,8,128]{2,1,0:T(8,128)S(1)}, u32[]{:S(2)}, u32[]{:S(2)}) collective-permute-start(f32[16,8,128]{2,1,0:T(8,128)S(1)} %summed.18), channel_id=1, source_target_pairs={{0,2},{1,3},{2,0},{3,1},{4,6},{5,7},{6,4},{7,5},{8,10},{9,11},{10,... | collective-permute-start | bytes 196616 | tf_op jit(solution)/shard_map/ppermute | solution.py:284
  17.5 5.5 %collective-permute-start.4 = (f32[16,8,128]{2,1,0:T(8,128)S(1)}, f32[16,8,128]{2,1,0:T(8,128)S(1)}, u32[]{:S(2)}, u32[]{:S(2)}) collective-permute-start(f32[16,8,128]{2,1,0:T(8,128)S(1)} %summed.13), channel_id=1, source_target_pairs={{0,2},{1,3},{2,0},{3,1},{4,6},{5,7},{6,4},{7,5},{8,10},{9,11},{10,... | collective-permute-start | bytes 196616 | tf_op jit(solution)/shard_map/ppermute | solution.py:284
  20.4 7.0 %collective-permute-start.11 = (f32[17,8,128]{2,1,0:T(8,128)S(1)}, f32[17,8,128]{2,1,0:T(8,128)S(1)}, u32[]{:S(2)}, u32[]{:S(2)}) collective-permute-start(f32[17,8,128]{2,1,0:T(8,128)S(1)} %summed.19), channel_id=1, source_target_pairs={{0,8},{1,9},{2,10},{3,11},{4,12},{5,13},{6,14},{7,15},{8,0},{9,1},... | collective-permute-start | bytes 208904 | tf_op jit(solution)/shard_map/ppermute | solution.py:284
  23.1 5.9 %collective-permute-start.5 = (f32[17,8,128]{2,1,0:T(8,128)S(1)}, f32[17,8,128]{2,1,0:T(8,128)S(1)}, u32[]{:S(2)}, u32[]{:S(2)}) collective-permute-start(f32[17,8,128]{2,1,0:T(8,128)S(1)} %summed.14), channel_id=1, source_target_pairs={{0,8},{1,9},{2,10},{3,11},{4,12},{5,13},{6,14},{7,15},{8,0},{9,1},... | collective-permute-start | bytes 208904 | tf_op jit(solution)/shard_map/ppermute | solution.py:284

commit v3 on v2

v3 whole, which is shorter than its diff:
```python
import functools

import jax
import jax.numpy as jnp
from jax import lax
from jax.experimental import pallas as pl
from jax.experimental.pallas import tpu as pltpu
from jax.sharding import PartitionSpec as P

epsilon = 1e-06
MIB = 1 << 20
CHUNKS = 2


def quad_bits(bits):
    return (1, 2) if bits > 2 else ()


def place_of(group, me, bits):
    quad = quad_bits(bits)
    place = 0
    for bit in reversed(quad):
        place = place * 2 + ((group >> bit) & 1)
    for bit in range(1, bits):
        if bit not in quad:
            place = place * 2 + (1 - (((group ^ me) >> bit) & 1))
    return place


def write_products(slots, rows, weights, served, out):
    users = rows.shape[0] // slots
    antennas = rows.shape[1] // 2
    blocks, steps = weights.shape[1] // 128, users // 8
    group = min(slots, 8)
    for base in range(0, slots, group):
        plain = rows[base * users:(base + group) * users, :]
        turned = jnp.concatenate([-plain[:, antennas:], plain[:, :antennas]], axis=1)
        both = jnp.concatenate([plain, turned], axis=0)
        value = jnp.dot(both, weights, preferred_element_type=jnp.float32)
        value = jnp.where(served, value, 0.0)
        for half in range(2):
            for slot in range(group):
                top = (half * group + slot) * users
                for block in range(blocks):
                    piece = value[top:top + users, block * 128:(block + 1) * 128]
                    start = (((base + slot) * 2 + half) * blocks + block) * steps
                    out[start:start + steps] = piece.reshape(steps, 8, 128)


def power_tile(weights, served):
    wide = weights.astype(jnp.float32)
    power = jnp.sum(wide * wide, axis=0, keepdims=True)
    power = jnp.where(served, power, 0.0)
    blocks = power.shape[1] // 128
    pieces = [power[:, block * 128:(block + 1) * 128] for block in range(blocks)]
    return jnp.concatenate(pieces + [jnp.zeros((8 - blocks, 128), jnp.float32)], axis=0)


def first_kernel(
    bits, visible, cluster, channel, precoder,
    out, rows, weights, served,
    seen, names, raw, sems,
):
    me = lax.axis_index("ap")
    held, users, antennas = raw.shape[1], raw.shape[3], raw.shape[4]
    columns = weights.shape[1]
    width = columns // CHUNKS
    slots = rows.shape[1] // users
    loads = [
        pltpu.make_async_copy(visible, seen, sems.at[0]),
        pltpu.make_async_copy(cluster, names, sems.at[1]),
        pltpu.make_async_copy(channel, raw, sems.at[2]),
    ]
    for chunk in range(CHUNKS):
        at = pl.ds(chunk * width, width)
        loads.append(
            pltpu.make_async_copy(precoder.at[:, at], weights.at[:, at], sems.at[3 + chunk])
        )
    for load in loads:
        load.start()
    rows[...] = jnp.zeros_like(rows)
    loads[0].wait()
    loads[1].wait()
    mask = jnp.max((names[...] == me).astype(jnp.float32), axis=0, keepdims=True)
    served[...] = mask
    loads[2].wait()
    for v in range(held):
        which = 1 - ((seen[0, v] ^ me) & 1)
        place = place_of(seen[0, v], me, bits)
        at = pl.ds(pl.multiple_of(place * users, users), users)
        rows[which, at, 0:antennas] = raw[0, v, 0]
        rows[which, at, antennas:2 * antennas] = raw[0, v, 1]
    loads[3].wait()
    mine = mask[:, 0:width] > 0.0
    chosen = weights[:, 0:width]
    write_products(slots, rows.at[0], chosen, mine, out)
    out[out.shape[0] - 1] = power_tile(chosen, mine)
    for load in loads[4:]:
        load.wait()


def next_kernel(bits, which, chunk, rows, weights, served, out):
    width = weights.shape[1] // CHUNKS
    at = slice(chunk * width, (chunk + 1) * width)
    mine = served[:, at] > 0.0
    chosen = weights[:, at]
    slots = 1 << (bits - 1)
    write_products(slots, rows.at[which], chosen, mine, out)
    out[out.shape[0] - 1] = power_tile(chosen, mine)


def message(tiles):
    return jax.ShapeDtypeStruct((tiles, 8, 128), jnp.float32)


def estimate(slots, users, antennas, columns):
    return pl.CostEstimate(
        flops=8 * slots * users * antennas * columns,
        bytes_accessed=slots * users * (antennas * 4 + columns * 8) + antennas * columns * 4,
        transcendentals=0,
    )


def first_products(bits, visible, cluster, channel, precoder):
    held, users, antennas = channel.shape[1], channel.shape[3], channel.shape[4]
    columns = precoder.shape[1]
    slots = 1 << (bits - 1)
    tiles = (users // 8) * (columns // CHUNKS // 128)
    hbm = pl.BlockSpec(memory_space=pltpu.HBM)
    vmem = pl.BlockSpec(memory_space=pltpu.VMEM)
    return pl.pallas_call(
        functools.partial(first_kernel, bits),
        out_shape=(
            message(2 * slots * tiles + 1),
            jax.ShapeDtypeStruct((2, slots * users, 2 * antennas), jnp.bfloat16),
            jax.ShapeDtypeStruct(precoder.shape, jnp.bfloat16),
            jax.ShapeDtypeStruct((1, columns), jnp.float32),
        ),
        in_specs=[hbm] * 4,
        out_specs=(vmem,) * 4,
        scratch_shapes=[
            pltpu.SMEM(visible.shape, jnp.int32),
            pltpu.VMEM(cluster.shape, jnp.int32),
            pltpu.VMEM(channel.shape, jnp.bfloat16),
            pltpu.SemaphoreType.DMA((3 + CHUNKS,)),
        ],
        compiler_params=pltpu.CompilerParams(vmem_limit_bytes=48 * MIB if slots > 8 else 24 * MIB),
        cost_estimate=estimate(slots, users, antennas, columns // CHUNKS),
        name="first_products",
    )(*[pltpu.with_memory_space_constraint(a, pltpu.HBM) for a in (visible, cluster, channel, precoder)])


def next_products(bits, which, chunk, rows, weights, served, users):
    slots = 1 << (bits - 1)
    antennas, columns = weights.shape[0] // 2, weights.shape[1]
    tiles = (users // 8) * (columns // CHUNKS // 128)
    vmem = pl.BlockSpec(memory_space=pltpu.VMEM)
    return pl.pallas_call(
        functools.partial(next_kernel, bits, which, chunk),
        out_shape=message(2 * slots * tiles + 1),
        in_specs=[vmem] * 3,
        out_specs=vmem,
        compiler_params=pltpu.CompilerParams(vmem_limit_bytes=48 * MIB if slots > 8 else 16 * MIB),
        cost_estimate=estimate(slots, users, antennas, columns // CHUNKS),
        name="next_products",
    )(rows, weights, served)


def add_up(refs, terms, count):
    total = refs[terms[0][0]][terms[0][1]:terms[0][1] + count]
    for ref, start in terms[1:]:
        total = total + refs[ref][start:start + count]
    return total


def sum_kernel(jobs, *refs):
    at = 0
    for terms, count in jobs:
        refs[-1][at:at + count] = add_up(refs, terms, count)
        at += count


def summed(arrays, jobs):
    size = sum(count for _, count in jobs)
    vmem = pl.BlockSpec(memory_space=pltpu.VMEM)
    reads = sum(len(terms) * count for terms, count in jobs)
    return pl.pallas_call(
        functools.partial(sum_kernel, jobs),
        out_shape=message(size),
        in_specs=[vmem] * len(arrays),
        out_specs=vmem,
        compiler_params=pltpu.CompilerParams(vmem_limit_bytes=8 * MIB),
        cost_estimate=pl.CostEstimate(
            flops=reads * 1024, bytes_accessed=(reads + size) * 4096, transcendentals=0
        ),
        name="summed",
    )(*arrays)


def final_kernel(jobs, users, *refs):
    out = refs[-1]
    blocks, steps = out.shape[2] // 128 // CHUNKS, users // 8
    for chunk, (terms, powers) in enumerate(jobs):
        scale = lax.rsqrt(add_up(refs, powers, 1)[0] + epsilon)
        total = add_up(refs, terms, 2 * blocks * steps)
        for half in range(2):
            for block in range(blocks):
                start = (half * blocks + block) * steps
                value = total[start:start + steps].reshape(users, 128)
                factor = scale[block:block + 1, :]
                value = jnp.where(factor > 0.0, value * factor, 0.0)
                left = (chunk * blocks + block) * 128
                out[:, half, left:left + 128] = value


def finish(arrays, jobs, users, columns):
    vmem = pl.BlockSpec(memory_space=pltpu.VMEM)
    return pl.pallas_call(
        functools.partial(final_kernel, jobs, users),
        out_shape=jax.ShapeDtypeStruct((users, 2, columns), jnp.float32),
        in_specs=[vmem] * len(arrays),
        out_specs=vmem,
        compiler_params=pltpu.CompilerParams(vmem_limit_bytes=8 * MIB),
        name="finish",
    )(*arrays)


def on_device(channel, precoder, visible, cluster):
    devices = lax.axis_size("ap")
    bits = devices.bit_length() - 1
    users, columns = channel.shape[3], precoder.shape[2]
    tiles = (users // 8) * (columns // CHUNKS // 128) * 2
    quad = quad_bits(bits)
    flat = precoder.reshape(-1, columns)

    def swap(value, bit):
        return lax.ppermute(value, "ap", [(i, i ^ (1 << bit)) for i in range(devices)])

    def square(value):
        low = 1 << quad[0]
        groups = [
            [i + low * member for member in range(4)]
            for i in range(devices) if (i >> quad[0]) & 3 == 0
        ]
        return lax.all_to_all(
            value, "ap", split_axis=0, concat_axis=0, axis_index_groups=groups, tiled=True
        )

    half = devices // 2
    sent, rows, weights, served = first_products(bits, visible, cluster.T, channel, flat)
    got = [swap(sent, 0)]
    for chunk in range(1, CHUNKS):
        got.append(swap(next_products(bits, 0, chunk, rows, weights, served, users), 0))
    lasts, jobs, base = [], [], 0
    for chunk in range(CHUNKS):
        kept = next_products(bits, 1, chunk, rows, weights, served, users)
        members = 4 if quad else 1
        slots = half // members
        count = slots * tiles
        power = ([(0, half * tiles), (1, half * tiles)], 1)
        sums = []
        for member in range(members):
            sums += [([(0, member * count), (1, member * count)], count), power]
        got_all = summed([kept, got[chunk]], sums)
        if quad:
            got_all = square(got_all)
        held = [got_all]
        left = [(0, member * (count + 1)) for member in range(members)]
        powers = [(0, member * (count + 1) + count) for member in range(members)]
        for bit in range(1, bits):
            if bit in quad:
                continue
            slots //= 2
            count = slots * tiles
            came = swap(summed(held, [(left, count), (powers, 1)]), bit)
            left = [(array, start + count) for array, start in left] + [(len(held), 0)]
            powers = powers + [(len(held), count)]
            held = held + [came]
        jobs.append((
            [(base + array, start) for array, start in left],
            [(base + array, start) for array, start in powers],
        ))
        base += len(held)
        lasts += held
    return finish(lasts, jobs, users, columns)


def solution(mesh):
    in_specs = (
        P(("parts", "ap"), None, None, None, None),
        P(None, ("parts", "ap"), None),
        P(("parts", "ap"), None),
        P("parts", None),
    )
    out_specs = P(("parts", "ap"), None, None)
    return jax.shard_map(
        on_device, mesh=mesh, in_specs=in_specs, out_specs=out_specs, check_vma=False
    )
```

time: 29.9 us -> 38 us (1.27)
  waiting for transfers between devices: 8.22 us -> 18.3 us
  starting transfers between devices: 17.4 us -> 13.8 us
  Pallas kernels: 4.07 us -> 5.66 us
    all_to_all x0 -> x2, waiting for transfers between devices: none -> 12.3 us  [square(): lax.all_to_all(value, 'ap', split_axis=0, concat_axis=0, axis_index_group...]
    ppermute x12 -> x4, starting transfers between devices: 17.4 us -> 5.14 us  [swap(): lax.ppermute(value, 'ap', [(i, i ^ 1 << bit) for i in range(devices)])]
    all_to_all x0 -> x2, starting transfers between devices: none -> 8.62 us  [square(): lax.all_to_all(value, 'ap', split_axis=0, concat_axis=0, axis_index_group...]
    ppermute x12 -> x4, waiting for transfers between devices: 8.22 us -> 5.99 us  [swap(): lax.ppermute(value, 'ap', [(i, i ^ 1 << bit) for i in range(devices)])]
    pallas_call x11 -> x5, Pallas kernels: 0.95 us -> 2.54 us  [the longest x4 1.78 us: summed(): pl.pallas_call(functools.partial(sum_kernel, jobs), out_shape=message(siz...]
  transfers between devices with their start and end apart: 12 -> 6, of which waited for: 6 -> 5; matrix products, arithmetic and copies ran while one was open for 0% -> 0% of each run, Pallas kernels for 4% -> 6%
where the time goes in v3:
time: 38 us; the launch traced here: 37.8 us
  waiting for transfers between devices  18.3 us (48%)
  starting transfers between devices  13.8 us (36%)
  Pallas kernels  5.66 us (15%)
    all_to_all x2, waiting for transfers between devices, square(): lax.all_to_all(value, 'ap', split_axis=0, concat_axis=0, axis_index_group...  12.3 us
    all_to_all x2, starting transfers between devices, square(): lax.all_to_all(value, 'ap', split_axis=0, concat_axis=0, axis_index_group...  8.62 us
    ppermute x4, waiting for transfers between devices, swap(): lax.ppermute(value, 'ap', [(i, i ^ 1 << bit) for i in range(devices)])  5.99 us
    ppermute x4, starting transfers between devices, swap(): lax.ppermute(value, 'ap', [(i, i ^ 1 << bit) for i in range(devices)])  5.14 us
    pallas_call x1, Pallas kernels, first_products(): pl.pallas_call(functools.partial(first_kernel, bits), out_shape=(message(...  1.79 us
    pallas_call x4, Pallas kernels, summed(): pl.pallas_call(functools.partial(sum_kernel, jobs), out_shape=message(siz...  1.78 us
    pallas_call x3, Pallas kernels, next_products(): pl.pallas_call(functools.partial(next_kernel, bits, which, chunk), out_sh...  1.32 us
    pallas_call x1, Pallas kernels, finish(): pl.pallas_call(functools.partial(final_kernel, jobs, users), out_shape=ja...  0.77 us
  transfers between devices with their start and end apart: 6, of which 5 were waited for; matrix products, arithmetic and copies ran while one was open for 0% of the time, Pallas kernels for 6%

profile of v3, /device:TPU:0, one launch (start us, length us, event | category | flops | bytes accessed | tf_op | source)
XLA Modules:
  0.0 37.8 jit_solution(9571968512875678924)
XLA Ops:
  0.0 1.8 %first_products.1 = (f32[129,8,128]{2,1,0:T(8,128)S(1)}, bf16[2,256,1024]{2,1,0:T(8,128)(2,1)S(1)}, bf16[1024,512]{1,0:T(8,128)(2,1)S(1)}, f32[1,512]{1,0:T(1,128)S(1)}) custom-call(s32[1,12]{1,0:T(1,128)} %visible.1, s32[4,512]{1,0:T(4,128)} %bitcast.3, bf16[1,12,2,32,512]{4,3,2,1,0:T(8,128)(2,1)} %channel.1, bf16[1024,512]{1,0:T(8,128)(2,1)} %bitcast.2), custom_call_target="tpu_custom_call" | custom-call | flops 268435456 | bytes 1572864 | tf_op jit(solution)/shard_map/first_products/pallas_call | solution.py:131
  1.8 0.5 %collective-permute-start = (f32[129,8,128]{2,1,0:T(8,128)S(1)}, f32[129,8,128]{2,1,0:T(8,128)S(1)}, u32[]{:S(2)}, u32[]{:S(2)}) collective-permute-start(f32[129,8,128]{2,1,0:T(8,128)S(1)} %get-tuple-element.12), channel_id=1, source_target_pairs={{0,1},{1,0},{2,3},{3,2},{4,5},{5,4},{6,7},{7,6},{8,9},{9,8},{10,11... | collective-permute-start | bytes 1585160 | tf_op jit(solution)/shard_map/ppermute | solution.py:237
  2.3 0.4 %next_products.3.refs_0_ = f32[129,8,128]{2,1,0:T(8,128)S(1)} custom-call(bf16[2,256,1024]{2,1,0:T(8,128)(2,1)S(1)} %get-tuple-element.9.rows, bf16[1024,512]{1,0:T(8,128)(2,1)S(1)} %get-tuple-element.10.weights, f32[1,512]{1,0:T(1,128)S(1)} %get-tuple-element.11.served), custom_call_target="tpu_custom_call" | custom-call | flops 268435456 | bytes 1572864 | tf_op jit(solution)/shard_map/next_products/pallas_call | solution.py:158
  2.8 1.1 %collective-permute-done.refs_1_ = f32[129,8,128]{2,1,0:T(8,128)S(1)} collective-permute-done((f32[129,8,128]{2,1,0:T(8,128)S(1)}, f32[129,8,128]{2,1,0:T(8,128)S(1)}, u32[]{:S(2)}, u32[]{:S(2)}) %collective-permute-start) | collective-permute-done | bytes 528416 | tf_op jit(solution)/shard_map/ppermute | solution.py:237
  3.9 0.9 %summed.4 = f32[132,8,128]{2,1,0:T(8,128)} custom-call(f32[129,8,128]{2,1,0:T(8,128)S(1)} %next_products.3.refs_0_, f32[129,8,128]{2,1,0:T(8,128)S(1)} %collective-permute-done.refs_1_), custom_call_target="tpu_custom_call" | custom-call | flops 270336 | bytes 1622016 | tf_op jit(solution)/shard_map/summed/pallas_call | solution.py:187
  4.7 5.1 %all-to-all-start = ((f32[132,8,128]{2,1,0:T(8,128)}), f32[132,8,128]{2,1,0:T(8,128)S(1)}, u32[]{:S(2)}, u32[]{:S(2)}) async-start(f32[132,8,128]{2,1,0:T(8,128)} %summed.4), calls=%async_computation | async-start | bytes 1081344 | tf_op jit(solution)/shard_map/all_to_all | solution.py:245
  9.9 0.4 %next_products.5 = f32[129,8,128]{2,1,0:T(8,128)S(1)} custom-call(bf16[2,256,1024]{2,1,0:T(8,128)(2,1)S(1)} %get-tuple-element.9.rows, bf16[1024,512]{1,0:T(8,128)(2,1)S(1)} %get-tuple-element.10.weights, f32[1,512]{1,0:T(1,128)S(1)} %get-tuple-element.11.served), custom_call_target="tpu_custom_call" | custom-call | flops 268435456 | bytes 1572864 | tf_op jit(solution)/shard_map/next_products/pallas_call | solution.py:158
  10.3 0.1 collective-permute-start.2
  10.4 0.4 %next_products.4.refs_0_ = f32[129,8,128]{2,1,0:T(8,128)S(1)} custom-call(bf16[2,256,1024]{2,1,0:T(8,128)(2,1)S(1)} %get-tuple-element.9.rows, bf16[1024,512]{1,0:T(8,128)(2,1)S(1)} %get-tuple-element.10.weights, f32[1,512]{1,0:T(1,128)S(1)} %get-tuple-element.11.served), custom_call_target="tpu_custom_call" | custom-call | flops 268435456 | bytes 1572864 | tf_op jit(solution)/shard_map/next_products/pallas_call | solution.py:158
  10.9 1.5 %collective-permute-done.2.refs_1_ = f32[129,8,128]{2,1,0:T(8,128)S(1)} collective-permute-done((f32[129,8,128]{2,1,0:T(8,128)S(1)}, f32[129,8,128]{2,1,0:T(8,128)S(1)}, u32[]{:S(2)}, u32[]{:S(2)}) %collective-permute-start.2) | collective-permute-done | bytes 528416 | tf_op jit(solution)/shard_map/ppermute | solution.py:237
  12.3 0.9 %summed.6 = f32[132,8,128]{2,1,0:T(8,128)} custom-call(f32[129,8,128]{2,1,0:T(8,128)S(1)} %next_products.4.refs_0_, f32[129,8,128]{2,1,0:T(8,128)S(1)} %collective-permute-done.2.refs_1_), custom_call_target="tpu_custom_call" | custom-call | flops 270336 | bytes 1622016 | tf_op jit(solution)/shard_map/summed/pallas_call | solution.py:187
  13.2 5.2 %all-to-all-done.refs_0_ = f32[132,8,128]{2,1,0:T(8,128)S(1)} async-done(((f32[132,8,128]{2,1,0:T(8,128)}), f32[132,8,128]{2,1,0:T(8,128)S(1)}, u32[]{:S(2)}, u32[]{:S(2)}) %all-to-all-start) | async-done | bytes 540704 | tf_op jit(solution)/shard_map/all_to_all | solution.py:245
  18.4 3.5 %all-to-all-start.1 = ((f32[132,8,128]{2,1,0:T(8,128)}), f32[132,8,128]{2,1,0:T(8,128)S(1)}, u32[]{:S(2)}, u32[]{:S(2)}) async-start(f32[132,8,128]{2,1,0:T(8,128)} %summed.6), calls=%async_computation.1 | async-start | bytes 1081344 | tf_op jit(solution)/shard_map/all_to_all | solution.py:245
  21.9 2.7 %collective-permute-start.1 = (f32[17,8,128]{2,1,0:T(8,128)S(1)}, f32[17,8,128]{2,1,0:T(8,128)S(1)}, u32[]{:S(2)}, u32[]{:S(2)}) collective-permute-start(f32[17,8,128]{2,1,0:T(8,128)S(1)} %summed.5), channel_id=1, source_target_pairs={{0,8},{1,9},{2,10},{3,11},{4,12},{5,13},{6,14},{7,15},{8,0},{9,1},... | collective-permute-start | bytes 208904 | tf_op jit(solution)/shard_map/ppermute | solution.py:237
  24.5 7.1 %all-to-all-done.1.refs_0_.refs_2_ = f32[132,8,128]{2,1,0:T(8,128)S(1)} async-done(((f32[132,8,128]{2,1,0:T(8,128)}), f32[132,8,128]{2,1,0:T(8,128)S(1)}, u32[]{:S(2)}, u32[]{:S(2)}) %all-to-all-start.1) | async-done | bytes 540704 | tf_op jit(solution)/shard_map/all_to_all | solution.py:245
  31.7 1.9 %collective-permute-start.3 = (f32[17,8,128]{2,1,0:T(8,128)S(1)}, f32[17,8,128]{2,1,0:T(8,128)S(1)}, u32[]{:S(2)}, u32[]{:S(2)}) collective-permute-start(f32[17,8,128]{2,1,0:T(8,128)S(1)} %summed.7), channel_id=1, source_target_pairs={{0,8},{1,9},{2,10},{3,11},{4,12},{5,13},{6,14},{7,15},{8,0},{9,1},... | collective-permute-start | bytes 208904 | tf_op jit(solution)/shard_map/ppermute | solution.py:237
  33.6 0.0 collective-permute-done.1.refs_1_
  33.6 3.4 %collective-permute-done.3.refs_3_ = f32[17,8,128]{2,1,0:T(8,128)S(1)} collective-permute-done((f32[17,8,128]{2,1,0:T(8,128)S(1)}, f32[17,8,128]{2,1,0:T(8,128)S(1)}, u32[]{:S(2)}, u32[]{:S(2)}) %collective-permute-start.3) | collective-permute-done | bytes 69664 | tf_op jit(solution)/shard_map/ppermute | solution.py:237
  37.0 0.8 %finish.1 = f32[32,2,512]{2,1,0:T(2,128)} custom-call(f32[132,8,128]{2,1,0:T(8,128)S(1)} %all-to-all-done.refs_0_, f32[17,8,128]{2,1,0:T(8,128)S(1)} %collective-permute-done.1.refs_1_, f32[132,8,128]{2,1,0:T(8,128)S(1)} %all-to-all-done.1.refs_0_.refs_2_, f32[17,8,128]{2,1,0:T(8,128)S(1)} %collective-permute-done.3.refs_3_), custom_call_target="tpu_custom_call" | custom-call | tf_op jit(solution)/shard_map/finish/pallas_call | solution.py:218
  (2 shorter events, 0.0 us)
Async XLA Ops:
  1.8 2.1 %collective-permute-start = (f32[129,8,128]{2,1,0:T(8,128)S(1)}, f32[129,8,128]{2,1,0:T(8,128)S(1)}, u32[]{:S(2)}, u32[]{:S(2)}) collective-permute-start(f32[129,8,128]{2,1,0:T(8,128)S(1)} %get-tuple-element.12), channel_id=1, source_target_pairs={{0,1},{1,0},{2,3},{3,2},{4,5},{5,4},{6,7},{7,6},{8,9},{9,8},{10,11... | collective-permute-start | bytes 1585160 | tf_op jit(solution)/shard_map/ppermute | solution.py:237
  4.7 13.6 %all-to-all-start = ((f32[132,8,128]{2,1,0:T(8,128)}), f32[132,8,128]{2,1,0:T(8,128)S(1)}, u32[]{:S(2)}, u32[]{:S(2)}) async-start(f32[132,8,128]{2,1,0:T(8,128)} %summed.4), calls=%async_computation | async-start | bytes 1081344 | tf_op jit(solution)/shard_map/all_to_all | solution.py:245
  10.3 2.0 %collective-permute-start.2 = (f32[129,8,128]{2,1,0:T(8,128)S(1)}, f32[129,8,128]{2,1,0:T(8,128)S(1)}, u32[]{:S(2)}, u32[]{:S(2)}) collective-permute-start(f32[129,8,128]{2,1,0:T(8,128)S(1)} %next_products.5), channel_id=1, source_target_pairs={{0,1},{1,0},{2,3},{3,2},{4,5},{5,4},{6,7},{7,6},{8,9},{9,8},{10,11... | collective-permute-start | bytes 1585160 | tf_op jit(solution)/shard_map/ppermute | solution.py:237
  18.4 13.3 %all-to-all-start.1 = ((f32[132,8,128]{2,1,0:T(8,128)}), f32[132,8,128]{2,1,0:T(8,128)S(1)}, u32[]{:S(2)}, u32[]{:S(2)}) async-start(f32[132,8,128]{2,1,0:T(8,128)} %summed.6), calls=%async_computation.1 | async-start | bytes 1081344 | tf_op jit(solution)/shard_map/all_to_all | solution.py:245
  21.9 11.7 %collective-permute-start.1 = (f32[17,8,128]{2,1,0:T(8,128)S(1)}, f32[17,8,128]{2,1,0:T(8,128)S(1)}, u32[]{:S(2)}, u32[]{:S(2)}) collective-permute-start(f32[17,8,128]{2,1,0:T(8,128)S(1)} %summed.5), channel_id=1, source_target_pairs={{0,8},{1,9},{2,10},{3,11},{4,12},{5,13},{6,14},{7,15},{8,0},{9,1},... | collective-permute-start | bytes 208904 | tf_op jit(solution)/shard_map/ppermute | solution.py:237
  31.7 5.3 %collective-permute-start.3 = (f32[17,8,128]{2,1,0:T(8,128)S(1)}, f32[17,8,128]{2,1,0:T(8,128)S(1)}, u32[]{:S(2)}, u32[]{:S(2)}) collective-permute-start(f32[17,8,128]{2,1,0:T(8,128)S(1)} %summed.7), channel_id=1, source_target_pairs={{0,8},{1,9},{2,10},{3,11},{4,12},{5,13},{6,14},{7,15},{8,0},{9,1},... | collective-permute-start | bytes 208904 | tf_op jit(solution)/shard_map/ppermute | solution.py:237

commit v4 on v3

v4 whole, which is shorter than its diff:
```python
import functools

import jax
import jax.numpy as jnp
from jax import lax
from jax.experimental import pallas as pl
from jax.experimental.pallas import tpu as pltpu
from jax.sharding import PartitionSpec as P

epsilon = 1e-06
MIB = 1 << 20
CHUNKS = 2


def chip_orders(bits):
    first = list(range(1, bits))
    second = list(first)
    if bits > 2:
        second[0], second[1] = second[1], second[0]
    return first, second


def place_of(group, me, core, bits):
    away = [1 - (((group ^ me) >> bit) & 1) for bit in range(1, bits)]
    if bits > 2:
        swapped = core == 1
        away[:2] = [jnp.where(swapped, away[1], away[0]), jnp.where(swapped, away[0], away[1])]
    place = 0
    for value in away:
        place = place * 2 + value
    return place * 2 + (1 - ((group ^ core) & 1))


def write_products(slots, rows, weights, served, out):
    users = rows.shape[0] // slots
    antennas = rows.shape[1] // 2
    blocks, steps = weights.shape[1] // 128, users // 8
    group = min(slots, 16)
    for base in range(0, slots, group):
        plain = rows[base * users:(base + group) * users, :]
        turned = jnp.concatenate([-plain[:, antennas:], plain[:, :antennas]], axis=1)
        both = jnp.concatenate([plain, turned], axis=0)
        value = jnp.dot(both, weights, preferred_element_type=jnp.float32)
        value = jnp.where(served, value, 0.0)
        for half in range(2):
            for slot in range(group):
                top = (half * group + slot) * users
                for block in range(blocks):
                    piece = value[top:top + users, block * 128:(block + 1) * 128]
                    start = (((base + slot) * 2 + half) * blocks + block) * steps
                    out[start:start + steps] = piece.reshape(steps, 8, 128)


def power_tile(weights, served):
    wide = weights.astype(jnp.float32)
    power = jnp.sum(wide * wide, axis=0, keepdims=True)
    power = jnp.where(served, power, 0.0)
    blocks = power.shape[1] // 128
    pieces = [power[:, block * 128:(block + 1) * 128] for block in range(blocks)]
    return jnp.concatenate(pieces + [jnp.zeros((8 - blocks, 128), jnp.float32)], axis=0)


def first_kernel(
    bits, visible, cluster, channel, precoder,
    out, rows, weights, served,
    seen, names, raw, sems,
):
    me = lax.axis_index("ap")
    core = me & 1
    held, users, antennas = raw.shape[1], raw.shape[3], raw.shape[4]
    width = weights.shape[2]
    slots = 1 << bits
    mine = users // CHUNKS
    loads = [
        pltpu.make_async_copy(visible, seen, sems.at[0]),
        pltpu.make_async_copy(channel, raw, sems.at[1]),
    ]
    for keep in range(2):
        start = pl.multiple_of((core if keep else 1 - core) * width, width)
        at = pl.ds(start, width)
        loads.append(pltpu.make_async_copy(cluster.at[:, at], names.at[keep], sems.at[2 + 2 * keep]))
        loads.append(pltpu.make_async_copy(precoder.at[:, at], weights.at[keep], sems.at[3 + 2 * keep]))
    for load in loads:
        load.start()
    rows[...] = jnp.zeros_like(rows)
    loads[0].wait()
    loads[1].wait()
    for v in range(held):
        for keep in range(2):
            place = place_of(seen[0, v], me, core if keep else 1 - core, bits)
            at = pl.ds(pl.multiple_of(place * mine, mine), mine)
            for chunk in range(CHUNKS):
                part = slice(chunk * mine, (chunk + 1) * mine)
                rows[keep, chunk, at, 0:antennas] = raw[0, v, 0, part]
                rows[keep, chunk, at, antennas:2 * antennas] = raw[0, v, 1, part]
    for keep in range(2):
        loads[2 + 2 * keep].wait()
        here = (names[keep] == me).astype(jnp.float32)
        served[keep] = jnp.max(here, axis=0, keepdims=True)
    loads[3].wait()
    chosen, mask = weights[0], served[0] > 0.0
    write_products(slots, rows.at[0, 0], chosen, mask, out)
    out[out.shape[0] - 1] = power_tile(chosen, mask)
    loads[5].wait()


def next_kernel(bits, keep, chunk, rows, weights, served, out):
    chosen, mask = weights[keep], served[keep] > 0.0
    write_products(1 << bits, rows.at[keep, chunk], chosen, mask, out)
    if chunk == 0:
        out[out.shape[0] - 1] = power_tile(chosen, mask)


def message(tiles):
    return jax.ShapeDtypeStruct((tiles, 8, 128), jnp.float32)


def estimate(rows, weights):
    return pl.CostEstimate(
        flops=8 * rows[2] * rows[3] * weights[2],
        bytes_accessed=rows[2] * (rows[3] * 2 + weights[2] * 8) + weights[1] * weights[2] * 2,
        transcendentals=0,
    )


def first_products(bits, visible, cluster, channel, precoder):
    users, antennas = channel.shape[3], channel.shape[4]
    width = precoder.shape[1] // 2
    slots = 1 << bits
    tiles = (users // CHUNKS // 8) * (width // 128) * 2
    rows = (2, CHUNKS, slots * users // CHUNKS, 2 * antennas)
    weights = (2, precoder.shape[0], width)
    vmem = pl.BlockSpec(memory_space=pltpu.VMEM)
    hbm = pl.BlockSpec(memory_space=pltpu.HBM)
    operands = (visible, cluster, channel, precoder)
    return pl.pallas_call(
        functools.partial(first_kernel, bits),
        out_shape=(
            message(slots * tiles + 1),
            jax.ShapeDtypeStruct(rows, jnp.bfloat16),
            jax.ShapeDtypeStruct(weights, jnp.bfloat16),
            jax.ShapeDtypeStruct((2, 1, width), jnp.float32),
        ),
        in_specs=[hbm] * 4,
        out_specs=(vmem,) * 4,
        scratch_shapes=[
            pltpu.SMEM(visible.shape, jnp.int32),
            pltpu.VMEM((2, cluster.shape[0], width), jnp.int32),
            pltpu.VMEM(channel.shape, jnp.bfloat16),
            pltpu.SemaphoreType.DMA((6,)),
        ],
        compiler_params=pltpu.CompilerParams(vmem_limit_bytes=52 * MIB if slots > 16 else 24 * MIB),
        cost_estimate=estimate(rows, weights),
        name="first_products",
    )(*[pltpu.with_memory_space_constraint(operand, pltpu.HBM) for operand in operands])


def next_products(bits, keep, chunk, rows, weights, served):
    slots = 1 << bits
    users = rows.shape[2] // slots
    tiles = (users // 8) * (weights.shape[2] // 128) * 2
    vmem = pl.BlockSpec(memory_space=pltpu.VMEM)
    return pl.pallas_call(
        functools.partial(next_kernel, bits, keep, chunk),
        out_shape=message(slots * tiles + (chunk == 0)),
        in_specs=[vmem] * 3,
        out_specs=vmem,
        compiler_params=pltpu.CompilerParams(vmem_limit_bytes=48 * MIB if slots > 16 else 16 * MIB),
        cost_estimate=estimate(rows.shape, weights.shape),
        name="next_products",
    )(rows, weights, served)


def add_up(refs, terms, count):
    total = refs[terms[0][0]][terms[0][1]:terms[0][1] + count]
    for ref, start in terms[1:]:
        total = total + refs[ref][start:start + count]
    return total


def sum_kernel(jobs, *refs):
    at = 0
    for terms, count in jobs:
        refs[-1][at:at + count] = add_up(refs, terms, count)
        at += count


def summed(arrays, jobs):
    size = sum(count for _, count in jobs)
    vmem = pl.BlockSpec(memory_space=pltpu.VMEM)
    reads = sum(len(terms) * count for terms, count in jobs)
    return pl.pallas_call(
        functools.partial(sum_kernel, jobs),
        out_shape=message(size),
        in_specs=[vmem] * len(arrays),
        out_specs=vmem,
        compiler_params=pltpu.CompilerParams(vmem_limit_bytes=8 * MIB),
        cost_estimate=pl.CostEstimate(
            flops=reads * 1024, bytes_accessed=(reads + size) * 4096, transcendentals=0
        ),
        name="summed",
    )(*arrays)


def scaled_slot(refs, terms, powers, blocks, steps):
    scale = lax.rsqrt(add_up(refs, powers, 1)[0] + epsilon)
    total = add_up(refs, terms, 2 * blocks * steps)
    pieces = []
    for half in range(2):
        for block in range(blocks):
            start = (half * blocks + block) * steps
            factor = scale[block:block + 1, :].reshape(1, 1, 128)
            piece = total[start:start + steps]
            pieces.append(jnp.where(factor > 0.0, piece * factor, 0.0))
    return jnp.concatenate(pieces, axis=0)


def cross_kernel(jobs, powers, blocks, steps, *refs):
    tiles = 2 * blocks * steps
    for chunk, terms in enumerate(jobs):
        refs[-1][chunk * tiles:(chunk + 1) * tiles] = scaled_slot(refs, terms, powers, blocks, steps)


def final_kernel(jobs, powers, blocks, steps, *refs):
    crossed, out = refs[-2], refs[-1]
    core = lax.axis_index("ap") & 1
    tiles, users = 2 * blocks * steps, steps * 8
    for chunk, terms in enumerate(jobs):
        own = scaled_slot(refs, terms, powers, blocks, steps)
        other = crossed[chunk * tiles:(chunk + 1) * tiles]
        for side, value in ((core, own), (1 - core, other)):
            for half in range(2):
                for block in range(blocks):
                    start = (half * blocks + block) * steps
                    left = pl.multiple_of((side * blocks + block) * 128, 128)
                    piece = value[start:start + steps].reshape(users, 128)
                    out[chunk * users:(chunk + 1) * users, half, pl.ds(left, 128)] = piece


def finished(body, name, arrays, shape):
    vmem = pl.BlockSpec(memory_space=pltpu.VMEM)
    return pl.pallas_call(
        body,
        out_shape=shape,
        in_specs=[vmem] * len(arrays),
        out_specs=vmem,
        compiler_params=pltpu.CompilerParams(vmem_limit_bytes=8 * MIB),
        name=name,
    )(*arrays)


def on_device(channel, precoder, visible, cluster):
    devices = lax.axis_size("ap")
    bits = devices.bit_length() - 1
    users, columns = channel.shape[3], precoder.shape[2]
    steps, blocks = users // CHUNKS // 8, columns // 2 // 128
    tiles = 2 * blocks * steps
    orders = chip_orders(bits)
    flat = precoder.reshape(-1, columns)

    def swap(value, bit_of):
        return lax.ppermute(value, "ap", [(i, i ^ (1 << bit_of[i & 1])) for i in range(devices)])

    sent, rows, weights, served = first_products(bits, visible, cluster.T, channel, flat)
    got = [swap(sent, (0, 0))]
    for chunk in range(1, CHUNKS):
        got.append(swap(next_products(bits, 0, chunk, rows, weights, served), (0, 0)))
    held = [
        [next_products(bits, 1, chunk, rows, weights, served), got[chunk]] for chunk in range(CHUNKS)
    ]
    slots = devices
    left = [[(0, 0), (1, 0)] for _ in range(CHUNKS)]
    powers = [(0, slots * tiles), (1, slots * tiles)]
    for step in range(bits - 1):
        slots //= 2
        count = slots * tiles
        for chunk in range(CHUNKS):
            jobs = [(left[chunk], count)] + ([(powers, 1)] if chunk == 0 else [])
            came = swap(summed(held[chunk], jobs), (orders[0][step], orders[1][step]))
            left[chunk] = [(array, start + count) for array, start in left[chunk]]
            left[chunk].append((len(held[chunk]), 0))
            held[chunk].append(came)
        powers = powers + [(step + 2, count)]
    arrays = [array for mine in held for array in mine]
    other, own, base = [], [], 0
    for chunk in range(CHUNKS):
        other.append([(base + array, start) for array, start in left[chunk]])
        own.append([(base + array, start + tiles) for array, start in left[chunk]])
        base += len(held[chunk])
    cross = finished(
        functools.partial(cross_kernel, other, powers, blocks, steps),
        "cross", arrays, message(CHUNKS * tiles),
    )
    crossed = swap(cross, (0, 0))
    return finished(
        functools.partial(final_kernel, own, powers, blocks, steps),
        "finish", arrays + [crossed], jax.ShapeDtypeStruct((users, 2, columns), jnp.float32),
    )


def solution(mesh):
    in_specs = (
        P(("parts", "ap"), None, None, None, None),
        P(None, ("parts", "ap"), None),
        P(("parts", "ap"), None),
        P("parts", None),
    )
    out_specs = P(("parts", "ap"), None, None)
    return jax.shard_map(
        on_device, mesh=mesh, in_specs=in_specs, out_specs=out_specs, check_vma=False
    )
```

time: 38 us -> 28.4 us (0.75)
  waiting for transfers between devices: 18.3 us -> 9.88 us
  Pallas kernels: 5.66 us -> 4.18 us
    all_to_all x2 -> x0, waiting for transfers between devices: 12.3 us -> none  [square(): lax.all_to_all(value, 'ap', split_axis=0, concat_axis=0, axis_index_group...]
    ppermute x4 -> x9, starting transfers between devices: 5.14 us -> 14.1 us  [swap(): lax.ppermute(value, 'ap', [(i, i ^ 1 << bit_of[i & 1]) for i in range(dev...]
    all_to_all x2 -> x0, starting transfers between devices: 8.62 us -> none  [square(): lax.all_to_all(value, 'ap', split_axis=0, concat_axis=0, axis_index_group...]
    ppermute x4 -> x9, waiting for transfers between devices: 5.99 us -> 9.88 us  [swap(): lax.ppermute(value, 'ap', [(i, i ^ 1 << bit_of[i & 1]) for i in range(dev...]
    pallas_call x4 -> x6, Pallas kernels: 1.78 us -> 0.15 us  [summed(): pl.pallas_call(functools.partial(sum_kernel, jobs), out_shape=message(siz...]
    pallas_call x4 -> x5, Pallas kernels: 2.09 us -> 2.11 us  [the longest x3 1.31 us: next_products(): pl.pallas_call(functools.partial(next_kernel, bits, keep, chunk), out_sha...]
  transfers between devices with their start and end apart: 6 -> 9, of which waited for: 5 -> 6; matrix products, arithmetic and copies ran while one was open for 0% -> 0% of each run, Pallas kernels for 6% -> 5%
where the time goes in v4:
time: 28.4 us; the launch traced here: 28.2 us
  starting transfers between devices  14.1 us (50%)
  waiting for transfers between devices  9.88 us (35%)
  Pallas kernels  4.18 us (15%)
    ppermute x9, starting transfers between devices, swap(): lax.ppermute(value, 'ap', [(i, i ^ 1 << bit_of[i & 1]) for i in range(dev...  14.1 us
    ppermute x9, waiting for transfers between devices, swap(): lax.ppermute(value, 'ap', [(i, i ^ 1 << bit_of[i & 1]) for i in range(dev...  9.88 us
    pallas_call x1, Pallas kernels, first_products(): pl.pallas_call(functools.partial(first_kernel, bits), out_shape=(message(...  1.92 us
    pallas_call x3, Pallas kernels, next_products(): pl.pallas_call(functools.partial(next_kernel, bits, keep, chunk), out_sha...  1.31 us
    pallas_call x2, Pallas kernels, finished(): pl.pallas_call(body, out_shape=shape, in_specs=[vmem] * len(arrays), out_...  0.8 us
  transfers between devices with their start and end apart: 9, of which 6 were waited for; matrix products, arithmetic and copies ran while one was open for 0% of the time, Pallas kernels for 5%

profile of v4, /device:TPU:0, one launch (start us, length us, event | category | flops | bytes accessed | tf_op | source)
XLA Modules:
  0.0 28.2 jit_solution(13115073437985831827)
XLA Ops:
  0.0 1.9 %first_products.1 = (f32[129,8,128]{2,1,0:T(8,128)S(1)}, bf16[2,2,256,1024]{3,2,1,0:T(8,128)(2,1)S(1)}, bf16[2,1024,256]{2,1,0:T(8,128)(2,1)S(1)}, f32[2,1,256]{2,1,0:T(1,128)S(1)}) custom-call(s32[1,12]{1,0:T(1,128)} %visible.1, s32[4,512]{1,0:T(4,128)} %bitcast.3, bf16[1,12,2,32,512]{4,3,2,1,0:T(8,128)(2,1)} %channel.1, bf16[1024,512]{1,0:T(8,128)(2,1)} %bitcast.2), custom_call_target="tpu_custom_call" | custom-call | flops 536870912 | bytes 1572864 | tf_op jit(solution)/shard_map/first_products/pallas_call | solution.py:136
  1.9 0.5 %collective-permute-start = (f32[129,8,128]{2,1,0:T(8,128)S(1)}, f32[129,8,128]{2,1,0:T(8,128)S(1)}, u32[]{:S(2)}, u32[]{:S(2)}) collective-permute-start(f32[129,8,128]{2,1,0:T(8,128)S(1)} %get-tuple-element.12), channel_id=1, source_target_pairs={{0,1},{1,0},{2,3},{3,2},{4,5},{5,4},{6,7},{7,6},{8,9},{9,8},{10,11... | collective-permute-start | bytes 1585160 | tf_op jit(solution)/shard_map/ppermute | solution.py:262
  2.4 0.4 %next_products.5 = f32[128,8,128]{2,1,0:T(8,128)S(1)} custom-call(bf16[2,2,256,1024]{3,2,1,0:T(8,128)(2,1)S(1)} %get-tuple-element.9.rows, bf16[2,1024,256]{2,1,0:T(8,128)(2,1)S(1)} %get-tuple-element.10.weights, f32[2,1,256]{2,1,0:T(1,128)S(1)} %get-tuple-element.11.served), custom_call_target="tpu_custom_call" | custom-call | flops 536870912 | bytes 1572864 | tf_op jit(solution)/shard_map/next_products/pallas_call | solution.py:163
  2.9 0.1 collective-permute-start.4
  3.0 0.4 %next_products.3.refs_0_ = f32[129,8,128]{2,1,0:T(8,128)S(1)} custom-call(bf16[2,2,256,1024]{3,2,1,0:T(8,128)(2,1)S(1)} %get-tuple-element.9.rows, bf16[2,1024,256]{2,1,0:T(8,128)(2,1)S(1)} %get-tuple-element.10.weights, f32[2,1,256]{2,1,0:T(1,128)S(1)} %get-tuple-element.11.served), custom_call_target="tpu_custom_call" | custom-call | flops 536870912 | bytes 1572864 | tf_op jit(solution)/shard_map/next_products/pallas_call | solution.py:163
  3.5 0.5 %collective-permute-done.refs_1_ = f32[129,8,128]{2,1,0:T(8,128)S(1)} collective-permute-done((f32[129,8,128]{2,1,0:T(8,128)S(1)}, f32[129,8,128]{2,1,0:T(8,128)S(1)}, u32[]{:S(2)}, u32[]{:S(2)}) %collective-permute-start) | collective-permute-done | bytes 528416 | tf_op jit(solution)/shard_map/ppermute | solution.py:262
  4.0 2.9 %collective-permute-start.1 = (f32[65,8,128]{2,1,0:T(8,128)S(1)}, f32[65,8,128]{2,1,0:T(8,128)S(1)}, u32[]{:S(2)}, u32[]{:S(2)}) collective-permute-start(f32[65,8,128]{2,1,0:T(8,128)S(1)} %summed.6), channel_id=1, source_target_pairs={{0,2},{1,5},{2,0},{3,7},{4,6},{5,1},{6,4},{7,3},{8,10},{9,13},{10,... | collective-permute-start | bytes 798728 | tf_op jit(solution)/shard_map/ppermute | solution.py:262
  7.0 0.4 %next_products.4.refs_0_.refs_5_ = f32[128,8,128]{2,1,0:T(8,128)S(1)} custom-call(bf16[2,2,256,1024]{3,2,1,0:T(8,128)(2,1)S(1)} %get-tuple-element.9.rows, bf16[2,1024,256]{2,1,0:T(8,128)(2,1)S(1)} %get-tuple-element.10.weights, f32[2,1,256]{2,1,0:T(1,128)S(1)} %get-tuple-element.11.served), custom_call_target="tpu_custom_call" | custom-call | flops 536870912 | bytes 1572864 | tf_op jit(solution)/shard_map/next_products/pallas_call | solution.py:163
  7.4 0.0 collective-permute-done.4.refs_1_.refs_6_
  7.4 0.3 collective-permute-start.5
  7.7 3.6 %collective-permute-done.1.refs_2_ = f32[65,8,128]{2,1,0:T(8,128)S(1)} collective-permute-done((f32[65,8,128]{2,1,0:T(8,128)S(1)}, f32[65,8,128]{2,1,0:T(8,128)S(1)}, u32[]{:S(2)}, u32[]{:S(2)}) %collective-permute-start.1) | collective-permute-done | bytes 266272 | tf_op jit(solution)/shard_map/ppermute | solution.py:262
  11.4 2.2 %collective-permute-start.2 = (f32[33,8,128]{2,1,0:T(8,128)S(1)}, f32[33,8,128]{2,1,0:T(8,128)S(1)}, u32[]{:S(2)}, u32[]{:S(2)}) collective-permute-start(f32[33,8,128]{2,1,0:T(8,128)S(1)} %summed.7), channel_id=1, source_target_pairs={{0,4},{1,3},{2,6},{3,1},{4,0},{5,7},{6,2},{7,5},{8,12},{9,11},{10,... | collective-permute-start | bytes 405512 | tf_op jit(solution)/shard_map/ppermute | solution.py:262
  13.5 1.0 %collective-permute-done.5.refs_2_.refs_7_ = f32[64,8,128]{2,1,0:T(8,128)S(1)} collective-permute-done((f32[64,8,128]{2,1,0:T(8,128)S(1)}, f32[64,8,128]{2,1,0:T(8,128)S(1)}, u32[]{:S(2)}, u32[]{:S(2)}) %collective-permute-start.5) | collective-permute-done | bytes 262176 | tf_op jit(solution)/shard_map/ppermute | solution.py:262
  14.6 2.5 %collective-permute-start.6 = (f32[32,8,128]{2,1,0:T(8,128)S(1)}, f32[32,8,128]{2,1,0:T(8,128)S(1)}, u32[]{:S(2)}, u32[]{:S(2)}) collective-permute-start(f32[32,8,128]{2,1,0:T(8,128)S(1)} %summed.10), channel_id=1, source_target_pairs={{0,4},{1,3},{2,6},{3,1},{4,0},{5,7},{6,2},{7,5},{8,12},{9,11},{10,... | collective-permute-start | bytes 393224 | tf_op jit(solution)/shard_map/ppermute | solution.py:262
  17.1 0.0 collective-permute-done.2.refs_3_
  17.2 2.7 %collective-permute-start.3 = (f32[17,8,128]{2,1,0:T(8,128)S(1)}, f32[17,8,128]{2,1,0:T(8,128)S(1)}, u32[]{:S(2)}, u32[]{:S(2)}) collective-permute-start(f32[17,8,128]{2,1,0:T(8,128)S(1)} %summed.8), channel_id=1, source_target_pairs={{0,8},{1,9},{2,10},{3,11},{4,12},{5,13},{6,14},{7,15},{8,0},{9,1},... | collective-permute-start | bytes 208904 | tf_op jit(solution)/shard_map/ppermute | solution.py:262
  19.8 1.0 %collective-permute-done.6.refs_3_.refs_8_ = f32[32,8,128]{2,1,0:T(8,128)S(1)} collective-permute-done((f32[32,8,128]{2,1,0:T(8,128)S(1)}, f32[32,8,128]{2,1,0:T(8,128)S(1)}, u32[]{:S(2)}, u32[]{:S(2)}) %collective-permute-start.6) | collective-permute-done | bytes 131104 | tf_op jit(solution)/shard_map/ppermute | solution.py:262
  20.8 2.8 %collective-permute-start.7 = (f32[16,8,128]{2,1,0:T(8,128)S(1)}, f32[16,8,128]{2,1,0:T(8,128)S(1)}, u32[]{:S(2)}, u32[]{:S(2)}) collective-permute-start(f32[16,8,128]{2,1,0:T(8,128)S(1)} %summed.11), channel_id=1, source_target_pairs={{0,8},{1,9},{2,10},{3,11},{4,12},{5,13},{6,14},{7,15},{8,0},{9,1},... | collective-permute-start | bytes 196616 | tf_op jit(solution)/shard_map/ppermute | solution.py:262
  23.6 2.4 %collective-permute-done.7.refs_9_ = f32[16,8,128]{2,1,0:T(8,128)S(1)} collective-permute-done((f32[16,8,128]{2,1,0:T(8,128)S(1)}, f32[16,8,128]{2,1,0:T(8,128)S(1)}, u32[]{:S(2)}, u32[]{:S(2)}) %collective-permute-start.7) | collective-permute-done | bytes 65568 | tf_op jit(solution)/shard_map/ppermute | solution.py:262
  26.1 0.0 collective-permute-done.3.refs_4_
  26.1 0.1 collective-permute-start.8
  26.2 1.2 %collective-permute-done.8.refs_10_ = f32[16,8,128]{2,1,0:T(8,128)S(1)} collective-permute-done((f32[16,8,128]{2,1,0:T(8,128)S(1)}, f32[16,8,128]{2,1,0:T(8,128)S(1)}, u32[]{:S(2)}, u32[]{:S(2)}) %collective-permute-start.8) | collective-permute-done | bytes 65568 | tf_op jit(solution)/shard_map/ppermute | solution.py:262
  27.4 0.8 %finish.1 = f32[32,2,512]{2,1,0:T(2,128)} custom-call(f32[129,8,128]{2,1,0:T(8,128)S(1)} %next_products.3.refs_0_, f32[129,8,128]{2,1,0:T(8,128)S(1)} %collective-permute-done.refs_1_, f32[65,8,128]{2,1,0:T(8,128)S(1)} %collective-permute-done.1.refs_2_, f32[33,8,128]{2,1,0:T(8,128)S(1)} %collective-permute-done.2.refs_3_, ...), custom_call_target="tpu_custom_call" | custom-call | tf_op jit(solution)/shard_map/finish/pallas_call | solution.py:242
  (7 shorter events, 0.2 us)
Async XLA Ops:
  1.9 2.1 %collective-permute-start = (f32[129,8,128]{2,1,0:T(8,128)S(1)}, f32[129,8,128]{2,1,0:T(8,128)S(1)}, u32[]{:S(2)}, u32[]{:S(2)}) collective-permute-start(f32[129,8,128]{2,1,0:T(8,128)S(1)} %get-tuple-element.12), channel_id=1, source_target_pairs={{0,1},{1,0},{2,3},{3,2},{4,5},{5,4},{6,7},{7,6},{8,9},{9,8},{10,11... | collective-permute-start | bytes 1585160 | tf_op jit(solution)/shard_map/ppermute | solution.py:262
  2.9 4.5 %collective-permute-start.4 = (f32[128,8,128]{2,1,0:T(8,128)S(1)}, f32[128,8,128]{2,1,0:T(8,128)S(1)}, u32[]{:S(2)}, u32[]{:S(2)}) collective-permute-start(f32[128,8,128]{2,1,0:T(8,128)S(1)} %next_products.5), channel_id=1, source_target_pairs={{0,1},{1,0},{2,3},{3,2},{4,5},{5,4},{6,7},{7,6},{8,9},{9,8},{10,11... | collective-permute-start | bytes 1572872 | tf_op jit(solution)/shard_map/ppermute | solution.py:262
  4.0 7.3 %collective-permute-start.1 = (f32[65,8,128]{2,1,0:T(8,128)S(1)}, f32[65,8,128]{2,1,0:T(8,128)S(1)}, u32[]{:S(2)}, u32[]{:S(2)}) collective-permute-start(f32[65,8,128]{2,1,0:T(8,128)S(1)} %summed.6), channel_id=1, source_target_pairs={{0,2},{1,5},{2,0},{3,7},{4,6},{5,1},{6,4},{7,3},{8,10},{9,13},{10,... | collective-permute-start | bytes 798728 | tf_op jit(solution)/shard_map/ppermute | solution.py:262
  7.4 7.1 %collective-permute-start.5 = (f32[64,8,128]{2,1,0:T(8,128)S(1)}, f32[64,8,128]{2,1,0:T(8,128)S(1)}, u32[]{:S(2)}, u32[]{:S(2)}) collective-permute-start(f32[64,8,128]{2,1,0:T(8,128)S(1)} %summed.9), channel_id=1, source_target_pairs={{0,2},{1,5},{2,0},{3,7},{4,6},{5,1},{6,4},{7,3},{8,10},{9,13},{10,... | collective-permute-start | bytes 786440 | tf_op jit(solution)/shard_map/ppermute | solution.py:262
  11.4 5.8 %collective-permute-start.2 = (f32[33,8,128]{2,1,0:T(8,128)S(1)}, f32[33,8,128]{2,1,0:T(8,128)S(1)}, u32[]{:S(2)}, u32[]{:S(2)}) collective-permute-start(f32[33,8,128]{2,1,0:T(8,128)S(1)} %summed.7), channel_id=1, source_target_pairs={{0,4},{1,3},{2,6},{3,1},{4,0},{5,7},{6,2},{7,5},{8,12},{9,11},{10,... | collective-permute-start | bytes 405512 | tf_op jit(solution)/shard_map/ppermute | solution.py:262
  14.6 6.2 %collective-permute-start.6 = (f32[32,8,128]{2,1,0:T(8,128)S(1)}, f32[32,8,128]{2,1,0:T(8,128)S(1)}, u32[]{:S(2)}, u32[]{:S(2)}) collective-permute-start(f32[32,8,128]{2,1,0:T(8,128)S(1)} %summed.10), channel_id=1, source_target_pairs={{0,4},{1,3},{2,6},{3,1},{4,0},{5,7},{6,2},{7,5},{8,12},{9,11},{10,... | collective-permute-start | bytes 393224 | tf_op jit(solution)/shard_map/ppermute | solution.py:262
  17.2 8.9 %collective-permute-start.3 = (f32[17,8,128]{2,1,0:T(8,128)S(1)}, f32[17,8,128]{2,1,0:T(8,128)S(1)}, u32[]{:S(2)}, u32[]{:S(2)}) collective-permute-start(f32[17,8,128]{2,1,0:T(8,128)S(1)} %summed.8), channel_id=1, source_target_pairs={{0,8},{1,9},{2,10},{3,11},{4,12},{5,13},{6,14},{7,15},{8,0},{9,1},... | collective-permute-start | bytes 208904 | tf_op jit(solution)/shard_map/ppermute | solution.py:262
  20.8 5.2 %collective-permute-start.7 = (f32[16,8,128]{2,1,0:T(8,128)S(1)}, f32[16,8,128]{2,1,0:T(8,128)S(1)}, u32[]{:S(2)}, u32[]{:S(2)}) collective-permute-start(f32[16,8,128]{2,1,0:T(8,128)S(1)} %summed.11), channel_id=1, source_target_pairs={{0,8},{1,9},{2,10},{3,11},{4,12},{5,13},{6,14},{7,15},{8,0},{9,1},... | collective-permute-start | bytes 196616 | tf_op jit(solution)/shard_map/ppermute | solution.py:262
  26.1 1.3 %collective-permute-start.8 = (f32[16,8,128]{2,1,0:T(8,128)S(1)}, f32[16,8,128]{2,1,0:T(8,128)S(1)}, u32[]{:S(2)}, u32[]{:S(2)}) collective-permute-start(f32[16,8,128]{2,1,0:T(8,128)S(1)} %cross.1), channel_id=1, source_target_pairs={{0,1},{1,0},{2,3},{3,2},{4,5},{5,4},{6,7},{7,6},{8,9},{9,8},{10,11... | collective-permute-start | bytes 196616 | tf_op jit(solution)/shard_map/ppermute | solution.py:262

commit v5 on v4

--- a/solution.py
+++ b/solution.py
@@ -17,13 +17,13 @@
     second = list(first)
     if bits > 2:
         second[0], second[1] = second[1], second[0]
-    return first, second
+    return second, first
 
 
 def place_of(group, me, core, bits):
     away = [1 - (((group ^ me) >> bit) & 1) for bit in range(1, bits)]
     if bits > 2:
-        swapped = core == 1
+        swapped = core == 0
         away[:2] = [jnp.where(swapped, away[1], away[0]), jnp.where(swapped, away[0], away[1])]
     place = 0
     for value in away:

time: 28.4 us -> 27.7 us (0.975)
  waiting for transfers between devices: 9.88 us -> 9.21 us
    ppermute x9, waiting for transfers between devices: 9.88 us -> 9.21 us  [swap(): lax.ppermute(value, 'ap', [(i, i ^ 1 << bit_of[i & 1]) for i in range(dev...]
where the time goes in v5:
time: 27.7 us; the launch traced here: 27.6 us
  starting transfers between devices  14.1 us (51%)
  waiting for transfers between devices  9.21 us (33%)
  Pallas kernels  4.18 us (15%)
    ppermute x9, starting transfers between devices, swap(): lax.ppermute(value, 'ap', [(i, i ^ 1 << bit_of[i & 1]) for i in range(dev...  14.1 us
    ppermute x9, waiting for transfers between devices, swap(): lax.ppermute(value, 'ap', [(i, i ^ 1 << bit_of[i & 1]) for i in range(dev...  9.21 us
    pallas_call x1, Pallas kernels, first_products(): pl.pallas_call(functools.partial(first_kernel, bits), out_shape=(message(...  1.92 us
    pallas_call x3, Pallas kernels, next_products(): pl.pallas_call(functools.partial(next_kernel, bits, keep, chunk), out_sha...  1.31 us
    pallas_call x2, Pallas kernels, finished(): pl.pallas_call(body, out_shape=shape, in_specs=[vmem] * len(arrays), out_...  0.8 us
  transfers between devices with their start and end apart: 9, of which 6 were waited for; matrix products, arithmetic and copies ran while one was open for 0% of the time, Pallas kernels for 5%

profile of v5, /device:TPU:0, one launch (start us, length us, event | category | flops | bytes accessed | tf_op | source)
XLA Modules:
  0.0 27.6 jit_solution(9650717625564191967)
XLA Ops:
  0.0 1.9 %first_products.1 = (f32[129,8,128]{2,1,0:T(8,128)S(1)}, bf16[2,2,256,1024]{3,2,1,0:T(8,128)(2,1)S(1)}, bf16[2,1024,256]{2,1,0:T(8,128)(2,1)S(1)}, f32[2,1,256]{2,1,0:T(1,128)S(1)}) custom-call(s32[1,12]{1,0:T(1,128)} %visible.1, s32[4,512]{1,0:T(4,128)} %bitcast.3, bf16[1,12,2,32,512]{4,3,2,1,0:T(8,128)(2,1)} %channel.1, bf16[1024,512]{1,0:T(8,128)(2,1)} %bitcast.2), custom_call_target="tpu_custom_call" | custom-call | flops 536870912 | bytes 1572864 | tf_op jit(solution)/shard_map/first_products/pallas_call | solution.py:136
  1.9 0.5 %collective-permute-start = (f32[129,8,128]{2,1,0:T(8,128)S(1)}, f32[129,8,128]{2,1,0:T(8,128)S(1)}, u32[]{:S(2)}, u32[]{:S(2)}) collective-permute-start(f32[129,8,128]{2,1,0:T(8,128)S(1)} %get-tuple-element.12), channel_id=1, source_target_pairs={{0,1},{1,0},{2,3},{3,2},{4,5},{5,4},{6,7},{7,6},{8,9},{9,8},{10,11... | collective-permute-start | bytes 1585160 | tf_op jit(solution)/shard_map/ppermute | solution.py:262
  2.4 0.4 %next_products.5 = f32[128,8,128]{2,1,0:T(8,128)S(1)} custom-call(bf16[2,2,256,1024]{3,2,1,0:T(8,128)(2,1)S(1)} %get-tuple-element.9.rows, bf16[2,1024,256]{2,1,0:T(8,128)(2,1)S(1)} %get-tuple-element.10.weights, f32[2,1,256]{2,1,0:T(1,128)S(1)} %get-tuple-element.11.served), custom_call_target="tpu_custom_call" | custom-call | flops 536870912 | bytes 1572864 | tf_op jit(solution)/shard_map/next_products/pallas_call | solution.py:163
  2.9 0.1 collective-permute-start.4
  3.0 0.4 %next_products.3.refs_0_ = f32[129,8,128]{2,1,0:T(8,128)S(1)} custom-call(bf16[2,2,256,1024]{3,2,1,0:T(8,128)(2,1)S(1)} %get-tuple-element.9.rows, bf16[2,1024,256]{2,1,0:T(8,128)(2,1)S(1)} %get-tuple-element.10.weights, f32[2,1,256]{2,1,0:T(1,128)S(1)} %get-tuple-element.11.served), custom_call_target="tpu_custom_call" | custom-call | flops 536870912 | bytes 1572864 | tf_op jit(solution)/shard_map/next_products/pallas_call | solution.py:163
  3.5 0.5 %collective-permute-done.refs_1_ = f32[129,8,128]{2,1,0:T(8,128)S(1)} collective-permute-done((f32[129,8,128]{2,1,0:T(8,128)S(1)}, f32[129,8,128]{2,1,0:T(8,128)S(1)}, u32[]{:S(2)}, u32[]{:S(2)}) %collective-permute-start) | collective-permute-done | bytes 528416 | tf_op jit(solution)/shard_map/ppermute | solution.py:262
  4.0 3.0 %collective-permute-start.1 = (f32[65,8,128]{2,1,0:T(8,128)S(1)}, f32[65,8,128]{2,1,0:T(8,128)S(1)}, u32[]{:S(2)}, u32[]{:S(2)}) collective-permute-start(f32[65,8,128]{2,1,0:T(8,128)S(1)} %summed.6), channel_id=1, source_target_pairs={{0,4},{1,3},{2,6},{3,1},{4,0},{5,7},{6,2},{7,5},{8,12},{9,11},{10,... | collective-permute-start | bytes 798728 | tf_op jit(solution)/shard_map/ppermute | solution.py:262
  7.0 0.4 %next_products.4.refs_0_.refs_5_ = f32[128,8,128]{2,1,0:T(8,128)S(1)} custom-call(bf16[2,2,256,1024]{3,2,1,0:T(8,128)(2,1)S(1)} %get-tuple-element.9.rows, bf16[2,1024,256]{2,1,0:T(8,128)(2,1)S(1)} %get-tuple-element.10.weights, f32[2,1,256]{2,1,0:T(1,128)S(1)} %get-tuple-element.11.served), custom_call_target="tpu_custom_call" | custom-call | flops 536870912 | bytes 1572864 | tf_op jit(solution)/shard_map/next_products/pallas_call | solution.py:163
  7.5 0.0 collective-permute-done.4.refs_1_.refs_6_
  7.5 0.3 collective-permute-start.5
  7.8 3.6 %collective-permute-done.1.refs_2_ = f32[65,8,128]{2,1,0:T(8,128)S(1)} collective-permute-done((f32[65,8,128]{2,1,0:T(8,128)S(1)}, f32[65,8,128]{2,1,0:T(8,128)S(1)}, u32[]{:S(2)}, u32[]{:S(2)}) %collective-permute-start.1) | collective-permute-done | bytes 266272 | tf_op jit(solution)/shard_map/ppermute | solution.py:262
  11.5 2.0 %collective-permute-start.2 = (f32[33,8,128]{2,1,0:T(8,128)S(1)}, f32[33,8,128]{2,1,0:T(8,128)S(1)}, u32[]{:S(2)}, u32[]{:S(2)}) collective-permute-start(f32[33,8,128]{2,1,0:T(8,128)S(1)} %summed.7), channel_id=1, source_target_pairs={{0,2},{1,5},{2,0},{3,7},{4,6},{5,1},{6,4},{7,3},{8,10},{9,13},{10,... | collective-permute-start | bytes 405512 | tf_op jit(solution)/shard_map/ppermute | solution.py:262
  13.5 1.3 %collective-permute-done.5.refs_2_.refs_7_ = f32[64,8,128]{2,1,0:T(8,128)S(1)} collective-permute-done((f32[64,8,128]{2,1,0:T(8,128)S(1)}, f32[64,8,128]{2,1,0:T(8,128)S(1)}, u32[]{:S(2)}, u32[]{:S(2)}) %collective-permute-start.5) | collective-permute-done | bytes 262176 | tf_op jit(solution)/shard_map/ppermute | solution.py:262
  14.8 2.3 %collective-permute-start.6 = (f32[32,8,128]{2,1,0:T(8,128)S(1)}, f32[32,8,128]{2,1,0:T(8,128)S(1)}, u32[]{:S(2)}, u32[]{:S(2)}) collective-permute-start(f32[32,8,128]{2,1,0:T(8,128)S(1)} %summed.10), channel_id=1, source_target_pairs={{0,2},{1,5},{2,0},{3,7},{4,6},{5,1},{6,4},{7,3},{8,10},{9,13},{10,... | collective-permute-start | bytes 393224 | tf_op jit(solution)/shard_map/ppermute | solution.py:262
  17.0 0.0 collective-permute-done.2.refs_3_
  17.1 2.7 %collective-permute-start.3 = (f32[17,8,128]{2,1,0:T(8,128)S(1)}, f32[17,8,128]{2,1,0:T(8,128)S(1)}, u32[]{:S(2)}, u32[]{:S(2)}) collective-permute-start(f32[17,8,128]{2,1,0:T(8,128)S(1)} %summed.8), channel_id=1, source_target_pairs={{0,8},{1,9},{2,10},{3,11},{4,12},{5,13},{6,14},{7,15},{8,0},{9,1},... | collective-permute-start | bytes 208904 | tf_op jit(solution)/shard_map/ppermute | solution.py:262
  19.7 0.3 collective-permute-done.6.refs_3_.refs_8_
  20.0 3.2 %collective-permute-start.7 = (f32[16,8,128]{2,1,0:T(8,128)S(1)}, f32[16,8,128]{2,1,0:T(8,128)S(1)}, u32[]{:S(2)}, u32[]{:S(2)}) collective-permute-start(f32[16,8,128]{2,1,0:T(8,128)S(1)} %summed.11), channel_id=1, source_target_pairs={{0,8},{1,9},{2,10},{3,11},{4,12},{5,13},{6,14},{7,15},{8,0},{9,1},... | collective-permute-start | bytes 196616 | tf_op jit(solution)/shard_map/ppermute | solution.py:262
  23.2 2.2 %collective-permute-done.7.refs_9_ = f32[16,8,128]{2,1,0:T(8,128)S(1)} collective-permute-done((f32[16,8,128]{2,1,0:T(8,128)S(1)}, f32[16,8,128]{2,1,0:T(8,128)S(1)}, u32[]{:S(2)}, u32[]{:S(2)}) %collective-permute-start.7) | collective-permute-done | bytes 65568 | tf_op jit(solution)/shard_map/ppermute | solution.py:262
  25.4 0.0 collective-permute-done.3.refs_4_
  25.5 0.1 collective-permute-start.8
  25.6 1.2 %collective-permute-done.8.refs_10_ = f32[16,8,128]{2,1,0:T(8,128)S(1)} collective-permute-done((f32[16,8,128]{2,1,0:T(8,128)S(1)}, f32[16,8,128]{2,1,0:T(8,128)S(1)}, u32[]{:S(2)}, u32[]{:S(2)}) %collective-permute-start.8) | collective-permute-done | bytes 65568 | tf_op jit(solution)/shard_map/ppermute | solution.py:262
  26.8 0.8 %finish.1 = f32[32,2,512]{2,1,0:T(2,128)} custom-call(f32[129,8,128]{2,1,0:T(8,128)S(1)} %next_products.3.refs_0_, f32[129,8,128]{2,1,0:T(8,128)S(1)} %collective-permute-done.refs_1_, f32[65,8,128]{2,1,0:T(8,128)S(1)} %collective-permute-done.1.refs_2_, f32[33,8,128]{2,1,0:T(8,128)S(1)} %collective-permute-done.2.refs_3_, ...), custom_call_target="tpu_custom_call" | custom-call | tf_op jit(solution)/shard_map/finish/pallas_call | solution.py:242
  (7 shorter events, 0.2 us)
Async XLA Ops:
  1.9 2.1 %collective-permute-start = (f32[129,8,128]{2,1,0:T(8,128)S(1)}, f32[129,8,128]{2,1,0:T(8,128)S(1)}, u32[]{:S(2)}, u32[]{:S(2)}) collective-permute-start(f32[129,8,128]{2,1,0:T(8,128)S(1)} %get-tuple-element.12), channel_id=1, source_target_pairs={{0,1},{1,0},{2,3},{3,2},{4,5},{5,4},{6,7},{7,6},{8,9},{9,8},{10,11... | collective-permute-start | bytes 1585160 | tf_op jit(solution)/shard_map/ppermute | solution.py:262
  2.9 4.6 %collective-permute-start.4 = (f32[128,8,128]{2,1,0:T(8,128)S(1)}, f32[128,8,128]{2,1,0:T(8,128)S(1)}, u32[]{:S(2)}, u32[]{:S(2)}) collective-permute-start(f32[128,8,128]{2,1,0:T(8,128)S(1)} %next_products.5), channel_id=1, source_target_pairs={{0,1},{1,0},{2,3},{3,2},{4,5},{5,4},{6,7},{7,6},{8,9},{9,8},{10,11... | collective-permute-start | bytes 1572872 | tf_op jit(solution)/shard_map/ppermute | solution.py:262
  4.0 7.4 %collective-permute-start.1 = (f32[65,8,128]{2,1,0:T(8,128)S(1)}, f32[65,8,128]{2,1,0:T(8,128)S(1)}, u32[]{:S(2)}, u32[]{:S(2)}) collective-permute-start(f32[65,8,128]{2,1,0:T(8,128)S(1)} %summed.6), channel_id=1, source_target_pairs={{0,4},{1,3},{2,6},{3,1},{4,0},{5,7},{6,2},{7,5},{8,12},{9,11},{10,... | collective-permute-start | bytes 798728 | tf_op jit(solution)/shard_map/ppermute | solution.py:262
  7.5 7.2 %collective-permute-start.5 = (f32[64,8,128]{2,1,0:T(8,128)S(1)}, f32[64,8,128]{2,1,0:T(8,128)S(1)}, u32[]{:S(2)}, u32[]{:S(2)}) collective-permute-start(f32[64,8,128]{2,1,0:T(8,128)S(1)} %summed.9), channel_id=1, source_target_pairs={{0,4},{1,3},{2,6},{3,1},{4,0},{5,7},{6,2},{7,5},{8,12},{9,11},{10,... | collective-permute-start | bytes 786440 | tf_op jit(solution)/shard_map/ppermute | solution.py:262
  11.5 5.6 %collective-permute-start.2 = (f32[33,8,128]{2,1,0:T(8,128)S(1)}, f32[33,8,128]{2,1,0:T(8,128)S(1)}, u32[]{:S(2)}, u32[]{:S(2)}) collective-permute-start(f32[33,8,128]{2,1,0:T(8,128)S(1)} %summed.7), channel_id=1, source_target_pairs={{0,2},{1,5},{2,0},{3,7},{4,6},{5,1},{6,4},{7,3},{8,10},{9,13},{10,... | collective-permute-start | bytes 405512 | tf_op jit(solution)/shard_map/ppermute | solution.py:262
  14.8 5.2 %collective-permute-start.6 = (f32[32,8,128]{2,1,0:T(8,128)S(1)}, f32[32,8,128]{2,1,0:T(8,128)S(1)}, u32[]{:S(2)}, u32[]{:S(2)}) collective-permute-start(f32[32,8,128]{2,1,0:T(8,128)S(1)} %summed.10), channel_id=1, source_target_pairs={{0,2},{1,5},{2,0},{3,7},{4,6},{5,1},{6,4},{7,3},{8,10},{9,13},{10,... | collective-permute-start | bytes 393224 | tf_op jit(solution)/shard_map/ppermute | solution.py:262
  17.1 8.4 %collective-permute-start.3 = (f32[17,8,128]{2,1,0:T(8,128)S(1)}, f32[17,8,128]{2,1,0:T(8,128)S(1)}, u32[]{:S(2)}, u32[]{:S(2)}) collective-permute-start(f32[17,8,128]{2,1,0:T(8,128)S(1)} %summed.8), channel_id=1, source_target_pairs={{0,8},{1,9},{2,10},{3,11},{4,12},{5,13},{6,14},{7,15},{8,0},{9,1},... | collective-permute-start | bytes 208904 | tf_op jit(solution)/shard_map/ppermute | solution.py:262
  20.0 5.4 %collective-permute-start.7 = (f32[16,8,128]{2,1,0:T(8,128)S(1)}, f32[16,8,128]{2,1,0:T(8,128)S(1)}, u32[]{:S(2)}, u32[]{:S(2)}) collective-permute-start(f32[16,8,128]{2,1,0:T(8,128)S(1)} %summed.11), channel_id=1, source_target_pairs={{0,8},{1,9},{2,10},{3,11},{4,12},{5,13},{6,14},{7,15},{8,0},{9,1},... | collective-permute-start | bytes 196616 | tf_op jit(solution)/shard_map/ppermute | solution.py:262
  25.5 1.3 %collective-permute-start.8 = (f32[16,8,128]{2,1,0:T(8,128)S(1)}, f32[16,8,128]{2,1,0:T(8,128)S(1)}, u32[]{:S(2)}, u32[]{:S(2)}) collective-permute-start(f32[16,8,128]{2,1,0:T(8,128)S(1)} %cross.1), channel_id=1, source_target_pairs={{0,1},{1,0},{2,3},{3,2},{4,5},{5,4},{6,7},{7,6},{8,9},{9,8},{10,11... | collective-permute-start | bytes 196616 | tf_op jit(solution)/shard_map/ppermute | solution.py:262

commit v6 on v5

--- a/solution.py
+++ b/solution.py
@@ -20,10 +20,10 @@
     return second, first
 
 
-def place_of(group, me, core, bits):
+def place_of(group, me, core, chunk, bits):
     away = [1 - (((group ^ me) >> bit) & 1) for bit in range(1, bits)]
     if bits > 2:
-        swapped = core == 0
+        swapped = core == chunk % 2
         away[:2] = [jnp.where(swapped, away[1], away[0]), jnp.where(swapped, away[0], away[1])]
     place = 0
     for value in away:
@@ -87,9 +87,9 @@
     loads[1].wait()
     for v in range(held):
         for keep in range(2):
-            place = place_of(seen[0, v], me, core if keep else 1 - core, bits)
-            at = pl.ds(pl.multiple_of(place * mine, mine), mine)
             for chunk in range(CHUNKS):
+                place = place_of(seen[0, v], me, core if keep else 1 - core, chunk, bits)
+                at = pl.ds(pl.multiple_of(place * mine, mine), mine)
                 part = slice(chunk * mine, (chunk + 1) * mine)
                 rows[keep, chunk, at, 0:antennas] = raw[0, v, 0, part]
                 rows[keep, chunk, at, antennas:2 * antennas] = raw[0, v, 1, part]
@@ -276,7 +276,7 @@
         count = slots * tiles
         for chunk in range(CHUNKS):
             jobs = [(left[chunk], count)] + ([(powers, 1)] if chunk == 0 else [])
-            came = swap(summed(held[chunk], jobs), (orders[0][step], orders[1][step]))
+            came = swap(summed(held[chunk], jobs), (orders[chunk % 2][step], orders[1 - chunk % 2][step]))
             left[chunk] = [(array, start + count) for array, start in left[chunk]]
             left[chunk].append((len(held[chunk]), 0))
             held[chunk].append(came)

time: 27.7 us -> 30.4 us (1.097)
  waiting for transfers between devices: 9.21 us -> 11.7 us
    ppermute x9, waiting for transfers between devices: 9.21 us -> 11.7 us  [swap(): lax.ppermute(value, 'ap', [(i, i ^ 1 << bit_of[i & 1]) for i in range(dev...]
  transfers between devices with their start and end apart: 9 -> 9, of which waited for: 6 -> 5; matrix products, arithmetic and copies ran while one was open for 0% -> 0% of each run, Pallas kernels for 5% -> 5%
where the time goes in v6:
time: 30.4 us; the launch traced here: 30.3 us
  starting transfers between devices  14.1 us (46%)
  waiting for transfers between devices  11.7 us (38%)
  Pallas kernels  4.33 us (14%)
    ppermute x9, starting transfers between devices, swap(): lax.ppermute(value, 'ap', [(i, i ^ 1 << bit_of[i & 1]) for i in range(dev...  14.1 us
    ppermute x9, waiting for transfers between devices, swap(): lax.ppermute(value, 'ap', [(i, i ^ 1 << bit_of[i & 1]) for i in range(dev...  11.7 us
    pallas_call x1, Pallas kernels, first_products(): pl.pallas_call(functools.partial(first_kernel, bits), out_shape=(message(...  2.07 us
    pallas_call x3, Pallas kernels, next_products(): pl.pallas_call(functools.partial(next_kernel, bits, keep, chunk), out_sha...  1.31 us
    pallas_call x2, Pallas kernels, finished(): pl.pallas_call(body, out_shape=shape, in_specs=[vmem] * len(arrays), out_...  0.8 us
  transfers between devices with their start and end apart: 9, of which 5 were waited for; matrix products, arithmetic and copies ran while one was open for 0% of the time, Pallas kernels for 5%

profile of v6, /device:TPU:0, one launch (start us, length us, event | category | flops | bytes accessed | tf_op | source)
XLA Modules:
  0.0 30.3 jit_solution(8031681566505117559)
XLA Ops:
  0.0 2.1 %first_products.1 = (f32[129,8,128]{2,1,0:T(8,128)S(1)}, bf16[2,2,256,1024]{3,2,1,0:T(8,128)(2,1)S(1)}, bf16[2,1024,256]{2,1,0:T(8,128)(2,1)S(1)}, f32[2,1,256]{2,1,0:T(1,128)S(1)}) custom-call(s32[1,12]{1,0:T(1,128)} %visible.1, s32[4,512]{1,0:T(4,128)} %bitcast.3, bf16[1,12,2,32,512]{4,3,2,1,0:T(8,128)(2,1)} %channel.1, bf16[1024,512]{1,0:T(8,128)(2,1)} %bitcast.2), custom_call_target="tpu_custom_call" | custom-call | flops 536870912 | bytes 1572864 | tf_op jit(solution)/shard_map/first_products/pallas_call | solution.py:136
  2.1 0.5 %collective-permute-start = (f32[129,8,128]{2,1,0:T(8,128)S(1)}, f32[129,8,128]{2,1,0:T(8,128)S(1)}, u32[]{:S(2)}, u32[]{:S(2)}) collective-permute-start(f32[129,8,128]{2,1,0:T(8,128)S(1)} %get-tuple-element.12), channel_id=1, source_target_pairs={{0,1},{1,0},{2,3},{3,2},{4,5},{5,4},{6,7},{7,6},{8,9},{9,8},{10,11... | collective-permute-start | bytes 1585160 | tf_op jit(solution)/shard_map/ppermute | solution.py:262
  2.6 0.4 %next_products.5 = f32[128,8,128]{2,1,0:T(8,128)S(1)} custom-call(bf16[2,2,256,1024]{3,2,1,0:T(8,128)(2,1)S(1)} %get-tuple-element.9.rows, bf16[2,1024,256]{2,1,0:T(8,128)(2,1)S(1)} %get-tuple-element.10.weights, f32[2,1,256]{2,1,0:T(1,128)S(1)} %get-tuple-element.11.served), custom_call_target="tpu_custom_call" | custom-call | flops 536870912 | bytes 1572864 | tf_op jit(solution)/shard_map/next_products/pallas_call | solution.py:163
  3.0 0.1 collective-permute-start.4
  3.2 0.4 %next_products.3.refs_0_ = f32[129,8,128]{2,1,0:T(8,128)S(1)} custom-call(bf16[2,2,256,1024]{3,2,1,0:T(8,128)(2,1)S(1)} %get-tuple-element.9.rows, bf16[2,1024,256]{2,1,0:T(8,128)(2,1)S(1)} %get-tuple-element.10.weights, f32[2,1,256]{2,1,0:T(1,128)S(1)} %get-tuple-element.11.served), custom_call_target="tpu_custom_call" | custom-call | flops 536870912 | bytes 1572864 | tf_op jit(solution)/shard_map/next_products/pallas_call | solution.py:163
  3.6 0.5 %collective-permute-done.refs_1_ = f32[129,8,128]{2,1,0:T(8,128)S(1)} collective-permute-done((f32[129,8,128]{2,1,0:T(8,128)S(1)}, f32[129,8,128]{2,1,0:T(8,128)S(1)}, u32[]{:S(2)}, u32[]{:S(2)}) %collective-permute-start) | collective-permute-done | bytes 528416 | tf_op jit(solution)/shard_map/ppermute | solution.py:262
  4.2 3.0 %collective-permute-start.1 = (f32[65,8,128]{2,1,0:T(8,128)S(1)}, f32[65,8,128]{2,1,0:T(8,128)S(1)}, u32[]{:S(2)}, u32[]{:S(2)}) collective-permute-start(f32[65,8,128]{2,1,0:T(8,128)S(1)} %summed.6), channel_id=1, source_target_pairs={{0,4},{1,3},{2,6},{3,1},{4,0},{5,7},{6,2},{7,5},{8,12},{9,11},{10,... | collective-permute-start | bytes 798728 | tf_op jit(solution)/shard_map/ppermute | solution.py:262
  7.2 0.4 %next_products.4.refs_0_.refs_5_ = f32[128,8,128]{2,1,0:T(8,128)S(1)} custom-call(bf16[2,2,256,1024]{3,2,1,0:T(8,128)(2,1)S(1)} %get-tuple-element.9.rows, bf16[2,1024,256]{2,1,0:T(8,128)(2,1)S(1)} %get-tuple-element.10.weights, f32[2,1,256]{2,1,0:T(1,128)S(1)} %get-tuple-element.11.served), custom_call_target="tpu_custom_call" | custom-call | flops 536870912 | bytes 1572864 | tf_op jit(solution)/shard_map/next_products/pallas_call | solution.py:163
  7.6 0.0 collective-permute-done.4.refs_1_.refs_6_
  7.7 1.6 %collective-permute-start.5 = (f32[64,8,128]{2,1,0:T(8,128)S(1)}, f32[64,8,128]{2,1,0:T(8,128)S(1)}, u32[]{:S(2)}, u32[]{:S(2)}) collective-permute-start(f32[64,8,128]{2,1,0:T(8,128)S(1)} %summed.9), channel_id=1, source_target_pairs={{0,2},{1,5},{2,0},{3,7},{4,6},{5,1},{6,4},{7,3},{8,10},{9,13},{10,... | collective-permute-start | bytes 786440 | tf_op jit(solution)/shard_map/ppermute | solution.py:262
  9.2 3.8 %collective-permute-done.1.refs_2_ = f32[65,8,128]{2,1,0:T(8,128)S(1)} collective-permute-done((f32[65,8,128]{2,1,0:T(8,128)S(1)}, f32[65,8,128]{2,1,0:T(8,128)S(1)}, u32[]{:S(2)}, u32[]{:S(2)}) %collective-permute-start.1) | collective-permute-done | bytes 266272 | tf_op jit(solution)/shard_map/ppermute | solution.py:262
  13.1 3.3 %collective-permute-start.2 = (f32[33,8,128]{2,1,0:T(8,128)S(1)}, f32[33,8,128]{2,1,0:T(8,128)S(1)}, u32[]{:S(2)}, u32[]{:S(2)}) collective-permute-start(f32[33,8,128]{2,1,0:T(8,128)S(1)} %summed.7), channel_id=1, source_target_pairs={{0,2},{1,5},{2,0},{3,7},{4,6},{5,1},{6,4},{7,3},{8,10},{9,13},{10,... | collective-permute-start | bytes 405512 | tf_op jit(solution)/shard_map/ppermute | solution.py:262
  16.4 0.0 collective-permute-done.5.refs_2_.refs_7_
  16.4 1.6 %collective-permute-start.6 = (f32[32,8,128]{2,1,0:T(8,128)S(1)}, f32[32,8,128]{2,1,0:T(8,128)S(1)}, u32[]{:S(2)}, u32[]{:S(2)}) collective-permute-start(f32[32,8,128]{2,1,0:T(8,128)S(1)} %summed.10), channel_id=1, source_target_pairs={{0,4},{1,3},{2,6},{3,1},{4,0},{5,7},{6,2},{7,5},{8,12},{9,11},{10,... | collective-permute-start | bytes 393224 | tf_op jit(solution)/shard_map/ppermute | solution.py:262
  18.1 2.1 %collective-permute-done.2.refs_3_ = f32[33,8,128]{2,1,0:T(8,128)S(1)} collective-permute-done((f32[33,8,128]{2,1,0:T(8,128)S(1)}, f32[33,8,128]{2,1,0:T(8,128)S(1)}, u32[]{:S(2)}, u32[]{:S(2)}) %collective-permute-start.2) | collective-permute-done | bytes 135200 | tf_op jit(solution)/shard_map/ppermute | solution.py:262
  20.2 2.7 %collective-permute-start.3 = (f32[17,8,128]{2,1,0:T(8,128)S(1)}, f32[17,8,128]{2,1,0:T(8,128)S(1)}, u32[]{:S(2)}, u32[]{:S(2)}) collective-permute-start(f32[17,8,128]{2,1,0:T(8,128)S(1)} %summed.8), channel_id=1, source_target_pairs={{0,8},{1,9},{2,10},{3,11},{4,12},{5,13},{6,14},{7,15},{8,0},{9,1},... | collective-permute-start | bytes 208904 | tf_op jit(solution)/shard_map/ppermute | solution.py:262
  22.9 0.0 collective-permute-done.6.refs_3_.refs_8_
  22.9 1.2 %collective-permute-start.7 = (f32[16,8,128]{2,1,0:T(8,128)S(1)}, f32[16,8,128]{2,1,0:T(8,128)S(1)}, u32[]{:S(2)}, u32[]{:S(2)}) collective-permute-start(f32[16,8,128]{2,1,0:T(8,128)S(1)} %summed.11), channel_id=1, source_target_pairs={{0,8},{1,9},{2,10},{3,11},{4,12},{5,13},{6,14},{7,15},{8,0},{9,1},... | collective-permute-start | bytes 196616 | tf_op jit(solution)/shard_map/ppermute | solution.py:262
  24.1 4.0 %collective-permute-done.7.refs_9_ = f32[16,8,128]{2,1,0:T(8,128)S(1)} collective-permute-done((f32[16,8,128]{2,1,0:T(8,128)S(1)}, f32[16,8,128]{2,1,0:T(8,128)S(1)}, u32[]{:S(2)}, u32[]{:S(2)}) %collective-permute-start.7) | collective-permute-done | bytes 65568 | tf_op jit(solution)/shard_map/ppermute | solution.py:262
  28.2 0.0 collective-permute-done.3.refs_4_
  28.2 0.1 collective-permute-start.8
  28.3 1.2 %collective-permute-done.8.refs_10_ = f32[16,8,128]{2,1,0:T(8,128)S(1)} collective-permute-done((f32[16,8,128]{2,1,0:T(8,128)S(1)}, f32[16,8,128]{2,1,0:T(8,128)S(1)}, u32[]{:S(2)}, u32[]{:S(2)}) %collective-permute-start.8) | collective-permute-done | bytes 65568 | tf_op jit(solution)/shard_map/ppermute | solution.py:262
  29.5 0.8 %finish.1 = f32[32,2,512]{2,1,0:T(2,128)} custom-call(f32[129,8,128]{2,1,0:T(8,128)S(1)} %next_products.3.refs_0_, f32[129,8,128]{2,1,0:T(8,128)S(1)} %collective-permute-done.refs_1_, f32[65,8,128]{2,1,0:T(8,128)S(1)} %collective-permute-done.1.refs_2_, f32[33,8,128]{2,1,0:T(8,128)S(1)} %collective-permute-done.2.refs_3_, ...), custom_call_target="tpu_custom_call" | custom-call | tf_op jit(solution)/shard_map/finish/pallas_call | solution.py:242
  (7 shorter events, 0.2 us)
Async XLA Ops:
  2.1 2.1 %collective-permute-start = (f32[129,8,128]{2,1,0:T(8,128)S(1)}, f32[129,8,128]{2,1,0:T(8,128)S(1)}, u32[]{:S(2)}, u32[]{:S(2)}) collective-permute-start(f32[129,8,128]{2,1,0:T(8,128)S(1)} %get-tuple-element.12), channel_id=1, source_target_pairs={{0,1},{1,0},{2,3},{3,2},{4,5},{5,4},{6,7},{7,6},{8,9},{9,8},{10,11... | collective-permute-start | bytes 1585160 | tf_op jit(solution)/shard_map/ppermute | solution.py:262
  3.0 4.6 %collective-permute-start.4 = (f32[128,8,128]{2,1,0:T(8,128)S(1)}, f32[128,8,128]{2,1,0:T(8,128)S(1)}, u32[]{:S(2)}, u32[]{:S(2)}) collective-permute-start(f32[128,8,128]{2,1,0:T(8,128)S(1)} %next_products.5), channel_id=1, source_target_pairs={{0,1},{1,0},{2,3},{3,2},{4,5},{5,4},{6,7},{7,6},{8,9},{9,8},{10,11... | collective-permute-start | bytes 1572872 | tf_op jit(solution)/shard_map/ppermute | solution.py:262
  4.2 8.9 %collective-permute-start.1 = (f32[65,8,128]{2,1,0:T(8,128)S(1)}, f32[65,8,128]{2,1,0:T(8,128)S(1)}, u32[]{:S(2)}, u32[]{:S(2)}) collective-permute-start(f32[65,8,128]{2,1,0:T(8,128)S(1)} %summed.6), channel_id=1, source_target_pairs={{0,4},{1,3},{2,6},{3,1},{4,0},{5,7},{6,2},{7,5},{8,12},{9,11},{10,... | collective-permute-start | bytes 798728 | tf_op jit(solution)/shard_map/ppermute | solution.py:262
  7.7 8.7 %collective-permute-start.5 = (f32[64,8,128]{2,1,0:T(8,128)S(1)}, f32[64,8,128]{2,1,0:T(8,128)S(1)}, u32[]{:S(2)}, u32[]{:S(2)}) collective-permute-start(f32[64,8,128]{2,1,0:T(8,128)S(1)} %summed.9), channel_id=1, source_target_pairs={{0,2},{1,5},{2,0},{3,7},{4,6},{5,1},{6,4},{7,3},{8,10},{9,13},{10,... | collective-permute-start | bytes 786440 | tf_op jit(solution)/shard_map/ppermute | solution.py:262
  13.1 7.2 %collective-permute-start.2 = (f32[33,8,128]{2,1,0:T(8,128)S(1)}, f32[33,8,128]{2,1,0:T(8,128)S(1)}, u32[]{:S(2)}, u32[]{:S(2)}) collective-permute-start(f32[33,8,128]{2,1,0:T(8,128)S(1)} %summed.7), channel_id=1, source_target_pairs={{0,2},{1,5},{2,0},{3,7},{4,6},{5,1},{6,4},{7,3},{8,10},{9,13},{10,... | collective-permute-start | bytes 405512 | tf_op jit(solution)/shard_map/ppermute | solution.py:262
  16.4 6.5 %collective-permute-start.6 = (f32[32,8,128]{2,1,0:T(8,128)S(1)}, f32[32,8,128]{2,1,0:T(8,128)S(1)}, u32[]{:S(2)}, u32[]{:S(2)}) collective-permute-start(f32[32,8,128]{2,1,0:T(8,128)S(1)} %summed.10), channel_id=1, source_target_pairs={{0,4},{1,3},{2,6},{3,1},{4,0},{5,7},{6,2},{7,5},{8,12},{9,11},{10,... | collective-permute-start | bytes 393224 | tf_op jit(solution)/shard_map/ppermute | solution.py:262
  20.2 7.9 %collective-permute-start.3 = (f32[17,8,128]{2,1,0:T(8,128)S(1)}, f32[17,8,128]{2,1,0:T(8,128)S(1)}, u32[]{:S(2)}, u32[]{:S(2)}) collective-permute-start(f32[17,8,128]{2,1,0:T(8,128)S(1)} %summed.8), channel_id=1, source_target_pairs={{0,8},{1,9},{2,10},{3,11},{4,12},{5,13},{6,14},{7,15},{8,0},{9,1},... | collective-permute-start | bytes 208904 | tf_op jit(solution)/shard_map/ppermute | solution.py:262
  22.9 5.2 %collective-permute-start.7 = (f32[16,8,128]{2,1,0:T(8,128)S(1)}, f32[16,8,128]{2,1,0:T(8,128)S(1)}, u32[]{:S(2)}, u32[]{:S(2)}) collective-permute-start(f32[16,8,128]{2,1,0:T(8,128)S(1)} %summed.11), channel_id=1, source_target_pairs={{0,8},{1,9},{2,10},{3,11},{4,12},{5,13},{6,14},{7,15},{8,0},{9,1},... | collective-permute-start | bytes 196616 | tf_op jit(solution)/shard_map/ppermute | solution.py:262
  28.2 1.3 %collective-permute-start.8 = (f32[16,8,128]{2,1,0:T(8,128)S(1)}, f32[16,8,128]{2,1,0:T(8,128)S(1)}, u32[]{:S(2)}, u32[]{:S(2)}) collective-permute-start(f32[16,8,128]{2,1,0:T(8,128)S(1)} %cross.1), channel_id=1, source_target_pairs={{0,1},{1,0},{2,3},{3,2},{4,5},{5,4},{6,7},{7,6},{8,9},{9,8},{10,11... | collective-permute-start | bytes 196616 | tf_op jit(solution)/shard_map/ppermute | solution.py:262

commit v7 on v5

v7 whole, which is shorter than its diff:
```python
import functools

import jax
import jax.numpy as jnp
from jax import lax
from jax.experimental import pallas as pl
from jax.experimental.pallas import tpu as pltpu
from jax.sharding import PartitionSpec as P

epsilon = 1e-06
MIB = 1 << 20


def chip_orders(bits):
    first = list(range(1, bits))
    second = list(first)
    if bits > 2:
        second[0], second[1] = second[1], second[0]
    return second, first


def place_of(group, me, core, bits):
    away = [1 - (((group ^ me) >> bit) & 1) for bit in range(1, bits)]
    if bits > 2:
        swapped = core == 0
        away[:2] = [jnp.where(swapped, away[1], away[0]), jnp.where(swapped, away[0], away[1])]
    place = 0
    for value in away:
        place = place * 2 + value
    return place * 2 + (1 - ((group ^ core) & 1))


def other_place(place, bits):
    away = [(place >> at) & 1 for at in reversed(range(bits))]
    if bits > 2:
        away[0], away[1] = away[1], away[0]
    away[-1] = 1 - away[-1]
    out = 0
    for value in away:
        out = out * 2 + value
    return out


def late_steps(users):
    return max(users // 32, 1)


def write_products(slots, rows, weights, served, out, put_late):
    users = rows.shape[0] // slots
    antennas = rows.shape[1] // 2
    blocks, steps = weights.shape[1] // 128, users // 8
    early = steps - late_steps(users)
    group = min(slots, 16)
    for base in range(0, slots, group):
        plain = rows[base * users:(base + group) * users, :]
        turned = jnp.concatenate([-plain[:, antennas:], plain[:, :antennas]], axis=1)
        both = jnp.concatenate([plain, turned], axis=0)
        value = jnp.dot(both, weights, preferred_element_type=jnp.float32)
        value = jnp.where(served, value, 0.0)
        for half in range(2):
            for slot in range(group):
                top = (half * group + slot) * users
                for block in range(blocks):
                    piece = value[top:top + users, block * 128:(block + 1) * 128]
                    piece = piece.reshape(steps, 8, 128)
                    start = (((base + slot) * 2 + half) * blocks + block) * early
                    out[start:start + early] = piece[:early]
                    put_late(base + slot, half * blocks + block, piece[early:])


def power_tile(weights, served):
    wide = weights.astype(jnp.float32)
    power = jnp.sum(wide * wide, axis=0, keepdims=True)
    power = jnp.where(served, power, 0.0)
    blocks = power.shape[1] // 128
    pieces = [power[:, block * 128:(block + 1) * 128] for block in range(blocks)]
    return jnp.concatenate(pieces + [jnp.zeros((8 - blocks, 128), jnp.float32)], axis=0)


def first_kernel(
    bits, visible, cluster, channel, precoder,
    out, late, rows, weights, served,
    seen, names, raw, sems,
):
    me = lax.axis_index("ap")
    core = me & 1
    held, users, antennas = raw.shape[1], raw.shape[3], raw.shape[4]
    width = weights.shape[2]
    slots = 1 << bits
    loads = [
        pltpu.make_async_copy(visible, seen, sems.at[0]),
        pltpu.make_async_copy(channel, raw, sems.at[1]),
    ]
    for keep in range(2):
        start = pl.multiple_of((core if keep else 1 - core) * width, width)
        at = pl.ds(start, width)
        loads.append(pltpu.make_async_copy(cluster.at[:, at], names.at[keep], sems.at[2 + 2 * keep]))
        loads.append(pltpu.make_async_copy(precoder.at[:, at], weights.at[keep], sems.at[3 + 2 * keep]))
    for load in loads:
        load.start()
    rows[...] = jnp.zeros_like(rows)
    loads[0].wait()
    loads[1].wait()
    for v in range(held):
        for keep in range(2):
            place = place_of(seen[0, v], me, core if keep else 1 - core, bits)
            at = pl.ds(pl.multiple_of(place * users, users), users)
            rows[keep, at, 0:antennas] = raw[0, v, 0]
            rows[keep, at, antennas:2 * antennas] = raw[0, v, 1]
    for keep in range(2):
        loads[2 + 2 * keep].wait()
        here = (names[keep] == me).astype(jnp.float32)
        served[keep] = jnp.max(here, axis=0, keepdims=True)
    loads[3].wait()
    chosen, mask = weights[0], served[0] > 0.0
    count = late.shape[0] // slots

    def put_late(place, block, piece):
        start = place * count + block * piece.shape[0]
        late[start:start + piece.shape[0]] = piece

    write_products(slots, rows.at[0], chosen, mask, out, put_late)
    out[out.shape[0] - 1] = power_tile(chosen, mask)
    loads[5].wait()


def next_kernel(bits, sent, early, rows, weights, served, out, late):
    core = lax.axis_index("ap") & 1
    slots = 1 << bits
    chosen, mask = weights[1], served[1] > 0.0
    count = early.shape[0] // slots

    def put_late(place, block, piece):
        size = piece.shape[0]
        turned = jnp.where(core == 0, other_place(place, bits), place)
        start = turned * (2 * count) + core * count + block * size
        late[pl.ds(start, size)] = piece

    write_products(slots, rows.at[1], chosen, mask, out, put_late)
    for place in range(slots):
        turned = jnp.where(core == 1, other_place(place, bits), place)
        start = turned * (2 * count) + (1 - core) * count
        late[pl.ds(start, count)] = early[place * count:(place + 1) * count]
    own = power_tile(chosen, mask)
    out[out.shape[0] - 1] = own
    late[late.shape[0] - 1] = jnp.where(core == 0, own, sent[sent.shape[0] - 1])


def message(tiles):
    return jax.ShapeDtypeStruct((tiles, 8, 128), jnp.float32)


def estimate(rows, weights):
    return pl.CostEstimate(
        flops=8 * rows[1] * rows[2] * weights[2],
        bytes_accessed=rows[1] * (rows[2] * 2 + weights[2] * 8) + weights[1] * weights[2] * 2,
        transcendentals=0,
    )


def first_products(bits, visible, cluster, channel, precoder):
    users, antennas = channel.shape[3], channel.shape[4]
    width = precoder.shape[1] // 2
    slots = 1 << bits
    late = late_steps(users) * (width // 128) * 2
    early = (users // 8) * (width // 128) * 2 - late
    rows = (2, slots * users, 2 * antennas)
    weights = (2, precoder.shape[0], width)
    vmem = pl.BlockSpec(memory_space=pltpu.VMEM)
    hbm = pl.BlockSpec(memory_space=pltpu.HBM)
    operands = (visible, cluster, channel, precoder)
    return pl.pallas_call(
        functools.partial(first_kernel, bits),
        out_shape=(
            message(slots * early + 1),
            message(slots * late),
            jax.ShapeDtypeStruct(rows, jnp.bfloat16),
            jax.ShapeDtypeStruct(weights, jnp.bfloat16),
            jax.ShapeDtypeStruct((2, 1, width), jnp.float32),
        ),
        in_specs=[hbm] * 4,
        out_specs=(vmem,) * 5,
        scratch_shapes=[
            pltpu.SMEM(visible.shape, jnp.int32),
            pltpu.VMEM((2, cluster.shape[0], width), jnp.int32),
            pltpu.VMEM(channel.shape, jnp.bfloat16),
            pltpu.SemaphoreType.DMA((6,)),
        ],
        compiler_params=pltpu.CompilerParams(vmem_limit_bytes=52 * MIB if slots > 16 else 24 * MIB),
        cost_estimate=estimate(rows, weights),
        name="first_products",
    )(*[pltpu.with_memory_space_constraint(operand, pltpu.HBM) for operand in operands])


def next_products(bits, sent, early, rows, weights, served):
    slots = 1 << bits
    vmem = pl.BlockSpec(memory_space=pltpu.VMEM)
    return pl.pallas_call(
        functools.partial(next_kernel, bits),
        out_shape=(message(sent.shape[0]), message(2 * early.shape[0] + 1)),
        in_specs=[vmem] * 5,
        out_specs=(vmem, vmem),
        compiler_params=pltpu.CompilerParams(vmem_limit_bytes=52 * MIB if slots > 16 else 16 * MIB),
        cost_estimate=estimate(rows.shape, weights.shape),
        name="next_products",
    )(sent, early, rows, weights, served)


def add_up(refs, terms, count):
    total = refs[terms[0][0]][terms[0][1]:terms[0][1] + count]
    for ref, start in terms[1:]:
        total = total + refs[ref][start:start + count]
    return total


def sum_kernel(jobs, *refs):
    at = 0
    for terms, count in jobs:
        refs[-1][at:at + count] = add_up(refs, terms, count)
        at += count


def summed(arrays, jobs):
    size = sum(count for _, count in jobs)
    vmem = pl.BlockSpec(memory_space=pltpu.VMEM)
    reads = sum(len(terms) * count for terms, count in jobs)
    return pl.pallas_call(
        functools.partial(sum_kernel, jobs),
        out_shape=message(size),
        in_specs=[vmem] * len(arrays),
        out_specs=vmem,
        compiler_params=pltpu.CompilerParams(vmem_limit_bytes=8 * MIB),
        cost_estimate=pl.CostEstimate(
            flops=reads * 1024, bytes_accessed=(reads + size) * 4096, transcendentals=0
        ),
        name="summed",
    )(*arrays)


def scaled_slot(refs, terms, scales, blocks, steps):
    total = add_up(refs, terms, 2 * len(scales) * blocks * steps)
    pieces = []
    for side, scale in enumerate(scales):
        for half in range(2):
            for block in range(blocks):
                start = ((side * 2 + half) * blocks + block) * steps
                factor = scale[block:block + 1, :].reshape(1, 1, 128)
                piece = total[start:start + steps]
                pieces.append(jnp.where(factor > 0.0, piece * factor, 0.0))
    return jnp.concatenate(pieces, axis=0)


def column_scale(refs, powers):
    return lax.rsqrt(add_up(refs, powers, 1)[0] + epsilon)


def both_slots(plan, blocks, steps, refs):
    (early, early_powers), (late, late_powers) = plan
    own, first = column_scale(refs, early_powers), column_scale(refs, late_powers)
    return (
        scaled_slot(refs, early, [own], blocks, steps[0]),
        scaled_slot(refs, late, [first, own], blocks, steps[1]),
    )


def cross_kernel(plan, blocks, steps, *refs):
    early, late = both_slots(plan, blocks, steps, refs)
    refs[-1][:early.shape[0]] = early
    refs[-1][early.shape[0]:] = late


def final_kernel(plan, blocks, steps, *refs):
    crossed, out = refs[-2], refs[-1]
    core = lax.axis_index("ap") & 1
    early, late = both_slots(plan, blocks, steps, refs)
    size = early.shape[0]
    late = jnp.where(core == 1, late, crossed[size:size + late.shape[0]])
    middle = steps[0] * 8

    def put(value, side, first, rows):
        count = rows // 8
        for half in range(2):
            for block in range(blocks):
                start = (half * blocks + block) * count
                left = pl.multiple_of((side * blocks + block) * 128, 128)
                piece = value[start:start + count].reshape(rows, 128)
                out[first:first + rows, half, pl.ds(left, 128)] = piece

    put(early, core, 0, middle)
    put(crossed[:size], 1 - core, 0, middle)
    for side in range(2):
        count = late.shape[0] // 2
        put(late[side * count:(side + 1) * count], side, middle, steps[1] * 8)


def finished(body, name, arrays, shape):
    vmem = pl.BlockSpec(memory_space=pltpu.VMEM)
    return pl.pallas_call(
        body,
        out_shape=shape,
        in_specs=[vmem] * len(arrays),
        out_specs=vmem,
        compiler_params=pltpu.CompilerParams(vmem_limit_bytes=8 * MIB),
        name=name,
    )(*arrays)


def on_device(channel, precoder, visible, cluster):
    devices = lax.axis_size("ap")
    bits = devices.bit_length() - 1
    users, columns = channel.shape[3], precoder.shape[2]
    blocks = columns // 2 // 128
    steps = (users // 8 - late_steps(users), late_steps(users))
    tiles = (2 * blocks * steps[0], 4 * blocks * steps[1])
    orders = chip_orders(bits)
    flat = precoder.reshape(-1, columns)

    def swap(value, bit_of, cores=(0, 1)):
        pairs = [(i, i ^ (1 << bit_of[i & 1])) for i in range(devices) if i & 1 in cores]
        return lax.ppermute(value, "ap", pairs)

    sent, early, rows, weights, served = first_products(bits, visible, cluster.T, channel, flat)
    got = swap(sent, (0, 0))
    kept, late = next_products(bits, sent, early, rows, weights, served)
    held = [[kept, got], [late, swap(late, (0, 0), (0,))]]
    slots = devices
    left = [[(0, 0), (1, 0)] for _ in range(2)]
    powers = [[(0, slots * count), (1, slots * count)] for count in tiles]
    for step in range(bits - 1):
        slots //= 2
        for chunk in range(2):
            count = slots * tiles[chunk]
            jobs = [(left[chunk], count), (powers[chunk], 1)]
            came = swap(
                summed(held[chunk], jobs), (orders[0][step], orders[1][step]), (0, 1)[chunk:]
            )
            left[chunk] = [(array, start + count) for array, start in left[chunk]]
            left[chunk].append((len(held[chunk]), 0))
            powers[chunk] = powers[chunk] + [(len(held[chunk]), count)]
            held[chunk].append(came)
    arrays = held[0] + held[1]
    other, own, base = [], [], 0
    for chunk in range(2):
        here = [(base + array, start) for array, start in powers[chunk]]
        other.append(([(base + array, start) for array, start in left[chunk]], here))
        own.append(([(base + array, start + tiles[chunk]) for array, start in left[chunk]], here))
        base += len(held[chunk])
    cross = finished(
        functools.partial(cross_kernel, other, blocks, steps),
        "cross", arrays, message(tiles[0] + tiles[1]),
    )
    crossed = swap(cross, (0, 0))
    return finished(
        functools.partial(final_kernel, own, blocks, steps),
        "finish", arrays + [crossed], jax.ShapeDtypeStruct((users, 2, columns), jnp.float32),
    )


def solution(mesh):
    in_specs = (
        P(("parts", "ap"), None, None, None, None),
        P(None, ("parts", "ap"), None),
        P(("parts", "ap"), None),
        P("parts", None),
    )
    out_specs = P(("parts", "ap"), None, None)
    return jax.shard_map(
        on_device, mesh=mesh, in_specs=in_specs, out_specs=out_specs, check_vma=False
    )
```

time: 27.7 us -> 29.9 us (1.079)
  waiting for transfers between devices: 9.21 us -> 11.2 us
  starting transfers between devices: 14.1 us -> 14.5 us
    ppermute x9, waiting for transfers between devices: 9.21 us -> 11.2 us  [swap(): return lax.ppermute(value, 'ap', pairs)]
    pallas_call x3 -> x1, Pallas kernels: 1.31 us -> 0.71 us  [next_products(): pl.pallas_call(functools.partial(next_kernel, bits), out_shape=(message(s...]
    ppermute x9, starting transfers between devices: 14.1 us -> 14.5 us  [swap(): return lax.ppermute(value, 'ap', pairs)]
  transfers between devices with their start and end apart: 9 -> 9, of which waited for: 6 -> 4; matrix products, arithmetic and copies ran while one was open for 0% -> 0% of each run, Pallas kernels for 5% -> 3%
where the time goes in v7:
time: 29.9 us; the launch traced here: 29.7 us
  starting transfers between devices  14.5 us (48%)
  waiting for transfers between devices  11.2 us (37%)
  Pallas kernels  3.94 us (13%)
    ppermute x9, starting transfers between devices, swap(): return lax.ppermute(value, 'ap', pairs)  14.5 us
    ppermute x9, waiting for transfers between devices, swap(): return lax.ppermute(value, 'ap', pairs)  11.2 us
    pallas_call x1, Pallas kernels, first_products(): pl.pallas_call(functools.partial(first_kernel, bits), out_shape=(message(...  2.2 us
    pallas_call x2, Pallas kernels, finished(): pl.pallas_call(body, out_shape=shape, in_specs=[vmem] * len(arrays), out_...  0.81 us
    pallas_call x1, Pallas kernels, next_products(): pl.pallas_call(functools.partial(next_kernel, bits), out_shape=(message(s...  0.71 us
  transfers between devices with their start and end apart: 9, of which 4 were waited for; matrix products, arithmetic and copies ran while one was open for 0% of the time, Pallas kernels for 3%

profile of v7, /device:TPU:0, one launch (start us, length us, event | category | flops | bytes accessed | tf_op | source)
XLA Modules:
  0.0 29.7 jit_solution(4555742817453289655)
XLA Ops:
  0.0 2.2 %first_products.1 = (f32[193,8,128]{2,1,0:T(8,128)S(1)}, f32[64,8,128]{2,1,0:T(8,128)S(1)}, bf16[2,512,1024]{2,1,0:T(8,128)(2,1)S(1)}, bf16[2,1024,256]{2,1,0:T(8,128)(2,1)S(1)}, f32[2,1,256]{2,1,0:T(1,128)S(1)}) custom-call(s32[1,12]{1,0:T(1,128)} %visible.1, s32[4,512]{1,0:T(4,128)} %bitcast.3, bf16[1,12,2,32,512]{4,3,2,1,0:T(8,128)(2,1)} %channel.1, ...), custom_call_target="tpu_custom_call" | custom-call | flops 1073741824 | bytes 2621440 | tf_op jit(solution)/shard_map/first_products/pallas_call | solution.py:172
  2.2 0.5 %collective-permute-start = (f32[193,8,128]{2,1,0:T(8,128)S(1)}, f32[193,8,128]{2,1,0:T(8,128)S(1)}, u32[]{:S(2)}, u32[]{:S(2)}) collective-permute-start(f32[193,8,128]{2,1,0:T(8,128)S(1)} %get-tuple-element.12.sent), channel_id=1, source_target_pairs={{0,1},{1,0},{2,3},{3,2},{4,5},{5,4},{6,7},{7,6},{8,9},{9,8},{10,11... | collective-permute-start | bytes 2371592 | tf_op jit(solution)/shard_map/ppermute | solution.py:320
  2.7 0.7 %next_products.1 = (f32[193,8,128]{2,1,0:T(8,128)S(1)}, f32[129,8,128]{2,1,0:T(8,128)S(1)}) custom-call(f32[193,8,128]{2,1,0:T(8,128)S(1)} %get-tuple-element.12.sent, f32[64,8,128]{2,1,0:T(8,128)S(1)} %get-tuple-element.13.early, bf16[2,512,1024]{2,1,0:T(8,128)(2,1)S(1)} %get-tuple-element.14.rows, bf16[2,1024,256]{2,1,0:T(8,128)(2,1)S(1)} %get-tuple-element.15.weights, ...), custom_call_target="tpu_custom_call" | custom-call | flops 1073741824 | bytes 2621440 | tf_op jit(solution)/shard_map/next_products/pallas_call | solution.py:198
  3.4 2.0 %collective-permute-start.4 = (f32[129,8,128]{2,1,0:T(8,128)S(1)}, f32[129,8,128]{2,1,0:T(8,128)S(1)}, u32[]{:S(2)}, u32[]{:S(2)}) collective-permute-start(f32[129,8,128]{2,1,0:T(8,128)S(1)} %get-tuple-element.18.refs_0_.refs_5_), channel_id=1, source_target_pairs={{0,1},{2,3},{4,5},{6,7},{8,9},{10,11},{12,13},{14,15},{16,17},{18,... | collective-permute-start | bytes 1585160 | tf_op jit(solution)/shard_map/ppermute | solution.py:320
  5.4 0.0 collective-permute-done.refs_1_
  5.5 0.1 summed.6
  5.5 3.1 %collective-permute-start.1 = (f32[97,8,128]{2,1,0:T(8,128)S(1)}, f32[97,8,128]{2,1,0:T(8,128)S(1)}, u32[]{:S(2)}, u32[]{:S(2)}) collective-permute-start(f32[97,8,128]{2,1,0:T(8,128)S(1)} %summed.6), channel_id=1, source_target_pairs={{0,4},{1,3},{2,6},{3,1},{4,0},{5,7},{6,2},{7,5},{8,12},{9,11},{10,... | collective-permute-start | bytes 1191944 | tf_op jit(solution)/shard_map/ppermute | solution.py:320
  8.6 0.0 collective-permute-done.4.refs_1_.refs_6_
  8.6 0.7 %collective-permute-start.5 = (f32[65,8,128]{2,1,0:T(8,128)S(1)}, f32[65,8,128]{2,1,0:T(8,128)S(1)}, u32[]{:S(2)}, u32[]{:S(2)}) collective-permute-start(f32[65,8,128]{2,1,0:T(8,128)S(1)} %summed.9), channel_id=1, source_target_pairs={{1,3},{3,1},{5,7},{7,5},{9,11},{11,9},{13,15},{15,13},{17,19},{19,... | collective-permute-start | bytes 798728 | tf_op jit(solution)/shard_map/ppermute | solution.py:320
  9.3 5.1 %collective-permute-done.1.refs_2_ = f32[97,8,128]{2,1,0:T(8,128)S(1)} collective-permute-done((f32[97,8,128]{2,1,0:T(8,128)S(1)}, f32[97,8,128]{2,1,0:T(8,128)S(1)}, u32[]{:S(2)}, u32[]{:S(2)}) %collective-permute-start.1) | collective-permute-done | bytes 397344 | tf_op jit(solution)/shard_map/ppermute | solution.py:320
  14.4 2.0 %collective-permute-start.2 = (f32[49,8,128]{2,1,0:T(8,128)S(1)}, f32[49,8,128]{2,1,0:T(8,128)S(1)}, u32[]{:S(2)}, u32[]{:S(2)}) collective-permute-start(f32[49,8,128]{2,1,0:T(8,128)S(1)} %summed.7), channel_id=1, source_target_pairs={{0,2},{1,5},{2,0},{3,7},{4,6},{5,1},{6,4},{7,3},{8,10},{9,13},{10,... | collective-permute-start | bytes 602120 | tf_op jit(solution)/shard_map/ppermute | solution.py:320
  16.4 0.0 collective-permute-done.5.refs_2_.refs_7_
  16.5 0.7 %collective-permute-start.6 = (f32[33,8,128]{2,1,0:T(8,128)S(1)}, f32[33,8,128]{2,1,0:T(8,128)S(1)}, u32[]{:S(2)}, u32[]{:S(2)}) collective-permute-start(f32[33,8,128]{2,1,0:T(8,128)S(1)} %summed.10), channel_id=1, source_target_pairs={{1,5},{3,7},{5,1},{7,3},{9,13},{11,15},{13,9},{15,11},{17,21},{19,... | collective-permute-start | bytes 405512 | tf_op jit(solution)/shard_map/ppermute | solution.py:320
  17.2 3.1 %collective-permute-done.2.refs_3_ = f32[49,8,128]{2,1,0:T(8,128)S(1)} collective-permute-done((f32[49,8,128]{2,1,0:T(8,128)S(1)}, f32[49,8,128]{2,1,0:T(8,128)S(1)}, u32[]{:S(2)}, u32[]{:S(2)}) %collective-permute-start.2) | collective-permute-done | bytes 200736 | tf_op jit(solution)/shard_map/ppermute | solution.py:320
  20.3 3.1 %collective-permute-start.3 = (f32[25,8,128]{2,1,0:T(8,128)S(1)}, f32[25,8,128]{2,1,0:T(8,128)S(1)}, u32[]{:S(2)}, u32[]{:S(2)}) collective-permute-start(f32[25,8,128]{2,1,0:T(8,128)S(1)} %summed.8), channel_id=1, source_target_pairs={{0,8},{1,9},{2,10},{3,11},{4,12},{5,13},{6,14},{7,15},{8,0},{9,1},... | collective-permute-start | bytes 307208 | tf_op jit(solution)/shard_map/ppermute | solution.py:320
  23.4 0.0 collective-permute-done.6.refs_3_.refs_8_
  23.4 0.7 %collective-permute-start.7 = (f32[17,8,128]{2,1,0:T(8,128)S(1)}, f32[17,8,128]{2,1,0:T(8,128)S(1)}, u32[]{:S(2)}, u32[]{:S(2)}) collective-permute-start(f32[17,8,128]{2,1,0:T(8,128)S(1)} %summed.11), channel_id=1, source_target_pairs={{1,9},{3,11},{5,13},{7,15},{9,1},{11,3},{13,5},{15,7},{17,25},{19,... | collective-permute-start | bytes 208904 | tf_op jit(solution)/shard_map/ppermute | solution.py:320
  24.1 0.0 collective-permute-done.7.refs_9_
  24.1 2.1 %collective-permute-done.3.refs_4_ = f32[25,8,128]{2,1,0:T(8,128)S(1)} collective-permute-done((f32[25,8,128]{2,1,0:T(8,128)S(1)}, f32[25,8,128]{2,1,0:T(8,128)S(1)}, u32[]{:S(2)}, u32[]{:S(2)}) %collective-permute-start.3) | collective-permute-done | bytes 102432 | tf_op jit(solution)/shard_map/ppermute | solution.py:320
  26.2 1.8 %collective-permute-start.8 = (f32[20,8,128]{2,1,0:T(8,128)S(1)}, f32[20,8,128]{2,1,0:T(8,128)S(1)}, u32[]{:S(2)}, u32[]{:S(2)}) collective-permute-start(f32[20,8,128]{2,1,0:T(8,128)S(1)} %cross.1), channel_id=1, source_target_pairs={{0,1},{1,0},{2,3},{3,2},{4,5},{5,4},{6,7},{7,6},{8,9},{9,8},{10,11... | collective-permute-start | bytes 245768 | tf_op jit(solution)/shard_map/ppermute | solution.py:320
  28.0 0.9 %collective-permute-done.8.refs_10_ = f32[20,8,128]{2,1,0:T(8,128)S(1)} collective-permute-done((f32[20,8,128]{2,1,0:T(8,128)S(1)}, f32[20,8,128]{2,1,0:T(8,128)S(1)}, u32[]{:S(2)}, u32[]{:S(2)}) %collective-permute-start.8) | collective-permute-done | bytes 81952 | tf_op jit(solution)/shard_map/ppermute | solution.py:320
  28.9 0.8 %finish.1 = f32[32,2,512]{2,1,0:T(2,128)} custom-call(f32[193,8,128]{2,1,0:T(8,128)S(1)} %get-tuple-element.17.refs_0_, f32[193,8,128]{2,1,0:T(8,128)S(1)} %collective-permute-done.refs_1_, f32[97,8,128]{2,1,0:T(8,128)S(1)} %collective-permute-done.1.refs_2_, f32[49,8,128]{2,1,0:T(8,128)S(1)} %collective-permute-done.2.refs_3_, ...), custom_call_target="tpu_custom_call" | custom-call | tf_op jit(solution)/shard_map/finish/pallas_call | solution.py:298
  (6 shorter events, 0.2 us)
Async XLA Ops:
  2.2 3.2 %collective-permute-start = (f32[193,8,128]{2,1,0:T(8,128)S(1)}, f32[193,8,128]{2,1,0:T(8,128)S(1)}, u32[]{:S(2)}, u32[]{:S(2)}) collective-permute-start(f32[193,8,128]{2,1,0:T(8,128)S(1)} %get-tuple-element.12.sent), channel_id=1, source_target_pairs={{0,1},{1,0},{2,3},{3,2},{4,5},{5,4},{6,7},{7,6},{8,9},{9,8},{10,11... | collective-permute-start | bytes 2371592 | tf_op jit(solution)/shard_map/ppermute | solution.py:320
  3.4 5.2 %collective-permute-start.4 = (f32[129,8,128]{2,1,0:T(8,128)S(1)}, f32[129,8,128]{2,1,0:T(8,128)S(1)}, u32[]{:S(2)}, u32[]{:S(2)}) collective-permute-start(f32[129,8,128]{2,1,0:T(8,128)S(1)} %get-tuple-element.18.refs_0_.refs_5_), channel_id=1, source_target_pairs={{0,1},{2,3},{4,5},{6,7},{8,9},{10,11},{12,13},{14,15},{16,17},{18,... | collective-permute-start | bytes 1585160 | tf_op jit(solution)/shard_map/ppermute | solution.py:320
  5.5 8.9 %collective-permute-start.1 = (f32[97,8,128]{2,1,0:T(8,128)S(1)}, f32[97,8,128]{2,1,0:T(8,128)S(1)}, u32[]{:S(2)}, u32[]{:S(2)}) collective-permute-start(f32[97,8,128]{2,1,0:T(8,128)S(1)} %summed.6), channel_id=1, source_target_pairs={{0,4},{1,3},{2,6},{3,1},{4,0},{5,7},{6,2},{7,5},{8,12},{9,11},{10,... | collective-permute-start | bytes 1191944 | tf_op jit(solution)/shard_map/ppermute | solution.py:320
  8.6 7.8 %collective-permute-start.5 = (f32[65,8,128]{2,1,0:T(8,128)S(1)}, f32[65,8,128]{2,1,0:T(8,128)S(1)}, u32[]{:S(2)}, u32[]{:S(2)}) collective-permute-start(f32[65,8,128]{2,1,0:T(8,128)S(1)} %summed.9), channel_id=1, source_target_pairs={{1,3},{3,1},{5,7},{7,5},{9,11},{11,9},{13,15},{15,13},{17,19},{19,... | collective-permute-start | bytes 798728 | tf_op jit(solution)/shard_map/ppermute | solution.py:320
  14.4 5.8 %collective-permute-start.2 = (f32[49,8,128]{2,1,0:T(8,128)S(1)}, f32[49,8,128]{2,1,0:T(8,128)S(1)}, u32[]{:S(2)}, u32[]{:S(2)}) collective-permute-start(f32[49,8,128]{2,1,0:T(8,128)S(1)} %summed.7), channel_id=1, source_target_pairs={{0,2},{1,5},{2,0},{3,7},{4,6},{5,1},{6,4},{7,3},{8,10},{9,13},{10,... | collective-permute-start | bytes 602120 | tf_op jit(solution)/shard_map/ppermute | solution.py:320
  16.5 6.9 %collective-permute-start.6 = (f32[33,8,128]{2,1,0:T(8,128)S(1)}, f32[33,8,128]{2,1,0:T(8,128)S(1)}, u32[]{:S(2)}, u32[]{:S(2)}) collective-permute-start(f32[33,8,128]{2,1,0:T(8,128)S(1)} %summed.10), channel_id=1, source_target_pairs={{1,5},{3,7},{5,1},{7,3},{9,13},{11,15},{13,9},{15,11},{17,21},{19,... | collective-permute-start | bytes 405512 | tf_op jit(solution)/shard_map/ppermute | solution.py:320
  20.3 5.9 %collective-permute-start.3 = (f32[25,8,128]{2,1,0:T(8,128)S(1)}, f32[25,8,128]{2,1,0:T(8,128)S(1)}, u32[]{:S(2)}, u32[]{:S(2)}) collective-permute-start(f32[25,8,128]{2,1,0:T(8,128)S(1)} %summed.8), channel_id=1, source_target_pairs={{0,8},{1,9},{2,10},{3,11},{4,12},{5,13},{6,14},{7,15},{8,0},{9,1},... | collective-permute-start | bytes 307208 | tf_op jit(solution)/shard_map/ppermute | solution.py:320
  23.4 0.7 %collective-permute-start.7 = (f32[17,8,128]{2,1,0:T(8,128)S(1)}, f32[17,8,128]{2,1,0:T(8,128)S(1)}, u32[]{:S(2)}, u32[]{:S(2)}) collective-permute-start(f32[17,8,128]{2,1,0:T(8,128)S(1)} %summed.11), channel_id=1, source_target_pairs={{1,9},{3,11},{5,13},{7,15},{9,1},{11,3},{13,5},{15,7},{17,25},{19,... | collective-permute-start | bytes 208904 | tf_op jit(solution)/shard_map/ppermute | solution.py:320
  26.2 2.8 %collective-permute-start.8 = (f32[20,8,128]{2,1,0:T(8,128)S(1)}, f32[20,8,128]{2,1,0:T(8,128)S(1)}, u32[]{:S(2)}, u32[]{:S(2)}) collective-permute-start(f32[20,8,128]{2,1,0:T(8,128)S(1)} %cross.1), channel_id=1, source_target_pairs={{0,1},{1,0},{2,3},{3,2},{4,5},{5,4},{6,7},{7,6},{8,9},{9,8},{10,11... | collective-permute-start | bytes 245768 | tf_op jit(solution)/shard_map/ppermute | solution.py:320

commit v8 on v5

v8 whole, which is shorter than its diff:
```python
import functools

import jax
import jax.numpy as jnp
from jax import lax
from jax.experimental import pallas as pl
from jax.experimental.pallas import tpu as pltpu
from jax.sharding import PartitionSpec as P

epsilon = 1e-06
MIB = 1 << 20
CHUNKS = 2


def chip_orders(bits):
    first = list(range(1, bits))
    second = list(first)
    if bits > 2:
        second[0], second[1] = second[1], second[0]
    return second, first


def place_of(group, me, core, bits):
    away = [1 - (((group ^ me) >> bit) & 1) for bit in range(1, bits)]
    if bits > 2:
        swapped = core == 0
        away[:2] = [jnp.where(swapped, away[1], away[0]), jnp.where(swapped, away[0], away[1])]
    place = 0
    for value in away:
        place = place * 2 + value
    return place


def write_products(slots, rows, weights, served, out):
    users = rows.shape[0] // slots
    antennas = rows.shape[1] // 2
    blocks, steps = weights.shape[1] // 128, users // 8
    group = min(slots, 8)
    for base in range(0, slots, group):
        plain = rows[base * users:(base + group) * users, :]
        turned = jnp.concatenate([-plain[:, antennas:], plain[:, :antennas]], axis=1)
        both = jnp.concatenate([plain, turned], axis=0)
        value = jnp.dot(both, weights, preferred_element_type=jnp.float32)
        value = jnp.where(served, value, 0.0)
        for half in range(2):
            for slot in range(group):
                top = (half * group + slot) * users
                for block in range(blocks):
                    piece = value[top:top + users, block * 128:(block + 1) * 128]
                    start = (((base + slot) * 2 + half) * blocks + block) * steps
                    out[start:start + steps] = piece.reshape(steps, 8, 128)


def power_tile(weights, served):
    wide = weights.astype(jnp.float32)
    power = jnp.sum(wide * wide, axis=0, keepdims=True)
    power = jnp.where(served, power, 0.0)
    blocks = power.shape[1] // 128
    pieces = [power[:, block * 128:(block + 1) * 128] for block in range(blocks)]
    return jnp.concatenate(pieces + [jnp.zeros((8 - blocks, 128), jnp.float32)], axis=0)


def first_kernel(
    bits, visible, cluster, channel, precoder,
    out, rows, weights, served,
    seen, names, raw, sems,
):
    me = lax.axis_index("ap")
    held, users, antennas = raw.shape[1], raw.shape[3], raw.shape[4]
    width = weights.shape[2]
    slots = 1 << (bits - 1)
    loads = [
        pltpu.make_async_copy(visible, seen, sems.at[0]),
        pltpu.make_async_copy(channel, raw, sems.at[1]),
        pltpu.make_async_copy(cluster, names, sems.at[2]),
    ]
    for chunk in range(CHUNKS):
        at = pl.ds(chunk * width, width)
        loads.append(pltpu.make_async_copy(precoder.at[:, at], weights.at[chunk], sems.at[3 + chunk]))
    for load in loads:
        load.start()
    rows[...] = jnp.zeros_like(rows)
    loads[0].wait()
    loads[1].wait()
    for v in range(held):
        core = seen[0, v] & 1
        keep = 1 - (core ^ (me & 1))
        at = pl.ds(pl.multiple_of(place_of(seen[0, v], me, core, bits) * users, users), users)
        rows[keep, at, 0:antennas] = raw[0, v, 0]
        rows[keep, at, antennas:2 * antennas] = raw[0, v, 1]
    loads[2].wait()
    here = jnp.max((names[...] == me).astype(jnp.float32), axis=0, keepdims=True)
    for chunk in range(CHUNKS):
        served[chunk] = here[:, chunk * width:(chunk + 1) * width]
    loads[3].wait()
    chosen, mask = weights[0], served[0] > 0.0
    write_products(slots, rows.at[0], chosen, mask, out)
    out[out.shape[0] - 1] = power_tile(chosen, mask)
    for load in loads[4:]:
        load.wait()


def next_kernel(bits, keep, chunk, rows, weights, served, out):
    chosen, mask = weights[chunk], served[chunk] > 0.0
    write_products(1 << (bits - 1), rows.at[keep], chosen, mask, out)
    out[out.shape[0] - 1] = power_tile(chosen, mask)


def message(tiles):
    return jax.ShapeDtypeStruct((tiles, 8, 128), jnp.float32)


def estimate(rows, weights):
    return pl.CostEstimate(
        flops=8 * rows[1] * rows[2] * weights[2],
        bytes_accessed=rows[1] * (rows[2] * 2 + weights[2] * 8) + weights[1] * weights[2] * 2,
        transcendentals=0,
    )


def first_products(bits, visible, cluster, channel, precoder):
    users, antennas = channel.shape[3], channel.shape[4]
    width = precoder.shape[1] // CHUNKS
    slots = 1 << (bits - 1)
    tiles = (users // 8) * (width // 128) * 2
    rows = (2, slots * users, 2 * antennas)
    weights = (CHUNKS, precoder.shape[0], width)
    vmem = pl.BlockSpec(memory_space=pltpu.VMEM)
    hbm = pl.BlockSpec(memory_space=pltpu.HBM)
    operands = (visible, cluster, channel, precoder)
    return pl.pallas_call(
        functools.partial(first_kernel, bits),
        out_shape=(
            message(slots * tiles + 1),
            jax.ShapeDtypeStruct(rows, jnp.bfloat16),
            jax.ShapeDtypeStruct(weights, jnp.bfloat16),
            jax.ShapeDtypeStruct((CHUNKS, 1, width), jnp.float32),
        ),
        in_specs=[hbm] * 4,
        out_specs=(vmem,) * 4,
        scratch_shapes=[
            pltpu.SMEM(visible.shape, jnp.int32),
            pltpu.VMEM(cluster.shape, jnp.int32),
            pltpu.VMEM(channel.shape, jnp.bfloat16),
            pltpu.SemaphoreType.DMA((3 + CHUNKS,)),
        ],
        compiler_params=pltpu.CompilerParams(vmem_limit_bytes=52 * MIB if slots > 8 else 24 * MIB),
        cost_estimate=estimate(rows, weights),
        name="first_products",
    )(*[pltpu.with_memory_space_constraint(operand, pltpu.HBM) for operand in operands])


def next_products(bits, keep, chunk, rows, weights, served):
    slots = 1 << (bits - 1)
    users = rows.shape[1] // slots
    tiles = (users // 8) * (weights.shape[2] // 128) * 2
    vmem = pl.BlockSpec(memory_space=pltpu.VMEM)
    return pl.pallas_call(
        functools.partial(next_kernel, bits, keep, chunk),
        out_shape=message(slots * tiles + 1),
        in_specs=[vmem] * 3,
        out_specs=vmem,
        compiler_params=pltpu.CompilerParams(vmem_limit_bytes=48 * MIB if slots > 8 else 16 * MIB),
        cost_estimate=estimate(rows.shape, weights.shape),
        name="next_products",
    )(rows, weights, served)


def add_up(refs, terms, count):
    total = refs[terms[0][0]][terms[0][1]:terms[0][1] + count]
    for ref, start in terms[1:]:
        total = total + refs[ref][start:start + count]
    return total


def sum_kernel(jobs, *refs):
    at = 0
    for terms, count in jobs:
        refs[-1][at:at + count] = add_up(refs, terms, count)
        at += count


def summed(arrays, jobs):
    size = sum(count for _, count in jobs)
    vmem = pl.BlockSpec(memory_space=pltpu.VMEM)
    reads = sum(len(terms) * count for terms, count in jobs)
    return pl.pallas_call(
        functools.partial(sum_kernel, jobs),
        out_shape=message(size),
        in_specs=[vmem] * len(arrays),
        out_specs=vmem,
        compiler_params=pltpu.CompilerParams(vmem_limit_bytes=8 * MIB),
        cost_estimate=pl.CostEstimate(
            flops=reads * 1024, bytes_accessed=(reads + size) * 4096, transcendentals=0
        ),
        name="summed",
    )(*arrays)


def final_kernel(jobs, *refs):
    out = refs[-1]
    users, blocks = out.shape[0], out.shape[2] // 128 // CHUNKS
    steps = users // 8
    for chunk, (terms, powers) in enumerate(jobs):
        scale = lax.rsqrt(add_up(refs, powers, 1)[0] + epsilon)
        total = add_up(refs, terms, 2 * blocks * steps)
        for half in range(2):
            for block in range(blocks):
                start = (half * blocks + block) * steps
                value = total[start:start + steps].reshape(users, 128)
                factor = scale[block:block + 1, :]
                value = jnp.where(factor > 0.0, value * factor, 0.0)
                left = (chunk * blocks + block) * 128
                out[:, half, left:left + 128] = value


def finish(arrays, jobs, users, columns):
    vmem = pl.BlockSpec(memory_space=pltpu.VMEM)
    return pl.pallas_call(
        functools.partial(final_kernel, jobs),
        out_shape=jax.ShapeDtypeStruct((users, 2, columns), jnp.float32),
        in_specs=[vmem] * len(arrays),
        out_specs=vmem,
        compiler_params=pltpu.CompilerParams(vmem_limit_bytes=8 * MIB),
        name="finish",
    )(*arrays)


def on_device(channel, precoder, visible, cluster):
    devices = lax.axis_size("ap")
    bits = devices.bit_length() - 1
    users, columns = channel.shape[3], precoder.shape[2]
    tiles = (users // 8) * (columns // CHUNKS // 128) * 2
    orders = chip_orders(bits)
    flat = precoder.reshape(-1, columns)

    def swap(value, bit_of):
        return lax.ppermute(value, "ap", [(i, i ^ (1 << bit_of[i & 1])) for i in range(devices)])

    sent, rows, weights, served = first_products(bits, visible, cluster.T, channel, flat)
    got = [swap(sent, (0, 0))]
    for chunk in range(1, CHUNKS):
        got.append(swap(next_products(bits, 0, chunk, rows, weights, served), (0, 0)))
    held = [
        [next_products(bits, 1, chunk, rows, weights, served), got[chunk]] for chunk in range(CHUNKS)
    ]
    slots = devices // 2
    left = [(0, 0), (1, 0)]
    powers = [(0, slots * tiles), (1, slots * tiles)]
    for step in range(bits - 1):
        slots //= 2
        count = slots * tiles
        for mine in held:
            message_now = summed(mine, [(left, count), (powers, 1)])
            mine.append(swap(message_now, (orders[0][step], orders[1][step])))
        left = [(array, start + count) for array, start in left] + [(step + 2, 0)]
        powers = powers + [(step + 2, count)]
    jobs = []
    for chunk, mine in enumerate(held):
        base = chunk * len(mine)
        jobs.append((
            [(base + array, start) for array, start in left],
            [(base + array, start) for array, start in powers],
        ))
    return finish([array for mine in held for array in mine], jobs, users, columns)


def solution(mesh):
    in_specs = (
        P(("parts", "ap"), None, None, None, None),
        P(None, ("parts", "ap"), None),
        P(("parts", "ap"), None),
        P("parts", None),
    )
    out_specs = P(("parts", "ap"), None, None)
    return jax.shard_map(
        on_device, mesh=mesh, in_specs=in_specs, out_specs=out_specs, check_vma=False
    )
```

time: 27.7 us -> 26.9 us (0.971)
  waiting for transfers between devices: 9.21 us -> 8.17 us
  starting transfers between devices: 14.1 us -> 14.4 us
    ppermute x9 -> x8, waiting for transfers between devices: 9.21 us -> 8.17 us  [swap(): lax.ppermute(value, 'ap', [(i, i ^ 1 << bit_of[i & 1]) for i in range(dev...]
    ppermute x9 -> x8, starting transfers between devices: 14.1 us -> 14.4 us  [swap(): lax.ppermute(value, 'ap', [(i, i ^ 1 << bit_of[i & 1]) for i in range(dev...]
    pallas_call x2 -> x1, Pallas kernels: 0.8 us -> 0.78 us  [finish(): pl.pallas_call(functools.partial(final_kernel, jobs), out_shape=jax.Shape...]
  transfers between devices with their start and end apart: 9 -> 8, of which waited for: 6 -> 5; matrix products, arithmetic and copies ran while one was open for 0% -> 0% of each run, Pallas kernels for 5% -> 4%
where the time goes in v8:
time: 26.9 us; the launch traced here: 26.7 us
  starting transfers between devices  14.4 us (54%)
  waiting for transfers between devices  8.17 us (30%)
  Pallas kernels  4.06 us (15%)
    ppermute x8, starting transfers between devices, swap(): lax.ppermute(value, 'ap', [(i, i ^ 1 << bit_of[i & 1]) for i in range(dev...  14.4 us
    ppermute x8, waiting for transfers between devices, swap(): lax.ppermute(value, 'ap', [(i, i ^ 1 << bit_of[i & 1]) for i in range(dev...  8.17 us
    pallas_call x1, Pallas kernels, first_products(): pl.pallas_call(functools.partial(first_kernel, bits), out_shape=(message(...  1.8 us
    pallas_call x3, Pallas kernels, next_products(): pl.pallas_call(functools.partial(next_kernel, bits, keep, chunk), out_sha...  1.32 us
    pallas_call x1, Pallas kernels, finish(): pl.pallas_call(functools.partial(final_kernel, jobs), out_shape=jax.Shape...  0.78 us
  transfers between devices with their start and end apart: 8, of which 5 were waited for; matrix products, arithmetic and copies ran while one was open for 0% of the time, Pallas kernels for 4%

profile of v8, /device:TPU:0, one launch (start us, length us, event | category | flops | bytes accessed | tf_op | source)
XLA Modules:
  0.0 26.7 jit_solution(8667037296204053119)
XLA Ops:
  0.0 1.8 %first_products.1 = (f32[129,8,128]{2,1,0:T(8,128)S(1)}, bf16[2,256,1024]{2,1,0:T(8,128)(2,1)S(1)}, bf16[2,1024,256]{2,1,0:T(8,128)(2,1)S(1)}, f32[2,1,256]{2,1,0:T(1,128)S(1)}) custom-call(s32[1,12]{1,0:T(1,128)} %visible.1, s32[4,512]{1,0:T(4,128)} %bitcast.3, bf16[1,12,2,32,512]{4,3,2,1,0:T(8,128)(2,1)} %channel.1, bf16[1024,512]{1,0:T(8,128)(2,1)} %bitcast.2), custom_call_target="tpu_custom_call" | custom-call | flops 536870912 | bytes 1572864 | tf_op jit(solution)/shard_map/first_products/pallas_call | solution.py:131
  1.8 0.4 %next_products.5 = f32[129,8,128]{2,1,0:T(8,128)S(1)} custom-call(bf16[2,256,1024]{2,1,0:T(8,128)(2,1)S(1)} %get-tuple-element.9.rows, bf16[2,1024,256]{2,1,0:T(8,128)(2,1)S(1)} %get-tuple-element.10.weights, f32[2,1,256]{2,1,0:T(1,128)S(1)} %get-tuple-element.11.served), custom_call_target="tpu_custom_call" | custom-call | flops 536870912 | bytes 1572864 | tf_op jit(solution)/shard_map/next_products/pallas_call | solution.py:158
  2.3 0.5 %collective-permute-start.4 = (f32[129,8,128]{2,1,0:T(8,128)S(1)}, f32[129,8,128]{2,1,0:T(8,128)S(1)}, u32[]{:S(2)}, u32[]{:S(2)}) collective-permute-start(f32[129,8,128]{2,1,0:T(8,128)S(1)} %next_products.5), channel_id=1, source_target_pairs={{0,1},{1,0},{2,3},{3,2},{4,5},{5,4},{6,7},{7,6},{8,9},{9,8},{10,11... | collective-permute-start | bytes 1585160 | tf_op jit(solution)/shard_map/ppermute | solution.py:238
  2.8 0.1 collective-permute-start
  2.9 0.4 %next_products.4.refs_0_.refs_5_ = f32[129,8,128]{2,1,0:T(8,128)S(1)} custom-call(bf16[2,256,1024]{2,1,0:T(8,128)(2,1)S(1)} %get-tuple-element.9.rows, bf16[2,1024,256]{2,1,0:T(8,128)(2,1)S(1)} %get-tuple-element.10.weights, f32[2,1,256]{2,1,0:T(1,128)S(1)} %get-tuple-element.11.served), custom_call_target="tpu_custom_call" | custom-call | flops 536870912 | bytes 1572864 | tf_op jit(solution)/shard_map/next_products/pallas_call | solution.py:158
  3.3 0.4 %next_products.3.refs_0_ = f32[129,8,128]{2,1,0:T(8,128)S(1)} custom-call(bf16[2,256,1024]{2,1,0:T(8,128)(2,1)S(1)} %get-tuple-element.9.rows, bf16[2,1024,256]{2,1,0:T(8,128)(2,1)S(1)} %get-tuple-element.10.weights, f32[2,1,256]{2,1,0:T(1,128)S(1)} %get-tuple-element.11.served), custom_call_target="tpu_custom_call" | custom-call | flops 536870912 | bytes 1572864 | tf_op jit(solution)/shard_map/next_products/pallas_call | solution.py:158
  3.7 0.6 %collective-permute-done.4.refs_1_.refs_6_ = f32[129,8,128]{2,1,0:T(8,128)S(1)} collective-permute-done((f32[129,8,128]{2,1,0:T(8,128)S(1)}, f32[129,8,128]{2,1,0:T(8,128)S(1)}, u32[]{:S(2)}, u32[]{:S(2)}) %collective-permute-start.4) | collective-permute-done | bytes 528416 | tf_op jit(solution)/shard_map/ppermute | solution.py:238
  4.4 3.0 %collective-permute-start.5 = (f32[65,8,128]{2,1,0:T(8,128)S(1)}, f32[65,8,128]{2,1,0:T(8,128)S(1)}, u32[]{:S(2)}, u32[]{:S(2)}) collective-permute-start(f32[65,8,128]{2,1,0:T(8,128)S(1)} %summed.9), channel_id=1, source_target_pairs={{0,4},{1,3},{2,6},{3,1},{4,0},{5,7},{6,2},{7,5},{8,12},{9,11},{10,... | collective-permute-start | bytes 798728 | tf_op jit(solution)/shard_map/ppermute | solution.py:238
  7.4 0.0 collective-permute-done.refs_1_
  7.4 0.7 %collective-permute-start.1 = (f32[65,8,128]{2,1,0:T(8,128)S(1)}, f32[65,8,128]{2,1,0:T(8,128)S(1)}, u32[]{:S(2)}, u32[]{:S(2)}) collective-permute-start(f32[65,8,128]{2,1,0:T(8,128)S(1)} %summed.6), channel_id=1, source_target_pairs={{0,4},{1,3},{2,6},{3,1},{4,0},{5,7},{6,2},{7,5},{8,12},{9,11},{10,... | collective-permute-start | bytes 798728 | tf_op jit(solution)/shard_map/ppermute | solution.py:238
  8.1 3.6 %collective-permute-done.5.refs_2_.refs_7_ = f32[65,8,128]{2,1,0:T(8,128)S(1)} collective-permute-done((f32[65,8,128]{2,1,0:T(8,128)S(1)}, f32[65,8,128]{2,1,0:T(8,128)S(1)}, u32[]{:S(2)}, u32[]{:S(2)}) %collective-permute-start.5) | collective-permute-done | bytes 266272 | tf_op jit(solution)/shard_map/ppermute | solution.py:238
  11.8 2.0 %collective-permute-start.6 = (f32[33,8,128]{2,1,0:T(8,128)S(1)}, f32[33,8,128]{2,1,0:T(8,128)S(1)}, u32[]{:S(2)}, u32[]{:S(2)}) collective-permute-start(f32[33,8,128]{2,1,0:T(8,128)S(1)} %summed.10), channel_id=1, source_target_pairs={{0,2},{1,5},{2,0},{3,7},{4,6},{5,1},{6,4},{7,3},{8,10},{9,13},{10,... | collective-permute-start | bytes 405512 | tf_op jit(solution)/shard_map/ppermute | solution.py:238
  13.8 1.4 %collective-permute-done.1.refs_2_ = f32[65,8,128]{2,1,0:T(8,128)S(1)} collective-permute-done((f32[65,8,128]{2,1,0:T(8,128)S(1)}, f32[65,8,128]{2,1,0:T(8,128)S(1)}, u32[]{:S(2)}, u32[]{:S(2)}) %collective-permute-start.1) | collective-permute-done | bytes 266272 | tf_op jit(solution)/shard_map/ppermute | solution.py:238
  15.2 2.3 %collective-permute-start.2 = (f32[33,8,128]{2,1,0:T(8,128)S(1)}, f32[33,8,128]{2,1,0:T(8,128)S(1)}, u32[]{:S(2)}, u32[]{:S(2)}) collective-permute-start(f32[33,8,128]{2,1,0:T(8,128)S(1)} %summed.7), channel_id=1, source_target_pairs={{0,2},{1,5},{2,0},{3,7},{4,6},{5,1},{6,4},{7,3},{8,10},{9,13},{10,... | collective-permute-start | bytes 405512 | tf_op jit(solution)/shard_map/ppermute | solution.py:238
  17.5 0.0 collective-permute-done.6.refs_3_.refs_8_
  17.5 2.7 %collective-permute-start.7 = (f32[17,8,128]{2,1,0:T(8,128)S(1)}, f32[17,8,128]{2,1,0:T(8,128)S(1)}, u32[]{:S(2)}, u32[]{:S(2)}) collective-permute-start(f32[17,8,128]{2,1,0:T(8,128)S(1)} %summed.11), channel_id=1, source_target_pairs={{0,8},{1,9},{2,10},{3,11},{4,12},{5,13},{6,14},{7,15},{8,0},{9,1},... | collective-permute-start | bytes 208904 | tf_op jit(solution)/shard_map/ppermute | solution.py:238
  20.1 0.3 %collective-permute-done.2.refs_3_ = f32[33,8,128]{2,1,0:T(8,128)S(1)} collective-permute-done((f32[33,8,128]{2,1,0:T(8,128)S(1)}, f32[33,8,128]{2,1,0:T(8,128)S(1)}, u32[]{:S(2)}, u32[]{:S(2)}) %collective-permute-start.2) | collective-permute-done | bytes 135200 | tf_op jit(solution)/shard_map/ppermute | solution.py:238
  20.5 3.2 %collective-permute-start.3 = (f32[17,8,128]{2,1,0:T(8,128)S(1)}, f32[17,8,128]{2,1,0:T(8,128)S(1)}, u32[]{:S(2)}, u32[]{:S(2)}) collective-permute-start(f32[17,8,128]{2,1,0:T(8,128)S(1)} %summed.8), channel_id=1, source_target_pairs={{0,8},{1,9},{2,10},{3,11},{4,12},{5,13},{6,14},{7,15},{8,0},{9,1},... | collective-permute-start | bytes 208904 | tf_op jit(solution)/shard_map/ppermute | solution.py:238
  23.7 0.0 collective-permute-done.7.refs_9_
  23.7 2.3 %collective-permute-done.3.refs_4_ = f32[17,8,128]{2,1,0:T(8,128)S(1)} collective-permute-done((f32[17,8,128]{2,1,0:T(8,128)S(1)}, f32[17,8,128]{2,1,0:T(8,128)S(1)}, u32[]{:S(2)}, u32[]{:S(2)}) %collective-permute-start.3) | collective-permute-done | bytes 69664 | tf_op jit(solution)/shard_map/ppermute | solution.py:238
  25.9 0.8 %finish.1 = f32[32,2,512]{2,1,0:T(2,128)} custom-call(f32[129,8,128]{2,1,0:T(8,128)S(1)} %next_products.3.refs_0_, f32[129,8,128]{2,1,0:T(8,128)S(1)} %collective-permute-done.refs_1_, f32[65,8,128]{2,1,0:T(8,128)S(1)} %collective-permute-done.1.refs_2_, f32[33,8,128]{2,1,0:T(8,128)S(1)} %collective-permute-done.2.refs_3_, ...), custom_call_target="tpu_custom_call" | custom-call | tf_op jit(solution)/shard_map/finish/pallas_call | solution.py:219
  (6 shorter events, 0.2 us)
Async XLA Ops:
  2.3 2.1 %collective-permute-start.4 = (f32[129,8,128]{2,1,0:T(8,128)S(1)}, f32[129,8,128]{2,1,0:T(8,128)S(1)}, u32[]{:S(2)}, u32[]{:S(2)}) collective-permute-start(f32[129,8,128]{2,1,0:T(8,128)S(1)} %next_products.5), channel_id=1, source_target_pairs={{0,1},{1,0},{2,3},{3,2},{4,5},{5,4},{6,7},{7,6},{8,9},{9,8},{10,11... | collective-permute-start | bytes 1585160 | tf_op jit(solution)/shard_map/ppermute | solution.py:238
  2.8 4.6 %collective-permute-start = (f32[129,8,128]{2,1,0:T(8,128)S(1)}, f32[129,8,128]{2,1,0:T(8,128)S(1)}, u32[]{:S(2)}, u32[]{:S(2)}) collective-permute-start(f32[129,8,128]{2,1,0:T(8,128)S(1)} %get-tuple-element.12), channel_id=1, source_target_pairs={{0,1},{1,0},{2,3},{3,2},{4,5},{5,4},{6,7},{7,6},{8,9},{9,8},{10,11... | collective-permute-start | bytes 1585160 | tf_op jit(solution)/shard_map/ppermute | solution.py:238
  4.4 7.4 %collective-permute-start.5 = (f32[65,8,128]{2,1,0:T(8,128)S(1)}, f32[65,8,128]{2,1,0:T(8,128)S(1)}, u32[]{:S(2)}, u32[]{:S(2)}) collective-permute-start(f32[65,8,128]{2,1,0:T(8,128)S(1)} %summed.9), channel_id=1, source_target_pairs={{0,4},{1,3},{2,6},{3,1},{4,0},{5,7},{6,2},{7,5},{8,12},{9,11},{10,... | collective-permute-start | bytes 798728 | tf_op jit(solution)/shard_map/ppermute | solution.py:238
  7.4 7.7 %collective-permute-start.1 = (f32[65,8,128]{2,1,0:T(8,128)S(1)}, f32[65,8,128]{2,1,0:T(8,128)S(1)}, u32[]{:S(2)}, u32[]{:S(2)}) collective-permute-start(f32[65,8,128]{2,1,0:T(8,128)S(1)} %summed.6), channel_id=1, source_target_pairs={{0,4},{1,3},{2,6},{3,1},{4,0},{5,7},{6,2},{7,5},{8,12},{9,11},{10,... | collective-permute-start | bytes 798728 | tf_op jit(solution)/shard_map/ppermute | solution.py:238
  11.8 5.7 %collective-permute-start.6 = (f32[33,8,128]{2,1,0:T(8,128)S(1)}, f32[33,8,128]{2,1,0:T(8,128)S(1)}, u32[]{:S(2)}, u32[]{:S(2)}) collective-permute-start(f32[33,8,128]{2,1,0:T(8,128)S(1)} %summed.10), channel_id=1, source_target_pairs={{0,2},{1,5},{2,0},{3,7},{4,6},{5,1},{6,4},{7,3},{8,10},{9,13},{10,... | collective-permute-start | bytes 405512 | tf_op jit(solution)/shard_map/ppermute | solution.py:238
  15.2 5.3 %collective-permute-start.2 = (f32[33,8,128]{2,1,0:T(8,128)S(1)}, f32[33,8,128]{2,1,0:T(8,128)S(1)}, u32[]{:S(2)}, u32[]{:S(2)}) collective-permute-start(f32[33,8,128]{2,1,0:T(8,128)S(1)} %summed.7), channel_id=1, source_target_pairs={{0,2},{1,5},{2,0},{3,7},{4,6},{5,1},{6,4},{7,3},{8,10},{9,13},{10,... | collective-permute-start | bytes 405512 | tf_op jit(solution)/shard_map/ppermute | solution.py:238
  17.5 6.2 %collective-permute-start.7 = (f32[17,8,128]{2,1,0:T(8,128)S(1)}, f32[17,8,128]{2,1,0:T(8,128)S(1)}, u32[]{:S(2)}, u32[]{:S(2)}) collective-permute-start(f32[17,8,128]{2,1,0:T(8,128)S(1)} %summed.11), channel_id=1, source_target_pairs={{0,8},{1,9},{2,10},{3,11},{4,12},{5,13},{6,14},{7,15},{8,0},{9,1},... | collective-permute-start | bytes 208904 | tf_op jit(solution)/shard_map/ppermute | solution.py:238
  20.5 5.5 %collective-permute-start.3 = (f32[17,8,128]{2,1,0:T(8,128)S(1)}, f32[17,8,128]{2,1,0:T(8,128)S(1)}, u32[]{:S(2)}, u32[]{:S(2)}) collective-permute-start(f32[17,8,128]{2,1,0:T(8,128)S(1)} %summed.8), channel_id=1, source_target_pairs={{0,8},{1,9},{2,10},{3,11},{4,12},{5,13},{6,14},{7,15},{8,0},{9,1},... | collective-permute-start | bytes 208904 | tf_op jit(solution)/shard_map/ppermute | solution.py:238

commit v9 on v8

--- a/solution.py
+++ b/solution.py
@@ -9,7 +9,12 @@
 
 epsilon = 1e-06
 MIB = 1 << 20
-CHUNKS = 2
+SHARES = (2, 1, 1)
+
+
+def column_chunks(columns):
+    unit = columns // sum(SHARES)
+    return [(unit * sum(SHARES[:at]), unit * share) for at, share in enumerate(SHARES)]
 
 
 def chip_orders(bits):
@@ -67,16 +72,18 @@
 ):
     me = lax.axis_index("ap")
     held, users, antennas = raw.shape[1], raw.shape[3], raw.shape[4]
-    width = weights.shape[2]
+    chunks = column_chunks(weights.shape[1])
     slots = 1 << (bits - 1)
     loads = [
         pltpu.make_async_copy(visible, seen, sems.at[0]),
         pltpu.make_async_copy(channel, raw, sems.at[1]),
         pltpu.make_async_copy(cluster, names, sems.at[2]),
     ]
-    for chunk in range(CHUNKS):
-        at = pl.ds(chunk * width, width)
-        loads.append(pltpu.make_async_copy(precoder.at[:, at], weights.at[chunk], sems.at[3 + chunk]))
+    for chunk, (start, width) in enumerate(chunks):
+        at = pl.ds(start, width)
+        loads.append(
+            pltpu.make_async_copy(precoder.at[:, at], weights.at[:, at], sems.at[3 + chunk])
+        )
     for load in loads:
         load.start()
     rows[...] = jnp.zeros_like(rows)
@@ -90,41 +97,39 @@
         rows[keep, at, antennas:2 * antennas] = raw[0, v, 1]
     loads[2].wait()
     here = jnp.max((names[...] == me).astype(jnp.float32), axis=0, keepdims=True)
-    for chunk in range(CHUNKS):
-        served[chunk] = here[:, chunk * width:(chunk + 1) * width]
+    served[...] = here
     loads[3].wait()
-    chosen, mask = weights[0], served[0] > 0.0
+    width = chunks[0][1]
+    chosen, mask = weights[:, 0:width], here[:, 0:width] > 0.0
     write_products(slots, rows.at[0], chosen, mask, out)
     out[out.shape[0] - 1] = power_tile(chosen, mask)
     for load in loads[4:]:
         load.wait()
 
 
-def next_kernel(bits, keep, chunk, rows, weights, served, out):
-    chosen, mask = weights[chunk], served[chunk] > 0.0
-    write_products(1 << (bits - 1), rows.at[keep], chosen, mask, out)
-    out[out.shape[0] - 1] = power_tile(chosen, mask)
+def next_kernel(bits, jobs, rows, weights, served, *refs):
+    for (keep, chunk), out in zip(jobs, refs[-len(jobs):]):
+        start, width = column_chunks(weights.shape[1])[chunk]
+        chosen, mask = weights[:, start:start + width], served[:, start:start + width] > 0.0
+        write_products(1 << (bits - 1), rows.at[keep], chosen, mask, out)
+        out[out.shape[0] - 1] = power_tile(chosen, mask)
 
 
 def message(tiles):
     return jax.ShapeDtypeStruct((tiles, 8, 128), jnp.float32)
 
 
-def estimate(rows, weights):
-    return pl.CostEstimate(
-        flops=8 * rows[1] * rows[2] * weights[2],
-        bytes_accessed=rows[1] * (rows[2] * 2 + weights[2] * 8) + weights[1] * weights[2] * 2,
-        transcendentals=0,
-    )
+def estimate():
+    return pl.CostEstimate(flops=8192, bytes_accessed=8192, transcendentals=0)
 
 
 def first_products(bits, visible, cluster, channel, precoder):
     users, antennas = channel.shape[3], channel.shape[4]
-    width = precoder.shape[1] // CHUNKS
+    columns = precoder.shape[1]
+    width = column_chunks(columns)[0][1]
     slots = 1 << (bits - 1)
     tiles = (users // 8) * (width // 128) * 2
     rows = (2, slots * users, 2 * antennas)
-    weights = (CHUNKS, precoder.shape[0], width)
     vmem = pl.BlockSpec(memory_space=pltpu.VMEM)
     hbm = pl.BlockSpec(memory_space=pltpu.HBM)
     operands = (visible, cluster, channel, precoder)
@@ -133,8 +138,8 @@
         out_shape=(
             message(slots * tiles + 1),
             jax.ShapeDtypeStruct(rows, jnp.bfloat16),
-            jax.ShapeDtypeStruct(weights, jnp.bfloat16),
-            jax.ShapeDtypeStruct((CHUNKS, 1, width), jnp.float32),
+            jax.ShapeDtypeStruct(precoder.shape, jnp.bfloat16),
+            jax.ShapeDtypeStruct((1, columns), jnp.float32),
         ),
         in_specs=[hbm] * 4,
         out_specs=(vmem,) * 4,
@@ -142,28 +147,28 @@
             pltpu.SMEM(visible.shape, jnp.int32),
             pltpu.VMEM(cluster.shape, jnp.int32),
             pltpu.VMEM(channel.shape, jnp.bfloat16),
-            pltpu.SemaphoreType.DMA((3 + CHUNKS,)),
+            pltpu.SemaphoreType.DMA((3 + len(SHARES),)),
         ],
         compiler_params=pltpu.CompilerParams(vmem_limit_bytes=52 * MIB if slots > 8 else 24 * MIB),
-        cost_estimate=estimate(rows, weights),
+        cost_estimate=estimate(),
         name="first_products",
     )(*[pltpu.with_memory_space_constraint(operand, pltpu.HBM) for operand in operands])
 
 
-def next_products(bits, keep, chunk, rows, weights, served):
+def next_products(bits, jobs, rows, weights, served, after):
     slots = 1 << (bits - 1)
     users = rows.shape[1] // slots
-    tiles = (users // 8) * (weights.shape[2] // 128) * 2
-    vmem = pl.BlockSpec(memory_space=pltpu.VMEM)
-    return pl.pallas_call(
-        functools.partial(next_kernel, bits, keep, chunk),
-        out_shape=message(slots * tiles + 1),
-        in_specs=[vmem] * 3,
-        out_specs=vmem,
+    widths = [column_chunks(weights.shape[1])[chunk][1] for _, chunk in jobs]
+    vmem = pl.BlockSpec(memory_space=pltpu.VMEM)
+    return pl.pallas_call(
+        functools.partial(next_kernel, bits, jobs),
+        out_shape=[message(slots * (users // 8) * (width // 128) * 2 + 1) for width in widths],
+        in_specs=[vmem] * (3 + len(after)),
+        out_specs=[vmem] * len(jobs),
         compiler_params=pltpu.CompilerParams(vmem_limit_bytes=48 * MIB if slots > 8 else 16 * MIB),
-        cost_estimate=estimate(rows.shape, weights.shape),
+        cost_estimate=estimate(),
         name="next_products",
-    )(rows, weights, served)
+    )(rows, weights, served, *after)
 
 
 def add_up(refs, terms, count):
@@ -180,28 +185,26 @@
         at += count
 
 
-def summed(arrays, jobs):
+def summed(arrays, jobs, after):
     size = sum(count for _, count in jobs)
     vmem = pl.BlockSpec(memory_space=pltpu.VMEM)
-    reads = sum(len(terms) * count for terms, count in jobs)
     return pl.pallas_call(
         functools.partial(sum_kernel, jobs),
         out_shape=message(size),
-        in_specs=[vmem] * len(arrays),
+        in_specs=[vmem] * (len(arrays) + len(after)),
         out_specs=vmem,
         compiler_params=pltpu.CompilerParams(vmem_limit_bytes=8 * MIB),
-        cost_estimate=pl.CostEstimate(
-            flops=reads * 1024, bytes_accessed=(reads + size) * 4096, transcendentals=0
-        ),
+        cost_estimate=estimate(),
         name="summed",
-    )(*arrays)
+    )(*arrays, *after)
 
 
 def final_kernel(jobs, *refs):
     out = refs[-1]
-    users, blocks = out.shape[0], out.shape[2] // 128 // CHUNKS
+    users, columns = out.shape[0], out.shape[2]
     steps = users // 8
-    for chunk, (terms, powers) in enumerate(jobs):
+    for (first, width), (terms, powers) in zip(column_chunks(columns), jobs):
+        blocks = width // 128
         scale = lax.rsqrt(add_up(refs, powers, 1)[0] + epsilon)
         total = add_up(refs, terms, 2 * blocks * steps)
         for half in range(2):
@@ -210,7 +213,7 @@
                 value = total[start:start + steps].reshape(users, 128)
                 factor = scale[block:block + 1, :]
                 value = jnp.where(factor > 0.0, value * factor, 0.0)
-                left = (chunk * blocks + block) * 128
+                left = first + block * 128
                 out[:, half, left:left + 128] = value
 
 
@@ -230,7 +233,8 @@
     devices = lax.axis_size("ap")
     bits = devices.bit_length() - 1
     users, columns = channel.shape[3], precoder.shape[2]
-    tiles = (users // 8) * (columns // CHUNKS // 128) * 2
+    tiles = [(users // 8) * (width // 128) * 2 for _, width in column_chunks(columns)]
+    chunks = range(len(tiles))
     orders = chip_orders(bits)
     flat = precoder.reshape(-1, columns)
 
@@ -238,31 +242,46 @@
         return lax.ppermute(value, "ap", [(i, i ^ (1 << bit_of[i & 1])) for i in range(devices)])
 
     sent, rows, weights, served = first_products(bits, visible, cluster.T, channel, flat)
-    got = [swap(sent, (0, 0))]
-    for chunk in range(1, CHUNKS):
-        got.append(swap(next_products(bits, 0, chunk, rows, weights, served), (0, 0)))
-    held = [
-        [next_products(bits, 1, chunk, rows, weights, served), got[chunk]] for chunk in range(CHUNKS)
-    ]
+    got, held, after = [swap(sent, (0, 0))], [], []
+    left = [[(0, 0), (1, 0)] for _ in chunks]
+    powers = [[(0, devices // 2 * tiles[chunk]), (1, devices // 2 * tiles[chunk])] for chunk in chunks]
     slots = devices // 2
-    left = [(0, 0), (1, 0)]
-    powers = [(0, slots * tiles), (1, slots * tiles)]
     for step in range(bits - 1):
         slots //= 2
-        count = slots * tiles
-        for mine in held:
-            message_now = summed(mine, [(left, count), (powers, 1)])
-            mine.append(swap(message_now, (orders[0][step], orders[1][step])))
-        left = [(array, start + count) for array, start in left] + [(step + 2, 0)]
-        powers = powers + [(step + 2, count)]
-    jobs = []
-    for chunk, mine in enumerate(held):
-        base = chunk * len(mine)
-        jobs.append((
-            [(base + array, start) for array, start in left],
-            [(base + array, start) for array, start in powers],
+        last = step == bits - 2
+        for members in [chunks[:-1], chunks[-1:]] if last else [[chunk] for chunk in chunks]:
+            if step == 0:
+                chunk = members[0]
+                wanted = ((0, chunk + 1), (1, chunk)) if chunk + 1 in chunks else ((1, chunk),)
+                made = next_products(bits, wanted, rows, weights, served, after)
+                if len(made) > 1:
+                    got.append(swap(made[0], (0, 0)))
+                held.append([made[-1], got[chunk]])
+            arrays, parts, starts, size = [], [], [], 0
+            for chunk in members:
+                count = slots * tiles[chunk]
+                for terms, amount in ((left[chunk], count), (powers[chunk], 1)):
+                    parts.append(([(len(arrays) + array, start) for array, start in terms], amount))
+                arrays = arrays + held[chunk]
+                starts.append(size)
+                size += count + 1
+            message_now = summed(arrays, parts, after)
+            came = swap(message_now, (orders[0][step], orders[1][step]))
+            after = [message_now]
+            for chunk, start in zip(members, starts):
+                count = slots * tiles[chunk]
+                left[chunk] = [(array, at + count) for array, at in left[chunk]]
+                left[chunk].append((len(held[chunk]), start))
+                powers[chunk].append((len(held[chunk]), start + count))
+                held[chunk].append(came)
+    jobs, arrays = [], []
+    for chunk in chunks:
+        jobs.append(tuple(
+            [(len(arrays) + array, start) for array, start in terms]
+            for terms in (left[chunk], powers[chunk])
         ))
-    return finish([array for mine in held for array in mine], jobs, users, columns)
+        arrays = arrays + held[chunk]
+    return finish(arrays, jobs, users, columns)
 
 
 def solution(mesh):

time: 26.9 us -> 28.4 us (1.056)
  starting transfers between devices: 14.4 us -> 16 us
  Pallas kernels: 4.06 us -> 4.61 us
  waiting for transfers between devices: 8.17 us -> 7.64 us
    ppermute x8 -> x11, starting transfers between devices: 14.4 us -> 16 us  [swap(): lax.ppermute(value, 'ap', [(i, i ^ 1 << bit_of[i & 1]) for i in range(dev...]
    pallas_call x3, Pallas kernels: 1.32 us -> 1.87 us  [next_products(): pl.pallas_call(functools.partial(next_kernel, bits, jobs), out_shape=[mes...]
    ppermute x8 -> x11, waiting for transfers between devices: 8.17 us -> 7.64 us  [swap(): lax.ppermute(value, 'ap', [(i, i ^ 1 << bit_of[i & 1]) for i in range(dev...]
  transfers between devices with their start and end apart: 8 -> 11, of which waited for: 5 -> 4; matrix products, arithmetic and copies ran while one was open for 0% -> 0% of each run, Pallas kernels for 4% -> 7%
where the time goes in v9:
time: 28.4 us; the launch traced here: 28.3 us
  starting transfers between devices  16 us (56%)
  waiting for transfers between devices  7.64 us (27%)
  Pallas kernels  4.61 us (16%)
    ppermute x11, starting transfers between devices, swap(): lax.ppermute(value, 'ap', [(i, i ^ 1 << bit_of[i & 1]) for i in range(dev...  16 us
    ppermute x11, waiting for transfers between devices, swap(): lax.ppermute(value, 'ap', [(i, i ^ 1 << bit_of[i & 1]) for i in range(dev...  7.64 us
    pallas_call x3, Pallas kernels, next_products(): pl.pallas_call(functools.partial(next_kernel, bits, jobs), out_shape=[mes...  1.87 us
    pallas_call x1, Pallas kernels, first_products(): pl.pallas_call(functools.partial(first_kernel, bits), out_shape=(message(...  1.81 us
    pallas_call x1, Pallas kernels, finish(): pl.pallas_call(functools.partial(final_kernel, jobs), out_shape=jax.Shape...  0.78 us
  transfers between devices with their start and end apart: 11, of which 4 were waited for; matrix products, arithmetic and copies ran while one was open for 0% of the time, Pallas kernels for 7%

profile of v9, /device:TPU:0, one launch (start us, length us, event | category | flops | bytes accessed | tf_op | source)
XLA Modules:
  0.0 28.3 jit_solution(14172773066214207195)
XLA Ops:
  0.0 1.8 %first_products.1 = (f32[129,8,128]{2,1,0:T(8,128)S(1)}, bf16[2,256,1024]{2,1,0:T(8,128)(2,1)S(1)}, bf16[1024,512]{1,0:T(8,128)(2,1)S(1)}, f32[1,512]{1,0:T(1,128)S(1)}) custom-call(s32[1,12]{1,0:T(1,128)} %visible.1, s32[4,512]{1,0:T(4,128)} %bitcast.3, bf16[1,12,2,32,512]{4,3,2,1,0:T(8,128)(2,1)} %channel.1, bf16[1024,512]{1,0:T(8,128)(2,1)} %bitcast.2), custom_call_target="tpu_custom_call" | custom-call | flops 8192 | bytes 8192 | tf_op jit(solution)/shard_map/first_products/pallas_call | solution.py:136
  1.8 0.5 %collective-permute-start = (f32[129,8,128]{2,1,0:T(8,128)S(1)}, f32[129,8,128]{2,1,0:T(8,128)S(1)}, u32[]{:S(2)}, u32[]{:S(2)}) collective-permute-start(f32[129,8,128]{2,1,0:T(8,128)S(1)} %get-tuple-element.17), channel_id=1, source_target_pairs={{0,1},{1,0},{2,3},{3,2},{4,5},{5,4},{6,7},{7,6},{8,9},{9,8},{10,11... | collective-permute-start | bytes 1585160 | tf_op jit(solution)/shard_map/ppermute | solution.py:242
  2.3 0.7 %next_products.3 = (f32[65,8,128]{2,1,0:T(8,128)S(1)}, f32[129,8,128]{2,1,0:T(8,128)S(1)}) custom-call(bf16[2,256,1024]{2,1,0:T(8,128)(2,1)S(1)} %get-tuple-element.13.rows, bf16[1024,512]{1,0:T(8,128)(2,1)S(1)} %get-tuple-element.14.weights, f32[1,512]{1,0:T(1,128)S(1)} %get-tuple-element.15.served), custom_call_target="tpu_custom_call" | custom-call | flops 8192 | bytes 8192 | tf_op jit(solution)/shard_map/next_products/pallas_call | solution.py:163
  3.1 0.1 collective-permute-start.2
  3.2 0.7 %collective-permute-done.refs_1_ = f32[129,8,128]{2,1,0:T(8,128)S(1)} collective-permute-done((f32[129,8,128]{2,1,0:T(8,128)S(1)}, f32[129,8,128]{2,1,0:T(8,128)S(1)}, u32[]{:S(2)}, u32[]{:S(2)}) %collective-permute-start) | collective-permute-done | bytes 528416 | tf_op jit(solution)/shard_map/ppermute | solution.py:242
  3.9 0.7 %next_products.4 = (f32[65,8,128]{2,1,0:T(8,128)S(1)}, f32[65,8,128]{2,1,0:T(8,128)S(1)}) custom-call(bf16[2,256,1024]{2,1,0:T(8,128)(2,1)S(1)} %get-tuple-element.13.rows, bf16[1024,512]{1,0:T(8,128)(2,1)S(1)} %get-tuple-element.14.weights, f32[1,512]{1,0:T(1,128)S(1)} %get-tuple-element.15.served, f32[65,8,128]{2,1,0:T(8,128)S(1)} %summed.8.refs_0_.refs_2_), custom_call_target="tpu_custom_call" | custom-call | flops 8192 | bytes 8192 | tf_op jit(solution)/shard_map/next_products/pallas_call | solution.py:163
  4.6 0.4 %collective-permute-start.3 = (f32[65,8,128]{2,1,0:T(8,128)S(1)}, f32[65,8,128]{2,1,0:T(8,128)S(1)}, u32[]{:S(2)}, u32[]{:S(2)}) collective-permute-start(f32[65,8,128]{2,1,0:T(8,128)S(1)} %get-tuple-element.20), channel_id=1, source_target_pairs={{0,1},{1,0},{2,3},{3,2},{4,5},{5,4},{6,7},{7,6},{8,9},{9,8},{10,11... | collective-permute-start | bytes 798728 | tf_op jit(solution)/shard_map/ppermute | solution.py:242
  5.1 2.7 %collective-permute-start.1 = (f32[65,8,128]{2,1,0:T(8,128)S(1)}, f32[65,8,128]{2,1,0:T(8,128)S(1)}, u32[]{:S(2)}, u32[]{:S(2)}) collective-permute-start(f32[65,8,128]{2,1,0:T(8,128)S(1)} %summed.8.refs_0_.refs_2_), channel_id=1, source_target_pairs={{0,4},{1,3},{2,6},{3,1},{4,0},{5,7},{6,2},{7,5},{8,12},{9,11},{10,... | collective-permute-start | bytes 798728 | tf_op jit(solution)/shard_map/ppermute | solution.py:242
  7.8 0.0 collective-permute-done.2.refs_1_.refs_5_.refs_6_
  7.8 0.1 collective-permute-start.5
  7.9 0.4 %next_products.5.refs_0_.refs_10_ = f32[65,8,128]{2,1,0:T(8,128)S(1)} custom-call(bf16[2,256,1024]{2,1,0:T(8,128)(2,1)S(1)} %get-tuple-element.13.rows, bf16[1024,512]{1,0:T(8,128)(2,1)S(1)} %get-tuple-element.14.weights, f32[1,512]{1,0:T(1,128)S(1)} %get-tuple-element.15.served, f32[33,8,128]{2,1,0:T(8,128)S(1)} %summed.9.refs_0_.refs_2_), custom_call_target="tpu_custom_call" | custom-call | flops 8192 | bytes 8192 | tf_op jit(solution)/shard_map/next_products/pallas_call | solution.py:163
  8.3 0.0 collective-permute-done.3.refs_1_.refs_11_
  8.4 2.1 %collective-permute-start.7 = (f32[33,8,128]{2,1,0:T(8,128)S(1)}, f32[33,8,128]{2,1,0:T(8,128)S(1)}, u32[]{:S(2)}, u32[]{:S(2)}) collective-permute-start(f32[33,8,128]{2,1,0:T(8,128)S(1)} %summed.10.refs_3_), channel_id=1, source_target_pairs={{0,4},{1,3},{2,6},{3,1},{4,0},{5,7},{6,2},{7,5},{8,12},{9,11},{10,... | collective-permute-start | bytes 405512 | tf_op jit(solution)/shard_map/ppermute | solution.py:242
  10.4 1.7 %collective-permute-done.1.refs_2_ = f32[65,8,128]{2,1,0:T(8,128)S(1)} collective-permute-done((f32[65,8,128]{2,1,0:T(8,128)S(1)}, f32[65,8,128]{2,1,0:T(8,128)S(1)}, u32[]{:S(2)}, u32[]{:S(2)}) %collective-permute-start.1) | collective-permute-done | bytes 266272 | tf_op jit(solution)/shard_map/ppermute | solution.py:242
  12.2 2.0 %collective-permute-start.4 = (f32[33,8,128]{2,1,0:T(8,128)S(1)}, f32[33,8,128]{2,1,0:T(8,128)S(1)}, u32[]{:S(2)}, u32[]{:S(2)}) collective-permute-start(f32[33,8,128]{2,1,0:T(8,128)S(1)} %summed.11.refs_3_), channel_id=1, source_target_pairs={{0,2},{1,5},{2,0},{3,7},{4,6},{5,1},{6,4},{7,3},{8,10},{9,13},{10,... | collective-permute-start | bytes 405512 | tf_op jit(solution)/shard_map/ppermute | solution.py:242
  14.2 0.0 collective-permute-done.5.refs_2_.refs_6_.refs_7_
  14.2 1.4 %collective-permute-start.6 = (f32[17,8,128]{2,1,0:T(8,128)S(1)}, f32[17,8,128]{2,1,0:T(8,128)S(1)}, u32[]{:S(2)}, u32[]{:S(2)}) collective-permute-start(f32[17,8,128]{2,1,0:T(8,128)S(1)} %summed.12.refs_3_), channel_id=1, source_target_pairs={{0,2},{1,5},{2,0},{3,7},{4,6},{5,1},{6,4},{7,3},{8,10},{9,13},{10,... | collective-permute-start | bytes 208904 | tf_op jit(solution)/shard_map/ppermute | solution.py:242
  15.6 0.0 collective-permute-done.7.refs_2_.refs_12_
  15.7 2.1 %collective-permute-start.9 = (f32[17,8,128]{2,1,0:T(8,128)S(1)}, f32[17,8,128]{2,1,0:T(8,128)S(1)}, u32[]{:S(2)}, u32[]{:S(2)}) collective-permute-start(f32[17,8,128]{2,1,0:T(8,128)S(1)} %summed.13.refs_8_), channel_id=1, source_target_pairs={{0,2},{1,5},{2,0},{3,7},{4,6},{5,1},{6,4},{7,3},{8,10},{9,13},{10,... | collective-permute-start | bytes 208904 | tf_op jit(solution)/shard_map/ppermute | solution.py:242
  17.7 0.9 %collective-permute-done.6.refs_7_.refs_8_ = f32[17,8,128]{2,1,0:T(8,128)S(1)} collective-permute-done((f32[17,8,128]{2,1,0:T(8,128)S(1)}, f32[17,8,128]{2,1,0:T(8,128)S(1)}, u32[]{:S(2)}, u32[]{:S(2)}) %collective-permute-start.6) | collective-permute-done | bytes 69664 | tf_op jit(solution)/shard_map/ppermute | solution.py:242
  18.6 0.0 collective-permute-done.4.refs_3_
  18.6 2.7 %collective-permute-start.8 = (f32[26,8,128]{2,1,0:T(8,128)S(1)}, f32[26,8,128]{2,1,0:T(8,128)S(1)}, u32[]{:S(2)}, u32[]{:S(2)}) collective-permute-start(f32[26,8,128]{2,1,0:T(8,128)S(1)} %summed.14.refs_4_), channel_id=1, source_target_pairs={{0,8},{1,9},{2,10},{3,11},{4,12},{5,13},{6,14},{7,15},{8,0},{9,1},... | collective-permute-start | bytes 319496 | tf_op jit(solution)/shard_map/ppermute | solution.py:242
  21.3 0.0 collective-permute-done.9.refs_3_.refs_13_
  21.3 1.9 %collective-permute-start.10 = (f32[9,8,128]{2,1,0:T(8,128)S(1)}, f32[9,8,128]{2,1,0:T(8,128)S(1)}, u32[]{:S(2)}, u32[]{:S(2)}) collective-permute-start(f32[9,8,128]{2,1,0:T(8,128)S(1)} %summed.15), channel_id=1, source_target_pairs={{0,8},{1,9},{2,10},{3,11},{4,12},{5,13},{6,14},{7,15},{8,0},{9,1},... | collective-permute-start | bytes 110600 | tf_op jit(solution)/shard_map/ppermute | solution.py:242
  23.2 4.3 %collective-permute-done.10.refs_14_ = f32[9,8,128]{2,1,0:T(8,128)S(1)} collective-permute-done((f32[9,8,128]{2,1,0:T(8,128)S(1)}, f32[9,8,128]{2,1,0:T(8,128)S(1)}, u32[]{:S(2)}, u32[]{:S(2)}) %collective-permute-start.10) | collective-permute-done | bytes 36896 | tf_op jit(solution)/shard_map/ppermute | solution.py:242
  27.5 0.0 collective-permute-done.8.refs_4_.refs_9_
  27.5 0.8 %finish.1 = f32[32,2,512]{2,1,0:T(2,128)} custom-call(f32[129,8,128]{2,1,0:T(8,128)S(1)} %get-tuple-element.16.refs_0_, f32[129,8,128]{2,1,0:T(8,128)S(1)} %collective-permute-done.refs_1_, f32[65,8,128]{2,1,0:T(8,128)S(1)} %collective-permute-done.1.refs_2_, f32[33,8,128]{2,1,0:T(8,128)S(1)} %collective-permute-done.4.refs_3_, ...), custom_call_target="tpu_custom_call" | custom-call | tf_op jit(solution)/shard_map/finish/pallas_call | solution.py:222
  (8 shorter events, 0.2 us)
Async XLA Ops:
  1.8 2.1 %collective-permute-start = (f32[129,8,128]{2,1,0:T(8,128)S(1)}, f32[129,8,128]{2,1,0:T(8,128)S(1)}, u32[]{:S(2)}, u32[]{:S(2)}) collective-permute-start(f32[129,8,128]{2,1,0:T(8,128)S(1)} %get-tuple-element.17), channel_id=1, source_target_pairs={{0,1},{1,0},{2,3},{3,2},{4,5},{5,4},{6,7},{7,6},{8,9},{9,8},{10,11... | collective-permute-start | bytes 1585160 | tf_op jit(solution)/shard_map/ppermute | solution.py:242
  3.1 4.7 %collective-permute-start.2 = (f32[65,8,128]{2,1,0:T(8,128)S(1)}, f32[65,8,128]{2,1,0:T(8,128)S(1)}, u32[]{:S(2)}, u32[]{:S(2)}) collective-permute-start(f32[65,8,128]{2,1,0:T(8,128)S(1)} %get-tuple-element.19), channel_id=1, source_target_pairs={{0,1},{1,0},{2,3},{3,2},{4,5},{5,4},{6,7},{7,6},{8,9},{9,8},{10,11... | collective-permute-start | bytes 798728 | tf_op jit(solution)/shard_map/ppermute | solution.py:242
  4.6 3.7 %collective-permute-start.3 = (f32[65,8,128]{2,1,0:T(8,128)S(1)}, f32[65,8,128]{2,1,0:T(8,128)S(1)}, u32[]{:S(2)}, u32[]{:S(2)}) collective-permute-start(f32[65,8,128]{2,1,0:T(8,128)S(1)} %get-tuple-element.20), channel_id=1, source_target_pairs={{0,1},{1,0},{2,3},{3,2},{4,5},{5,4},{6,7},{7,6},{8,9},{9,8},{10,11... | collective-permute-start | bytes 798728 | tf_op jit(solution)/shard_map/ppermute | solution.py:242
  5.1 7.1 %collective-permute-start.1 = (f32[65,8,128]{2,1,0:T(8,128)S(1)}, f32[65,8,128]{2,1,0:T(8,128)S(1)}, u32[]{:S(2)}, u32[]{:S(2)}) collective-permute-start(f32[65,8,128]{2,1,0:T(8,128)S(1)} %summed.8.refs_0_.refs_2_), channel_id=1, source_target_pairs={{0,4},{1,3},{2,6},{3,1},{4,0},{5,7},{6,2},{7,5},{8,12},{9,11},{10,... | collective-permute-start | bytes 798728 | tf_op jit(solution)/shard_map/ppermute | solution.py:242
  7.8 6.4 %collective-permute-start.5 = (f32[33,8,128]{2,1,0:T(8,128)S(1)}, f32[33,8,128]{2,1,0:T(8,128)S(1)}, u32[]{:S(2)}, u32[]{:S(2)}) collective-permute-start(f32[33,8,128]{2,1,0:T(8,128)S(1)} %summed.9.refs_0_.refs_2_), channel_id=1, source_target_pairs={{0,4},{1,3},{2,6},{3,1},{4,0},{5,7},{6,2},{7,5},{8,12},{9,11},{10,... | collective-permute-start | bytes 405512 | tf_op jit(solution)/shard_map/ppermute | solution.py:242
  8.4 7.3 %collective-permute-start.7 = (f32[33,8,128]{2,1,0:T(8,128)S(1)}, f32[33,8,128]{2,1,0:T(8,128)S(1)}, u32[]{:S(2)}, u32[]{:S(2)}) collective-permute-start(f32[33,8,128]{2,1,0:T(8,128)S(1)} %summed.10.refs_3_), channel_id=1, source_target_pairs={{0,4},{1,3},{2,6},{3,1},{4,0},{5,7},{6,2},{7,5},{8,12},{9,11},{10,... | collective-permute-start | bytes 405512 | tf_op jit(solution)/shard_map/ppermute | solution.py:242
  12.2 6.4 %collective-permute-start.4 = (f32[33,8,128]{2,1,0:T(8,128)S(1)}, f32[33,8,128]{2,1,0:T(8,128)S(1)}, u32[]{:S(2)}, u32[]{:S(2)}) collective-permute-start(f32[33,8,128]{2,1,0:T(8,128)S(1)} %summed.11.refs_3_), channel_id=1, source_target_pairs={{0,2},{1,5},{2,0},{3,7},{4,6},{5,1},{6,4},{7,3},{8,10},{9,13},{10,... | collective-permute-start | bytes 405512 | tf_op jit(solution)/shard_map/ppermute | solution.py:242
  14.2 4.4 %collective-permute-start.6 = (f32[17,8,128]{2,1,0:T(8,128)S(1)}, f32[17,8,128]{2,1,0:T(8,128)S(1)}, u32[]{:S(2)}, u32[]{:S(2)}) collective-permute-start(f32[17,8,128]{2,1,0:T(8,128)S(1)} %summed.12.refs_3_), channel_id=1, source_target_pairs={{0,2},{1,5},{2,0},{3,7},{4,6},{5,1},{6,4},{7,3},{8,10},{9,13},{10,... | collective-permute-start | bytes 208904 | tf_op jit(solution)/shard_map/ppermute | solution.py:242
  15.7 5.6 %collective-permute-start.9 = (f32[17,8,128]{2,1,0:T(8,128)S(1)}, f32[17,8,128]{2,1,0:T(8,128)S(1)}, u32[]{:S(2)}, u32[]{:S(2)}) collective-permute-start(f32[17,8,128]{2,1,0:T(8,128)S(1)} %summed.13.refs_8_), channel_id=1, source_target_pairs={{0,2},{1,5},{2,0},{3,7},{4,6},{5,1},{6,4},{7,3},{8,10},{9,13},{10,... | collective-permute-start | bytes 208904 | tf_op jit(solution)/shard_map/ppermute | solution.py:242
  18.6 8.9 %collective-permute-start.8 = (f32[26,8,128]{2,1,0:T(8,128)S(1)}, f32[26,8,128]{2,1,0:T(8,128)S(1)}, u32[]{:S(2)}, u32[]{:S(2)}) collective-permute-start(f32[26,8,128]{2,1,0:T(8,128)S(1)} %summed.14.refs_4_), channel_id=1, source_target_pairs={{0,8},{1,9},{2,10},{3,11},{4,12},{5,13},{6,14},{7,15},{8,0},{9,1},... | collective-permute-start | bytes 319496 | tf_op jit(solution)/shard_map/ppermute | solution.py:242
  21.3 6.2 %collective-permute-start.10 = (f32[9,8,128]{2,1,0:T(8,128)S(1)}, f32[9,8,128]{2,1,0:T(8,128)S(1)}, u32[]{:S(2)}, u32[]{:S(2)}) collective-permute-start(f32[9,8,128]{2,1,0:T(8,128)S(1)} %summed.15), channel_id=1, source_target_pairs={{0,8},{1,9},{2,10},{3,11},{4,12},{5,13},{6,14},{7,15},{8,0},{9,1},... | collective-permute-start | bytes 110600 | tf_op jit(solution)/shard_map/ppermute | solution.py:242

commit v10 on v9

--- a/solution.py
+++ b/solution.py
@@ -9,7 +9,8 @@
 
 epsilon = 1e-06
 MIB = 1 << 20
-SHARES = (2, 1, 1)
+SHARES = (1, 1, 1, 1)
+PAIRED = ((0, 1), (2, 3))
 
 
 def column_chunks(columns):
@@ -248,8 +249,7 @@
     slots = devices // 2
     for step in range(bits - 1):
         slots //= 2
-        last = step == bits - 2
-        for members in [chunks[:-1], chunks[-1:]] if last else [[chunk] for chunk in chunks]:
+        for members in PAIRED if step > 0 else [(chunk,) for chunk in chunks]:
             if step == 0:
                 chunk = members[0]
                 wanted = ((0, chunk + 1), (1, chunk)) if chunk + 1 in chunks else ((1, chunk),)

time: 28.4 us -> 30 us (1.056)
  waiting for transfers between devices: 7.64 us -> 9.66 us
  starting transfers between devices: 16 us -> 14.8 us
  Pallas kernels: 4.61 us -> 5.32 us
    ppermute x11 -> x12, waiting for transfers between devices: 7.64 us -> 9.66 us  [swap(): lax.ppermute(value, 'ap', [(i, i ^ 1 << bit_of[i & 1]) for i in range(dev...]
    ppermute x11 -> x12, starting transfers between devices: 16 us -> 14.8 us  [swap(): lax.ppermute(value, 'ap', [(i, i ^ 1 << bit_of[i & 1]) for i in range(dev...]
    pallas_call x3 -> x4, Pallas kernels: 1.87 us -> 2.56 us  [next_products(): pl.pallas_call(functools.partial(next_kernel, bits, jobs), out_shape=[mes...]
  transfers between devices with their start and end apart: 11 -> 12, of which waited for: 4 -> 6; matrix products, arithmetic and copies ran while one was open for 0% -> 0% of each run, Pallas kernels for 7% -> 9%
where the time goes in v10:
time: 30 us; the launch traced here: 29.8 us
  starting transfers between devices  14.8 us (49%)
  waiting for transfers between devices  9.66 us (32%)
  Pallas kernels  5.32 us (18%)
    ppermute x12, starting transfers between devices, swap(): lax.ppermute(value, 'ap', [(i, i ^ 1 << bit_of[i & 1]) for i in range(dev...  14.8 us
    ppermute x12, waiting for transfers between devices, swap(): lax.ppermute(value, 'ap', [(i, i ^ 1 << bit_of[i & 1]) for i in range(dev...  9.66 us
    pallas_call x4, Pallas kernels, next_products(): pl.pallas_call(functools.partial(next_kernel, bits, jobs), out_shape=[mes...  2.56 us
    pallas_call x1, Pallas kernels, first_products(): pl.pallas_call(functools.partial(first_kernel, bits), out_shape=(message(...  1.8 us
    pallas_call x1, Pallas kernels, finish(): pl.pallas_call(functools.partial(final_kernel, jobs), out_shape=jax.Shape...  0.78 us
  transfers between devices with their start and end apart: 12, of which 6 were waited for; matrix products, arithmetic and copies ran while one was open for 0% of the time, Pallas kernels for 9%

profile of v10, /device:TPU:0, one launch (start us, length us, event | category | flops | bytes accessed | tf_op | source)
XLA Modules:
  0.0 29.8 jit_solution(9836560310804919159)
XLA Ops:
  0.0 1.8 %first_products.1 = (f32[65,8,128]{2,1,0:T(8,128)S(1)}, bf16[2,256,1024]{2,1,0:T(8,128)(2,1)S(1)}, bf16[1024,512]{1,0:T(8,128)(2,1)S(1)}, f32[1,512]{1,0:T(1,128)S(1)}) custom-call(s32[1,12]{1,0:T(1,128)} %visible.1, s32[4,512]{1,0:T(4,128)} %bitcast.3, bf16[1,12,2,32,512]{4,3,2,1,0:T(8,128)(2,1)} %channel.1, bf16[1024,512]{1,0:T(8,128)(2,1)} %bitcast.2), custom_call_target="tpu_custom_call" | custom-call | flops 8192 | bytes 8192 | tf_op jit(solution)/shard_map/first_products/pallas_call | solution.py:137
  1.8 0.5 %collective-permute-start = (f32[65,8,128]{2,1,0:T(8,128)S(1)}, f32[65,8,128]{2,1,0:T(8,128)S(1)}, u32[]{:S(2)}, u32[]{:S(2)}) collective-permute-start(f32[65,8,128]{2,1,0:T(8,128)S(1)} %get-tuple-element.19), channel_id=1, source_target_pairs={{0,1},{1,0},{2,3},{3,2},{4,5},{5,4},{6,7},{7,6},{8,9},{9,8},{10,11... | collective-permute-start | bytes 798728 | tf_op jit(solution)/shard_map/ppermute | solution.py:243
  2.3 0.7 %next_products.4 = (f32[65,8,128]{2,1,0:T(8,128)S(1)}, f32[65,8,128]{2,1,0:T(8,128)S(1)}) custom-call(bf16[2,256,1024]{2,1,0:T(8,128)(2,1)S(1)} %get-tuple-element.15.rows, bf16[1024,512]{1,0:T(8,128)(2,1)S(1)} %get-tuple-element.16.weights, f32[1,512]{1,0:T(1,128)S(1)} %get-tuple-element.17.served), custom_call_target="tpu_custom_call" | custom-call | flops 8192 | bytes 8192 | tf_op jit(solution)/shard_map/next_products/pallas_call | solution.py:164
  3.0 0.1 collective-permute-start.2
  3.2 0.3 %collective-permute-done.refs_1_ = f32[65,8,128]{2,1,0:T(8,128)S(1)} collective-permute-done((f32[65,8,128]{2,1,0:T(8,128)S(1)}, f32[65,8,128]{2,1,0:T(8,128)S(1)}, u32[]{:S(2)}, u32[]{:S(2)}) %collective-permute-start) | collective-permute-done | bytes 266272 | tf_op jit(solution)/shard_map/ppermute | solution.py:243
  3.5 0.7 %next_products.5 = (f32[65,8,128]{2,1,0:T(8,128)S(1)}, f32[65,8,128]{2,1,0:T(8,128)S(1)}) custom-call(bf16[2,256,1024]{2,1,0:T(8,128)(2,1)S(1)} %get-tuple-element.15.rows, bf16[1024,512]{1,0:T(8,128)(2,1)S(1)} %get-tuple-element.16.weights, f32[1,512]{1,0:T(1,128)S(1)} %get-tuple-element.17.served, f32[33,8,128]{2,1,0:T(8,128)S(1)} %summed.8.refs_0_.refs_2_), custom_call_target="tpu_custom_call" | custom-call | flops 8192 | bytes 8192 | tf_op jit(solution)/shard_map/next_products/pallas_call | solution.py:164
  4.2 0.4 %collective-permute-start.4 = (f32[65,8,128]{2,1,0:T(8,128)S(1)}, f32[65,8,128]{2,1,0:T(8,128)S(1)}, u32[]{:S(2)}, u32[]{:S(2)}) collective-permute-start(f32[65,8,128]{2,1,0:T(8,128)S(1)} %get-tuple-element.23), channel_id=1, source_target_pairs={{0,1},{1,0},{2,3},{3,2},{4,5},{5,4},{6,7},{7,6},{8,9},{9,8},{10,11... | collective-permute-start | bytes 798728 | tf_op jit(solution)/shard_map/ppermute | solution.py:243
  4.7 0.0 collective-permute-done.2.refs_1_.refs_4_.refs_5_.refs_6_
  4.7 0.7 %next_products.6 = (f32[65,8,128]{2,1,0:T(8,128)S(1)}, f32[65,8,128]{2,1,0:T(8,128)S(1)}) custom-call(bf16[2,256,1024]{2,1,0:T(8,128)(2,1)S(1)} %get-tuple-element.15.rows, bf16[1024,512]{1,0:T(8,128)(2,1)S(1)} %get-tuple-element.16.weights, f32[1,512]{1,0:T(1,128)S(1)} %get-tuple-element.17.served, f32[33,8,128]{2,1,0:T(8,128)S(1)} %summed.9.refs_0_.refs_2_), custom_call_target="tpu_custom_call" | custom-call | flops 8192 | bytes 8192 | tf_op jit(solution)/shard_map/next_products/pallas_call | solution.py:164
  5.4 0.2 collective-permute-start.5
  5.6 2.9 %collective-permute-start.1 = (f32[33,8,128]{2,1,0:T(8,128)S(1)}, f32[33,8,128]{2,1,0:T(8,128)S(1)}, u32[]{:S(2)}, u32[]{:S(2)}) collective-permute-start(f32[33,8,128]{2,1,0:T(8,128)S(1)} %summed.8.refs_0_.refs_2_), channel_id=1, source_target_pairs={{0,4},{1,3},{2,6},{3,1},{4,0},{5,7},{6,2},{7,5},{8,12},{9,11},{10,... | collective-permute-start | bytes 405512 | tf_op jit(solution)/shard_map/ppermute | solution.py:243
  8.5 0.0 collective-permute-done.4.refs_1_.refs_11_
  8.6 0.3 collective-permute-start.3
  8.9 0.4 %next_products.7.refs_0_.refs_3_.refs_4_.refs_15_ = f32[65,8,128]{2,1,0:T(8,128)S(1)} custom-call(bf16[2,256,1024]{2,1,0:T(8,128)(2,1)S(1)} %get-tuple-element.15.rows, bf16[1024,512]{1,0:T(8,128)(2,1)S(1)} %get-tuple-element.16.weights, f32[1,512]{1,0:T(1,128)S(1)} %get-tuple-element.17.served, f32[33,8,128]{2,1,0:T(8,128)S(1)} %summed.10.refs_0_.refs_2_), custom_call_target="tpu_custom_call" | custom-call | flops 8192 | bytes 8192 | tf_op jit(solution)/shard_map/next_products/pallas_call | solution.py:164
  9.3 1.9 %collective-permute-start.7 = (f32[33,8,128]{2,1,0:T(8,128)S(1)}, f32[33,8,128]{2,1,0:T(8,128)S(1)}, u32[]{:S(2)}, u32[]{:S(2)}) collective-permute-start(f32[33,8,128]{2,1,0:T(8,128)S(1)} %summed.10.refs_0_.refs_2_), channel_id=1, source_target_pairs={{0,4},{1,3},{2,6},{3,1},{4,0},{5,7},{6,2},{7,5},{8,12},{9,11},{10,... | collective-permute-start | bytes 405512 | tf_op jit(solution)/shard_map/ppermute | solution.py:243
  11.2 0.0 collective-permute-done.5.refs_1_.refs_4_.refs_5_.refs_16_
  11.2 0.3 collective-permute-start.8
  11.5 0.0 collective-permute-done.1.refs_2_
  11.5 2.1 %collective-permute-done.3.refs_5_.refs_6_.refs_7_ = f32[33,8,128]{2,1,0:T(8,128)S(1)} collective-permute-done((f32[33,8,128]{2,1,0:T(8,128)S(1)}, f32[33,8,128]{2,1,0:T(8,128)S(1)}, u32[]{:S(2)}, u32[]{:S(2)}) %collective-permute-start.3) | collective-permute-done | bytes 135200 | tf_op jit(solution)/shard_map/ppermute | solution.py:243
  13.7 1.6 %collective-permute-start.6 = (f32[34,8,128]{2,1,0:T(8,128)S(1)}, f32[34,8,128]{2,1,0:T(8,128)S(1)}, u32[]{:S(2)}, u32[]{:S(2)}) collective-permute-start(f32[34,8,128]{2,1,0:T(8,128)S(1)} %summed.12.refs_6_), channel_id=1, source_target_pairs={{0,2},{1,5},{2,0},{3,7},{4,6},{5,1},{6,4},{7,3},{8,10},{9,13},{10,... | collective-permute-start | bytes 417800 | tf_op jit(solution)/shard_map/ppermute | solution.py:243
  15.2 0.0 collective-permute-done.7.refs_2_.refs_12_
  15.2 2.5 %collective-permute-done.8.refs_5_.refs_6_.refs_17_ = f32[33,8,128]{2,1,0:T(8,128)S(1)} collective-permute-done((f32[33,8,128]{2,1,0:T(8,128)S(1)}, f32[33,8,128]{2,1,0:T(8,128)S(1)}, u32[]{:S(2)}, u32[]{:S(2)}) %collective-permute-start.8) | collective-permute-done | bytes 135200 | tf_op jit(solution)/shard_map/ppermute | solution.py:243
  17.8 1.4 %collective-permute-start.10 = (f32[34,8,128]{2,1,0:T(8,128)S(1)}, f32[34,8,128]{2,1,0:T(8,128)S(1)}, u32[]{:S(2)}, u32[]{:S(2)}) collective-permute-start(f32[34,8,128]{2,1,0:T(8,128)S(1)} %summed.13.refs_8_), channel_id=1, source_target_pairs={{0,2},{1,5},{2,0},{3,7},{4,6},{5,1},{6,4},{7,3},{8,10},{9,13},{10,... | collective-permute-start | bytes 417800 | tf_op jit(solution)/shard_map/ppermute | solution.py:243
  19.2 0.0 collective-permute-done.6.refs_3_.refs_7_.refs_8_
  19.2 2.7 %collective-permute-start.9 = (f32[18,8,128]{2,1,0:T(8,128)S(1)}, f32[18,8,128]{2,1,0:T(8,128)S(1)}, u32[]{:S(2)}, u32[]{:S(2)}) collective-permute-start(f32[18,8,128]{2,1,0:T(8,128)S(1)} %summed.14.refs_8_), channel_id=1, source_target_pairs={{0,8},{1,9},{2,10},{3,11},{4,12},{5,13},{6,14},{7,15},{8,0},{9,1},... | collective-permute-start | bytes 221192 | tf_op jit(solution)/shard_map/ppermute | solution.py:243
  21.9 1.0 %collective-permute-done.10.refs_3_.refs_7_.refs_13_.refs_18_ = f32[34,8,128]{2,1,0:T(8,128)S(1)} collective-permute-done((f32[34,8,128]{2,1,0:T(8,128)S(1)}, f32[34,8,128]{2,1,0:T(8,128)S(1)}, u32[]{:S(2)}, u32[]{:S(2)}) %collective-permute-start.10) | collective-permute-done | bytes 139296 | tf_op jit(solution)/shard_map/ppermute | solution.py:243
  22.9 2.5 %collective-permute-start.11 = (f32[18,8,128]{2,1,0:T(8,128)S(1)}, f32[18,8,128]{2,1,0:T(8,128)S(1)}, u32[]{:S(2)}, u32[]{:S(2)}) collective-permute-start(f32[18,8,128]{2,1,0:T(8,128)S(1)} %summed.15), channel_id=1, source_target_pairs={{0,8},{1,9},{2,10},{3,11},{4,12},{5,13},{6,14},{7,15},{8,0},{9,1},... | collective-permute-start | bytes 221192 | tf_op jit(solution)/shard_map/ppermute | solution.py:243
  25.4 1.2 %collective-permute-done.9.refs_4_.refs_9_ = f32[18,8,128]{2,1,0:T(8,128)S(1)} collective-permute-done((f32[18,8,128]{2,1,0:T(8,128)S(1)}, f32[18,8,128]{2,1,0:T(8,128)S(1)}, u32[]{:S(2)}, u32[]{:S(2)}) %collective-permute-start.9) | collective-permute-done | bytes 73760 | tf_op jit(solution)/shard_map/ppermute | solution.py:243
  26.6 2.4 %collective-permute-done.11.refs_14_.refs_19_ = f32[18,8,128]{2,1,0:T(8,128)S(1)} collective-permute-done((f32[18,8,128]{2,1,0:T(8,128)S(1)}, f32[18,8,128]{2,1,0:T(8,128)S(1)}, u32[]{:S(2)}, u32[]{:S(2)}) %collective-permute-start.11) | collective-permute-done | bytes 73760 | tf_op jit(solution)/shard_map/ppermute | solution.py:243
  29.0 0.8 %finish.1 = f32[32,2,512]{2,1,0:T(2,128)} custom-call(f32[65,8,128]{2,1,0:T(8,128)S(1)} %get-tuple-element.18.refs_0_, f32[65,8,128]{2,1,0:T(8,128)S(1)} %collective-permute-done.refs_1_, f32[33,8,128]{2,1,0:T(8,128)S(1)} %collective-permute-done.1.refs_2_, f32[34,8,128]{2,1,0:T(8,128)S(1)} %collective-permute-done.6.refs_3_.refs_7_.refs_8_, ...), custom_call_target="tpu_custom_call" | custom-call | tf_op jit(solution)/shard_map/finish/pallas_call | solution.py:223
  (8 shorter events, 0.2 us)
Async XLA Ops:
  1.8 1.7 %collective-permute-start = (f32[65,8,128]{2,1,0:T(8,128)S(1)}, f32[65,8,128]{2,1,0:T(8,128)S(1)}, u32[]{:S(2)}, u32[]{:S(2)}) collective-permute-start(f32[65,8,128]{2,1,0:T(8,128)S(1)} %get-tuple-element.19), channel_id=1, source_target_pairs={{0,1},{1,0},{2,3},{3,2},{4,5},{5,4},{6,7},{7,6},{8,9},{9,8},{10,11... | collective-permute-start | bytes 798728 | tf_op jit(solution)/shard_map/ppermute | solution.py:243
  3.0 1.6 %collective-permute-start.2 = (f32[65,8,128]{2,1,0:T(8,128)S(1)}, f32[65,8,128]{2,1,0:T(8,128)S(1)}, u32[]{:S(2)}, u32[]{:S(2)}) collective-permute-start(f32[65,8,128]{2,1,0:T(8,128)S(1)} %get-tuple-element.21), channel_id=1, source_target_pairs={{0,1},{1,0},{2,3},{3,2},{4,5},{5,4},{6,7},{7,6},{8,9},{9,8},{10,11... | collective-permute-start | bytes 798728 | tf_op jit(solution)/shard_map/ppermute | solution.py:243
  4.2 4.3 %collective-permute-start.4 = (f32[65,8,128]{2,1,0:T(8,128)S(1)}, f32[65,8,128]{2,1,0:T(8,128)S(1)}, u32[]{:S(2)}, u32[]{:S(2)}) collective-permute-start(f32[65,8,128]{2,1,0:T(8,128)S(1)} %get-tuple-element.23), channel_id=1, source_target_pairs={{0,1},{1,0},{2,3},{3,2},{4,5},{5,4},{6,7},{7,6},{8,9},{9,8},{10,11... | collective-permute-start | bytes 798728 | tf_op jit(solution)/shard_map/ppermute | solution.py:243
  5.4 5.8 %collective-permute-start.5 = (f32[65,8,128]{2,1,0:T(8,128)S(1)}, f32[65,8,128]{2,1,0:T(8,128)S(1)}, u32[]{:S(2)}, u32[]{:S(2)}) collective-permute-start(f32[65,8,128]{2,1,0:T(8,128)S(1)} %get-tuple-element.24), channel_id=1, source_target_pairs={{0,1},{1,0},{2,3},{3,2},{4,5},{5,4},{6,7},{7,6},{8,9},{9,8},{10,11... | collective-permute-start | bytes 798728 | tf_op jit(solution)/shard_map/ppermute | solution.py:243
  5.6 5.9 %collective-permute-start.1 = (f32[33,8,128]{2,1,0:T(8,128)S(1)}, f32[33,8,128]{2,1,0:T(8,128)S(1)}, u32[]{:S(2)}, u32[]{:S(2)}) collective-permute-start(f32[33,8,128]{2,1,0:T(8,128)S(1)} %summed.8.refs_0_.refs_2_), channel_id=1, source_target_pairs={{0,4},{1,3},{2,6},{3,1},{4,0},{5,7},{6,2},{7,5},{8,12},{9,11},{10,... | collective-permute-start | bytes 405512 | tf_op jit(solution)/shard_map/ppermute | solution.py:243
  8.6 5.1 %collective-permute-start.3 = (f32[33,8,128]{2,1,0:T(8,128)S(1)}, f32[33,8,128]{2,1,0:T(8,128)S(1)}, u32[]{:S(2)}, u32[]{:S(2)}) collective-permute-start(f32[33,8,128]{2,1,0:T(8,128)S(1)} %summed.9.refs_0_.refs_2_), channel_id=1, source_target_pairs={{0,4},{1,3},{2,6},{3,1},{4,0},{5,7},{6,2},{7,5},{8,12},{9,11},{10,... | collective-permute-start | bytes 405512 | tf_op jit(solution)/shard_map/ppermute | solution.py:243
  9.3 5.9 %collective-permute-start.7 = (f32[33,8,128]{2,1,0:T(8,128)S(1)}, f32[33,8,128]{2,1,0:T(8,128)S(1)}, u32[]{:S(2)}, u32[]{:S(2)}) collective-permute-start(f32[33,8,128]{2,1,0:T(8,128)S(1)} %summed.10.refs_0_.refs_2_), channel_id=1, source_target_pairs={{0,4},{1,3},{2,6},{3,1},{4,0},{5,7},{6,2},{7,5},{8,12},{9,11},{10,... | collective-permute-start | bytes 405512 | tf_op jit(solution)/shard_map/ppermute | solution.py:243
  11.2 6.6 %collective-permute-start.8 = (f32[33,8,128]{2,1,0:T(8,128)S(1)}, f32[33,8,128]{2,1,0:T(8,128)S(1)}, u32[]{:S(2)}, u32[]{:S(2)}) collective-permute-start(f32[33,8,128]{2,1,0:T(8,128)S(1)} %summed.11.refs_6_), channel_id=1, source_target_pairs={{0,4},{1,3},{2,6},{3,1},{4,0},{5,7},{6,2},{7,5},{8,12},{9,11},{10,... | collective-permute-start | bytes 405512 | tf_op jit(solution)/shard_map/ppermute | solution.py:243
  13.7 5.5 %collective-permute-start.6 = (f32[34,8,128]{2,1,0:T(8,128)S(1)}, f32[34,8,128]{2,1,0:T(8,128)S(1)}, u32[]{:S(2)}, u32[]{:S(2)}) collective-permute-start(f32[34,8,128]{2,1,0:T(8,128)S(1)} %summed.12.refs_6_), channel_id=1, source_target_pairs={{0,2},{1,5},{2,0},{3,7},{4,6},{5,1},{6,4},{7,3},{8,10},{9,13},{10,... | collective-permute-start | bytes 417800 | tf_op jit(solution)/shard_map/ppermute | solution.py:243
  17.8 5.1 %collective-permute-start.10 = (f32[34,8,128]{2,1,0:T(8,128)S(1)}, f32[34,8,128]{2,1,0:T(8,128)S(1)}, u32[]{:S(2)}, u32[]{:S(2)}) collective-permute-start(f32[34,8,128]{2,1,0:T(8,128)S(1)} %summed.13.refs_8_), channel_id=1, source_target_pairs={{0,2},{1,5},{2,0},{3,7},{4,6},{5,1},{6,4},{7,3},{8,10},{9,13},{10,... | collective-permute-start | bytes 417800 | tf_op jit(solution)/shard_map/ppermute | solution.py:243
  19.2 7.4 %collective-permute-start.9 = (f32[18,8,128]{2,1,0:T(8,128)S(1)}, f32[18,8,128]{2,1,0:T(8,128)S(1)}, u32[]{:S(2)}, u32[]{:S(2)}) collective-permute-start(f32[18,8,128]{2,1,0:T(8,128)S(1)} %summed.14.refs_8_), channel_id=1, source_target_pairs={{0,8},{1,9},{2,10},{3,11},{4,12},{5,13},{6,14},{7,15},{8,0},{9,1},... | collective-permute-start | bytes 221192 | tf_op jit(solution)/shard_map/ppermute | solution.py:243
  22.9 6.1 %collective-permute-start.11 = (f32[18,8,128]{2,1,0:T(8,128)S(1)}, f32[18,8,128]{2,1,0:T(8,128)S(1)}, u32[]{:S(2)}, u32[]{:S(2)}) collective-permute-start(f32[18,8,128]{2,1,0:T(8,128)S(1)} %summed.15), channel_id=1, source_target_pairs={{0,8},{1,9},{2,10},{3,11},{4,12},{5,13},{6,14},{7,15},{8,0},{9,1},... | collective-permute-start | bytes 221192 | tf_op jit(solution)/shard_map/ppermute | solution.py:243

commit v11 on v10

--- a/solution.py
+++ b/solution.py
@@ -9,8 +9,8 @@
 
 epsilon = 1e-06
 MIB = 1 << 20
-SHARES = (1, 1, 1, 1)
-PAIRED = ((0, 1), (2, 3))
+SHARES = (1, 1)
+PAIRED = ((0,), (1,))
 
 
 def column_chunks(columns):

time: 30 us -> 26.4 us (0.88)
  waiting for transfers between devices: 9.66 us -> 8.16 us
  Pallas kernels: 5.32 us -> 3.87 us
  starting transfers between devices: 14.8 us -> 14.2 us
    ppermute x12 -> x8, waiting for transfers between devices: 9.66 us -> 8.16 us  [swap(): lax.ppermute(value, 'ap', [(i, i ^ 1 << bit_of[i & 1]) for i in range(dev...]
    pallas_call x4 -> x2, Pallas kernels: 2.56 us -> 1.14 us  [next_products(): pl.pallas_call(functools.partial(next_kernel, bits, jobs), out_shape=[mes...]
    ppermute x12 -> x8, starting transfers between devices: 14.8 us -> 14.2 us  [swap(): lax.ppermute(value, 'ap', [(i, i ^ 1 << bit_of[i & 1]) for i in range(dev...]
  transfers between devices with their start and end apart: 12 -> 8, of which waited for: 6 -> 5; matrix products, arithmetic and copies ran while one was open for 0% -> 0% of each run, Pallas kernels for 9% -> 5%
where the time goes in v11:
time: 26.4 us; the launch traced here: 26.3 us
  starting transfers between devices  14.2 us (54%)
  waiting for transfers between devices  8.16 us (31%)
  Pallas kernels  3.87 us (15%)
    ppermute x8, starting transfers between devices, swap(): lax.ppermute(value, 'ap', [(i, i ^ 1 << bit_of[i & 1]) for i in range(dev...  14.2 us
    ppermute x8, waiting for transfers between devices, swap(): lax.ppermute(value, 'ap', [(i, i ^ 1 << bit_of[i & 1]) for i in range(dev...  8.16 us
    pallas_call x1, Pallas kernels, first_products(): pl.pallas_call(functools.partial(first_kernel, bits), out_shape=(message(...  1.8 us
    pallas_call x2, Pallas kernels, next_products(): pl.pallas_call(functools.partial(next_kernel, bits, jobs), out_shape=[mes...  1.14 us
    pallas_call x1, Pallas kernels, finish(): pl.pallas_call(functools.partial(final_kernel, jobs), out_shape=jax.Shape...  0.78 us
  transfers between devices with their start and end apart: 8, of which 5 were waited for; matrix products, arithmetic and copies ran while one was open for 0% of the time, Pallas kernels for 5%

profile of v11, /device:TPU:0, one launch (start us, length us, event | category | flops | bytes accessed | tf_op | source)
XLA Modules:
  0.0 26.3 jit_solution(11826391134383648639)
XLA Ops:
  0.0 1.8 %first_products.1 = (f32[129,8,128]{2,1,0:T(8,128)S(1)}, bf16[2,256,1024]{2,1,0:T(8,128)(2,1)S(1)}, bf16[1024,512]{1,0:T(8,128)(2,1)S(1)}, f32[1,512]{1,0:T(1,128)S(1)}) custom-call(s32[1,12]{1,0:T(1,128)} %visible.1, s32[4,512]{1,0:T(4,128)} %bitcast.3, bf16[1,12,2,32,512]{4,3,2,1,0:T(8,128)(2,1)} %channel.1, bf16[1024,512]{1,0:T(8,128)(2,1)} %bitcast.2), custom_call_target="tpu_custom_call" | custom-call | flops 8192 | bytes 8192 | tf_op jit(solution)/shard_map/first_products/pallas_call | solution.py:137
  1.8 0.5 %collective-permute-start = (f32[129,8,128]{2,1,0:T(8,128)S(1)}, f32[129,8,128]{2,1,0:T(8,128)S(1)}, u32[]{:S(2)}, u32[]{:S(2)}) collective-permute-start(f32[129,8,128]{2,1,0:T(8,128)S(1)} %get-tuple-element.15), channel_id=1, source_target_pairs={{0,1},{1,0},{2,3},{3,2},{4,5},{5,4},{6,7},{7,6},{8,9},{9,8},{10,11... | collective-permute-start | bytes 1585160 | tf_op jit(solution)/shard_map/ppermute | solution.py:243
  2.3 0.7 %next_products.2 = (f32[129,8,128]{2,1,0:T(8,128)S(1)}, f32[129,8,128]{2,1,0:T(8,128)S(1)}) custom-call(bf16[2,256,1024]{2,1,0:T(8,128)(2,1)S(1)} %get-tuple-element.11.rows, bf16[1024,512]{1,0:T(8,128)(2,1)S(1)} %get-tuple-element.12.weights, f32[1,512]{1,0:T(1,128)S(1)} %get-tuple-element.13.served), custom_call_target="tpu_custom_call" | custom-call | flops 8192 | bytes 8192 | tf_op jit(solution)/shard_map/next_products/pallas_call | solution.py:164
  3.0 0.1 collective-permute-start.2
  3.2 0.7 %collective-permute-done.refs_1_ = f32[129,8,128]{2,1,0:T(8,128)S(1)} collective-permute-done((f32[129,8,128]{2,1,0:T(8,128)S(1)}, f32[129,8,128]{2,1,0:T(8,128)S(1)}, u32[]{:S(2)}, u32[]{:S(2)}) %collective-permute-start) | collective-permute-done | bytes 528416 | tf_op jit(solution)/shard_map/ppermute | solution.py:243
  3.9 3.0 %collective-permute-start.1 = (f32[65,8,128]{2,1,0:T(8,128)S(1)}, f32[65,8,128]{2,1,0:T(8,128)S(1)}, u32[]{:S(2)}, u32[]{:S(2)}) collective-permute-start(f32[65,8,128]{2,1,0:T(8,128)S(1)} %summed.6.refs_0_.refs_2_), channel_id=1, source_target_pairs={{0,4},{1,3},{2,6},{3,1},{4,0},{5,7},{6,2},{7,5},{8,12},{9,11},{10,... | collective-permute-start | bytes 798728 | tf_op jit(solution)/shard_map/ppermute | solution.py:243
  6.9 0.4 %next_products.3.refs_0_.refs_5_ = f32[129,8,128]{2,1,0:T(8,128)S(1)} custom-call(bf16[2,256,1024]{2,1,0:T(8,128)(2,1)S(1)} %get-tuple-element.11.rows, bf16[1024,512]{1,0:T(8,128)(2,1)S(1)} %get-tuple-element.12.weights, f32[1,512]{1,0:T(1,128)S(1)} %get-tuple-element.13.served, f32[65,8,128]{2,1,0:T(8,128)S(1)} %summed.6.refs_0_.refs_2_), custom_call_target="tpu_custom_call" | custom-call | flops 8192 | bytes 8192 | tf_op jit(solution)/shard_map/next_products/pallas_call | solution.py:164
  7.4 0.0 collective-permute-done.2.refs_1_.refs_6_
  7.4 0.4 %collective-permute-start.4 = (f32[65,8,128]{2,1,0:T(8,128)S(1)}, f32[65,8,128]{2,1,0:T(8,128)S(1)}, u32[]{:S(2)}, u32[]{:S(2)}) collective-permute-start(f32[65,8,128]{2,1,0:T(8,128)S(1)} %summed.7.refs_3_), channel_id=1, source_target_pairs={{0,4},{1,3},{2,6},{3,1},{4,0},{5,7},{6,2},{7,5},{8,12},{9,11},{10,... | collective-permute-start | bytes 798728 | tf_op jit(solution)/shard_map/ppermute | solution.py:243
  7.8 3.5 %collective-permute-done.1.refs_2_ = f32[65,8,128]{2,1,0:T(8,128)S(1)} collective-permute-done((f32[65,8,128]{2,1,0:T(8,128)S(1)}, f32[65,8,128]{2,1,0:T(8,128)S(1)}, u32[]{:S(2)}, u32[]{:S(2)}) %collective-permute-start.1) | collective-permute-done | bytes 266272 | tf_op jit(solution)/shard_map/ppermute | solution.py:243
  11.3 2.0 %collective-permute-start.3 = (f32[33,8,128]{2,1,0:T(8,128)S(1)}, f32[33,8,128]{2,1,0:T(8,128)S(1)}, u32[]{:S(2)}, u32[]{:S(2)}) collective-permute-start(f32[33,8,128]{2,1,0:T(8,128)S(1)} %summed.8.refs_3_), channel_id=1, source_target_pairs={{0,2},{1,5},{2,0},{3,7},{4,6},{5,1},{6,4},{7,3},{8,10},{9,13},{10,... | collective-permute-start | bytes 405512 | tf_op jit(solution)/shard_map/ppermute | solution.py:243
  13.3 1.4 %collective-permute-done.4.refs_2_.refs_7_ = f32[65,8,128]{2,1,0:T(8,128)S(1)} collective-permute-done((f32[65,8,128]{2,1,0:T(8,128)S(1)}, f32[65,8,128]{2,1,0:T(8,128)S(1)}, u32[]{:S(2)}, u32[]{:S(2)}) %collective-permute-start.4) | collective-permute-done | bytes 266272 | tf_op jit(solution)/shard_map/ppermute | solution.py:243
  14.7 2.3 %collective-permute-start.6 = (f32[33,8,128]{2,1,0:T(8,128)S(1)}, f32[33,8,128]{2,1,0:T(8,128)S(1)}, u32[]{:S(2)}, u32[]{:S(2)}) collective-permute-start(f32[33,8,128]{2,1,0:T(8,128)S(1)} %summed.9.refs_4_), channel_id=1, source_target_pairs={{0,2},{1,5},{2,0},{3,7},{4,6},{5,1},{6,4},{7,3},{8,10},{9,13},{10,... | collective-permute-start | bytes 405512 | tf_op jit(solution)/shard_map/ppermute | solution.py:243
  17.0 0.0 collective-permute-done.3.refs_3_
  17.0 2.7 %collective-permute-start.5 = (f32[17,8,128]{2,1,0:T(8,128)S(1)}, f32[17,8,128]{2,1,0:T(8,128)S(1)}, u32[]{:S(2)}, u32[]{:S(2)}) collective-permute-start(f32[17,8,128]{2,1,0:T(8,128)S(1)} %summed.10.refs_4_), channel_id=1, source_target_pairs={{0,8},{1,9},{2,10},{3,11},{4,12},{5,13},{6,14},{7,15},{8,0},{9,1},... | collective-permute-start | bytes 208904 | tf_op jit(solution)/shard_map/ppermute | solution.py:243
  19.7 0.3 %collective-permute-done.6.refs_3_.refs_8_ = f32[33,8,128]{2,1,0:T(8,128)S(1)} collective-permute-done((f32[33,8,128]{2,1,0:T(8,128)S(1)}, f32[33,8,128]{2,1,0:T(8,128)S(1)}, u32[]{:S(2)}, u32[]{:S(2)}) %collective-permute-start.6) | collective-permute-done | bytes 135200 | tf_op jit(solution)/shard_map/ppermute | solution.py:243
  20.0 3.2 %collective-permute-start.7 = (f32[17,8,128]{2,1,0:T(8,128)S(1)}, f32[17,8,128]{2,1,0:T(8,128)S(1)}, u32[]{:S(2)}, u32[]{:S(2)}) collective-permute-start(f32[17,8,128]{2,1,0:T(8,128)S(1)} %summed.11), channel_id=1, source_target_pairs={{0,8},{1,9},{2,10},{3,11},{4,12},{5,13},{6,14},{7,15},{8,0},{9,1},... | collective-permute-start | bytes 208904 | tf_op jit(solution)/shard_map/ppermute | solution.py:243
  23.2 0.0 collective-permute-done.5.refs_4_
  23.2 2.3 %collective-permute-done.7.refs_9_ = f32[17,8,128]{2,1,0:T(8,128)S(1)} collective-permute-done((f32[17,8,128]{2,1,0:T(8,128)S(1)}, f32[17,8,128]{2,1,0:T(8,128)S(1)}, u32[]{:S(2)}, u32[]{:S(2)}) %collective-permute-start.7) | collective-permute-done | bytes 69664 | tf_op jit(solution)/shard_map/ppermute | solution.py:243
  25.5 0.8 %finish.1 = f32[32,2,512]{2,1,0:T(2,128)} custom-call(f32[129,8,128]{2,1,0:T(8,128)S(1)} %get-tuple-element.14.refs_0_, f32[129,8,128]{2,1,0:T(8,128)S(1)} %collective-permute-done.refs_1_, f32[65,8,128]{2,1,0:T(8,128)S(1)} %collective-permute-done.1.refs_2_, f32[33,8,128]{2,1,0:T(8,128)S(1)} %collective-permute-done.3.refs_3_, ...), custom_call_target="tpu_custom_call" | custom-call | tf_op jit(solution)/shard_map/finish/pallas_call | solution.py:223
  (6 shorter events, 0.1 us)
Async XLA Ops:
  1.8 2.1 %collective-permute-start = (f32[129,8,128]{2,1,0:T(8,128)S(1)}, f32[129,8,128]{2,1,0:T(8,128)S(1)}, u32[]{:S(2)}, u32[]{:S(2)}) collective-permute-start(f32[129,8,128]{2,1,0:T(8,128)S(1)} %get-tuple-element.15), channel_id=1, source_target_pairs={{0,1},{1,0},{2,3},{3,2},{4,5},{5,4},{6,7},{7,6},{8,9},{9,8},{10,11... | collective-permute-start | bytes 1585160 | tf_op jit(solution)/shard_map/ppermute | solution.py:243
  3.0 4.3 %collective-permute-start.2 = (f32[129,8,128]{2,1,0:T(8,128)S(1)}, f32[129,8,128]{2,1,0:T(8,128)S(1)}, u32[]{:S(2)}, u32[]{:S(2)}) collective-permute-start(f32[129,8,128]{2,1,0:T(8,128)S(1)} %get-tuple-element.16), channel_id=1, source_target_pairs={{0,1},{1,0},{2,3},{3,2},{4,5},{5,4},{6,7},{7,6},{8,9},{9,8},{10,11... | collective-permute-start | bytes 1585160 | tf_op jit(solution)/shard_map/ppermute | solution.py:243
  3.9 7.4 %collective-permute-start.1 = (f32[65,8,128]{2,1,0:T(8,128)S(1)}, f32[65,8,128]{2,1,0:T(8,128)S(1)}, u32[]{:S(2)}, u32[]{:S(2)}) collective-permute-start(f32[65,8,128]{2,1,0:T(8,128)S(1)} %summed.6.refs_0_.refs_2_), channel_id=1, source_target_pairs={{0,4},{1,3},{2,6},{3,1},{4,0},{5,7},{6,2},{7,5},{8,12},{9,11},{10,... | collective-permute-start | bytes 798728 | tf_op jit(solution)/shard_map/ppermute | solution.py:243
  7.4 7.3 %collective-permute-start.4 = (f32[65,8,128]{2,1,0:T(8,128)S(1)}, f32[65,8,128]{2,1,0:T(8,128)S(1)}, u32[]{:S(2)}, u32[]{:S(2)}) collective-permute-start(f32[65,8,128]{2,1,0:T(8,128)S(1)} %summed.7.refs_3_), channel_id=1, source_target_pairs={{0,4},{1,3},{2,6},{3,1},{4,0},{5,7},{6,2},{7,5},{8,12},{9,11},{10,... | collective-permute-start | bytes 798728 | tf_op jit(solution)/shard_map/ppermute | solution.py:243
  11.3 5.7 %collective-permute-start.3 = (f32[33,8,128]{2,1,0:T(8,128)S(1)}, f32[33,8,128]{2,1,0:T(8,128)S(1)}, u32[]{:S(2)}, u32[]{:S(2)}) collective-permute-start(f32[33,8,128]{2,1,0:T(8,128)S(1)} %summed.8.refs_3_), channel_id=1, source_target_pairs={{0,2},{1,5},{2,0},{3,7},{4,6},{5,1},{6,4},{7,3},{8,10},{9,13},{10,... | collective-permute-start | bytes 405512 | tf_op jit(solution)/shard_map/ppermute | solution.py:243
  14.7 5.3 %collective-permute-start.6 = (f32[33,8,128]{2,1,0:T(8,128)S(1)}, f32[33,8,128]{2,1,0:T(8,128)S(1)}, u32[]{:S(2)}, u32[]{:S(2)}) collective-permute-start(f32[33,8,128]{2,1,0:T(8,128)S(1)} %summed.9.refs_4_), channel_id=1, source_target_pairs={{0,2},{1,5},{2,0},{3,7},{4,6},{5,1},{6,4},{7,3},{8,10},{9,13},{10,... | collective-permute-start | bytes 405512 | tf_op jit(solution)/shard_map/ppermute | solution.py:243
  17.0 6.2 %collective-permute-start.5 = (f32[17,8,128]{2,1,0:T(8,128)S(1)}, f32[17,8,128]{2,1,0:T(8,128)S(1)}, u32[]{:S(2)}, u32[]{:S(2)}) collective-permute-start(f32[17,8,128]{2,1,0:T(8,128)S(1)} %summed.10.refs_4_), channel_id=1, source_target_pairs={{0,8},{1,9},{2,10},{3,11},{4,12},{5,13},{6,14},{7,15},{8,0},{9,1},... | collective-permute-start | bytes 208904 | tf_op jit(solution)/shard_map/ppermute | solution.py:243
  20.0 5.5 %collective-permute-start.7 = (f32[17,8,128]{2,1,0:T(8,128)S(1)}, f32[17,8,128]{2,1,0:T(8,128)S(1)}, u32[]{:S(2)}, u32[]{:S(2)}) collective-permute-start(f32[17,8,128]{2,1,0:T(8,128)S(1)} %summed.11), channel_id=1, source_target_pairs={{0,8},{1,9},{2,10},{3,11},{4,12},{5,13},{6,14},{7,15},{8,0},{9,1},... | collective-permute-start | bytes 208904 | tf_op jit(solution)/shard_map/ppermute | solution.py:243

commit v12 on v8

v12 whole, which is shorter than its diff:
```python
import functools

import jax
import jax.numpy as jnp
from jax import lax
from jax.experimental import pallas as pl
from jax.experimental.pallas import tpu as pltpu
from jax.sharding import PartitionSpec as P

epsilon = 1e-06
MIB = 1 << 20


def chip_orders(bits):
    first = list(range(1, bits))
    second = list(first)
    if bits > 2:
        second[0], second[1] = second[1], second[0]
    return second, first


def place_of(group, me, core, bits):
    away = [1 - (((group ^ me) >> bit) & 1) for bit in range(1, bits)]
    if bits > 2:
        swapped = core == 0
        away[:2] = [jnp.where(swapped, away[1], away[0]), jnp.where(swapped, away[0], away[1])]
    place = 0
    for value in away:
        place = place * 2 + value
    return place


def write_products(users, rows, weights, served, out):
    slots, antennas = rows.shape[0] // users, rows.shape[1] // 2
    blocks, steps = weights.shape[1] // 128, users // 8
    group = min(slots, 8)
    for base in range(0, slots, group):
        plain = rows[base * users:(base + group) * users, :]
        turned = jnp.concatenate([-plain[:, antennas:], plain[:, :antennas]], axis=1)
        both = jnp.concatenate([plain, turned], axis=0)
        value = jnp.dot(both, weights, preferred_element_type=jnp.float32)
        value = jnp.where(served, value, 0.0)
        for half in range(2):
            for slot in range(group):
                top = (half * group + slot) * users
                for block in range(blocks):
                    piece = value[top:top + users, block * 128:(block + 1) * 128]
                    start = (((base + slot) * 2 + half) * blocks + block) * steps
                    out[start:start + steps] = piece.reshape(steps, 8, 128)


def power_tile(weights, served):
    wide = weights.astype(jnp.float32)
    power = jnp.sum(wide * wide, axis=0, keepdims=True)
    power = jnp.where(served, power, 0.0)
    blocks = power.shape[1] // 128
    pieces = [power[:, block * 128:(block + 1) * 128] for block in range(blocks)]
    return jnp.concatenate(pieces + [jnp.zeros((8 - blocks, 128), jnp.float32)], axis=0)


def first_kernel(
    bits, visible, cluster, channel, precoder,
    out, rows, weights, served,
    seen, names, raw, sems,
):
    me = lax.axis_index("ap")
    held, users, antennas = raw.shape[1], raw.shape[3], raw.shape[4]
    loads = [
        pltpu.make_async_copy(visible, seen, sems.at[0]),
        pltpu.make_async_copy(channel, raw, sems.at[1]),
        pltpu.make_async_copy(cluster, names, sems.at[2]),
        pltpu.make_async_copy(precoder, weights, sems.at[3]),
    ]
    for load in loads:
        load.start()
    rows[...] = jnp.zeros_like(rows)
    loads[0].wait()
    loads[1].wait()
    for v in range(held):
        core = seen[0, v] & 1
        keep = 1 - (core ^ (me & 1))
        at = pl.ds(pl.multiple_of(place_of(seen[0, v], me, core, bits) * users, users), users)
        rows[keep, at, 0:antennas] = raw[0, v, 0]
        rows[keep, at, antennas:2 * antennas] = raw[0, v, 1]
    loads[2].wait()
    here = jnp.max((names[...] == me).astype(jnp.float32), axis=0, keepdims=True)
    served[...] = here
    loads[3].wait()
    mask = here > 0.0
    write_products(users, rows.at[0, 0:rows.shape[1] // 2], weights[...], mask, out)
    out[out.shape[0] - 1] = power_tile(weights[...], mask)


def next_kernel(users, keep, region, rows, weights, served, *refs):
    size = rows.shape[1] // 2
    mine = rows.at[keep, region * size:(region + 1) * size]
    write_products(users, mine, weights[...], served[...] > 0.0, refs[-1])


def message(tiles):
    return jax.ShapeDtypeStruct((tiles, 8, 128), jnp.float32)


def estimate(size=8192):
    return pl.CostEstimate(flops=size, bytes_accessed=size, transcendentals=0)


def first_products(bits, visible, cluster, channel, precoder):
    users, antennas = channel.shape[3], channel.shape[4]
    columns = precoder.shape[1]
    slots = 1 << (bits - 1)
    vmem = pl.BlockSpec(memory_space=pltpu.VMEM)
    hbm = pl.BlockSpec(memory_space=pltpu.HBM)
    operands = (visible, cluster, channel, precoder)
    return pl.pallas_call(
        functools.partial(first_kernel, bits),
        out_shape=(
            message(slots * (users // 8) * (columns // 128) + 1),
            jax.ShapeDtypeStruct((2, slots * users, 2 * antennas), jnp.bfloat16),
            jax.ShapeDtypeStruct(precoder.shape, jnp.bfloat16),
            jax.ShapeDtypeStruct((1, columns), jnp.float32),
        ),
        in_specs=[hbm] * 4,
        out_specs=(vmem,) * 4,
        scratch_shapes=[
            pltpu.SMEM(visible.shape, jnp.int32),
            pltpu.VMEM(cluster.shape, jnp.int32),
            pltpu.VMEM(channel.shape, jnp.bfloat16),
            pltpu.SemaphoreType.DMA((4,)),
        ],
        compiler_params=pltpu.CompilerParams(vmem_limit_bytes=52 * MIB if slots > 8 else 24 * MIB),
        cost_estimate=estimate(),
        name="first_products",
    )(*[pltpu.with_memory_space_constraint(operand, pltpu.HBM) for operand in operands])


def next_products(users, keep, region, rows, weights, served):
    slots = rows.shape[1] // users
    vmem = pl.BlockSpec(memory_space=pltpu.VMEM)
    return pl.pallas_call(
        functools.partial(next_kernel, users, keep, region),
        out_shape=message(slots * (users // 8) * (weights.shape[1] // 128)),
        in_specs=[vmem] * 3,
        out_specs=vmem,
        compiler_params=pltpu.CompilerParams(vmem_limit_bytes=48 * MIB if slots > 8 else 16 * MIB),
        cost_estimate=estimate(),
        name="next_products",
    )(rows, weights, served)


def add_up(refs, terms, count):
    total = refs[terms[0][0]][terms[0][1]:terms[0][1] + count]
    for ref, start in terms[1:]:
        total = total + refs[ref][start:start + count]
    return total


def sum_kernel(jobs, *refs):
    at = 0
    for terms, count in jobs:
        refs[-1][at:at + count] = add_up(refs, terms, count)
        at += count


def summed(arrays, jobs, cost):
    size = sum(count for _, count in jobs)
    vmem = pl.BlockSpec(memory_space=pltpu.VMEM)
    return pl.pallas_call(
        functools.partial(sum_kernel, jobs),
        out_shape=message(size),
        in_specs=[vmem] * len(arrays),
        out_specs=vmem,
        compiler_params=pltpu.CompilerParams(vmem_limit_bytes=8 * MIB),
        cost_estimate=estimate(cost),
        name="summed",
    )(*arrays)


def final_kernel(terms, powers, *refs):
    out = refs[-1]
    users, blocks = out.shape[0], out.shape[2] // 128
    steps = users // 8
    scale = lax.rsqrt(add_up(refs, powers, 1)[0] + epsilon)
    total = add_up(refs, terms, 2 * blocks * steps)
    for half in range(2):
        for block in range(blocks):
            start = (half * blocks + block) * steps
            value = total[start:start + steps].reshape(users, 128)
            factor = scale[block:block + 1, :]
            value = jnp.where(factor > 0.0, value * factor, 0.0)
            out[:, half, block * 128:(block + 1) * 128] = value


def finish(arrays, terms, powers, users, columns):
    vmem = pl.BlockSpec(memory_space=pltpu.VMEM)
    return pl.pallas_call(
        functools.partial(final_kernel, terms, powers),
        out_shape=jax.ShapeDtypeStruct((users, 2, columns), jnp.float32),
        in_specs=[vmem] * len(arrays),
        out_specs=vmem,
        compiler_params=pltpu.CompilerParams(vmem_limit_bytes=8 * MIB),
        name="finish",
    )(*arrays)


def message_order(chips):
    steps = []
    for step in range(chips):
        size = 1 << (chips - 1 - step)
        first = (1 << chips) - 2 * size
        steps.append(list(range(first, first + size)))
    if chips < 3:
        return [(step, slots) for step, slots in enumerate(steps)]
    quarter, half = len(steps[0]) // 4, len(steps[1]) // 2
    order = [
        (0, steps[0][:quarter]),
        (0, steps[0][quarter:3 * quarter]),
        (1, steps[1][:half]),
        (0, steps[0][3 * quarter:]),
        (1, steps[1][half:]),
    ]
    return order + [(step, steps[step]) for step in range(2, chips)]


def on_device(channel, precoder, visible, cluster):
    devices = lax.axis_size("ap")
    bits = devices.bit_length() - 1
    users, columns = channel.shape[3], precoder.shape[2]
    tiles = (users // 8) * (columns // 128) * 2
    orders = chip_orders(bits)
    flat = precoder.reshape(-1, columns)
    half = devices // 4

    def swap(value, bit_of):
        return lax.ppermute(value, "ap", [(i, i ^ (1 << bit_of[i & 1])) for i in range(devices)])

    arrays = []
    terms = [[] for _ in range(2 * half)]
    powers = []

    def add(array, slots, power):
        for at, slot in enumerate(slots):
            terms[slot].append((len(arrays), at * tiles))
        if power:
            powers.append((len(arrays), len(slots) * tiles))
        arrays.append(array)

    def total(slots, power, cost=8192):
        jobs = [(list(terms[slot]), tiles) for slot in slots] + ([(list(powers), 1)] if power else [])
        used = sorted({array for parts, _ in jobs for array, _ in parts})
        jobs = [([(used.index(array), start) for array, start in parts], count) for parts, count in jobs]
        return summed([arrays[array] for array in used], jobs, cost)

    sent, rows, weights, served = first_products(bits, visible, cluster.T, channel, flat)
    came = swap(sent, (0, 0))
    later = next_products(users, 0, 1, rows, weights, served)
    came_later = swap(later, (0, 0))
    add(sent, [], False)
    powers.append((0, half * tiles))
    add(next_products(users, 1, 0, rows, weights, served), range(half), False)
    add(came, range(half), True)
    add(next_products(users, 1, 1, rows, weights, served), range(half, 2 * half), False)
    add(came_later, range(half, 2 * half), False)
    with_power = set()
    last = 2 * half - 1
    for step, slots in message_order(bits - 1):
        power = step not in with_power
        with_power.add(step)
        came = swap(total(slots, power), (orders[0][step], orders[1][step]))
        slots = [slot + (1 << (bits - 2 - step)) for slot in slots]
        add(came, slots, power)
        if last in slots and step < bits - 2:
            own = total([last], False, 64 * MIB)
            terms[last] = []
            add(own, [last], False)
    used = sorted({array for array, _ in terms[last] + powers})
    return finish(
        [arrays[array] for array in used],
        [(used.index(array), start) for array, start in terms[last]],
        [(used.index(array), start) for array, start in powers],
        users, columns,
    )


def solution(mesh):
    in_specs = (
        P(("parts", "ap"), None, None, None, None),
        P(None, ("parts", "ap"), None),
        P(("parts", "ap"), None),
        P("parts", None),
    )
    out_specs = P(("parts", "ap"), None, None)
    return jax.shard_map(
        on_device, mesh=mesh, in_specs=in_specs, out_specs=out_specs, check_vma=False
    )
```

time: 26.9 us -> 25.4 us (0.944)
  starting transfers between devices: 14.4 us -> 11.7 us
  waiting for transfers between devices: 8.17 us -> 9.33 us
    ppermute x8, starting transfers between devices: 14.4 us -> 11.7 us  [swap(): lax.ppermute(value, 'ap', [(i, i ^ 1 << bit_of[i & 1]) for i in range(dev...]
    ppermute x8, waiting for transfers between devices: 8.17 us -> 9.33 us  [swap(): lax.ppermute(value, 'ap', [(i, i ^ 1 << bit_of[i & 1]) for i in range(dev...]
  transfers between devices with their start and end apart: 8 -> 8, of which waited for: 5 -> 6; matrix products, arithmetic and copies ran while one was open for 0% -> 0% of each run, Pallas kernels for 4% -> 6%
where the time goes in v12:
time: 25.4 us; the launch traced here: 25.2 us
  starting transfers between devices  11.7 us (46%)
  waiting for transfers between devices  9.33 us (37%)
  Pallas kernels  4.2 us (17%)
    ppermute x8, starting transfers between devices, swap(): lax.ppermute(value, 'ap', [(i, i ^ 1 << bit_of[i & 1]) for i in range(dev...  11.7 us
    ppermute x8, waiting for transfers between devices, swap(): lax.ppermute(value, 'ap', [(i, i ^ 1 << bit_of[i & 1]) for i in range(dev...  9.33 us
    pallas_call x1, Pallas kernels, first_products(): pl.pallas_call(functools.partial(first_kernel, bits), out_shape=(message(...  1.96 us
    pallas_call x3, Pallas kernels, next_products(): pl.pallas_call(functools.partial(next_kernel, users, keep, region), out_s...  1.29 us
    pallas_call x1, Pallas kernels, finish(): pl.pallas_call(functools.partial(final_kernel, terms, powers), out_shape=...  0.75 us
  transfers between devices with their start and end apart: 8, of which 6 were waited for; matrix products, arithmetic and copies ran while one was open for 0% of the time, Pallas kernels for 6%

profile of v12, /device:TPU:0, one launch (start us, length us, event | category | flops | bytes accessed | tf_op | source)
XLA Modules:
  0.0 25.2 jit_solution(17157905904736548535)
XLA Ops:
  0.0 2.0 %first_products.1 = (f32[129,8,128]{2,1,0:T(8,128)S(1)}, bf16[2,256,1024]{2,1,0:T(8,128)(2,1)S(1)}, bf16[1024,512]{1,0:T(8,128)(2,1)S(1)}, f32[1,512]{1,0:T(1,128)S(1)}) custom-call(s32[1,12]{1,0:T(1,128)} %visible.1, s32[4,512]{1,0:T(4,128)} %bitcast.3, bf16[1,12,2,32,512]{4,3,2,1,0:T(8,128)(2,1)} %channel.1, bf16[1024,512]{1,0:T(8,128)(2,1)} %bitcast.2), custom_call_target="tpu_custom_call" | custom-call | flops 8192 | bytes 8192 | tf_op jit(solution)/shard_map/first_products/pallas_call | solution.py:115
  2.0 0.5 %collective-permute-start = (f32[129,8,128]{2,1,0:T(8,128)S(1)}, f32[129,8,128]{2,1,0:T(8,128)S(1)}, u32[]{:S(2)}, u32[]{:S(2)}) collective-permute-start(f32[129,8,128]{2,1,0:T(8,128)S(1)} %get-tuple-element.9.refs_0_), channel_id=1, source_target_pairs={{0,1},{1,0},{2,3},{3,2},{4,5},{5,4},{6,7},{7,6},{8,9},{9,8},{10,11... | collective-permute-start | bytes 1585160 | tf_op jit(solution)/shard_map/ppermute | solution.py:235
  2.5 0.4 %next_products.5 = f32[128,8,128]{2,1,0:T(8,128)S(1)} custom-call(bf16[2,256,1024]{2,1,0:T(8,128)(2,1)S(1)} %get-tuple-element.10.rows, bf16[1024,512]{1,0:T(8,128)(2,1)S(1)} %get-tuple-element.11.weights, f32[1,512]{1,0:T(1,128)S(1)} %get-tuple-element.12.served), custom_call_target="tpu_custom_call" | custom-call | flops 8192 | bytes 8192 | tf_op jit(solution)/shard_map/next_products/pallas_call | solution.py:140
  2.9 0.1 collective-permute-start.2
  3.0 0.4 %next_products.3.refs_1_.refs_0_ = f32[128,8,128]{2,1,0:T(8,128)S(1)} custom-call(bf16[2,256,1024]{2,1,0:T(8,128)(2,1)S(1)} %get-tuple-element.10.rows, bf16[1024,512]{1,0:T(8,128)(2,1)S(1)} %get-tuple-element.11.weights, f32[1,512]{1,0:T(1,128)S(1)} %get-tuple-element.12.served), custom_call_target="tpu_custom_call" | custom-call | flops 8192 | bytes 8192 | tf_op jit(solution)/shard_map/next_products/pallas_call | solution.py:140
  3.5 0.5 %collective-permute-done.refs_2_.refs_1_ = f32[129,8,128]{2,1,0:T(8,128)S(1)} collective-permute-done((f32[129,8,128]{2,1,0:T(8,128)S(1)}, f32[129,8,128]{2,1,0:T(8,128)S(1)}, u32[]{:S(2)}, u32[]{:S(2)}) %collective-permute-start) | collective-permute-done | bytes 528416 | tf_op jit(solution)/shard_map/ppermute | solution.py:235
  4.0 3.0 %collective-permute-start.1 = (f32[33,8,128]{2,1,0:T(8,128)S(1)}, f32[33,8,128]{2,1,0:T(8,128)S(1)}, u32[]{:S(2)}, u32[]{:S(2)}) collective-permute-start(f32[33,8,128]{2,1,0:T(8,128)S(1)} %summed.8), channel_id=1, source_target_pairs={{0,4},{1,3},{2,6},{3,1},{4,0},{5,7},{6,2},{7,5},{8,12},{9,11},{10,... | collective-permute-start | bytes 405512 | tf_op jit(solution)/shard_map/ppermute | solution.py:235
  7.1 0.1 collective-permute-start.5
  7.2 0.4 %next_products.4.refs_2_.refs_0_ = f32[128,8,128]{2,1,0:T(8,128)S(1)} custom-call(bf16[2,256,1024]{2,1,0:T(8,128)(2,1)S(1)} %get-tuple-element.10.rows, bf16[1024,512]{1,0:T(8,128)(2,1)S(1)} %get-tuple-element.11.weights, f32[1,512]{1,0:T(1,128)S(1)} %get-tuple-element.12.served), custom_call_target="tpu_custom_call" | custom-call | flops 8192 | bytes 8192 | tf_op jit(solution)/shard_map/next_products/pallas_call | solution.py:140
  7.6 0.0 collective-permute-done.2.refs_3_.refs_1_
  7.6 2.4 %collective-permute-done.1.refs_4_.refs_2_ = f32[33,8,128]{2,1,0:T(8,128)S(1)} collective-permute-done((f32[33,8,128]{2,1,0:T(8,128)S(1)}, f32[33,8,128]{2,1,0:T(8,128)S(1)}, u32[]{:S(2)}, u32[]{:S(2)}) %collective-permute-start.1) | collective-permute-done | bytes 135200 | tf_op jit(solution)/shard_map/ppermute | solution.py:235
  10.1 2.0 %collective-permute-start.3 = (f32[33,8,128]{2,1,0:T(8,128)S(1)}, f32[33,8,128]{2,1,0:T(8,128)S(1)}, u32[]{:S(2)}, u32[]{:S(2)}) collective-permute-start(f32[33,8,128]{2,1,0:T(8,128)S(1)} %summed.9), channel_id=1, source_target_pairs={{0,2},{1,5},{2,0},{3,7},{4,6},{5,1},{6,4},{7,3},{8,10},{9,13},{10,... | collective-permute-start | bytes 405512 | tf_op jit(solution)/shard_map/ppermute | solution.py:235
  12.1 1.6 %collective-permute-start.4 = (f32[32,8,128]{2,1,0:T(8,128)S(1)}, f32[32,8,128]{2,1,0:T(8,128)S(1)}, u32[]{:S(2)}, u32[]{:S(2)}) collective-permute-start(f32[32,8,128]{2,1,0:T(8,128)S(1)} %summed.10), channel_id=1, source_target_pairs={{0,4},{1,3},{2,6},{3,1},{4,0},{5,7},{6,2},{7,5},{8,12},{9,11},{10,... | collective-permute-start | bytes 393224 | tf_op jit(solution)/shard_map/ppermute | solution.py:235
  13.7 1.0 %collective-permute-done.5.refs_2_.refs_5_ = f32[64,8,128]{2,1,0:T(8,128)S(1)} collective-permute-done((f32[64,8,128]{2,1,0:T(8,128)S(1)}, f32[64,8,128]{2,1,0:T(8,128)S(1)}, u32[]{:S(2)}, u32[]{:S(2)}) %collective-permute-start.5) | collective-permute-done | bytes 262176 | tf_op jit(solution)/shard_map/ppermute | solution.py:235
  14.7 1.4 %collective-permute-start.6 = (f32[32,8,128]{2,1,0:T(8,128)S(1)}, f32[32,8,128]{2,1,0:T(8,128)S(1)}, u32[]{:S(2)}, u32[]{:S(2)}) collective-permute-start(f32[32,8,128]{2,1,0:T(8,128)S(1)} %summed.13), channel_id=1, source_target_pairs={{0,2},{1,5},{2,0},{3,7},{4,6},{5,1},{6,4},{7,3},{8,10},{9,13},{10,... | collective-permute-start | bytes 393224 | tf_op jit(solution)/shard_map/ppermute | solution.py:235
  16.1 0.3 %collective-permute-done.3.refs_6_.refs_3_ = f32[33,8,128]{2,1,0:T(8,128)S(1)} collective-permute-done((f32[33,8,128]{2,1,0:T(8,128)S(1)}, f32[33,8,128]{2,1,0:T(8,128)S(1)}, u32[]{:S(2)}, u32[]{:S(2)}) %collective-permute-start.3) | collective-permute-done | bytes 135200 | tf_op jit(solution)/shard_map/ppermute | solution.py:235
  16.5 2.9 %collective-permute-start.7 = (f32[33,8,128]{2,1,0:T(8,128)S(1)}, f32[33,8,128]{2,1,0:T(8,128)S(1)}, u32[]{:S(2)}, u32[]{:S(2)}) collective-permute-start(f32[33,8,128]{2,1,0:T(8,128)S(1)} %summed.15), channel_id=1, source_target_pairs={{0,8},{1,9},{2,10},{3,11},{4,12},{5,13},{6,14},{7,15},{8,0},{9,1},... | collective-permute-start | bytes 405512 | tf_op jit(solution)/shard_map/ppermute | solution.py:235
  19.4 0.0 collective-permute-done.4.refs_2_
  19.4 0.3 %collective-permute-done.6.refs_1_ = f32[32,8,128]{2,1,0:T(8,128)S(1)} collective-permute-done((f32[32,8,128]{2,1,0:T(8,128)S(1)}, f32[32,8,128]{2,1,0:T(8,128)S(1)}, u32[]{:S(2)}, u32[]{:S(2)}) %collective-permute-start.6) | collective-permute-done | bytes 131104 | tf_op jit(solution)/shard_map/ppermute | solution.py:235
  19.8 4.7 %collective-permute-done.7.refs_5_ = f32[33,8,128]{2,1,0:T(8,128)S(1)} collective-permute-done((f32[33,8,128]{2,1,0:T(8,128)S(1)}, f32[33,8,128]{2,1,0:T(8,128)S(1)}, u32[]{:S(2)}, u32[]{:S(2)}) %collective-permute-start.7) | collective-permute-done | bytes 135200 | tf_op jit(solution)/shard_map/ppermute | solution.py:235
  24.5 0.8 %finish.1 = f32[32,2,512]{2,1,0:T(2,128)} custom-call(f32[129,8,128]{2,1,0:T(8,128)S(1)} %get-tuple-element.9.refs_0_, f32[129,8,128]{2,1,0:T(8,128)S(1)} %collective-permute-done.refs_2_.refs_1_, f32[33,8,128]{2,1,0:T(8,128)S(1)} %collective-permute-done.1.refs_4_.refs_2_, f32[33,8,128]{2,1,0:T(8,128)S(1)} %collective-permute-done.3.refs_6_.refs_3_, ...), custom_call_target="tpu_custom_call" | custom-call | tf_op jit(solution)/shard_map/finish/pallas_call | solution.py:196
  (8 shorter events, 0.2 us)
Async XLA Ops:
  2.0 2.1 %collective-permute-start = (f32[129,8,128]{2,1,0:T(8,128)S(1)}, f32[129,8,128]{2,1,0:T(8,128)S(1)}, u32[]{:S(2)}, u32[]{:S(2)}) collective-permute-start(f32[129,8,128]{2,1,0:T(8,128)S(1)} %get-tuple-element.9.refs_0_), channel_id=1, source_target_pairs={{0,1},{1,0},{2,3},{3,2},{4,5},{5,4},{6,7},{7,6},{8,9},{9,8},{10,11... | collective-permute-start | bytes 1585160 | tf_op jit(solution)/shard_map/ppermute | solution.py:235
  2.9 4.7 %collective-permute-start.2 = (f32[128,8,128]{2,1,0:T(8,128)S(1)}, f32[128,8,128]{2,1,0:T(8,128)S(1)}, u32[]{:S(2)}, u32[]{:S(2)}) collective-permute-start(f32[128,8,128]{2,1,0:T(8,128)S(1)} %next_products.5), channel_id=1, source_target_pairs={{0,1},{1,0},{2,3},{3,2},{4,5},{5,4},{6,7},{7,6},{8,9},{9,8},{10,11... | collective-permute-start | bytes 1572872 | tf_op jit(solution)/shard_map/ppermute | solution.py:235
  4.0 6.0 %collective-permute-start.1 = (f32[33,8,128]{2,1,0:T(8,128)S(1)}, f32[33,8,128]{2,1,0:T(8,128)S(1)}, u32[]{:S(2)}, u32[]{:S(2)}) collective-permute-start(f32[33,8,128]{2,1,0:T(8,128)S(1)} %summed.8), channel_id=1, source_target_pairs={{0,4},{1,3},{2,6},{3,1},{4,0},{5,7},{6,2},{7,5},{8,12},{9,11},{10,... | collective-permute-start | bytes 405512 | tf_op jit(solution)/shard_map/ppermute | solution.py:235
  7.1 7.6 %collective-permute-start.5 = (f32[64,8,128]{2,1,0:T(8,128)S(1)}, f32[64,8,128]{2,1,0:T(8,128)S(1)}, u32[]{:S(2)}, u32[]{:S(2)}) collective-permute-start(f32[64,8,128]{2,1,0:T(8,128)S(1)} %summed.12), channel_id=1, source_target_pairs={{0,4},{1,3},{2,6},{3,1},{4,0},{5,7},{6,2},{7,5},{8,12},{9,11},{10,... | collective-permute-start | bytes 786440 | tf_op jit(solution)/shard_map/ppermute | solution.py:235
  10.1 6.4 %collective-permute-start.3 = (f32[33,8,128]{2,1,0:T(8,128)S(1)}, f32[33,8,128]{2,1,0:T(8,128)S(1)}, u32[]{:S(2)}, u32[]{:S(2)}) collective-permute-start(f32[33,8,128]{2,1,0:T(8,128)S(1)} %summed.9), channel_id=1, source_target_pairs={{0,2},{1,5},{2,0},{3,7},{4,6},{5,1},{6,4},{7,3},{8,10},{9,13},{10,... | collective-permute-start | bytes 405512 | tf_op jit(solution)/shard_map/ppermute | solution.py:235
  12.1 7.3 %collective-permute-start.4 = (f32[32,8,128]{2,1,0:T(8,128)S(1)}, f32[32,8,128]{2,1,0:T(8,128)S(1)}, u32[]{:S(2)}, u32[]{:S(2)}) collective-permute-start(f32[32,8,128]{2,1,0:T(8,128)S(1)} %summed.10), channel_id=1, source_target_pairs={{0,4},{1,3},{2,6},{3,1},{4,0},{5,7},{6,2},{7,5},{8,12},{9,11},{10,... | collective-permute-start | bytes 393224 | tf_op jit(solution)/shard_map/ppermute | solution.py:235
  14.7 5.0 %collective-permute-start.6 = (f32[32,8,128]{2,1,0:T(8,128)S(1)}, f32[32,8,128]{2,1,0:T(8,128)S(1)}, u32[]{:S(2)}, u32[]{:S(2)}) collective-permute-start(f32[32,8,128]{2,1,0:T(8,128)S(1)} %summed.13), channel_id=1, source_target_pairs={{0,2},{1,5},{2,0},{3,7},{4,6},{5,1},{6,4},{7,3},{8,10},{9,13},{10,... | collective-permute-start | bytes 393224 | tf_op jit(solution)/shard_map/ppermute | solution.py:235
  16.5 8.0 %collective-permute-start.7 = (f32[33,8,128]{2,1,0:T(8,128)S(1)}, f32[33,8,128]{2,1,0:T(8,128)S(1)}, u32[]{:S(2)}, u32[]{:S(2)}) collective-permute-start(f32[33,8,128]{2,1,0:T(8,128)S(1)} %summed.15), channel_id=1, source_target_pairs={{0,8},{1,9},{2,10},{3,11},{4,12},{5,13},{6,14},{7,15},{8,0},{9,1},... | collective-permute-start | bytes 405512 | tf_op jit(solution)/shard_map/ppermute | solution.py:235

commit v13 on v12

--- a/solution.py
+++ b/solution.py
@@ -162,18 +162,18 @@
         at += count
 
 
-def summed(arrays, jobs, cost):
+def summed(arrays, jobs, cost, after):
     size = sum(count for _, count in jobs)
     vmem = pl.BlockSpec(memory_space=pltpu.VMEM)
     return pl.pallas_call(
         functools.partial(sum_kernel, jobs),
         out_shape=message(size),
-        in_specs=[vmem] * len(arrays),
+        in_specs=[vmem] * (len(arrays) + len(after)),
         out_specs=vmem,
         compiler_params=pltpu.CompilerParams(vmem_limit_bytes=8 * MIB),
         cost_estimate=estimate(cost),
         name="summed",
-    )(*arrays)
+    )(*arrays, *after)
 
 
 def final_kernel(terms, powers, *refs):
@@ -181,10 +181,10 @@
     users, blocks = out.shape[0], out.shape[2] // 128
     steps = users // 8
     scale = lax.rsqrt(add_up(refs, powers, 1)[0] + epsilon)
-    total = add_up(refs, terms, 2 * blocks * steps)
     for half in range(2):
+        total = add_up(refs, terms[half], blocks * steps)
         for block in range(blocks):
-            start = (half * blocks + block) * steps
+            start = block * steps
             value = total[start:start + steps].reshape(users, 128)
             factor = scale[block:block + 1, :]
             value = jnp.where(factor > 0.0, value * factor, 0.0)
@@ -208,25 +208,27 @@
     for step in range(chips):
         size = 1 << (chips - 1 - step)
         first = (1 << chips) - 2 * size
-        steps.append(list(range(first, first + size)))
+        steps.append([(slot, part) for slot in range(first, first + size) for part in range(2)])
     if chips < 3:
-        return [(step, slots) for step, slots in enumerate(steps)]
+        return [(step, pieces) for step, pieces in enumerate(steps)]
     quarter, half = len(steps[0]) // 4, len(steps[1]) // 2
+    parts = [steps[0][at * quarter:(at + 1) * quarter] for at in range(4)]
     order = [
-        (0, steps[0][:quarter]),
-        (0, steps[0][quarter:3 * quarter]),
+        (0, parts[0]),
+        (0, parts[2] + parts[1][::2]),
         (1, steps[1][:half]),
-        (0, steps[0][3 * quarter:]),
+        (0, parts[1][1::2] + parts[3]),
+        (2, steps[2]),
         (1, steps[1][half:]),
     ]
-    return order + [(step, steps[step]) for step in range(2, chips)]
+    return order + [(step, steps[step]) for step in range(3, chips)]
 
 
 def on_device(channel, precoder, visible, cluster):
     devices = lax.axis_size("ap")
     bits = devices.bit_length() - 1
     users, columns = channel.shape[3], precoder.shape[2]
-    tiles = (users // 8) * (columns // 128) * 2
+    tiles = (users // 8) * (columns // 128)
     orders = chip_orders(bits)
     flat = precoder.reshape(-1, columns)
     half = devices // 4
@@ -235,48 +237,51 @@
         return lax.ppermute(value, "ap", [(i, i ^ (1 << bit_of[i & 1])) for i in range(devices)])
 
     arrays = []
-    terms = [[] for _ in range(2 * half)]
+    terms = {(slot, part): [] for slot in range(2 * half) for part in range(2)}
     powers = []
 
-    def add(array, slots, power):
-        for at, slot in enumerate(slots):
-            terms[slot].append((len(arrays), at * tiles))
+    def add(array, pieces, power):
+        for at, piece in enumerate(pieces):
+            terms[piece].append((len(arrays), at * tiles))
         if power:
-            powers.append((len(arrays), len(slots) * tiles))
+            powers.append((len(arrays), len(pieces) * tiles))
         arrays.append(array)
 
-    def total(slots, power, cost=8192):
-        jobs = [(list(terms[slot]), tiles) for slot in slots] + ([(list(powers), 1)] if power else [])
+    def total(pieces, power, cost, after):
+        jobs = [(list(terms[piece]), tiles) for piece in pieces]
+        jobs += [(list(powers), 1)] * int(power)
         used = sorted({array for parts, _ in jobs for array, _ in parts})
         jobs = [([(used.index(array), start) for array, start in parts], count) for parts, count in jobs]
-        return summed([arrays[array] for array in used], jobs, cost)
+        return summed([arrays[array] for array in used], jobs, cost, after)
+
+    def region(first):
+        return [(slot, part) for slot in range(first, first + half) for part in range(2)]
 
     sent, rows, weights, served = first_products(bits, visible, cluster.T, channel, flat)
     came = swap(sent, (0, 0))
     later = next_products(users, 0, 1, rows, weights, served)
     came_later = swap(later, (0, 0))
     add(sent, [], False)
-    powers.append((0, half * tiles))
-    add(next_products(users, 1, 0, rows, weights, served), range(half), False)
-    add(came, range(half), True)
-    add(next_products(users, 1, 1, rows, weights, served), range(half, 2 * half), False)
-    add(came_later, range(half, 2 * half), False)
-    with_power = set()
-    last = 2 * half - 1
-    for step, slots in message_order(bits - 1):
+    powers.append((0, 2 * half * tiles))
+    add(next_products(users, 1, 0, rows, weights, served), region(0), False)
+    add(came, region(0), True)
+    add(next_products(users, 1, 1, rows, weights, served), region(half), False)
+    add(came_later, region(half), False)
+    last = [(2 * half - 1, 0), (2 * half - 1, 1)]
+    with_power, after = set(), []
+    for step, pieces in message_order(bits - 1):
         power = step not in with_power
         with_power.add(step)
-        came = swap(total(slots, power), (orders[0][step], orders[1][step]))
-        slots = [slot + (1 << (bits - 2 - step)) for slot in slots]
-        add(came, slots, power)
-        if last in slots and step < bits - 2:
-            own = total([last], False, 64 * MIB)
-            terms[last] = []
-            add(own, [last], False)
-    used = sorted({array for array, _ in terms[last] + powers})
+        now = total(pieces, power, 4096 * MIB if step == 2 else 8192, after)
+        came = swap(now, (orders[0][step], orders[1][step]))
+        after = [now] if step > 0 else []
+        pieces = [(slot + (1 << (bits - 2 - step)), part) for slot, part in pieces]
+        add(came, pieces, power)
+    jobs = [(terms[piece], tiles) for piece in last]
+    used = sorted({array for parts, _ in jobs + [(powers, 1)] for array, _ in parts})
     return finish(
         [arrays[array] for array in used],
-        [(used.index(array), start) for array, start in terms[last]],
+        [[(used.index(array), start) for array, start in parts] for parts, _ in jobs],
         [(used.index(array), start) for array, start in powers],
         users, columns,
     )

time: 25.4 us -> 25.7 us (1.012)
  starting transfers between devices: 11.7 us -> 12.2 us
    ppermute x8, starting transfers between devices: 11.7 us -> 12.2 us  [swap(): lax.ppermute(value, 'ap', [(i, i ^ 1 << bit_of[i & 1]) for i in range(dev...]
  transfers between devices with their start and end apart: 8 -> 8, of which waited for: 6 -> 5; matrix products, arithmetic and copies ran while one was open for 0% -> 0% of each run, Pallas kernels for 6% -> 6%
where the time goes in v13:
time: 25.7 us; the launch traced here: 25.6 us
  starting transfers between devices  12.2 us (47%)
  waiting for transfers between devices  9.16 us (36%)
  Pallas kernels  4.19 us (16%)
    ppermute x8, starting transfers between devices, swap(): lax.ppermute(value, 'ap', [(i, i ^ 1 << bit_of[i & 1]) for i in range(dev...  12.2 us
    ppermute x8, waiting for transfers between devices, swap(): lax.ppermute(value, 'ap', [(i, i ^ 1 << bit_of[i & 1]) for i in range(dev...  9.16 us
    pallas_call x1, Pallas kernels, first_products(): pl.pallas_call(functools.partial(first_kernel, bits), out_shape=(message(...  1.96 us
    pallas_call x3, Pallas kernels, next_products(): pl.pallas_call(functools.partial(next_kernel, users, keep, region), out_s...  1.29 us
    pallas_call x1, Pallas kernels, finish(): pl.pallas_call(functools.partial(final_kernel, terms, powers), out_shape=...  0.77 us
  transfers between devices with their start and end apart: 8, of which 5 were waited for; matrix products, arithmetic and copies ran while one was open for 0% of the time, Pallas kernels for 6%

profile of v13, /device:TPU:0, one launch (start us, length us, event | category | flops | bytes accessed | tf_op | source)
XLA Modules:
  0.0 25.6 jit_solution(5959991619261824744)
XLA Ops:
  0.0 2.0 %first_products.1 = (f32[129,8,128]{2,1,0:T(8,128)S(1)}, bf16[2,256,1024]{2,1,0:T(8,128)(2,1)S(1)}, bf16[1024,512]{1,0:T(8,128)(2,1)S(1)}, f32[1,512]{1,0:T(1,128)S(1)}) custom-call(s32[1,12]{1,0:T(1,128)} %visible.1, s32[4,512]{1,0:T(4,128)} %bitcast.3, bf16[1,12,2,32,512]{4,3,2,1,0:T(8,128)(2,1)} %channel.1, bf16[1024,512]{1,0:T(8,128)(2,1)} %bitcast.2), custom_call_target="tpu_custom_call" | custom-call | flops 8192 | bytes 8192 | tf_op jit(solution)/shard_map/first_products/pallas_call | solution.py:115
  2.0 0.5 %collective-permute-start = (f32[129,8,128]{2,1,0:T(8,128)S(1)}, f32[129,8,128]{2,1,0:T(8,128)S(1)}, u32[]{:S(2)}, u32[]{:S(2)}) collective-permute-start(f32[129,8,128]{2,1,0:T(8,128)S(1)} %get-tuple-element.9.refs_0_), channel_id=1, source_target_pairs={{0,1},{1,0},{2,3},{3,2},{4,5},{5,4},{6,7},{7,6},{8,9},{9,8},{10,11... | collective-permute-start | bytes 1585160 | tf_op jit(solution)/shard_map/ppermute | solution.py:237
  2.5 0.4 %next_products.4 = f32[128,8,128]{2,1,0:T(8,128)S(1)} custom-call(bf16[2,256,1024]{2,1,0:T(8,128)(2,1)S(1)} %get-tuple-element.10.rows, bf16[1024,512]{1,0:T(8,128)(2,1)S(1)} %get-tuple-element.11.weights, f32[1,512]{1,0:T(1,128)S(1)} %get-tuple-element.12.served), custom_call_target="tpu_custom_call" | custom-call | flops 8192 | bytes 8192 | tf_op jit(solution)/shard_map/next_products/pallas_call | solution.py:140
  2.9 0.1 collective-permute-start.1
  3.0 0.4 %next_products.5.refs_1_.refs_0_ = f32[128,8,128]{2,1,0:T(8,128)S(1)} custom-call(bf16[2,256,1024]{2,1,0:T(8,128)(2,1)S(1)} %get-tuple-element.10.rows, bf16[1024,512]{1,0:T(8,128)(2,1)S(1)} %get-tuple-element.11.weights, f32[1,512]{1,0:T(1,128)S(1)} %get-tuple-element.12.served), custom_call_target="tpu_custom_call" | custom-call | flops 8192 | bytes 8192 | tf_op jit(solution)/shard_map/next_products/pallas_call | solution.py:140
  3.5 0.5 %collective-permute-done.refs_2_.refs_1_ = f32[129,8,128]{2,1,0:T(8,128)S(1)} collective-permute-done((f32[129,8,128]{2,1,0:T(8,128)S(1)}, f32[129,8,128]{2,1,0:T(8,128)S(1)}, u32[]{:S(2)}, u32[]{:S(2)}) %collective-permute-start) | collective-permute-done | bytes 528416 | tf_op jit(solution)/shard_map/ppermute | solution.py:237
  4.0 3.0 %collective-permute-start.2 = (f32[33,8,128]{2,1,0:T(8,128)S(1)}, f32[33,8,128]{2,1,0:T(8,128)S(1)}, u32[]{:S(2)}, u32[]{:S(2)}) collective-permute-start(f32[33,8,128]{2,1,0:T(8,128)S(1)} %summed.6), channel_id=1, source_target_pairs={{0,4},{1,3},{2,6},{3,1},{4,0},{5,7},{6,2},{7,5},{8,12},{9,11},{10,... | collective-permute-start | bytes 405512 | tf_op jit(solution)/shard_map/ppermute | solution.py:237
  7.1 0.1 collective-permute-start.5
  7.2 0.4 %next_products.3.refs_2_.refs_0_ = f32[128,8,128]{2,1,0:T(8,128)S(1)} custom-call(bf16[2,256,1024]{2,1,0:T(8,128)(2,1)S(1)} %get-tuple-element.10.rows, bf16[1024,512]{1,0:T(8,128)(2,1)S(1)} %get-tuple-element.11.weights, f32[1,512]{1,0:T(1,128)S(1)} %get-tuple-element.12.served), custom_call_target="tpu_custom_call" | custom-call | flops 8192 | bytes 8192 | tf_op jit(solution)/shard_map/next_products/pallas_call | solution.py:140
  7.6 0.0 collective-permute-done.1.refs_3_.refs_1_
  7.6 2.4 %collective-permute-done.2.refs_4_ = f32[33,8,128]{2,1,0:T(8,128)S(1)} collective-permute-done((f32[33,8,128]{2,1,0:T(8,128)S(1)}, f32[33,8,128]{2,1,0:T(8,128)S(1)}, u32[]{:S(2)}, u32[]{:S(2)}) %collective-permute-start.2) | collective-permute-done | bytes 135200 | tf_op jit(solution)/shard_map/ppermute | solution.py:237
  10.1 2.0 %collective-permute-start.3 = (f32[33,8,128]{2,1,0:T(8,128)S(1)}, f32[33,8,128]{2,1,0:T(8,128)S(1)}, u32[]{:S(2)}, u32[]{:S(2)}) collective-permute-start(f32[33,8,128]{2,1,0:T(8,128)S(1)} %summed.7.refs_2_), channel_id=1, source_target_pairs={{0,2},{1,5},{2,0},{3,7},{4,6},{5,1},{6,4},{7,3},{8,10},{9,13},{10,... | collective-permute-start | bytes 405512 | tf_op jit(solution)/shard_map/ppermute | solution.py:237
  12.1 1.6 %collective-permute-start.4 = (f32[48,8,128]{2,1,0:T(8,128)S(1)}, f32[48,8,128]{2,1,0:T(8,128)S(1)}, u32[]{:S(2)}, u32[]{:S(2)}) collective-permute-start(f32[48,8,128]{2,1,0:T(8,128)S(1)} %summed.8), channel_id=1, source_target_pairs={{0,4},{1,3},{2,6},{3,1},{4,0},{5,7},{6,2},{7,5},{8,12},{9,11},{10,... | collective-permute-start | bytes 589832 | tf_op jit(solution)/shard_map/ppermute | solution.py:237
  13.7 0.0 collective-permute-done.5.refs_5_.refs_2_
  13.8 2.7 %collective-permute-done.3.refs_6_.refs_5_ = f32[33,8,128]{2,1,0:T(8,128)S(1)} collective-permute-done((f32[33,8,128]{2,1,0:T(8,128)S(1)}, f32[33,8,128]{2,1,0:T(8,128)S(1)}, u32[]{:S(2)}, u32[]{:S(2)}) %collective-permute-start.3) | collective-permute-done | bytes 135200 | tf_op jit(solution)/shard_map/ppermute | solution.py:237
  16.5 3.2 %collective-permute-start.6 = (f32[33,8,128]{2,1,0:T(8,128)S(1)}, f32[33,8,128]{2,1,0:T(8,128)S(1)}, u32[]{:S(2)}, u32[]{:S(2)}) collective-permute-start(f32[33,8,128]{2,1,0:T(8,128)S(1)} %summed.10.refs_4_), channel_id=1, source_target_pairs={{0,8},{1,9},{2,10},{3,11},{4,12},{5,13},{6,14},{7,15},{8,0},{9,1},... | collective-permute-start | bytes 405512 | tf_op jit(solution)/shard_map/ppermute | solution.py:237
  19.7 0.0 collective-permute-done.4.refs_3_.refs_6_
  19.8 1.6 %collective-permute-start.7 = (f32[32,8,128]{2,1,0:T(8,128)S(1)}, f32[32,8,128]{2,1,0:T(8,128)S(1)}, u32[]{:S(2)}, u32[]{:S(2)}) collective-permute-start(f32[32,8,128]{2,1,0:T(8,128)S(1)} %summed.11), channel_id=1, source_target_pairs={{0,2},{1,5},{2,0},{3,7},{4,6},{5,1},{6,4},{7,3},{8,10},{9,13},{10,... | collective-permute-start | bytes 393224 | tf_op jit(solution)/shard_map/ppermute | solution.py:237
  21.3 2.9 %collective-permute-done.6.refs_7_ = f32[33,8,128]{2,1,0:T(8,128)S(1)} collective-permute-done((f32[33,8,128]{2,1,0:T(8,128)S(1)}, f32[33,8,128]{2,1,0:T(8,128)S(1)}, u32[]{:S(2)}, u32[]{:S(2)}) %collective-permute-start.6) | collective-permute-done | bytes 135200 | tf_op jit(solution)/shard_map/ppermute | solution.py:237
  24.2 0.6 %collective-permute-done.7.refs_8_ = f32[32,8,128]{2,1,0:T(8,128)S(1)} collective-permute-done((f32[32,8,128]{2,1,0:T(8,128)S(1)}, f32[32,8,128]{2,1,0:T(8,128)S(1)}, u32[]{:S(2)}, u32[]{:S(2)}) %collective-permute-start.7) | collective-permute-done | bytes 131104 | tf_op jit(solution)/shard_map/ppermute | solution.py:237
  24.8 0.8 %finish.1 = f32[32,2,512]{2,1,0:T(2,128)} custom-call(f32[129,8,128]{2,1,0:T(8,128)S(1)} %get-tuple-element.9.refs_0_, f32[129,8,128]{2,1,0:T(8,128)S(1)} %collective-permute-done.refs_2_.refs_1_, f32[128,8,128]{2,1,0:T(8,128)S(1)} %next_products.3.refs_2_.refs_0_, f32[128,8,128]{2,1,0:T(8,128)S(1)} %collective-permute-done.1.refs_3_.refs_1_, ...), custom_call_target="tpu_custom_call" | custom-call | tf_op jit(solution)/shard_map/finish/pallas_call | solution.py:196
  (6 shorter events, 0.2 us)
Async XLA Ops:
  2.0 2.1 %collective-permute-start = (f32[129,8,128]{2,1,0:T(8,128)S(1)}, f32[129,8,128]{2,1,0:T(8,128)S(1)}, u32[]{:S(2)}, u32[]{:S(2)}) collective-permute-start(f32[129,8,128]{2,1,0:T(8,128)S(1)} %get-tuple-element.9.refs_0_), channel_id=1, source_target_pairs={{0,1},{1,0},{2,3},{3,2},{4,5},{5,4},{6,7},{7,6},{8,9},{9,8},{10,11... | collective-permute-start | bytes 1585160 | tf_op jit(solution)/shard_map/ppermute | solution.py:237
  2.9 4.7 %collective-permute-start.1 = (f32[128,8,128]{2,1,0:T(8,128)S(1)}, f32[128,8,128]{2,1,0:T(8,128)S(1)}, u32[]{:S(2)}, u32[]{:S(2)}) collective-permute-start(f32[128,8,128]{2,1,0:T(8,128)S(1)} %next_products.4), channel_id=1, source_target_pairs={{0,1},{1,0},{2,3},{3,2},{4,5},{5,4},{6,7},{7,6},{8,9},{9,8},{10,11... | collective-permute-start | bytes 1572872 | tf_op jit(solution)/shard_map/ppermute | solution.py:237
  4.0 6.0 %collective-permute-start.2 = (f32[33,8,128]{2,1,0:T(8,128)S(1)}, f32[33,8,128]{2,1,0:T(8,128)S(1)}, u32[]{:S(2)}, u32[]{:S(2)}) collective-permute-start(f32[33,8,128]{2,1,0:T(8,128)S(1)} %summed.6), channel_id=1, source_target_pairs={{0,4},{1,3},{2,6},{3,1},{4,0},{5,7},{6,2},{7,5},{8,12},{9,11},{10,... | collective-permute-start | bytes 405512 | tf_op jit(solution)/shard_map/ppermute | solution.py:237
  7.1 6.7 %collective-permute-start.5 = (f32[48,8,128]{2,1,0:T(8,128)S(1)}, f32[48,8,128]{2,1,0:T(8,128)S(1)}, u32[]{:S(2)}, u32[]{:S(2)}) collective-permute-start(f32[48,8,128]{2,1,0:T(8,128)S(1)} %summed.9), channel_id=1, source_target_pairs={{0,4},{1,3},{2,6},{3,1},{4,0},{5,7},{6,2},{7,5},{8,12},{9,11},{10,... | collective-permute-start | bytes 589832 | tf_op jit(solution)/shard_map/ppermute | solution.py:237
  10.1 6.4 %collective-permute-start.3 = (f32[33,8,128]{2,1,0:T(8,128)S(1)}, f32[33,8,128]{2,1,0:T(8,128)S(1)}, u32[]{:S(2)}, u32[]{:S(2)}) collective-permute-start(f32[33,8,128]{2,1,0:T(8,128)S(1)} %summed.7.refs_2_), channel_id=1, source_target_pairs={{0,2},{1,5},{2,0},{3,7},{4,6},{5,1},{6,4},{7,3},{8,10},{9,13},{10,... | collective-permute-start | bytes 405512 | tf_op jit(solution)/shard_map/ppermute | solution.py:237
  12.1 7.6 %collective-permute-start.4 = (f32[48,8,128]{2,1,0:T(8,128)S(1)}, f32[48,8,128]{2,1,0:T(8,128)S(1)}, u32[]{:S(2)}, u32[]{:S(2)}) collective-permute-start(f32[48,8,128]{2,1,0:T(8,128)S(1)} %summed.8), channel_id=1, source_target_pairs={{0,4},{1,3},{2,6},{3,1},{4,0},{5,7},{6,2},{7,5},{8,12},{9,11},{10,... | collective-permute-start | bytes 589832 | tf_op jit(solution)/shard_map/ppermute | solution.py:237
  16.5 7.7 %collective-permute-start.6 = (f32[33,8,128]{2,1,0:T(8,128)S(1)}, f32[33,8,128]{2,1,0:T(8,128)S(1)}, u32[]{:S(2)}, u32[]{:S(2)}) collective-permute-start(f32[33,8,128]{2,1,0:T(8,128)S(1)} %summed.10.refs_4_), channel_id=1, source_target_pairs={{0,8},{1,9},{2,10},{3,11},{4,12},{5,13},{6,14},{7,15},{8,0},{9,1},... | collective-permute-start | bytes 405512 | tf_op jit(solution)/shard_map/ppermute | solution.py:237
  19.8 5.0 %collective-permute-start.7 = (f32[32,8,128]{2,1,0:T(8,128)S(1)}, f32[32,8,128]{2,1,0:T(8,128)S(1)}, u32[]{:S(2)}, u32[]{:S(2)}) collective-permute-start(f32[32,8,128]{2,1,0:T(8,128)S(1)} %summed.11), channel_id=1, source_target_pairs={{0,2},{1,5},{2,0},{3,7},{4,6},{5,1},{6,4},{7,3},{8,10},{9,13},{10,... | collective-permute-start | bytes 393224 | tf_op jit(solution)/shard_map/ppermute | solution.py:237

commit v14 on v12

--- a/solution.py
+++ b/solution.py
@@ -33,7 +33,7 @@
 def write_products(users, rows, weights, served, out):
     slots, antennas = rows.shape[0] // users, rows.shape[1] // 2
     blocks, steps = weights.shape[1] // 128, users // 8
-    group = min(slots, 8)
+    group = max(size for size in range(1, 9) if slots % size == 0)
     for base in range(0, slots, group):
         plain = rows[base * users:(base + group) * users, :]
         turned = jnp.concatenate([-plain[:, antennas:], plain[:, :antennas]], axis=1)
@@ -60,7 +60,7 @@
 
 def first_kernel(
     bits, visible, cluster, channel, precoder,
-    out, rows, weights, served,
+    out, kept, rows, weights, served,
     seen, names, raw, sems,
 ):
     me = lax.axis_index("ap")
@@ -87,13 +87,14 @@
     served[...] = here
     loads[3].wait()
     mask = here > 0.0
-    write_products(users, rows.at[0, 0:rows.shape[1] // 2], weights[...], mask, out)
+    size = (kept.shape[0] // (weights.shape[1] // 128) // 2) * 8
+    write_products(users, rows.at[0, 0:size], weights[...], mask, out)
     out[out.shape[0] - 1] = power_tile(weights[...], mask)
-
-
-def next_kernel(users, keep, region, rows, weights, served, *refs):
-    size = rows.shape[1] // 2
-    mine = rows.at[keep, region * size:(region + 1) * size]
+    write_products(users, rows.at[1, 0:size], weights[...], mask, kept)
+
+
+def next_kernel(users, keep, first, slots, rows, weights, served, *refs):
+    mine = rows.at[keep, first * users:(first + slots) * users]
     write_products(users, mine, weights[...], served[...] > 0.0, refs[-1])
 
 
@@ -105,23 +106,25 @@
     return pl.CostEstimate(flops=size, bytes_accessed=size, transcendentals=0)
 
 
-def first_products(bits, visible, cluster, channel, precoder):
+def first_products(bits, first, visible, cluster, channel, precoder):
     users, antennas = channel.shape[3], channel.shape[4]
     columns = precoder.shape[1]
     slots = 1 << (bits - 1)
+    tiles = first * (users // 8) * (columns // 128) * 2
     vmem = pl.BlockSpec(memory_space=pltpu.VMEM)
     hbm = pl.BlockSpec(memory_space=pltpu.HBM)
     operands = (visible, cluster, channel, precoder)
     return pl.pallas_call(
         functools.partial(first_kernel, bits),
         out_shape=(
-            message(slots * (users // 8) * (columns // 128) + 1),
+            message(tiles + 1),
+            message(tiles),
             jax.ShapeDtypeStruct((2, slots * users, 2 * antennas), jnp.bfloat16),
             jax.ShapeDtypeStruct(precoder.shape, jnp.bfloat16),
             jax.ShapeDtypeStruct((1, columns), jnp.float32),
         ),
         in_specs=[hbm] * 4,
-        out_specs=(vmem,) * 4,
+        out_specs=(vmem,) * 5,
         scratch_shapes=[
             pltpu.SMEM(visible.shape, jnp.int32),
             pltpu.VMEM(cluster.shape, jnp.int32),
@@ -134,15 +137,15 @@
     )(*[pltpu.with_memory_space_constraint(operand, pltpu.HBM) for operand in operands])
 
 
-def next_products(users, keep, region, rows, weights, served):
-    slots = rows.shape[1] // users
+def next_products(users, keep, first, slots, rows, weights, served):
     vmem = pl.BlockSpec(memory_space=pltpu.VMEM)
+    big = slots > 8
     return pl.pallas_call(
-        functools.partial(next_kernel, users, keep, region),
-        out_shape=message(slots * (users // 8) * (weights.shape[1] // 128)),
+        functools.partial(next_kernel, users, keep, first, slots),
+        out_shape=message(slots * (users // 8) * (weights.shape[1] // 128) * 2),
         in_specs=[vmem] * 3,
         out_specs=vmem,
-        compiler_params=pltpu.CompilerParams(vmem_limit_bytes=48 * MIB if slots > 8 else 16 * MIB),
+        compiler_params=pltpu.CompilerParams(vmem_limit_bytes=48 * MIB if big else 16 * MIB),
         cost_estimate=estimate(),
         name="next_products",
     )(rows, weights, served)
@@ -251,22 +254,27 @@
         jobs = [([(used.index(array), start) for array, start in parts], count) for parts, count in jobs]
         return summed([arrays[array] for array in used], jobs, cost)
 
-    sent, rows, weights, served = first_products(bits, visible, cluster.T, channel, flat)
+    quarter = half // 4
+    sent, kept, rows, weights, served = first_products(
+        bits, quarter, visible, cluster.T, channel, flat
+    )
     came = swap(sent, (0, 0))
-    later = next_products(users, 0, 1, rows, weights, served)
-    came_later = swap(later, (0, 0))
     add(sent, [], False)
-    powers.append((0, half * tiles))
-    add(next_products(users, 1, 0, rows, weights, served), range(half), False)
-    add(came, range(half), True)
-    add(next_products(users, 1, 1, rows, weights, served), range(half, 2 * half), False)
-    add(came_later, range(half, 2 * half), False)
+    powers.append((0, quarter * tiles))
+    add(kept, range(quarter), False)
+    add(came, range(quarter), True)
+    products = functools.partial(next_products, users, rows=rows, weights=weights, served=served)
+    rest = range(quarter, 2 * half)
+    later = swap(products(0, quarter, len(rest)), (0, 0))
+    add(products(1, quarter, len(rest)), rest, False)
+    add(later, rest, False)
     with_power = set()
     last = 2 * half - 1
-    for step, slots in message_order(bits - 1):
+    for number, (step, slots) in enumerate(message_order(bits - 1)):
         power = step not in with_power
         with_power.add(step)
-        came = swap(total(slots, power), (orders[0][step], orders[1][step]))
+        now = total(slots, power, 65536 * MIB if number == 0 else 8192)
+        came = swap(now, (orders[0][step], orders[1][step]))
         slots = [slot + (1 << (bits - 2 - step)) for slot in slots]
         add(came, slots, power)
         if last in slots and step < bits - 2:

time: 25.4 us -> 25.3 us (level)
  waiting for transfers between devices: 9.33 us -> 8.09 us
  starting transfers between devices: 11.7 us -> 12.8 us
    ppermute x8, waiting for transfers between devices: 9.33 us -> 8.09 us  [swap(): lax.ppermute(value, 'ap', [(i, i ^ 1 << bit_of[i & 1]) for i in range(dev...]
    ppermute x8, starting transfers between devices: 11.7 us -> 12.8 us  [swap(): lax.ppermute(value, 'ap', [(i, i ^ 1 << bit_of[i & 1]) for i in range(dev...]
    pallas_call x3 -> x2, Pallas kernels: 1.29 us -> 1.27 us  [next_products(): pl.pallas_call(functools.partial(next_kernel, users, keep, first, slots),...]
  transfers between devices with their start and end apart: 8 -> 8, of which waited for: 6 -> 5; matrix products, arithmetic and copies ran while one was open for 0% -> 0% of each run, Pallas kernels for 6% -> 6%
where the time goes in v14:
time: 25.3 us; the launch traced here: 25.1 us
  starting transfers between devices  12.8 us (51%)
  waiting for transfers between devices  8.09 us (32%)
  Pallas kernels  4.21 us (17%)
    ppermute x8, starting transfers between devices, swap(): lax.ppermute(value, 'ap', [(i, i ^ 1 << bit_of[i & 1]) for i in range(dev...  12.8 us
    ppermute x8, waiting for transfers between devices, swap(): lax.ppermute(value, 'ap', [(i, i ^ 1 << bit_of[i & 1]) for i in range(dev...  8.09 us
    pallas_call x1, Pallas kernels, first_products(): pl.pallas_call(functools.partial(first_kernel, bits), out_shape=(message(...  2 us
    pallas_call x2, Pallas kernels, next_products(): pl.pallas_call(functools.partial(next_kernel, users, keep, first, slots),...  1.27 us
    pallas_call x1, Pallas kernels, finish(): pl.pallas_call(functools.partial(final_kernel, terms, powers), out_shape=...  0.75 us
  transfers between devices with their start and end apart: 8, of which 5 were waited for; matrix products, arithmetic and copies ran while one was open for 0% of the time, Pallas kernels for 6%

profile of v14, /device:TPU:0, one launch (start us, length us, event | category | flops | bytes accessed | tf_op | source)
XLA Modules:
  0.0 25.1 jit_solution(21179119426975027)
XLA Ops:
  0.0 2.0 %first_products.1 = (f32[33,8,128]{2,1,0:T(8,128)S(1)}, f32[32,8,128]{2,1,0:T(8,128)S(1)}, bf16[2,256,1024]{2,1,0:T(8,128)(2,1)S(1)}, bf16[1024,512]{1,0:T(8,128)(2,1)S(1)}, f32[1,512]{1,0:T(1,128)S(1)}) custom-call(s32[1,12]{1,0:T(1,128)} %visible.1, s32[4,512]{1,0:T(4,128)} %bitcast.3, bf16[1,12,2,32,512]{4,3,2,1,0:T(8,128)(2,1)} %channel.1, ...), custom_call_target="tpu_custom_call" | custom-call | flops 8192 | bytes 8192 | tf_op jit(solution)/shard_map/first_products/pallas_call | solution.py:117
  2.0 0.5 %collective-permute-start = (f32[33,8,128]{2,1,0:T(8,128)S(1)}, f32[33,8,128]{2,1,0:T(8,128)S(1)}, u32[]{:S(2)}, u32[]{:S(2)}) collective-permute-start(f32[33,8,128]{2,1,0:T(8,128)S(1)} %get-tuple-element.10.refs_0_), channel_id=1, source_target_pairs={{0,1},{1,0},{2,3},{3,2},{4,5},{5,4},{6,7},{7,6},{8,9},{9,8},{10,11... | collective-permute-start | bytes 405512 | tf_op jit(solution)/shard_map/ppermute | solution.py:238
  2.5 0.6 %next_products.3 = f32[224,8,128]{2,1,0:T(8,128)S(1)} custom-call(bf16[2,256,1024]{2,1,0:T(8,128)(2,1)S(1)} %get-tuple-element.12.rows, bf16[1024,512]{1,0:T(8,128)(2,1)S(1)} %get-tuple-element.13.weights, f32[1,512]{1,0:T(1,128)S(1)} %get-tuple-element.14.served), custom_call_target="tpu_custom_call" | custom-call | flops 8192 | bytes 8192 | tf_op jit(solution)/shard_map/next_products/pallas_call | solution.py:143
  3.2 0.1 collective-permute-start.2
  3.3 0.2 collective-permute-done.refs_2_.refs_1_
  3.5 3.0 %collective-permute-start.1 = (f32[33,8,128]{2,1,0:T(8,128)S(1)}, f32[33,8,128]{2,1,0:T(8,128)S(1)}, u32[]{:S(2)}, u32[]{:S(2)}) collective-permute-start(f32[33,8,128]{2,1,0:T(8,128)S(1)} %summed.8), channel_id=1, source_target_pairs={{0,4},{1,3},{2,6},{3,1},{4,0},{5,7},{6,2},{7,5},{8,12},{9,11},{10,... | collective-permute-start | bytes 405512 | tf_op jit(solution)/shard_map/ppermute | solution.py:238
  6.5 0.6 %next_products.2.refs_2_.refs_0_ = f32[224,8,128]{2,1,0:T(8,128)S(1)} custom-call(bf16[2,256,1024]{2,1,0:T(8,128)(2,1)S(1)} %get-tuple-element.12.rows, bf16[1024,512]{1,0:T(8,128)(2,1)S(1)} %get-tuple-element.13.weights, f32[1,512]{1,0:T(1,128)S(1)} %get-tuple-element.14.served), custom_call_target="tpu_custom_call" | custom-call | flops 8192 | bytes 8192 | tf_op jit(solution)/shard_map/next_products/pallas_call | solution.py:143
  7.2 0.0 collective-permute-done.2.refs_3_.refs_1_
  7.2 1.3 %collective-permute-start.5 = (f32[64,8,128]{2,1,0:T(8,128)S(1)}, f32[64,8,128]{2,1,0:T(8,128)S(1)}, u32[]{:S(2)}, u32[]{:S(2)}) collective-permute-start(f32[64,8,128]{2,1,0:T(8,128)S(1)} %summed.12), channel_id=1, source_target_pairs={{0,4},{1,3},{2,6},{3,1},{4,0},{5,7},{6,2},{7,5},{8,12},{9,11},{10,... | collective-permute-start | bytes 786440 | tf_op jit(solution)/shard_map/ppermute | solution.py:238
  8.5 1.0 %collective-permute-done.1.refs_4_.refs_2_ = f32[33,8,128]{2,1,0:T(8,128)S(1)} collective-permute-done((f32[33,8,128]{2,1,0:T(8,128)S(1)}, f32[33,8,128]{2,1,0:T(8,128)S(1)}, u32[]{:S(2)}, u32[]{:S(2)}) %collective-permute-start.1) | collective-permute-done | bytes 135200 | tf_op jit(solution)/shard_map/ppermute | solution.py:238
  9.6 2.0 %collective-permute-start.3 = (f32[33,8,128]{2,1,0:T(8,128)S(1)}, f32[33,8,128]{2,1,0:T(8,128)S(1)}, u32[]{:S(2)}, u32[]{:S(2)}) collective-permute-start(f32[33,8,128]{2,1,0:T(8,128)S(1)} %summed.9), channel_id=1, source_target_pairs={{0,2},{1,5},{2,0},{3,7},{4,6},{5,1},{6,4},{7,3},{8,10},{9,13},{10,... | collective-permute-start | bytes 405512 | tf_op jit(solution)/shard_map/ppermute | solution.py:238
  11.6 1.6 %collective-permute-start.4 = (f32[32,8,128]{2,1,0:T(8,128)S(1)}, f32[32,8,128]{2,1,0:T(8,128)S(1)}, u32[]{:S(2)}, u32[]{:S(2)}) collective-permute-start(f32[32,8,128]{2,1,0:T(8,128)S(1)} %summed.10), channel_id=1, source_target_pairs={{0,4},{1,3},{2,6},{3,1},{4,0},{5,7},{6,2},{7,5},{8,12},{9,11},{10,... | collective-permute-start | bytes 393224 | tf_op jit(solution)/shard_map/ppermute | solution.py:238
  13.2 1.9 %collective-permute-done.5.refs_2_.refs_5_ = f32[64,8,128]{2,1,0:T(8,128)S(1)} collective-permute-done((f32[64,8,128]{2,1,0:T(8,128)S(1)}, f32[64,8,128]{2,1,0:T(8,128)S(1)}, u32[]{:S(2)}, u32[]{:S(2)}) %collective-permute-start.5) | collective-permute-done | bytes 262176 | tf_op jit(solution)/shard_map/ppermute | solution.py:238
  15.1 1.6 %collective-permute-start.6 = (f32[32,8,128]{2,1,0:T(8,128)S(1)}, f32[32,8,128]{2,1,0:T(8,128)S(1)}, u32[]{:S(2)}, u32[]{:S(2)}) collective-permute-start(f32[32,8,128]{2,1,0:T(8,128)S(1)} %summed.13), channel_id=1, source_target_pairs={{0,2},{1,5},{2,0},{3,7},{4,6},{5,1},{6,4},{7,3},{8,10},{9,13},{10,... | collective-permute-start | bytes 393224 | tf_op jit(solution)/shard_map/ppermute | solution.py:238
  16.7 0.0 collective-permute-done.3.refs_6_.refs_3_
  16.7 2.7 %collective-permute-start.7 = (f32[33,8,128]{2,1,0:T(8,128)S(1)}, f32[33,8,128]{2,1,0:T(8,128)S(1)}, u32[]{:S(2)}, u32[]{:S(2)}) collective-permute-start(f32[33,8,128]{2,1,0:T(8,128)S(1)} %summed.15), channel_id=1, source_target_pairs={{0,8},{1,9},{2,10},{3,11},{4,12},{5,13},{6,14},{7,15},{8,0},{9,1},... | collective-permute-start | bytes 405512 | tf_op jit(solution)/shard_map/ppermute | solution.py:238
  19.4 0.0 collective-permute-done.4.refs_2_
  19.4 0.7 %collective-permute-done.6.refs_1_ = f32[32,8,128]{2,1,0:T(8,128)S(1)} collective-permute-done((f32[32,8,128]{2,1,0:T(8,128)S(1)}, f32[32,8,128]{2,1,0:T(8,128)S(1)}, u32[]{:S(2)}, u32[]{:S(2)}) %collective-permute-start.6) | collective-permute-done | bytes 131104 | tf_op jit(solution)/shard_map/ppermute | solution.py:238
  20.2 4.2 %collective-permute-done.7.refs_5_ = f32[33,8,128]{2,1,0:T(8,128)S(1)} collective-permute-done((f32[33,8,128]{2,1,0:T(8,128)S(1)}, f32[33,8,128]{2,1,0:T(8,128)S(1)}, u32[]{:S(2)}, u32[]{:S(2)}) %collective-permute-start.7) | collective-permute-done | bytes 135200 | tf_op jit(solution)/shard_map/ppermute | solution.py:238
  24.4 0.8 %finish.1 = f32[32,2,512]{2,1,0:T(2,128)} custom-call(f32[33,8,128]{2,1,0:T(8,128)S(1)} %get-tuple-element.10.refs_0_, f32[33,8,128]{2,1,0:T(8,128)S(1)} %collective-permute-done.refs_2_.refs_1_, f32[33,8,128]{2,1,0:T(8,128)S(1)} %collective-permute-done.1.refs_4_.refs_2_, f32[33,8,128]{2,1,0:T(8,128)S(1)} %collective-permute-done.3.refs_6_.refs_3_, ...), custom_call_target="tpu_custom_call" | custom-call | tf_op jit(solution)/shard_map/finish/pallas_call | solution.py:199
  (8 shorter events, 0.2 us)
Async XLA Ops:
  2.0 1.5 %collective-permute-start = (f32[33,8,128]{2,1,0:T(8,128)S(1)}, f32[33,8,128]{2,1,0:T(8,128)S(1)}, u32[]{:S(2)}, u32[]{:S(2)}) collective-permute-start(f32[33,8,128]{2,1,0:T(8,128)S(1)} %get-tuple-element.10.refs_0_), channel_id=1, source_target_pairs={{0,1},{1,0},{2,3},{3,2},{4,5},{5,4},{6,7},{7,6},{8,9},{9,8},{10,11... | collective-permute-start | bytes 405512 | tf_op jit(solution)/shard_map/ppermute | solution.py:238
  3.2 4.0 %collective-permute-start.2 = (f32[224,8,128]{2,1,0:T(8,128)S(1)}, f32[224,8,128]{2,1,0:T(8,128)S(1)}, u32[]{:S(2)}, u32[]{:S(2)}) collective-permute-start(f32[224,8,128]{2,1,0:T(8,128)S(1)} %next_products.3), channel_id=1, source_target_pairs={{0,1},{1,0},{2,3},{3,2},{4,5},{5,4},{6,7},{7,6},{8,9},{9,8},{10,11... | collective-permute-start | bytes 2752520 | tf_op jit(solution)/shard_map/ppermute | solution.py:238
  3.5 6.0 %collective-permute-start.1 = (f32[33,8,128]{2,1,0:T(8,128)S(1)}, f32[33,8,128]{2,1,0:T(8,128)S(1)}, u32[]{:S(2)}, u32[]{:S(2)}) collective-permute-start(f32[33,8,128]{2,1,0:T(8,128)S(1)} %summed.8), channel_id=1, source_target_pairs={{0,4},{1,3},{2,6},{3,1},{4,0},{5,7},{6,2},{7,5},{8,12},{9,11},{10,... | collective-permute-start | bytes 405512 | tf_op jit(solution)/shard_map/ppermute | solution.py:238
  7.2 7.9 %collective-permute-start.5 = (f32[64,8,128]{2,1,0:T(8,128)S(1)}, f32[64,8,128]{2,1,0:T(8,128)S(1)}, u32[]{:S(2)}, u32[]{:S(2)}) collective-permute-start(f32[64,8,128]{2,1,0:T(8,128)S(1)} %summed.12), channel_id=1, source_target_pairs={{0,4},{1,3},{2,6},{3,1},{4,0},{5,7},{6,2},{7,5},{8,12},{9,11},{10,... | collective-permute-start | bytes 786440 | tf_op jit(solution)/shard_map/ppermute | solution.py:238
  9.6 7.1 %collective-permute-start.3 = (f32[33,8,128]{2,1,0:T(8,128)S(1)}, f32[33,8,128]{2,1,0:T(8,128)S(1)}, u32[]{:S(2)}, u32[]{:S(2)}) collective-permute-start(f32[33,8,128]{2,1,0:T(8,128)S(1)} %summed.9), channel_id=1, source_target_pairs={{0,2},{1,5},{2,0},{3,7},{4,6},{5,1},{6,4},{7,3},{8,10},{9,13},{10,... | collective-permute-start | bytes 405512 | tf_op jit(solution)/shard_map/ppermute | solution.py:238
  11.6 7.8 %collective-permute-start.4 = (f32[32,8,128]{2,1,0:T(8,128)S(1)}, f32[32,8,128]{2,1,0:T(8,128)S(1)}, u32[]{:S(2)}, u32[]{:S(2)}) collective-permute-start(f32[32,8,128]{2,1,0:T(8,128)S(1)} %summed.10), channel_id=1, source_target_pairs={{0,4},{1,3},{2,6},{3,1},{4,0},{5,7},{6,2},{7,5},{8,12},{9,11},{10,... | collective-permute-start | bytes 393224 | tf_op jit(solution)/shard_map/ppermute | solution.py:238
  15.1 5.0 %collective-permute-start.6 = (f32[32,8,128]{2,1,0:T(8,128)S(1)}, f32[32,8,128]{2,1,0:T(8,128)S(1)}, u32[]{:S(2)}, u32[]{:S(2)}) collective-permute-start(f32[32,8,128]{2,1,0:T(8,128)S(1)} %summed.13), channel_id=1, source_target_pairs={{0,2},{1,5},{2,0},{3,7},{4,6},{5,1},{6,4},{7,3},{8,10},{9,13},{10,... | collective-permute-start | bytes 393224 | tf_op jit(solution)/shard_map/ppermute | solution.py:238
  16.7 7.6 %collective-permute-start.7 = (f32[33,8,128]{2,1,0:T(8,128)S(1)}, f32[33,8,128]{2,1,0:T(8,128)S(1)}, u32[]{:S(2)}, u32[]{:S(2)}) collective-permute-start(f32[33,8,128]{2,1,0:T(8,128)S(1)} %summed.15), channel_id=1, source_target_pairs={{0,8},{1,9},{2,10},{3,11},{4,12},{5,13},{6,14},{7,15},{8,0},{9,1},... | collective-permute-start | bytes 405512 | tf_op jit(solution)/shard_map/ppermute | solution.py:238

commit v15 on v14

--- a/solution.py
+++ b/solution.py
@@ -165,18 +165,18 @@
         at += count
 
 
-def summed(arrays, jobs, cost):
+def summed(arrays, jobs, cost, after):
     size = sum(count for _, count in jobs)
     vmem = pl.BlockSpec(memory_space=pltpu.VMEM)
     return pl.pallas_call(
         functools.partial(sum_kernel, jobs),
         out_shape=message(size),
-        in_specs=[vmem] * len(arrays),
+        in_specs=[vmem] * (len(arrays) + len(after)),
         out_specs=vmem,
         compiler_params=pltpu.CompilerParams(vmem_limit_bytes=8 * MIB),
         cost_estimate=estimate(cost),
         name="summed",
-    )(*arrays)
+    )(*arrays, *after)
 
 
 def final_kernel(terms, powers, *refs):
@@ -220,9 +220,10 @@
         (0, steps[0][quarter:3 * quarter]),
         (1, steps[1][:half]),
         (0, steps[0][3 * quarter:]),
+        (2, steps[2]),
         (1, steps[1][half:]),
     ]
-    return order + [(step, steps[step]) for step in range(2, chips)]
+    return order + [(step, steps[step]) for step in range(3, chips)]
 
 
 def on_device(channel, precoder, visible, cluster):
@@ -248,11 +249,11 @@
             powers.append((len(arrays), len(slots) * tiles))
         arrays.append(array)
 
-    def total(slots, power, cost=8192):
+    def total(slots, power, cost=8192, after=()):
         jobs = [(list(terms[slot]), tiles) for slot in slots] + ([(list(powers), 1)] if power else [])
         used = sorted({array for parts, _ in jobs for array, _ in parts})
         jobs = [([(used.index(array), start) for array, start in parts], count) for parts, count in jobs]
-        return summed([arrays[array] for array in used], jobs, cost)
+        return summed([arrays[array] for array in used], jobs, cost, after)
 
     quarter = half // 4
     sent, kept, rows, weights, served = first_products(
@@ -273,12 +274,13 @@
     for number, (step, slots) in enumerate(message_order(bits - 1)):
         power = step not in with_power
         with_power.add(step)
-        now = total(slots, power, 65536 * MIB if number == 0 else 8192)
+        after = [now] if number == 5 else []
+        now = total(slots, power, 65536 * MIB if number == 0 else 8192, after)
         came = swap(now, (orders[0][step], orders[1][step]))
         slots = [slot + (1 << (bits - 2 - step)) for slot in slots]
         add(came, slots, power)
-        if last in slots and step < bits - 2:
-            own = total([last], False, 64 * MIB)
+        if last in slots and number == 3:
+            own = total([last], False, 256 * MIB)
             terms[last] = []
             add(own, [last], False)
     used = sorted({array for array, _ in terms[last] + powers})

time: 25.3 us -> 25.2 us (level)
  waiting for transfers between devices: 8.09 us -> 7.79 us
    ppermute x8, waiting for transfers between devices: 8.09 us -> 7.79 us  [swap(): lax.ppermute(value, 'ap', [(i, i ^ 1 << bit_of[i & 1]) for i in range(dev...]
where the time goes in v15:
time: 25.2 us; the launch traced here: 25.1 us
  starting transfers between devices  13 us (52%)
  waiting for transfers between devices  7.79 us (31%)
  Pallas kernels  4.21 us (17%)
    ppermute x8, starting transfers between devices, swap(): lax.ppermute(value, 'ap', [(i, i ^ 1 << bit_of[i & 1]) for i in range(dev...  13 us
    ppermute x8, waiting for transfers between devices, swap(): lax.ppermute(value, 'ap', [(i, i ^ 1 << bit_of[i & 1]) for i in range(dev...  7.79 us
    pallas_call x1, Pallas kernels, first_products(): pl.pallas_call(functools.partial(first_kernel, bits), out_shape=(message(...  2 us
    pallas_call x2, Pallas kernels, next_products(): pl.pallas_call(functools.partial(next_kernel, users, keep, first, slots),...  1.27 us
    pallas_call x1, Pallas kernels, finish(): pl.pallas_call(functools.partial(final_kernel, terms, powers), out_shape=...  0.76 us
  transfers between devices with their start and end apart: 8, of which 5 were waited for; matrix products, arithmetic and copies ran while one was open for 0% of the time, Pallas kernels for 6%

profile of v15, /device:TPU:0, one launch (start us, length us, event | category | flops | bytes accessed | tf_op | source)
XLA Modules:
  0.0 25.1 jit_solution(6679116500790111821)
XLA Ops:
  0.0 2.0 %first_products.1 = (f32[33,8,128]{2,1,0:T(8,128)S(1)}, f32[32,8,128]{2,1,0:T(8,128)S(1)}, bf16[2,256,1024]{2,1,0:T(8,128)(2,1)S(1)}, bf16[1024,512]{1,0:T(8,128)(2,1)S(1)}, f32[1,512]{1,0:T(1,128)S(1)}) custom-call(s32[1,12]{1,0:T(1,128)} %visible.1, s32[4,512]{1,0:T(4,128)} %bitcast.3, bf16[1,12,2,32,512]{4,3,2,1,0:T(8,128)(2,1)} %channel.1, ...), custom_call_target="tpu_custom_call" | custom-call | flops 8192 | bytes 8192 | tf_op jit(solution)/shard_map/first_products/pallas_call | solution.py:117
  2.0 0.5 %collective-permute-start = (f32[33,8,128]{2,1,0:T(8,128)S(1)}, f32[33,8,128]{2,1,0:T(8,128)S(1)}, u32[]{:S(2)}, u32[]{:S(2)}) collective-permute-start(f32[33,8,128]{2,1,0:T(8,128)S(1)} %get-tuple-element.10.refs_0_), channel_id=1, source_target_pairs={{0,1},{1,0},{2,3},{3,2},{4,5},{5,4},{6,7},{7,6},{8,9},{9,8},{10,11... | collective-permute-start | bytes 405512 | tf_op jit(solution)/shard_map/ppermute | solution.py:239
  2.5 0.6 %next_products.3 = f32[224,8,128]{2,1,0:T(8,128)S(1)} custom-call(bf16[2,256,1024]{2,1,0:T(8,128)(2,1)S(1)} %get-tuple-element.12.rows, bf16[1024,512]{1,0:T(8,128)(2,1)S(1)} %get-tuple-element.13.weights, f32[1,512]{1,0:T(1,128)S(1)} %get-tuple-element.14.served), custom_call_target="tpu_custom_call" | custom-call | flops 8192 | bytes 8192 | tf_op jit(solution)/shard_map/next_products/pallas_call | solution.py:143
  3.2 0.1 collective-permute-start.2
  3.3 0.2 collective-permute-done.refs_2_.refs_1_
  3.5 3.0 %collective-permute-start.1 = (f32[33,8,128]{2,1,0:T(8,128)S(1)}, f32[33,8,128]{2,1,0:T(8,128)S(1)}, u32[]{:S(2)}, u32[]{:S(2)}) collective-permute-start(f32[33,8,128]{2,1,0:T(8,128)S(1)} %summed.7), channel_id=1, source_target_pairs={{0,4},{1,3},{2,6},{3,1},{4,0},{5,7},{6,2},{7,5},{8,12},{9,11},{10,... | collective-permute-start | bytes 405512 | tf_op jit(solution)/shard_map/ppermute | solution.py:239
  6.5 0.6 %next_products.2.refs_2_.refs_0_ = f32[224,8,128]{2,1,0:T(8,128)S(1)} custom-call(bf16[2,256,1024]{2,1,0:T(8,128)(2,1)S(1)} %get-tuple-element.12.rows, bf16[1024,512]{1,0:T(8,128)(2,1)S(1)} %get-tuple-element.13.weights, f32[1,512]{1,0:T(1,128)S(1)} %get-tuple-element.14.served), custom_call_target="tpu_custom_call" | custom-call | flops 8192 | bytes 8192 | tf_op jit(solution)/shard_map/next_products/pallas_call | solution.py:143
  7.2 0.0 collective-permute-done.2.refs_3_.refs_1_
  7.2 1.3 %collective-permute-start.5 = (f32[64,8,128]{2,1,0:T(8,128)S(1)}, f32[64,8,128]{2,1,0:T(8,128)S(1)}, u32[]{:S(2)}, u32[]{:S(2)}) collective-permute-start(f32[64,8,128]{2,1,0:T(8,128)S(1)} %summed.11), channel_id=1, source_target_pairs={{0,4},{1,3},{2,6},{3,1},{4,0},{5,7},{6,2},{7,5},{8,12},{9,11},{10,... | collective-permute-start | bytes 786440 | tf_op jit(solution)/shard_map/ppermute | solution.py:239
  8.5 1.0 %collective-permute-done.1.refs_4_.refs_2_ = f32[33,8,128]{2,1,0:T(8,128)S(1)} collective-permute-done((f32[33,8,128]{2,1,0:T(8,128)S(1)}, f32[33,8,128]{2,1,0:T(8,128)S(1)}, u32[]{:S(2)}, u32[]{:S(2)}) %collective-permute-start.1) | collective-permute-done | bytes 135200 | tf_op jit(solution)/shard_map/ppermute | solution.py:239
  9.6 2.0 %collective-permute-start.3 = (f32[33,8,128]{2,1,0:T(8,128)S(1)}, f32[33,8,128]{2,1,0:T(8,128)S(1)}, u32[]{:S(2)}, u32[]{:S(2)}) collective-permute-start(f32[33,8,128]{2,1,0:T(8,128)S(1)} %summed.8), channel_id=1, source_target_pairs={{0,2},{1,5},{2,0},{3,7},{4,6},{5,1},{6,4},{7,3},{8,10},{9,13},{10,... | collective-permute-start | bytes 405512 | tf_op jit(solution)/shard_map/ppermute | solution.py:239
  11.6 1.6 %collective-permute-start.4 = (f32[32,8,128]{2,1,0:T(8,128)S(1)}, f32[32,8,128]{2,1,0:T(8,128)S(1)}, u32[]{:S(2)}, u32[]{:S(2)}) collective-permute-start(f32[32,8,128]{2,1,0:T(8,128)S(1)} %summed.9), channel_id=1, source_target_pairs={{0,4},{1,3},{2,6},{3,1},{4,0},{5,7},{6,2},{7,5},{8,12},{9,11},{10,... | collective-permute-start | bytes 393224 | tf_op jit(solution)/shard_map/ppermute | solution.py:239
  13.2 2.7 %collective-permute-done.3.refs_6_.refs_3_ = f32[33,8,128]{2,1,0:T(8,128)S(1)} collective-permute-done((f32[33,8,128]{2,1,0:T(8,128)S(1)}, f32[33,8,128]{2,1,0:T(8,128)S(1)}, u32[]{:S(2)}, u32[]{:S(2)}) %collective-permute-start.3) | collective-permute-done | bytes 135200 | tf_op jit(solution)/shard_map/ppermute | solution.py:239
  15.9 0.0 collective-permute-done.5.refs_5_.refs_2_
  16.0 2.9 %collective-permute-start.6 = (f32[33,8,128]{2,1,0:T(8,128)S(1)}, f32[33,8,128]{2,1,0:T(8,128)S(1)}, u32[]{:S(2)}, u32[]{:S(2)}) collective-permute-start(f32[33,8,128]{2,1,0:T(8,128)S(1)} %summed.12.refs_3_), channel_id=1, source_target_pairs={{0,8},{1,9},{2,10},{3,11},{4,12},{5,13},{6,14},{7,15},{8,0},{9,1},... | collective-permute-start | bytes 405512 | tf_op jit(solution)/shard_map/ppermute | solution.py:239
  18.9 1.6 %collective-permute-start.7 = (f32[32,8,128]{2,1,0:T(8,128)S(1)}, f32[32,8,128]{2,1,0:T(8,128)S(1)}, u32[]{:S(2)}, u32[]{:S(2)}) collective-permute-start(f32[32,8,128]{2,1,0:T(8,128)S(1)} %summed.13), channel_id=1, source_target_pairs={{0,2},{1,5},{2,0},{3,7},{4,6},{5,1},{6,4},{7,3},{8,10},{9,13},{10,... | collective-permute-start | bytes 393224 | tf_op jit(solution)/shard_map/ppermute | solution.py:239
  20.5 0.0 collective-permute-done.4.refs_2_
  20.5 3.4 %collective-permute-done.7.refs_6_ = f32[32,8,128]{2,1,0:T(8,128)S(1)} collective-permute-done((f32[32,8,128]{2,1,0:T(8,128)S(1)}, f32[32,8,128]{2,1,0:T(8,128)S(1)}, u32[]{:S(2)}, u32[]{:S(2)}) %collective-permute-start.7) | collective-permute-done | bytes 131104 | tf_op jit(solution)/shard_map/ppermute | solution.py:239
  23.9 0.4 %collective-permute-done.6.refs_5_ = f32[33,8,128]{2,1,0:T(8,128)S(1)} collective-permute-done((f32[33,8,128]{2,1,0:T(8,128)S(1)}, f32[33,8,128]{2,1,0:T(8,128)S(1)}, u32[]{:S(2)}, u32[]{:S(2)}) %collective-permute-start.6) | collective-permute-done | bytes 135200 | tf_op jit(solution)/shard_map/ppermute | solution.py:239
  24.3 0.8 %finish.1 = f32[32,2,512]{2,1,0:T(2,128)} custom-call(f32[33,8,128]{2,1,0:T(8,128)S(1)} %get-tuple-element.10.refs_0_, f32[33,8,128]{2,1,0:T(8,128)S(1)} %collective-permute-done.refs_2_.refs_1_, f32[33,8,128]{2,1,0:T(8,128)S(1)} %collective-permute-done.1.refs_4_.refs_2_, f32[33,8,128]{2,1,0:T(8,128)S(1)} %collective-permute-done.3.refs_6_.refs_3_, ...), custom_call_target="tpu_custom_call" | custom-call | tf_op jit(solution)/shard_map/finish/pallas_call | solution.py:199
  (7 shorter events, 0.2 us)
Async XLA Ops:
  2.0 1.5 %collective-permute-start = (f32[33,8,128]{2,1,0:T(8,128)S(1)}, f32[33,8,128]{2,1,0:T(8,128)S(1)}, u32[]{:S(2)}, u32[]{:S(2)}) collective-permute-start(f32[33,8,128]{2,1,0:T(8,128)S(1)} %get-tuple-element.10.refs_0_), channel_id=1, source_target_pairs={{0,1},{1,0},{2,3},{3,2},{4,5},{5,4},{6,7},{7,6},{8,9},{9,8},{10,11... | collective-permute-start | bytes 405512 | tf_op jit(solution)/shard_map/ppermute | solution.py:239
  3.2 4.0 %collective-permute-start.2 = (f32[224,8,128]{2,1,0:T(8,128)S(1)}, f32[224,8,128]{2,1,0:T(8,128)S(1)}, u32[]{:S(2)}, u32[]{:S(2)}) collective-permute-start(f32[224,8,128]{2,1,0:T(8,128)S(1)} %next_products.3), channel_id=1, source_target_pairs={{0,1},{1,0},{2,3},{3,2},{4,5},{5,4},{6,7},{7,6},{8,9},{9,8},{10,11... | collective-permute-start | bytes 2752520 | tf_op jit(solution)/shard_map/ppermute | solution.py:239
  3.5 6.0 %collective-permute-start.1 = (f32[33,8,128]{2,1,0:T(8,128)S(1)}, f32[33,8,128]{2,1,0:T(8,128)S(1)}, u32[]{:S(2)}, u32[]{:S(2)}) collective-permute-start(f32[33,8,128]{2,1,0:T(8,128)S(1)} %summed.7), channel_id=1, source_target_pairs={{0,4},{1,3},{2,6},{3,1},{4,0},{5,7},{6,2},{7,5},{8,12},{9,11},{10,... | collective-permute-start | bytes 405512 | tf_op jit(solution)/shard_map/ppermute | solution.py:239
  7.2 8.7 %collective-permute-start.5 = (f32[64,8,128]{2,1,0:T(8,128)S(1)}, f32[64,8,128]{2,1,0:T(8,128)S(1)}, u32[]{:S(2)}, u32[]{:S(2)}) collective-permute-start(f32[64,8,128]{2,1,0:T(8,128)S(1)} %summed.11), channel_id=1, source_target_pairs={{0,4},{1,3},{2,6},{3,1},{4,0},{5,7},{6,2},{7,5},{8,12},{9,11},{10,... | collective-permute-start | bytes 786440 | tf_op jit(solution)/shard_map/ppermute | solution.py:239
  9.6 6.4 %collective-permute-start.3 = (f32[33,8,128]{2,1,0:T(8,128)S(1)}, f32[33,8,128]{2,1,0:T(8,128)S(1)}, u32[]{:S(2)}, u32[]{:S(2)}) collective-permute-start(f32[33,8,128]{2,1,0:T(8,128)S(1)} %summed.8), channel_id=1, source_target_pairs={{0,2},{1,5},{2,0},{3,7},{4,6},{5,1},{6,4},{7,3},{8,10},{9,13},{10,... | collective-permute-start | bytes 405512 | tf_op jit(solution)/shard_map/ppermute | solution.py:239
  11.6 8.9 %collective-permute-start.4 = (f32[32,8,128]{2,1,0:T(8,128)S(1)}, f32[32,8,128]{2,1,0:T(8,128)S(1)}, u32[]{:S(2)}, u32[]{:S(2)}) collective-permute-start(f32[32,8,128]{2,1,0:T(8,128)S(1)} %summed.9), channel_id=1, source_target_pairs={{0,4},{1,3},{2,6},{3,1},{4,0},{5,7},{6,2},{7,5},{8,12},{9,11},{10,... | collective-permute-start | bytes 393224 | tf_op jit(solution)/shard_map/ppermute | solution.py:239
  16.0 8.3 %collective-permute-start.6 = (f32[33,8,128]{2,1,0:T(8,128)S(1)}, f32[33,8,128]{2,1,0:T(8,128)S(1)}, u32[]{:S(2)}, u32[]{:S(2)}) collective-permute-start(f32[33,8,128]{2,1,0:T(8,128)S(1)} %summed.12.refs_3_), channel_id=1, source_target_pairs={{0,8},{1,9},{2,10},{3,11},{4,12},{5,13},{6,14},{7,15},{8,0},{9,1},... | collective-permute-start | bytes 405512 | tf_op jit(solution)/shard_map/ppermute | solution.py:239
  18.9 5.0 %collective-permute-start.7 = (f32[32,8,128]{2,1,0:T(8,128)S(1)}, f32[32,8,128]{2,1,0:T(8,128)S(1)}, u32[]{:S(2)}, u32[]{:S(2)}) collective-permute-start(f32[32,8,128]{2,1,0:T(8,128)S(1)} %summed.13), channel_id=1, source_target_pairs={{0,2},{1,5},{2,0},{3,7},{4,6},{5,1},{6,4},{7,3},{8,10},{9,13},{10,... | collective-permute-start | bytes 393224 | tf_op jit(solution)/shard_map/ppermute | solution.py:239

commit v16 on v15

--- a/solution.py
+++ b/solution.py
@@ -9,6 +9,11 @@
 
 epsilon = 1e-06
 MIB = 1 << 20
+
+
+COSTS = (8192, 64 * MIB, 65536 * MIB, 8192 * MIB) + (
+    64 * MIB, 1024 * MIB, 1024 * MIB, 65536 * MIB, 1024 * MIB, 8192 * MIB
+)
 
 
 def chip_orders(bits):
@@ -137,7 +142,7 @@
     )(*[pltpu.with_memory_space_constraint(operand, pltpu.HBM) for operand in operands])
 
 
-def next_products(users, keep, first, slots, rows, weights, served):
+def next_products(users, keep, first, slots, cost, rows, weights, served):
     vmem = pl.BlockSpec(memory_space=pltpu.VMEM)
     big = slots > 8
     return pl.pallas_call(
@@ -146,7 +151,7 @@
         in_specs=[vmem] * 3,
         out_specs=vmem,
         compiler_params=pltpu.CompilerParams(vmem_limit_bytes=48 * MIB if big else 16 * MIB),
-        cost_estimate=estimate(),
+        cost_estimate=estimate(cost),
         name="next_products",
     )(rows, weights, served)
 
@@ -215,11 +220,12 @@
     if chips < 3:
         return [(step, slots) for step, slots in enumerate(steps)]
     quarter, half = len(steps[0]) // 4, len(steps[1]) // 2
+    parts = [steps[0][at * quarter:(at + 1) * quarter] for at in range(4)]
     order = [
-        (0, steps[0][:quarter]),
-        (0, steps[0][quarter:3 * quarter]),
+        (0, parts[0]),
+        (0, parts[2]),
         (1, steps[1][:half]),
-        (0, steps[0][3 * quarter:]),
+        (0, parts[1] + parts[3]),
         (2, steps[2]),
         (1, steps[1][half:]),
     ]
@@ -265,24 +271,21 @@
     add(kept, range(quarter), False)
     add(came, range(quarter), True)
     products = functools.partial(next_products, users, rows=rows, weights=weights, served=served)
-    rest = range(quarter, 2 * half)
-    later = swap(products(0, quarter, len(rest)), (0, 0))
-    add(products(1, quarter, len(rest)), rest, False)
-    add(later, rest, False)
+    for at, (first, count) in enumerate(((quarter, 4 * quarter), (5 * quarter, 3 * quarter))):
+        slots = range(first, first + count)
+        come = swap(products(0, first, count, cost=COSTS[2 * at]), (0, 0))
+        add(products(1, first, count, cost=COSTS[2 * at + 1]), slots, False)
+        add(come, slots, False)
     with_power = set()
     last = 2 * half - 1
     for number, (step, slots) in enumerate(message_order(bits - 1)):
         power = step not in with_power
         with_power.add(step)
-        after = [now] if number == 5 else []
-        now = total(slots, power, 65536 * MIB if number == 0 else 8192, after)
+        after = [now] if number in (3, 5) else []
+        now = total(slots, power, COSTS[4 + number] if number < 6 else 8192, after)
         came = swap(now, (orders[0][step], orders[1][step]))
         slots = [slot + (1 << (bits - 2 - step)) for slot in slots]
         add(came, slots, power)
-        if last in slots and number == 3:
-            own = total([last], False, 256 * MIB)
-            terms[last] = []
-            add(own, [last], False)
     used = sorted({array for array, _ in terms[last] + powers})
     return finish(
         [arrays[array] for array in used],

time: 25.2 us -> 25.2 us (level)
  waiting for transfers between devices: 7.79 us -> 6.84 us
  starting transfers between devices: 13 us -> 13.6 us
  Pallas kernels: 4.21 us -> 4.51 us
    ppermute x8 -> x9, waiting for transfers between devices: 7.79 us -> 6.84 us  [swap(): lax.ppermute(value, 'ap', [(i, i ^ 1 << bit_of[i & 1]) for i in range(dev...]
    ppermute x8 -> x9, starting transfers between devices: 13 us -> 13.6 us  [swap(): lax.ppermute(value, 'ap', [(i, i ^ 1 << bit_of[i & 1]) for i in range(dev...]
    pallas_call x2 -> x4, Pallas kernels: 1.27 us -> 1.6 us  [next_products(): pl.pallas_call(functools.partial(next_kernel, users, keep, first, slots),...]
  transfers between devices with their start and end apart: 8 -> 9, of which waited for: 5 -> 5; matrix products, arithmetic and copies ran while one was open for 0% -> 0% of each run, Pallas kernels for 6% -> 7%
where the time goes in v16:
time: 25.2 us; the launch traced here: 25 us
  starting transfers between devices  13.6 us (54%)
  waiting for transfers between devices  6.84 us (27%)
  Pallas kernels  4.51 us (18%)
    ppermute x9, starting transfers between devices, swap(): lax.ppermute(value, 'ap', [(i, i ^ 1 << bit_of[i & 1]) for i in range(dev...  13.6 us
    ppermute x9, waiting for transfers between devices, swap(): lax.ppermute(value, 'ap', [(i, i ^ 1 << bit_of[i & 1]) for i in range(dev...  6.84 us
    pallas_call x1, Pallas kernels, first_products(): pl.pallas_call(functools.partial(first_kernel, bits), out_shape=(message(...  2 us
    pallas_call x4, Pallas kernels, next_products(): pl.pallas_call(functools.partial(next_kernel, users, keep, first, slots),...  1.6 us
    pallas_call x1, Pallas kernels, finish(): pl.pallas_call(functools.partial(final_kernel, terms, powers), out_shape=...  0.76 us
  transfers between devices with their start and end apart: 9, of which 5 were waited for; matrix products, arithmetic and copies ran while one was open for 0% of the time, Pallas kernels for 7%

profile of v16, /device:TPU:0, one launch (start us, length us, event | category | flops | bytes accessed | tf_op | source)
XLA Modules:
  0.0 25.0 jit_solution(13653237316691798059)
XLA Ops:
  0.0 2.0 %first_products.1 = (f32[33,8,128]{2,1,0:T(8,128)S(1)}, f32[32,8,128]{2,1,0:T(8,128)S(1)}, bf16[2,256,1024]{2,1,0:T(8,128)(2,1)S(1)}, bf16[1024,512]{1,0:T(8,128)(2,1)S(1)}, f32[1,512]{1,0:T(1,128)S(1)}) custom-call(s32[1,12]{1,0:T(1,128)} %visible.1, s32[4,512]{1,0:T(4,128)} %bitcast.3, bf16[1,12,2,32,512]{4,3,2,1,0:T(8,128)(2,1)} %channel.1, ...), custom_call_target="tpu_custom_call" | custom-call | flops 8192 | bytes 8192 | tf_op jit(solution)/shard_map/first_products/pallas_call | solution.py:122
  2.0 0.5 %collective-permute-start = (f32[33,8,128]{2,1,0:T(8,128)S(1)}, f32[33,8,128]{2,1,0:T(8,128)S(1)}, u32[]{:S(2)}, u32[]{:S(2)}) collective-permute-start(f32[33,8,128]{2,1,0:T(8,128)S(1)} %get-tuple-element.10.refs_0_), channel_id=1, source_target_pairs={{0,1},{1,0},{2,3},{3,2},{4,5},{5,4},{6,7},{7,6},{8,9},{9,8},{10,11... | collective-permute-start | bytes 405512 | tf_op jit(solution)/shard_map/ppermute | solution.py:245
  2.5 0.4 %next_products.7 = f32[128,8,128]{2,1,0:T(8,128)S(1)} custom-call(bf16[2,256,1024]{2,1,0:T(8,128)(2,1)S(1)} %get-tuple-element.11.rows, bf16[1024,512]{1,0:T(8,128)(2,1)S(1)} %get-tuple-element.12.weights, f32[1,512]{1,0:T(1,128)S(1)} %get-tuple-element.13.served), custom_call_target="tpu_custom_call" | custom-call | flops 8192 | bytes 8192 | tf_op jit(solution)/shard_map/next_products/pallas_call | solution.py:148
  3.0 0.1 collective-permute-start.3
  3.1 0.4 %collective-permute-done.refs_2_.refs_1_ = f32[33,8,128]{2,1,0:T(8,128)S(1)} collective-permute-done((f32[33,8,128]{2,1,0:T(8,128)S(1)}, f32[33,8,128]{2,1,0:T(8,128)S(1)}, u32[]{:S(2)}, u32[]{:S(2)}) %collective-permute-start) | collective-permute-done | bytes 135200 | tf_op jit(solution)/shard_map/ppermute | solution.py:245
  3.5 3.0 %collective-permute-start.2 = (f32[33,8,128]{2,1,0:T(8,128)S(1)}, f32[33,8,128]{2,1,0:T(8,128)S(1)}, u32[]{:S(2)}, u32[]{:S(2)}) collective-permute-start(f32[33,8,128]{2,1,0:T(8,128)S(1)} %summed.6), channel_id=1, source_target_pairs={{0,4},{1,3},{2,6},{3,1},{4,0},{5,7},{6,2},{7,5},{8,12},{9,11},{10,... | collective-permute-start | bytes 405512 | tf_op jit(solution)/shard_map/ppermute | solution.py:245
  6.5 0.4 %next_products.5 = f32[96,8,128]{2,1,0:T(8,128)S(1)} custom-call(bf16[2,256,1024]{2,1,0:T(8,128)(2,1)S(1)} %get-tuple-element.11.rows, bf16[1024,512]{1,0:T(8,128)(2,1)S(1)} %get-tuple-element.12.weights, f32[1,512]{1,0:T(1,128)S(1)} %get-tuple-element.13.served), custom_call_target="tpu_custom_call" | custom-call | flops 68719476736 | bytes 68719476736 | tf_op jit(solution)/shard_map/next_products/pallas_call | solution.py:148
  6.9 0.1 collective-permute-start.1
  7.0 0.4 %next_products.6.refs_2_.refs_0_ = f32[128,8,128]{2,1,0:T(8,128)S(1)} custom-call(bf16[2,256,1024]{2,1,0:T(8,128)(2,1)S(1)} %get-tuple-element.11.rows, bf16[1024,512]{1,0:T(8,128)(2,1)S(1)} %get-tuple-element.12.weights, f32[1,512]{1,0:T(1,128)S(1)} %get-tuple-element.13.served), custom_call_target="tpu_custom_call" | custom-call | flops 67108864 | bytes 67108864 | tf_op jit(solution)/shard_map/next_products/pallas_call | solution.py:148
  7.4 0.0 collective-permute-done.3.refs_3_.refs_1_
  7.5 1.4 %collective-permute-start.6 = (f32[32,8,128]{2,1,0:T(8,128)S(1)}, f32[32,8,128]{2,1,0:T(8,128)S(1)}, u32[]{:S(2)}, u32[]{:S(2)}) collective-permute-start(f32[32,8,128]{2,1,0:T(8,128)S(1)} %summed.9), channel_id=1, source_target_pairs={{0,4},{1,3},{2,6},{3,1},{4,0},{5,7},{6,2},{7,5},{8,12},{9,11},{10,... | collective-permute-start | bytes 393224 | tf_op jit(solution)/shard_map/ppermute | solution.py:245
  8.9 0.7 %collective-permute-done.2.refs_4_ = f32[33,8,128]{2,1,0:T(8,128)S(1)} collective-permute-done((f32[33,8,128]{2,1,0:T(8,128)S(1)}, f32[33,8,128]{2,1,0:T(8,128)S(1)}, u32[]{:S(2)}, u32[]{:S(2)}) %collective-permute-start.2) | collective-permute-done | bytes 135200 | tf_op jit(solution)/shard_map/ppermute | solution.py:245
  9.6 2.0 %collective-permute-start.4 = (f32[33,8,128]{2,1,0:T(8,128)S(1)}, f32[33,8,128]{2,1,0:T(8,128)S(1)}, u32[]{:S(2)}, u32[]{:S(2)}) collective-permute-start(f32[33,8,128]{2,1,0:T(8,128)S(1)} %summed.7.refs_2_), channel_id=1, source_target_pairs={{0,2},{1,5},{2,0},{3,7},{4,6},{5,1},{6,4},{7,3},{8,10},{9,13},{10,... | collective-permute-start | bytes 405512 | tf_op jit(solution)/shard_map/ppermute | solution.py:245
  11.6 1.6 %collective-permute-start.5 = (f32[64,8,128]{2,1,0:T(8,128)S(1)}, f32[64,8,128]{2,1,0:T(8,128)S(1)}, u32[]{:S(2)}, u32[]{:S(2)}) collective-permute-start(f32[64,8,128]{2,1,0:T(8,128)S(1)} %summed.8), channel_id=1, source_target_pairs={{0,4},{1,3},{2,6},{3,1},{4,0},{5,7},{6,2},{7,5},{8,12},{9,11},{10,... | collective-permute-start | bytes 786440 | tf_op jit(solution)/shard_map/ppermute | solution.py:245
  13.2 0.4 %next_products.4.refs_2_.refs_0_ = f32[96,8,128]{2,1,0:T(8,128)S(1)} custom-call(bf16[2,256,1024]{2,1,0:T(8,128)(2,1)S(1)} %get-tuple-element.11.rows, bf16[1024,512]{1,0:T(8,128)(2,1)S(1)} %get-tuple-element.12.weights, f32[1,512]{1,0:T(1,128)S(1)} %get-tuple-element.13.served), custom_call_target="tpu_custom_call" | custom-call | flops 8589934592 | bytes 8589934592 | tf_op jit(solution)/shard_map/next_products/pallas_call | solution.py:148
  13.6 0.0 collective-permute-done.1.refs_3_.refs_1_
  13.6 0.0 collective-permute-done.6.refs_5_
  13.6 2.3 %collective-permute-done.4.refs_6_.refs_5_ = f32[33,8,128]{2,1,0:T(8,128)S(1)} collective-permute-done((f32[33,8,128]{2,1,0:T(8,128)S(1)}, f32[33,8,128]{2,1,0:T(8,128)S(1)}, u32[]{:S(2)}, u32[]{:S(2)}) %collective-permute-start.4) | collective-permute-done | bytes 135200 | tf_op jit(solution)/shard_map/ppermute | solution.py:245
  15.9 3.3 %collective-permute-start.7 = (f32[33,8,128]{2,1,0:T(8,128)S(1)}, f32[33,8,128]{2,1,0:T(8,128)S(1)}, u32[]{:S(2)}, u32[]{:S(2)}) collective-permute-start(f32[33,8,128]{2,1,0:T(8,128)S(1)} %summed.10.refs_3_), channel_id=1, source_target_pairs={{0,8},{1,9},{2,10},{3,11},{4,12},{5,13},{6,14},{7,15},{8,0},{9,1},... | collective-permute-start | bytes 405512 | tf_op jit(solution)/shard_map/ppermute | solution.py:245
  19.2 0.0 collective-permute-done.5.refs_2_.refs_6_
  19.2 1.6 %collective-permute-start.8 = (f32[32,8,128]{2,1,0:T(8,128)S(1)}, f32[32,8,128]{2,1,0:T(8,128)S(1)}, u32[]{:S(2)}, u32[]{:S(2)}) collective-permute-start(f32[32,8,128]{2,1,0:T(8,128)S(1)} %summed.11), channel_id=1, source_target_pairs={{0,2},{1,5},{2,0},{3,7},{4,6},{5,1},{6,4},{7,3},{8,10},{9,13},{10,... | collective-permute-start | bytes 393224 | tf_op jit(solution)/shard_map/ppermute | solution.py:245
  20.8 2.5 %collective-permute-done.7.refs_7_ = f32[33,8,128]{2,1,0:T(8,128)S(1)} collective-permute-done((f32[33,8,128]{2,1,0:T(8,128)S(1)}, f32[33,8,128]{2,1,0:T(8,128)S(1)}, u32[]{:S(2)}, u32[]{:S(2)}) %collective-permute-start.7) | collective-permute-done | bytes 135200 | tf_op jit(solution)/shard_map/ppermute | solution.py:245
  23.3 1.0 %collective-permute-done.8.refs_8_ = f32[32,8,128]{2,1,0:T(8,128)S(1)} collective-permute-done((f32[32,8,128]{2,1,0:T(8,128)S(1)}, f32[32,8,128]{2,1,0:T(8,128)S(1)}, u32[]{:S(2)}, u32[]{:S(2)}) %collective-permute-start.8) | collective-permute-done | bytes 131104 | tf_op jit(solution)/shard_map/ppermute | solution.py:245
  24.3 0.8 %finish.1 = f32[32,2,512]{2,1,0:T(2,128)} custom-call(f32[33,8,128]{2,1,0:T(8,128)S(1)} %get-tuple-element.10.refs_0_, f32[33,8,128]{2,1,0:T(8,128)S(1)} %collective-permute-done.refs_2_.refs_1_, f32[96,8,128]{2,1,0:T(8,128)S(1)} %next_products.4.refs_2_.refs_0_, f32[96,8,128]{2,1,0:T(8,128)S(1)} %collective-permute-done.1.refs_3_.refs_1_, ...), custom_call_target="tpu_custom_call" | custom-call | tf_op jit(solution)/shard_map/finish/pallas_call | solution.py:204
  (6 shorter events, 0.2 us)
Async XLA Ops:
  2.0 1.5 %collective-permute-start = (f32[33,8,128]{2,1,0:T(8,128)S(1)}, f32[33,8,128]{2,1,0:T(8,128)S(1)}, u32[]{:S(2)}, u32[]{:S(2)}) collective-permute-start(f32[33,8,128]{2,1,0:T(8,128)S(1)} %get-tuple-element.10.refs_0_), channel_id=1, source_target_pairs={{0,1},{1,0},{2,3},{3,2},{4,5},{5,4},{6,7},{7,6},{8,9},{9,8},{10,11... | collective-permute-start | bytes 405512 | tf_op jit(solution)/shard_map/ppermute | solution.py:245
  3.0 4.5 %collective-permute-start.3 = (f32[128,8,128]{2,1,0:T(8,128)S(1)}, f32[128,8,128]{2,1,0:T(8,128)S(1)}, u32[]{:S(2)}, u32[]{:S(2)}) collective-permute-start(f32[128,8,128]{2,1,0:T(8,128)S(1)} %next_products.7), channel_id=1, source_target_pairs={{0,1},{1,0},{2,3},{3,2},{4,5},{5,4},{6,7},{7,6},{8,9},{9,8},{10,11... | collective-permute-start | bytes 1572872 | tf_op jit(solution)/shard_map/ppermute | solution.py:245
  3.5 6.0 %collective-permute-start.2 = (f32[33,8,128]{2,1,0:T(8,128)S(1)}, f32[33,8,128]{2,1,0:T(8,128)S(1)}, u32[]{:S(2)}, u32[]{:S(2)}) collective-permute-start(f32[33,8,128]{2,1,0:T(8,128)S(1)} %summed.6), channel_id=1, source_target_pairs={{0,4},{1,3},{2,6},{3,1},{4,0},{5,7},{6,2},{7,5},{8,12},{9,11},{10,... | collective-permute-start | bytes 405512 | tf_op jit(solution)/shard_map/ppermute | solution.py:245
  6.9 6.7 %collective-permute-start.1 = (f32[96,8,128]{2,1,0:T(8,128)S(1)}, f32[96,8,128]{2,1,0:T(8,128)S(1)}, u32[]{:S(2)}, u32[]{:S(2)}) collective-permute-start(f32[96,8,128]{2,1,0:T(8,128)S(1)} %next_products.5), channel_id=1, source_target_pairs={{0,1},{1,0},{2,3},{3,2},{4,5},{5,4},{6,7},{7,6},{8,9},{9,8},{10,11... | collective-permute-start | bytes 1179656 | tf_op jit(solution)/shard_map/ppermute | solution.py:245
  7.5 6.2 %collective-permute-start.6 = (f32[32,8,128]{2,1,0:T(8,128)S(1)}, f32[32,8,128]{2,1,0:T(8,128)S(1)}, u32[]{:S(2)}, u32[]{:S(2)}) collective-permute-start(f32[32,8,128]{2,1,0:T(8,128)S(1)} %summed.9), channel_id=1, source_target_pairs={{0,4},{1,3},{2,6},{3,1},{4,0},{5,7},{6,2},{7,5},{8,12},{9,11},{10,... | collective-permute-start | bytes 393224 | tf_op jit(solution)/shard_map/ppermute | solution.py:245
  9.6 6.4 %collective-permute-start.4 = (f32[33,8,128]{2,1,0:T(8,128)S(1)}, f32[33,8,128]{2,1,0:T(8,128)S(1)}, u32[]{:S(2)}, u32[]{:S(2)}) collective-permute-start(f32[33,8,128]{2,1,0:T(8,128)S(1)} %summed.7.refs_2_), channel_id=1, source_target_pairs={{0,2},{1,5},{2,0},{3,7},{4,6},{5,1},{6,4},{7,3},{8,10},{9,13},{10,... | collective-permute-start | bytes 405512 | tf_op jit(solution)/shard_map/ppermute | solution.py:245
  11.6 7.6 %collective-permute-start.5 = (f32[64,8,128]{2,1,0:T(8,128)S(1)}, f32[64,8,128]{2,1,0:T(8,128)S(1)}, u32[]{:S(2)}, u32[]{:S(2)}) collective-permute-start(f32[64,8,128]{2,1,0:T(8,128)S(1)} %summed.8), channel_id=1, source_target_pairs={{0,4},{1,3},{2,6},{3,1},{4,0},{5,7},{6,2},{7,5},{8,12},{9,11},{10,... | collective-permute-start | bytes 786440 | tf_op jit(solution)/shard_map/ppermute | solution.py:245
  15.9 7.3 %collective-permute-start.7 = (f32[33,8,128]{2,1,0:T(8,128)S(1)}, f32[33,8,128]{2,1,0:T(8,128)S(1)}, u32[]{:S(2)}, u32[]{:S(2)}) collective-permute-start(f32[33,8,128]{2,1,0:T(8,128)S(1)} %summed.10.refs_3_), channel_id=1, source_target_pairs={{0,8},{1,9},{2,10},{3,11},{4,12},{5,13},{6,14},{7,15},{8,0},{9,1},... | collective-permute-start | bytes 405512 | tf_op jit(solution)/shard_map/ppermute | solution.py:245
  19.2 5.0 %collective-permute-start.8 = (f32[32,8,128]{2,1,0:T(8,128)S(1)}, f32[32,8,128]{2,1,0:T(8,128)S(1)}, u32[]{:S(2)}, u32[]{:S(2)}) collective-permute-start(f32[32,8,128]{2,1,0:T(8,128)S(1)} %summed.11), channel_id=1, source_target_pairs={{0,2},{1,5},{2,0},{3,7},{4,6},{5,1},{6,4},{7,3},{8,10},{9,13},{10,... | collective-permute-start | bytes 393224 | tf_op jit(solution)/shard_map/ppermute | solution.py:245

commit v17 on v16

--- a/solution.py
+++ b/solution.py
@@ -16,22 +16,10 @@
 )
 
 
-def chip_orders(bits):
-    first = list(range(1, bits))
-    second = list(first)
-    if bits > 2:
-        second[0], second[1] = second[1], second[0]
-    return second, first
-
-
-def place_of(group, me, core, bits):
-    away = [1 - (((group ^ me) >> bit) & 1) for bit in range(1, bits)]
-    if bits > 2:
-        swapped = core == 0
-        away[:2] = [jnp.where(swapped, away[1], away[0]), jnp.where(swapped, away[0], away[1])]
+def place_of(group, me, bits):
     place = 0
-    for value in away:
-        place = place * 2 + value
+    for bit in range(1, bits):
+        place = place * 2 + (1 - (((group ^ me) >> bit) & 1))
     return place
 
 
@@ -82,9 +70,8 @@
     loads[0].wait()
     loads[1].wait()
     for v in range(held):
-        core = seen[0, v] & 1
-        keep = 1 - (core ^ (me & 1))
-        at = pl.ds(pl.multiple_of(place_of(seen[0, v], me, core, bits) * users, users), users)
+        keep = 1 - ((seen[0, v] ^ me) & 1)
+        at = pl.ds(pl.multiple_of(place_of(seen[0, v], me, bits) * users, users), users)
         rows[keep, at, 0:antennas] = raw[0, v, 0]
         rows[keep, at, antennas:2 * antennas] = raw[0, v, 1]
     loads[2].wait()
@@ -237,12 +224,11 @@
     bits = devices.bit_length() - 1
     users, columns = channel.shape[3], precoder.shape[2]
     tiles = (users // 8) * (columns // 128) * 2
-    orders = chip_orders(bits)
     flat = precoder.reshape(-1, columns)
     half = devices // 4
 
-    def swap(value, bit_of):
-        return lax.ppermute(value, "ap", [(i, i ^ (1 << bit_of[i & 1])) for i in range(devices)])
+    def swap(value, bit):
+        return lax.ppermute(value, "ap", [(i, i ^ (1 << bit)) for i in range(devices)])
 
     arrays = []
     terms = [[] for _ in range(2 * half)]
@@ -265,7 +251,7 @@
     sent, kept, rows, weights, served = first_products(
         bits, quarter, visible, cluster.T, channel, flat
     )
-    came = swap(sent, (0, 0))
+    came = swap(sent, 0)
     add(sent, [], False)
     powers.append((0, quarter * tiles))
     add(kept, range(quarter), False)
@@ -273,7 +259,7 @@
     products = functools.partial(next_products, users, rows=rows, weights=weights, served=served)
     for at, (first, count) in enumerate(((quarter, 4 * quarter), (5 * quarter, 3 * quarter))):
         slots = range(first, first + count)
-        come = swap(products(0, first, count, cost=COSTS[2 * at]), (0, 0))
+        come = swap(products(0, first, count, cost=COSTS[2 * at]), 0)
         add(products(1, first, count, cost=COSTS[2 * at + 1]), slots, False)
         add(come, slots, False)
     with_power = set()
@@ -283,7 +269,7 @@
         with_power.add(step)
         after = [now] if number in (3, 5) else []
         now = total(slots, power, COSTS[4 + number] if number < 6 else 8192, after)
-        came = swap(now, (orders[0][step], orders[1][step]))
+        came = swap(now, step + 1)
         slots = [slot + (1 << (bits - 2 - step)) for slot in slots]
         add(came, slots, power)
     used = sorted({array for array, _ in terms[last] + powers})

time: 25.2 us -> 26 us (1.032)
  waiting for transfers between devices: 6.84 us -> 9.27 us
  starting transfers between devices: 13.6 us -> 11.9 us
    ppermute x9, waiting for transfers between devices: 6.84 us -> 9.27 us  [swap(): lax.ppermute(value, 'ap', [(i, i ^ 1 << bit) for i in range(devices)])]
    ppermute x9, starting transfers between devices: 13.6 us -> 11.9 us  [swap(): lax.ppermute(value, 'ap', [(i, i ^ 1 << bit) for i in range(devices)])]
  transfers between devices with their start and end apart: 9 -> 9, of which waited for: 5 -> 6; matrix products, arithmetic and copies ran while one was open for 0% -> 0% of each run, Pallas kernels for 7% -> 7%
where the time goes in v17:
time: 26 us; the launch traced here: 25.8 us
  starting transfers between devices  11.9 us (46%)
  waiting for transfers between devices  9.27 us (36%)
  Pallas kernels  4.52 us (17%)
    ppermute x9, starting transfers between devices, swap(): lax.ppermute(value, 'ap', [(i, i ^ 1 << bit) for i in range(devices)])  11.9 us
    ppermute x9, waiting for transfers between devices, swap(): lax.ppermute(value, 'ap', [(i, i ^ 1 << bit) for i in range(devices)])  9.27 us
    pallas_call x1, Pallas kernels, first_products(): pl.pallas_call(functools.partial(first_kernel, bits), out_shape=(message(...  2 us
    pallas_call x4, Pallas kernels, next_products(): pl.pallas_call(functools.partial(next_kernel, users, keep, first, slots),...  1.61 us
    pallas_call x1, Pallas kernels, finish(): pl.pallas_call(functools.partial(final_kernel, terms, powers), out_shape=...  0.76 us
  transfers between devices with their start and end apart: 9, of which 6 were waited for; matrix products, arithmetic and copies ran while one was open for 0% of the time, Pallas kernels for 7%

profile of v17, /device:TPU:0, one launch (start us, length us, event | category | flops | bytes accessed | tf_op | source)
XLA Modules:
  0.0 25.8 jit_solution(1153901067153770320)
XLA Ops:
  0.0 2.0 %first_products.1 = (f32[33,8,128]{2,1,0:T(8,128)S(1)}, f32[32,8,128]{2,1,0:T(8,128)S(1)}, bf16[2,256,1024]{2,1,0:T(8,128)(2,1)S(1)}, bf16[1024,512]{1,0:T(8,128)(2,1)S(1)}, f32[1,512]{1,0:T(1,128)S(1)}) custom-call(s32[1,12]{1,0:T(1,128)} %visible.1, s32[4,512]{1,0:T(4,128)} %bitcast.3, bf16[1,12,2,32,512]{4,3,2,1,0:T(8,128)(2,1)} %channel.1, ...), custom_call_target="tpu_custom_call" | custom-call | flops 8192 | bytes 8192 | tf_op jit(solution)/shard_map/first_products/pallas_call | solution.py:109
  2.0 0.5 %collective-permute-start = (f32[33,8,128]{2,1,0:T(8,128)S(1)}, f32[33,8,128]{2,1,0:T(8,128)S(1)}, u32[]{:S(2)}, u32[]{:S(2)}) collective-permute-start(f32[33,8,128]{2,1,0:T(8,128)S(1)} %get-tuple-element.10.refs_0_), channel_id=1, source_target_pairs={{0,1},{1,0},{2,3},{3,2},{4,5},{5,4},{6,7},{7,6},{8,9},{9,8},{10,11... | collective-permute-start | bytes 405512 | tf_op jit(solution)/shard_map/ppermute | solution.py:231
  2.5 0.4 %next_products.7 = f32[128,8,128]{2,1,0:T(8,128)S(1)} custom-call(bf16[2,256,1024]{2,1,0:T(8,128)(2,1)S(1)} %get-tuple-element.11.rows, bf16[1024,512]{1,0:T(8,128)(2,1)S(1)} %get-tuple-element.12.weights, f32[1,512]{1,0:T(1,128)S(1)} %get-tuple-element.13.served), custom_call_target="tpu_custom_call" | custom-call | flops 8192 | bytes 8192 | tf_op jit(solution)/shard_map/next_products/pallas_call | solution.py:135
  3.0 0.1 collective-permute-start.3
  3.1 0.4 %collective-permute-done.refs_2_.refs_1_ = f32[33,8,128]{2,1,0:T(8,128)S(1)} collective-permute-done((f32[33,8,128]{2,1,0:T(8,128)S(1)}, f32[33,8,128]{2,1,0:T(8,128)S(1)}, u32[]{:S(2)}, u32[]{:S(2)}) %collective-permute-start) | collective-permute-done | bytes 135200 | tf_op jit(solution)/shard_map/ppermute | solution.py:231
  3.5 2.9 %collective-permute-start.2 = (f32[33,8,128]{2,1,0:T(8,128)S(1)}, f32[33,8,128]{2,1,0:T(8,128)S(1)}, u32[]{:S(2)}, u32[]{:S(2)}) collective-permute-start(f32[33,8,128]{2,1,0:T(8,128)S(1)} %summed.6), channel_id=1, source_target_pairs={{0,2},{1,3},{2,0},{3,1},{4,6},{5,7},{6,4},{7,5},{8,10},{9,11},{10,... | collective-permute-start | bytes 405512 | tf_op jit(solution)/shard_map/ppermute | solution.py:231
  6.5 0.4 %next_products.5 = f32[96,8,128]{2,1,0:T(8,128)S(1)} custom-call(bf16[2,256,1024]{2,1,0:T(8,128)(2,1)S(1)} %get-tuple-element.11.rows, bf16[1024,512]{1,0:T(8,128)(2,1)S(1)} %get-tuple-element.12.weights, f32[1,512]{1,0:T(1,128)S(1)} %get-tuple-element.13.served), custom_call_target="tpu_custom_call" | custom-call | flops 68719476736 | bytes 68719476736 | tf_op jit(solution)/shard_map/next_products/pallas_call | solution.py:135
  6.8 0.1 collective-permute-start.1
  6.9 0.4 %next_products.6.refs_2_.refs_0_ = f32[128,8,128]{2,1,0:T(8,128)S(1)} custom-call(bf16[2,256,1024]{2,1,0:T(8,128)(2,1)S(1)} %get-tuple-element.11.rows, bf16[1024,512]{1,0:T(8,128)(2,1)S(1)} %get-tuple-element.12.weights, f32[1,512]{1,0:T(1,128)S(1)} %get-tuple-element.13.served), custom_call_target="tpu_custom_call" | custom-call | flops 67108864 | bytes 67108864 | tf_op jit(solution)/shard_map/next_products/pallas_call | solution.py:135
  7.4 0.0 collective-permute-done.3.refs_3_.refs_1_
  7.4 0.3 %collective-permute-start.6 = (f32[32,8,128]{2,1,0:T(8,128)S(1)}, f32[32,8,128]{2,1,0:T(8,128)S(1)}, u32[]{:S(2)}, u32[]{:S(2)}) collective-permute-start(f32[32,8,128]{2,1,0:T(8,128)S(1)} %summed.9), channel_id=1, source_target_pairs={{0,2},{1,3},{2,0},{3,1},{4,6},{5,7},{6,4},{7,5},{8,10},{9,11},{10,... | collective-permute-start | bytes 393224 | tf_op jit(solution)/shard_map/ppermute | solution.py:231
  7.7 2.7 %collective-permute-done.2.refs_4_ = f32[33,8,128]{2,1,0:T(8,128)S(1)} collective-permute-done((f32[33,8,128]{2,1,0:T(8,128)S(1)}, f32[33,8,128]{2,1,0:T(8,128)S(1)}, u32[]{:S(2)}, u32[]{:S(2)}) %collective-permute-start.2) | collective-permute-done | bytes 135200 | tf_op jit(solution)/shard_map/ppermute | solution.py:231
  10.4 1.8 %collective-permute-start.4 = (f32[33,8,128]{2,1,0:T(8,128)S(1)}, f32[33,8,128]{2,1,0:T(8,128)S(1)}, u32[]{:S(2)}, u32[]{:S(2)}) collective-permute-start(f32[33,8,128]{2,1,0:T(8,128)S(1)} %summed.7.refs_2_), channel_id=1, source_target_pairs={{0,4},{1,5},{2,6},{3,7},{4,0},{5,1},{6,2},{7,3},{8,12},{9,13},{10,... | collective-permute-start | bytes 405512 | tf_op jit(solution)/shard_map/ppermute | solution.py:231
  12.3 2.3 %collective-permute-start.5 = (f32[64,8,128]{2,1,0:T(8,128)S(1)}, f32[64,8,128]{2,1,0:T(8,128)S(1)}, u32[]{:S(2)}, u32[]{:S(2)}) collective-permute-start(f32[64,8,128]{2,1,0:T(8,128)S(1)} %summed.8), channel_id=1, source_target_pairs={{0,2},{1,3},{2,0},{3,1},{4,6},{5,7},{6,4},{7,5},{8,10},{9,11},{10,... | collective-permute-start | bytes 786440 | tf_op jit(solution)/shard_map/ppermute | solution.py:231
  14.7 0.4 %next_products.4.refs_2_.refs_0_ = f32[96,8,128]{2,1,0:T(8,128)S(1)} custom-call(bf16[2,256,1024]{2,1,0:T(8,128)(2,1)S(1)} %get-tuple-element.11.rows, bf16[1024,512]{1,0:T(8,128)(2,1)S(1)} %get-tuple-element.12.weights, f32[1,512]{1,0:T(1,128)S(1)} %get-tuple-element.13.served), custom_call_target="tpu_custom_call" | custom-call | flops 8589934592 | bytes 8589934592 | tf_op jit(solution)/shard_map/next_products/pallas_call | solution.py:135
  15.0 0.0 collective-permute-done.1.refs_3_.refs_1_
  15.0 0.0 collective-permute-done.6.refs_5_
  15.1 0.5 %collective-permute-done.4.refs_6_.refs_5_ = f32[33,8,128]{2,1,0:T(8,128)S(1)} collective-permute-done((f32[33,8,128]{2,1,0:T(8,128)S(1)}, f32[33,8,128]{2,1,0:T(8,128)S(1)}, u32[]{:S(2)}, u32[]{:S(2)}) %collective-permute-start.4) | collective-permute-done | bytes 135200 | tf_op jit(solution)/shard_map/ppermute | solution.py:231
  15.6 2.8 %collective-permute-start.7 = (f32[33,8,128]{2,1,0:T(8,128)S(1)}, f32[33,8,128]{2,1,0:T(8,128)S(1)}, u32[]{:S(2)}, u32[]{:S(2)}) collective-permute-start(f32[33,8,128]{2,1,0:T(8,128)S(1)} %summed.10.refs_3_), channel_id=1, source_target_pairs={{0,8},{1,9},{2,10},{3,11},{4,12},{5,13},{6,14},{7,15},{8,0},{9,1},... | collective-permute-start | bytes 405512 | tf_op jit(solution)/shard_map/ppermute | solution.py:231
  18.4 1.2 %collective-permute-done.5.refs_2_.refs_6_ = f32[64,8,128]{2,1,0:T(8,128)S(1)} collective-permute-done((f32[64,8,128]{2,1,0:T(8,128)S(1)}, f32[64,8,128]{2,1,0:T(8,128)S(1)}, u32[]{:S(2)}, u32[]{:S(2)}) %collective-permute-start.5) | collective-permute-done | bytes 262176 | tf_op jit(solution)/shard_map/ppermute | solution.py:231
  19.6 1.0 %collective-permute-start.8 = (f32[32,8,128]{2,1,0:T(8,128)S(1)}, f32[32,8,128]{2,1,0:T(8,128)S(1)}, u32[]{:S(2)}, u32[]{:S(2)}) collective-permute-start(f32[32,8,128]{2,1,0:T(8,128)S(1)} %summed.11), channel_id=1, source_target_pairs={{0,4},{1,5},{2,6},{3,7},{4,0},{5,1},{6,2},{7,3},{8,12},{9,13},{10,... | collective-permute-start | bytes 393224 | tf_op jit(solution)/shard_map/ppermute | solution.py:231
  20.7 3.0 %collective-permute-done.7.refs_7_ = f32[33,8,128]{2,1,0:T(8,128)S(1)} collective-permute-done((f32[33,8,128]{2,1,0:T(8,128)S(1)}, f32[33,8,128]{2,1,0:T(8,128)S(1)}, u32[]{:S(2)}, u32[]{:S(2)}) %collective-permute-start.7) | collective-permute-done | bytes 135200 | tf_op jit(solution)/shard_map/ppermute | solution.py:231
  23.7 1.4 %collective-permute-done.8.refs_8_ = f32[32,8,128]{2,1,0:T(8,128)S(1)} collective-permute-done((f32[32,8,128]{2,1,0:T(8,128)S(1)}, f32[32,8,128]{2,1,0:T(8,128)S(1)}, u32[]{:S(2)}, u32[]{:S(2)}) %collective-permute-start.8) | collective-permute-done | bytes 131104 | tf_op jit(solution)/shard_map/ppermute | solution.py:231
  25.0 0.8 %finish.1 = f32[32,2,512]{2,1,0:T(2,128)} custom-call(f32[33,8,128]{2,1,0:T(8,128)S(1)} %get-tuple-element.10.refs_0_, f32[33,8,128]{2,1,0:T(8,128)S(1)} %collective-permute-done.refs_2_.refs_1_, f32[96,8,128]{2,1,0:T(8,128)S(1)} %next_products.4.refs_2_.refs_0_, f32[96,8,128]{2,1,0:T(8,128)S(1)} %collective-permute-done.1.refs_3_.refs_1_, ...), custom_call_target="tpu_custom_call" | custom-call | tf_op jit(solution)/shard_map/finish/pallas_call | solution.py:191
  (6 shorter events, 0.2 us)
Async XLA Ops:
  2.0 1.5 %collective-permute-start = (f32[33,8,128]{2,1,0:T(8,128)S(1)}, f32[33,8,128]{2,1,0:T(8,128)S(1)}, u32[]{:S(2)}, u32[]{:S(2)}) collective-permute-start(f32[33,8,128]{2,1,0:T(8,128)S(1)} %get-tuple-element.10.refs_0_), channel_id=1, source_target_pairs={{0,1},{1,0},{2,3},{3,2},{4,5},{5,4},{6,7},{7,6},{8,9},{9,8},{10,11... | collective-permute-start | bytes 405512 | tf_op jit(solution)/shard_map/ppermute | solution.py:231
  3.0 4.4 %collective-permute-start.3 = (f32[128,8,128]{2,1,0:T(8,128)S(1)}, f32[128,8,128]{2,1,0:T(8,128)S(1)}, u32[]{:S(2)}, u32[]{:S(2)}) collective-permute-start(f32[128,8,128]{2,1,0:T(8,128)S(1)} %next_products.7), channel_id=1, source_target_pairs={{0,1},{1,0},{2,3},{3,2},{4,5},{5,4},{6,7},{7,6},{8,9},{9,8},{10,11... | collective-permute-start | bytes 1572872 | tf_op jit(solution)/shard_map/ppermute | solution.py:231
  3.5 6.9 %collective-permute-start.2 = (f32[33,8,128]{2,1,0:T(8,128)S(1)}, f32[33,8,128]{2,1,0:T(8,128)S(1)}, u32[]{:S(2)}, u32[]{:S(2)}) collective-permute-start(f32[33,8,128]{2,1,0:T(8,128)S(1)} %summed.6), channel_id=1, source_target_pairs={{0,2},{1,3},{2,0},{3,1},{4,6},{5,7},{6,4},{7,5},{8,10},{9,11},{10,... | collective-permute-start | bytes 405512 | tf_op jit(solution)/shard_map/ppermute | solution.py:231
  6.8 8.2 %collective-permute-start.1 = (f32[96,8,128]{2,1,0:T(8,128)S(1)}, f32[96,8,128]{2,1,0:T(8,128)S(1)}, u32[]{:S(2)}, u32[]{:S(2)}) collective-permute-start(f32[96,8,128]{2,1,0:T(8,128)S(1)} %next_products.5), channel_id=1, source_target_pairs={{0,1},{1,0},{2,3},{3,2},{4,5},{5,4},{6,7},{7,6},{8,9},{9,8},{10,11... | collective-permute-start | bytes 1179656 | tf_op jit(solution)/shard_map/ppermute | solution.py:231
  7.4 7.7 %collective-permute-start.6 = (f32[32,8,128]{2,1,0:T(8,128)S(1)}, f32[32,8,128]{2,1,0:T(8,128)S(1)}, u32[]{:S(2)}, u32[]{:S(2)}) collective-permute-start(f32[32,8,128]{2,1,0:T(8,128)S(1)} %summed.9), channel_id=1, source_target_pairs={{0,2},{1,3},{2,0},{3,1},{4,6},{5,7},{6,4},{7,5},{8,10},{9,11},{10,... | collective-permute-start | bytes 393224 | tf_op jit(solution)/shard_map/ppermute | solution.py:231
  10.4 5.1 %collective-permute-start.4 = (f32[33,8,128]{2,1,0:T(8,128)S(1)}, f32[33,8,128]{2,1,0:T(8,128)S(1)}, u32[]{:S(2)}, u32[]{:S(2)}) collective-permute-start(f32[33,8,128]{2,1,0:T(8,128)S(1)} %summed.7.refs_2_), channel_id=1, source_target_pairs={{0,4},{1,5},{2,6},{3,7},{4,0},{5,1},{6,2},{7,3},{8,12},{9,13},{10,... | collective-permute-start | bytes 405512 | tf_op jit(solution)/shard_map/ppermute | solution.py:231
  12.3 7.3 %collective-permute-start.5 = (f32[64,8,128]{2,1,0:T(8,128)S(1)}, f32[64,8,128]{2,1,0:T(8,128)S(1)}, u32[]{:S(2)}, u32[]{:S(2)}) collective-permute-start(f32[64,8,128]{2,1,0:T(8,128)S(1)} %summed.8), channel_id=1, source_target_pairs={{0,2},{1,3},{2,0},{3,1},{4,6},{5,7},{6,4},{7,5},{8,10},{9,11},{10,... | collective-permute-start | bytes 786440 | tf_op jit(solution)/shard_map/ppermute | solution.py:231
  15.6 8.1 %collective-permute-start.7 = (f32[33,8,128]{2,1,0:T(8,128)S(1)}, f32[33,8,128]{2,1,0:T(8,128)S(1)}, u32[]{:S(2)}, u32[]{:S(2)}) collective-permute-start(f32[33,8,128]{2,1,0:T(8,128)S(1)} %summed.10.refs_3_), channel_id=1, source_target_pairs={{0,8},{1,9},{2,10},{3,11},{4,12},{5,13},{6,14},{7,15},{8,0},{9,1},... | collective-permute-start | bytes 405512 | tf_op jit(solution)/shard_map/ppermute | solution.py:231
  19.6 5.4 %collective-permute-start.8 = (f32[32,8,128]{2,1,0:T(8,128)S(1)}, f32[32,8,128]{2,1,0:T(8,128)S(1)}, u32[]{:S(2)}, u32[]{:S(2)}) collective-permute-start(f32[32,8,128]{2,1,0:T(8,128)S(1)} %summed.11), channel_id=1, source_target_pairs={{0,4},{1,5},{2,6},{3,7},{4,0},{5,1},{6,2},{7,3},{8,12},{9,13},{10,... | collective-permute-start | bytes 393224 | tf_op jit(solution)/shard_map/ppermute | solution.py:231

commit v18 on v16

--- a/solution.py
+++ b/solution.py
@@ -65,7 +65,7 @@
 
 def first_kernel(
     bits, visible, cluster, channel, precoder,
-    out, kept, rows, weights, served,
+    out, rows, weights, served,
     seen, names, raw, sems,
 ):
     me = lax.axis_index("ap")
@@ -80,11 +80,13 @@
         load.start()
     rows[...] = jnp.zeros_like(rows)
     loads[0].wait()
-    loads[1].wait()
+    places = []
     for v in range(held):
         core = seen[0, v] & 1
-        keep = 1 - (core ^ (me & 1))
-        at = pl.ds(pl.multiple_of(place_of(seen[0, v], me, core, bits) * users, users), users)
+        places.append((1 - (core ^ (me & 1)), place_of(seen[0, v], me, core, bits) * users))
+    loads[1].wait()
+    for v, (keep, place) in enumerate(places):
+        at = pl.ds(pl.multiple_of(place, users), users)
         rows[keep, at, 0:antennas] = raw[0, v, 0]
         rows[keep, at, antennas:2 * antennas] = raw[0, v, 1]
     loads[2].wait()
@@ -92,15 +94,15 @@
     served[...] = here
     loads[3].wait()
     mask = here > 0.0
-    size = (kept.shape[0] // (weights.shape[1] // 128) // 2) * 8
+    size = (out.shape[0] // (weights.shape[1] // 128) // 2) * 8
     write_products(users, rows.at[0, 0:size], weights[...], mask, out)
     out[out.shape[0] - 1] = power_tile(weights[...], mask)
-    write_products(users, rows.at[1, 0:size], weights[...], mask, kept)
-
-
-def next_kernel(users, keep, first, slots, rows, weights, served, *refs):
-    mine = rows.at[keep, first * users:(first + slots) * users]
-    write_products(users, mine, weights[...], served[...] > 0.0, refs[-1])
+
+
+def next_kernel(users, jobs, rows, weights, served, *outs):
+    for (keep, first, slots), out in zip(jobs, outs):
+        mine = rows.at[keep, first * users:(first + slots) * users]
+        write_products(users, mine, weights[...], served[...] > 0.0, out)
 
 
 def message(tiles):
@@ -123,13 +125,12 @@
         functools.partial(first_kernel, bits),
         out_shape=(
             message(tiles + 1),
-            message(tiles),
             jax.ShapeDtypeStruct((2, slots * users, 2 * antennas), jnp.bfloat16),
             jax.ShapeDtypeStruct(precoder.shape, jnp.bfloat16),
             jax.ShapeDtypeStruct((1, columns), jnp.float32),
         ),
         in_specs=[hbm] * 4,
-        out_specs=(vmem,) * 5,
+        out_specs=(vmem,) * 4,
         scratch_shapes=[
             pltpu.SMEM(visible.shape, jnp.int32),
             pltpu.VMEM(cluster.shape, jnp.int32),
@@ -142,14 +143,15 @@
     )(*[pltpu.with_memory_space_constraint(operand, pltpu.HBM) for operand in operands])
 
 
-def next_products(users, keep, first, slots, cost, rows, weights, served):
+def next_products(users, jobs, cost, rows, weights, served):
     vmem = pl.BlockSpec(memory_space=pltpu.VMEM)
-    big = slots > 8
+    big = max(slots for _, _, slots in jobs) > 8
+    tiles = (users // 8) * (weights.shape[1] // 128) * 2
     return pl.pallas_call(
-        functools.partial(next_kernel, users, keep, first, slots),
-        out_shape=message(slots * (users // 8) * (weights.shape[1] // 128) * 2),
+        functools.partial(next_kernel, users, jobs),
+        out_shape=[message(slots * tiles) for _, _, slots in jobs],
         in_specs=[vmem] * 3,
-        out_specs=vmem,
+        out_specs=[vmem] * len(jobs),
         compiler_params=pltpu.CompilerParams(vmem_limit_bytes=48 * MIB if big else 16 * MIB),
         cost_estimate=estimate(cost),
         name="next_products",
@@ -262,20 +264,22 @@
         return summed([arrays[array] for array in used], jobs, cost, after)
 
     quarter = half // 4
-    sent, kept, rows, weights, served = first_products(
-        bits, quarter, visible, cluster.T, channel, flat
-    )
+    sent, rows, weights, served = first_products(bits, quarter, visible, cluster.T, channel, flat)
     came = swap(sent, (0, 0))
     add(sent, [], False)
     powers.append((0, quarter * tiles))
+    products = functools.partial(next_products, users, rows=rows, weights=weights, served=served)
+    first, count = quarter, 4 * quarter
+    send, kept = products(((0, first, count), (1, 0, quarter)), cost=COSTS[0])
     add(kept, range(quarter), False)
     add(came, range(quarter), True)
-    products = functools.partial(next_products, users, rows=rows, weights=weights, served=served)
-    for at, (first, count) in enumerate(((quarter, 4 * quarter), (5 * quarter, 3 * quarter))):
-        slots = range(first, first + count)
-        come = swap(products(0, first, count, cost=COSTS[2 * at]), (0, 0))
-        add(products(1, first, count, cost=COSTS[2 * at + 1]), slots, False)
-        add(come, slots, False)
+    come = swap(send, (0, 0))
+    add(products(((1, first, count),), cost=COSTS[1])[0], range(first, first + count), False)
+    add(come, range(first, first + count), False)
+    first, count = 5 * quarter, 3 * quarter
+    come = swap(products(((0, first, count),), cost=COSTS[2])[0], (0, 0))
+    add(products(((1, first, count),), cost=COSTS[3])[0], range(first, first + count), False)
+    add(come, range(first, first + count), False)
     with_power = set()
     last = 2 * half - 1
     for number, (step, slots) in enumerate(message_order(bits - 1)):

time: 25.2 us -> 25 us (level)
  transfers between devices with their start and end apart: 9 -> 9, of which waited for: 5 -> 5; matrix products, arithmetic and copies ran while one was open for 0% -> 0% of each run, Pallas kernels for 7% -> 8%
where the time goes in v18:
time: 25 us; the launch traced here: 24.9 us
  starting transfers between devices  13.6 us (54%)
  waiting for transfers between devices  6.71 us (27%)
  Pallas kernels  4.48 us (18%)
    ppermute x9, starting transfers between devices, swap(): lax.ppermute(value, 'ap', [(i, i ^ 1 << bit_of[i & 1]) for i in range(dev...  13.6 us
    ppermute x9, waiting for transfers between devices, swap(): lax.ppermute(value, 'ap', [(i, i ^ 1 << bit_of[i & 1]) for i in range(dev...  6.71 us
    pallas_call x1, Pallas kernels, first_products(): pl.pallas_call(functools.partial(first_kernel, bits), out_shape=(message(...  1.82 us
    pallas_call x4, Pallas kernels, next_products(): pl.pallas_call(functools.partial(next_kernel, users, jobs), out_shape=[me...  1.74 us
    pallas_call x1, Pallas kernels, finish(): pl.pallas_call(functools.partial(final_kernel, terms, powers), out_shape=...  0.76 us
  transfers between devices with their start and end apart: 9, of which 5 were waited for; matrix products, arithmetic and copies ran while one was open for 0% of the time, Pallas kernels for 8%

profile of v18, /device:TPU:0, one launch (start us, length us, event | category | flops | bytes accessed | tf_op | source)
XLA Modules:
  0.0 24.9 jit_solution(1279787498286517342)
XLA Ops:
  0.0 1.8 %first_products.1 = (f32[33,8,128]{2,1,0:T(8,128)S(1)}, bf16[2,256,1024]{2,1,0:T(8,128)(2,1)S(1)}, bf16[1024,512]{1,0:T(8,128)(2,1)S(1)}, f32[1,512]{1,0:T(1,128)S(1)}) custom-call(s32[1,12]{1,0:T(1,128)} %visible.1, s32[4,512]{1,0:T(4,128)} %bitcast.3, bf16[1,12,2,32,512]{4,3,2,1,0:T(8,128)(2,1)} %channel.1, bf16[1024,512]{1,0:T(8,128)(2,1)} %bitcast.2), custom_call_target="tpu_custom_call" | custom-call | flops 8192 | bytes 8192 | tf_op jit(solution)/shard_map/first_products/pallas_call | solution.py:124
  1.8 0.5 %collective-permute-start = (f32[33,8,128]{2,1,0:T(8,128)S(1)}, f32[33,8,128]{2,1,0:T(8,128)S(1)}, u32[]{:S(2)}, u32[]{:S(2)}) collective-permute-start(f32[33,8,128]{2,1,0:T(8,128)S(1)} %get-tuple-element.11.refs_0_), channel_id=1, source_target_pairs={{0,1},{1,0},{2,3},{3,2},{4,5},{5,4},{6,7},{7,6},{8,9},{9,8},{10,11... | collective-permute-start | bytes 405512 | tf_op jit(solution)/shard_map/ppermute | solution.py:247
  2.3 0.6 %next_products.6 = (f32[128,8,128]{2,1,0:T(8,128)S(1)}, f32[32,8,128]{2,1,0:T(8,128)S(1)}) custom-call(bf16[2,256,1024]{2,1,0:T(8,128)(2,1)S(1)} %get-tuple-element.12.rows, bf16[1024,512]{1,0:T(8,128)(2,1)S(1)} %get-tuple-element.13.weights, f32[1,512]{1,0:T(1,128)S(1)} %get-tuple-element.14.served), custom_call_target="tpu_custom_call" | custom-call | flops 8192 | bytes 8192 | tf_op jit(solution)/shard_map/next_products/pallas_call | solution.py:150
  2.9 0.1 collective-permute-start.3
  3.1 0.3 %collective-permute-done.refs_2_.refs_1_ = f32[33,8,128]{2,1,0:T(8,128)S(1)} collective-permute-done((f32[33,8,128]{2,1,0:T(8,128)S(1)}, f32[33,8,128]{2,1,0:T(8,128)S(1)}, u32[]{:S(2)}, u32[]{:S(2)}) %collective-permute-start) | collective-permute-done | bytes 135200 | tf_op jit(solution)/shard_map/ppermute | solution.py:247
  3.4 3.0 %collective-permute-start.2 = (f32[33,8,128]{2,1,0:T(8,128)S(1)}, f32[33,8,128]{2,1,0:T(8,128)S(1)}, u32[]{:S(2)}, u32[]{:S(2)}) collective-permute-start(f32[33,8,128]{2,1,0:T(8,128)S(1)} %summed.6), channel_id=1, source_target_pairs={{0,4},{1,3},{2,6},{3,1},{4,0},{5,7},{6,2},{7,5},{8,12},{9,11},{10,... | collective-permute-start | bytes 405512 | tf_op jit(solution)/shard_map/ppermute | solution.py:247
  6.4 0.4 %next_products.5 = f32[96,8,128]{2,1,0:T(8,128)S(1)} custom-call(bf16[2,256,1024]{2,1,0:T(8,128)(2,1)S(1)} %get-tuple-element.12.rows, bf16[1024,512]{1,0:T(8,128)(2,1)S(1)} %get-tuple-element.13.weights, f32[1,512]{1,0:T(1,128)S(1)} %get-tuple-element.14.served), custom_call_target="tpu_custom_call" | custom-call | flops 68719476736 | bytes 68719476736 | tf_op jit(solution)/shard_map/next_products/pallas_call | solution.py:150
  6.7 0.1 collective-permute-start.1
  6.8 0.4 %next_products.7.refs_2_.refs_0_ = f32[128,8,128]{2,1,0:T(8,128)S(1)} custom-call(bf16[2,256,1024]{2,1,0:T(8,128)(2,1)S(1)} %get-tuple-element.12.rows, bf16[1024,512]{1,0:T(8,128)(2,1)S(1)} %get-tuple-element.13.weights, f32[1,512]{1,0:T(1,128)S(1)} %get-tuple-element.14.served), custom_call_target="tpu_custom_call" | custom-call | flops 67108864 | bytes 67108864 | tf_op jit(solution)/shard_map/next_products/pallas_call | solution.py:150
  7.3 0.0 collective-permute-done.3.refs_3_.refs_1_
  7.3 1.4 %collective-permute-start.6 = (f32[32,8,128]{2,1,0:T(8,128)S(1)}, f32[32,8,128]{2,1,0:T(8,128)S(1)}, u32[]{:S(2)}, u32[]{:S(2)}) collective-permute-start(f32[32,8,128]{2,1,0:T(8,128)S(1)} %summed.9), channel_id=1, source_target_pairs={{0,4},{1,3},{2,6},{3,1},{4,0},{5,7},{6,2},{7,5},{8,12},{9,11},{10,... | collective-permute-start | bytes 393224 | tf_op jit(solution)/shard_map/ppermute | solution.py:247
  8.7 0.7 %collective-permute-done.2.refs_4_ = f32[33,8,128]{2,1,0:T(8,128)S(1)} collective-permute-done((f32[33,8,128]{2,1,0:T(8,128)S(1)}, f32[33,8,128]{2,1,0:T(8,128)S(1)}, u32[]{:S(2)}, u32[]{:S(2)}) %collective-permute-start.2) | collective-permute-done | bytes 135200 | tf_op jit(solution)/shard_map/ppermute | solution.py:247
  9.4 2.0 %collective-permute-start.4 = (f32[33,8,128]{2,1,0:T(8,128)S(1)}, f32[33,8,128]{2,1,0:T(8,128)S(1)}, u32[]{:S(2)}, u32[]{:S(2)}) collective-permute-start(f32[33,8,128]{2,1,0:T(8,128)S(1)} %summed.7.refs_2_), channel_id=1, source_target_pairs={{0,2},{1,5},{2,0},{3,7},{4,6},{5,1},{6,4},{7,3},{8,10},{9,13},{10,... | collective-permute-start | bytes 405512 | tf_op jit(solution)/shard_map/ppermute | solution.py:247
  11.4 1.6 %collective-permute-start.5 = (f32[64,8,128]{2,1,0:T(8,128)S(1)}, f32[64,8,128]{2,1,0:T(8,128)S(1)}, u32[]{:S(2)}, u32[]{:S(2)}) collective-permute-start(f32[64,8,128]{2,1,0:T(8,128)S(1)} %summed.8), channel_id=1, source_target_pairs={{0,4},{1,3},{2,6},{3,1},{4,0},{5,7},{6,2},{7,5},{8,12},{9,11},{10,... | collective-permute-start | bytes 786440 | tf_op jit(solution)/shard_map/ppermute | solution.py:247
  13.0 0.4 %next_products.4.refs_2_.refs_0_ = f32[96,8,128]{2,1,0:T(8,128)S(1)} custom-call(bf16[2,256,1024]{2,1,0:T(8,128)(2,1)S(1)} %get-tuple-element.12.rows, bf16[1024,512]{1,0:T(8,128)(2,1)S(1)} %get-tuple-element.13.weights, f32[1,512]{1,0:T(1,128)S(1)} %get-tuple-element.14.served), custom_call_target="tpu_custom_call" | custom-call | flops 8589934592 | bytes 8589934592 | tf_op jit(solution)/shard_map/next_products/pallas_call | solution.py:150
  13.4 0.0 collective-permute-done.1.refs_3_.refs_1_
  13.4 0.0 collective-permute-done.6.refs_5_
  13.4 2.3 %collective-permute-done.4.refs_6_.refs_5_ = f32[33,8,128]{2,1,0:T(8,128)S(1)} collective-permute-done((f32[33,8,128]{2,1,0:T(8,128)S(1)}, f32[33,8,128]{2,1,0:T(8,128)S(1)}, u32[]{:S(2)}, u32[]{:S(2)}) %collective-permute-start.4) | collective-permute-done | bytes 135200 | tf_op jit(solution)/shard_map/ppermute | solution.py:247
  15.8 3.3 %collective-permute-start.7 = (f32[33,8,128]{2,1,0:T(8,128)S(1)}, f32[33,8,128]{2,1,0:T(8,128)S(1)}, u32[]{:S(2)}, u32[]{:S(2)}) collective-permute-start(f32[33,8,128]{2,1,0:T(8,128)S(1)} %summed.10.refs_3_), channel_id=1, source_target_pairs={{0,8},{1,9},{2,10},{3,11},{4,12},{5,13},{6,14},{7,15},{8,0},{9,1},... | collective-permute-start | bytes 405512 | tf_op jit(solution)/shard_map/ppermute | solution.py:247
  19.0 0.0 collective-permute-done.5.refs_2_.refs_6_
  19.1 1.6 %collective-permute-start.8 = (f32[32,8,128]{2,1,0:T(8,128)S(1)}, f32[32,8,128]{2,1,0:T(8,128)S(1)}, u32[]{:S(2)}, u32[]{:S(2)}) collective-permute-start(f32[32,8,128]{2,1,0:T(8,128)S(1)} %summed.11), channel_id=1, source_target_pairs={{0,2},{1,5},{2,0},{3,7},{4,6},{5,1},{6,4},{7,3},{8,10},{9,13},{10,... | collective-permute-start | bytes 393224 | tf_op jit(solution)/shard_map/ppermute | solution.py:247
  20.6 2.5 %collective-permute-done.7.refs_7_ = f32[33,8,128]{2,1,0:T(8,128)S(1)} collective-permute-done((f32[33,8,128]{2,1,0:T(8,128)S(1)}, f32[33,8,128]{2,1,0:T(8,128)S(1)}, u32[]{:S(2)}, u32[]{:S(2)}) %collective-permute-start.7) | collective-permute-done | bytes 135200 | tf_op jit(solution)/shard_map/ppermute | solution.py:247
  23.1 1.0 %collective-permute-done.8.refs_8_ = f32[32,8,128]{2,1,0:T(8,128)S(1)} collective-permute-done((f32[32,8,128]{2,1,0:T(8,128)S(1)}, f32[32,8,128]{2,1,0:T(8,128)S(1)}, u32[]{:S(2)}, u32[]{:S(2)}) %collective-permute-start.8) | collective-permute-done | bytes 131104 | tf_op jit(solution)/shard_map/ppermute | solution.py:247
  24.1 0.8 %finish.1 = f32[32,2,512]{2,1,0:T(2,128)} custom-call(f32[33,8,128]{2,1,0:T(8,128)S(1)} %get-tuple-element.11.refs_0_, f32[33,8,128]{2,1,0:T(8,128)S(1)} %collective-permute-done.refs_2_.refs_1_, f32[96,8,128]{2,1,0:T(8,128)S(1)} %next_products.4.refs_2_.refs_0_, f32[96,8,128]{2,1,0:T(8,128)S(1)} %collective-permute-done.1.refs_3_.refs_1_, ...), custom_call_target="tpu_custom_call" | custom-call | tf_op jit(solution)/shard_map/finish/pallas_call | solution.py:206
  (6 shorter events, 0.2 us)
Async XLA Ops:
  1.8 1.5 %collective-permute-start = (f32[33,8,128]{2,1,0:T(8,128)S(1)}, f32[33,8,128]{2,1,0:T(8,128)S(1)}, u32[]{:S(2)}, u32[]{:S(2)}) collective-permute-start(f32[33,8,128]{2,1,0:T(8,128)S(1)} %get-tuple-element.11.refs_0_), channel_id=1, source_target_pairs={{0,1},{1,0},{2,3},{3,2},{4,5},{5,4},{6,7},{7,6},{8,9},{9,8},{10,11... | collective-permute-start | bytes 405512 | tf_op jit(solution)/shard_map/ppermute | solution.py:247
  2.9 4.3 %collective-permute-start.3 = (f32[128,8,128]{2,1,0:T(8,128)S(1)}, f32[128,8,128]{2,1,0:T(8,128)S(1)}, u32[]{:S(2)}, u32[]{:S(2)}) collective-permute-start(f32[128,8,128]{2,1,0:T(8,128)S(1)} %get-tuple-element.16), channel_id=1, source_target_pairs={{0,1},{1,0},{2,3},{3,2},{4,5},{5,4},{6,7},{7,6},{8,9},{9,8},{10,11... | collective-permute-start | bytes 1572872 | tf_op jit(solution)/shard_map/ppermute | solution.py:247
  3.4 6.0 %collective-permute-start.2 = (f32[33,8,128]{2,1,0:T(8,128)S(1)}, f32[33,8,128]{2,1,0:T(8,128)S(1)}, u32[]{:S(2)}, u32[]{:S(2)}) collective-permute-start(f32[33,8,128]{2,1,0:T(8,128)S(1)} %summed.6), channel_id=1, source_target_pairs={{0,4},{1,3},{2,6},{3,1},{4,0},{5,7},{6,2},{7,5},{8,12},{9,11},{10,... | collective-permute-start | bytes 405512 | tf_op jit(solution)/shard_map/ppermute | solution.py:247
  6.7 6.7 %collective-permute-start.1 = (f32[96,8,128]{2,1,0:T(8,128)S(1)}, f32[96,8,128]{2,1,0:T(8,128)S(1)}, u32[]{:S(2)}, u32[]{:S(2)}) collective-permute-start(f32[96,8,128]{2,1,0:T(8,128)S(1)} %next_products.5), channel_id=1, source_target_pairs={{0,1},{1,0},{2,3},{3,2},{4,5},{5,4},{6,7},{7,6},{8,9},{9,8},{10,11... | collective-permute-start | bytes 1179656 | tf_op jit(solution)/shard_map/ppermute | solution.py:247
  7.3 6.2 %collective-permute-start.6 = (f32[32,8,128]{2,1,0:T(8,128)S(1)}, f32[32,8,128]{2,1,0:T(8,128)S(1)}, u32[]{:S(2)}, u32[]{:S(2)}) collective-permute-start(f32[32,8,128]{2,1,0:T(8,128)S(1)} %summed.9), channel_id=1, source_target_pairs={{0,4},{1,3},{2,6},{3,1},{4,0},{5,7},{6,2},{7,5},{8,12},{9,11},{10,... | collective-permute-start | bytes 393224 | tf_op jit(solution)/shard_map/ppermute | solution.py:247
  9.4 6.4 %collective-permute-start.4 = (f32[33,8,128]{2,1,0:T(8,128)S(1)}, f32[33,8,128]{2,1,0:T(8,128)S(1)}, u32[]{:S(2)}, u32[]{:S(2)}) collective-permute-start(f32[33,8,128]{2,1,0:T(8,128)S(1)} %summed.7.refs_2_), channel_id=1, source_target_pairs={{0,2},{1,5},{2,0},{3,7},{4,6},{5,1},{6,4},{7,3},{8,10},{9,13},{10,... | collective-permute-start | bytes 405512 | tf_op jit(solution)/shard_map/ppermute | solution.py:247
  11.4 7.6 %collective-permute-start.5 = (f32[64,8,128]{2,1,0:T(8,128)S(1)}, f32[64,8,128]{2,1,0:T(8,128)S(1)}, u32[]{:S(2)}, u32[]{:S(2)}) collective-permute-start(f32[64,8,128]{2,1,0:T(8,128)S(1)} %summed.8), channel_id=1, source_target_pairs={{0,4},{1,3},{2,6},{3,1},{4,0},{5,7},{6,2},{7,5},{8,12},{9,11},{10,... | collective-permute-start | bytes 786440 | tf_op jit(solution)/shard_map/ppermute | solution.py:247
  15.8 7.3 %collective-permute-start.7 = (f32[33,8,128]{2,1,0:T(8,128)S(1)}, f32[33,8,128]{2,1,0:T(8,128)S(1)}, u32[]{:S(2)}, u32[]{:S(2)}) collective-permute-start(f32[33,8,128]{2,1,0:T(8,128)S(1)} %summed.10.refs_3_), channel_id=1, source_target_pairs={{0,8},{1,9},{2,10},{3,11},{4,12},{5,13},{6,14},{7,15},{8,0},{9,1},... | collective-permute-start | bytes 405512 | tf_op jit(solution)/shard_map/ppermute | solution.py:247
  19.1 5.0 %collective-permute-start.8 = (f32[32,8,128]{2,1,0:T(8,128)S(1)}, f32[32,8,128]{2,1,0:T(8,128)S(1)}, u32[]{:S(2)}, u32[]{:S(2)}) collective-permute-start(f32[32,8,128]{2,1,0:T(8,128)S(1)} %summed.11), channel_id=1, source_target_pairs={{0,2},{1,5},{2,0},{3,7},{4,6},{5,1},{6,4},{7,3},{8,10},{9,13},{10,... | collective-permute-start | bytes 393224 | tf_op jit(solution)/shard_map/ppermute | solution.py:247

commit v19 on v18

--- a/solution.py
+++ b/solution.py
@@ -11,8 +11,8 @@
 MIB = 1 << 20
 
 
-COSTS = (8192, 64 * MIB, 65536 * MIB, 8192 * MIB) + (
-    64 * MIB, 1024 * MIB, 1024 * MIB, 65536 * MIB, 1024 * MIB, 8192 * MIB
+COSTS = (8192 * MIB, 65536 * MIB, 64 * MIB, 64 * MIB) + (
+    1024 * MIB, 64 * MIB, 64 * MIB, 65536 * MIB, 65536 * MIB, 1024 * MIB
 )
 
 
@@ -285,9 +285,11 @@
     for number, (step, slots) in enumerate(message_order(bits - 1)):
         power = step not in with_power
         with_power.add(step)
-        after = [now] if number in (3, 5) else []
+        after = [now, came_second] if number == 3 else [now] if number == 5 else []
         now = total(slots, power, COSTS[4 + number] if number < 6 else 8192, after)
         came = swap(now, (orders[0][step], orders[1][step]))
+        if number == 1:
+            came_second = came
         slots = [slot + (1 << (bits - 2 - step)) for slot in slots]
         add(came, slots, power)
     used = sorted({array for array, _ in terms[last] + powers})

time: 25 us -> 25.9 us (1.036)
  waiting for transfers between devices: 6.71 us -> 8.52 us
  starting transfers between devices: 13.6 us -> 12.6 us
    ppermute x9, waiting for transfers between devices: 6.71 us -> 8.52 us  [swap(): lax.ppermute(value, 'ap', [(i, i ^ 1 << bit_of[i & 1]) for i in range(dev...]
    ppermute x9, starting transfers between devices: 13.6 us -> 12.6 us  [swap(): lax.ppermute(value, 'ap', [(i, i ^ 1 << bit_of[i & 1]) for i in range(dev...]
  transfers between devices with their start and end apart: 9 -> 9, of which waited for: 5 -> 7; matrix products, arithmetic and copies ran while one was open for 0% -> 0% of each run, Pallas kernels for 8% -> 7%
where the time goes in v19:
time: 25.9 us; the launch traced here: 25.7 us
  starting transfers between devices  12.6 us (49%)
  waiting for transfers between devices  8.52 us (33%)
  Pallas kernels  4.51 us (17%)
    ppermute x9, starting transfers between devices, swap(): lax.ppermute(value, 'ap', [(i, i ^ 1 << bit_of[i & 1]) for i in range(dev...  12.6 us
    ppermute x9, waiting for transfers between devices, swap(): lax.ppermute(value, 'ap', [(i, i ^ 1 << bit_of[i & 1]) for i in range(dev...  8.52 us
    pallas_call x1, Pallas kernels, first_products(): pl.pallas_call(functools.partial(first_kernel, bits), out_shape=(message(...  1.82 us
    pallas_call x4, Pallas kernels, next_products(): pl.pallas_call(functools.partial(next_kernel, users, jobs), out_shape=[me...  1.74 us
    pallas_call x1, Pallas kernels, finish(): pl.pallas_call(functools.partial(final_kernel, terms, powers), out_shape=...  0.78 us
  transfers between devices with their start and end apart: 9, of which 7 were waited for; matrix products, arithmetic and copies ran while one was open for 0% of the time, Pallas kernels for 7%

profile of v19, /device:TPU:0, one launch (start us, length us, event | category | flops | bytes accessed | tf_op | source)
XLA Modules:
  0.0 25.7 jit_solution(13119586197176303338)
XLA Ops:
  0.0 1.8 %first_products.1 = (f32[33,8,128]{2,1,0:T(8,128)S(1)}, bf16[2,256,1024]{2,1,0:T(8,128)(2,1)S(1)}, bf16[1024,512]{1,0:T(8,128)(2,1)S(1)}, f32[1,512]{1,0:T(1,128)S(1)}) custom-call(s32[1,12]{1,0:T(1,128)} %visible.1, s32[4,512]{1,0:T(4,128)} %bitcast.3, bf16[1,12,2,32,512]{4,3,2,1,0:T(8,128)(2,1)} %channel.1, bf16[1024,512]{1,0:T(8,128)(2,1)} %bitcast.2), custom_call_target="tpu_custom_call" | custom-call | flops 8192 | bytes 8192 | tf_op jit(solution)/shard_map/first_products/pallas_call | solution.py:124
  1.8 0.5 %collective-permute-start = (f32[33,8,128]{2,1,0:T(8,128)S(1)}, f32[33,8,128]{2,1,0:T(8,128)S(1)}, u32[]{:S(2)}, u32[]{:S(2)}) collective-permute-start(f32[33,8,128]{2,1,0:T(8,128)S(1)} %get-tuple-element.11.refs_0_), channel_id=1, source_target_pairs={{0,1},{1,0},{2,3},{3,2},{4,5},{5,4},{6,7},{7,6},{8,9},{9,8},{10,11... | collective-permute-start | bytes 405512 | tf_op jit(solution)/shard_map/ppermute | solution.py:247
  2.3 0.6 %next_products.6 = (f32[128,8,128]{2,1,0:T(8,128)S(1)}, f32[32,8,128]{2,1,0:T(8,128)S(1)}) custom-call(bf16[2,256,1024]{2,1,0:T(8,128)(2,1)S(1)} %get-tuple-element.12.rows, bf16[1024,512]{1,0:T(8,128)(2,1)S(1)} %get-tuple-element.13.weights, f32[1,512]{1,0:T(1,128)S(1)} %get-tuple-element.14.served), custom_call_target="tpu_custom_call" | custom-call | flops 8589934592 | bytes 8589934592 | tf_op jit(solution)/shard_map/next_products/pallas_call | solution.py:150
  2.9 0.1 collective-permute-start.3
  3.1 0.3 %collective-permute-done.refs_2_.refs_1_ = f32[33,8,128]{2,1,0:T(8,128)S(1)} collective-permute-done((f32[33,8,128]{2,1,0:T(8,128)S(1)}, f32[33,8,128]{2,1,0:T(8,128)S(1)}, u32[]{:S(2)}, u32[]{:S(2)}) %collective-permute-start) | collective-permute-done | bytes 135200 | tf_op jit(solution)/shard_map/ppermute | solution.py:247
  3.4 3.0 %collective-permute-start.2 = (f32[33,8,128]{2,1,0:T(8,128)S(1)}, f32[33,8,128]{2,1,0:T(8,128)S(1)}, u32[]{:S(2)}, u32[]{:S(2)}) collective-permute-start(f32[33,8,128]{2,1,0:T(8,128)S(1)} %summed.6), channel_id=1, source_target_pairs={{0,4},{1,3},{2,6},{3,1},{4,0},{5,7},{6,2},{7,5},{8,12},{9,11},{10,... | collective-permute-start | bytes 405512 | tf_op jit(solution)/shard_map/ppermute | solution.py:247
  6.4 0.4 %next_products.7.refs_2_.refs_0_ = f32[128,8,128]{2,1,0:T(8,128)S(1)} custom-call(bf16[2,256,1024]{2,1,0:T(8,128)(2,1)S(1)} %get-tuple-element.12.rows, bf16[1024,512]{1,0:T(8,128)(2,1)S(1)} %get-tuple-element.13.weights, f32[1,512]{1,0:T(1,128)S(1)} %get-tuple-element.14.served), custom_call_target="tpu_custom_call" | custom-call | flops 68719476736 | bytes 68719476736 | tf_op jit(solution)/shard_map/next_products/pallas_call | solution.py:150
  6.8 0.0 collective-permute-done.3.refs_3_.refs_1_
  6.8 0.9 %collective-permute-start.5 = (f32[32,8,128]{2,1,0:T(8,128)S(1)}, f32[32,8,128]{2,1,0:T(8,128)S(1)}, u32[]{:S(2)}, u32[]{:S(2)}) collective-permute-start(f32[32,8,128]{2,1,0:T(8,128)S(1)} %summed.8), channel_id=1, source_target_pairs={{0,4},{1,3},{2,6},{3,1},{4,0},{5,7},{6,2},{7,5},{8,12},{9,11},{10,... | collective-permute-start | bytes 393224 | tf_op jit(solution)/shard_map/ppermute | solution.py:247
  7.7 0.4 %next_products.5 = f32[96,8,128]{2,1,0:T(8,128)S(1)} custom-call(bf16[2,256,1024]{2,1,0:T(8,128)(2,1)S(1)} %get-tuple-element.12.rows, bf16[1024,512]{1,0:T(8,128)(2,1)S(1)} %get-tuple-element.13.weights, f32[1,512]{1,0:T(1,128)S(1)} %get-tuple-element.14.served), custom_call_target="tpu_custom_call" | custom-call | flops 67108864 | bytes 67108864 | tf_op jit(solution)/shard_map/next_products/pallas_call | solution.py:150
  8.1 0.1 collective-permute-start.1
  8.2 0.4 %next_products.4.refs_2_.refs_0_ = f32[96,8,128]{2,1,0:T(8,128)S(1)} custom-call(bf16[2,256,1024]{2,1,0:T(8,128)(2,1)S(1)} %get-tuple-element.12.rows, bf16[1024,512]{1,0:T(8,128)(2,1)S(1)} %get-tuple-element.13.weights, f32[1,512]{1,0:T(1,128)S(1)} %get-tuple-element.14.served), custom_call_target="tpu_custom_call" | custom-call | flops 67108864 | bytes 67108864 | tf_op jit(solution)/shard_map/next_products/pallas_call | solution.py:150
  8.5 0.8 %collective-permute-done.2.refs_4_ = f32[33,8,128]{2,1,0:T(8,128)S(1)} collective-permute-done((f32[33,8,128]{2,1,0:T(8,128)S(1)}, f32[33,8,128]{2,1,0:T(8,128)S(1)}, u32[]{:S(2)}, u32[]{:S(2)}) %collective-permute-start.2) | collective-permute-done | bytes 135200 | tf_op jit(solution)/shard_map/ppermute | solution.py:247
  9.4 2.0 %collective-permute-start.4 = (f32[33,8,128]{2,1,0:T(8,128)S(1)}, f32[33,8,128]{2,1,0:T(8,128)S(1)}, u32[]{:S(2)}, u32[]{:S(2)}) collective-permute-start(f32[33,8,128]{2,1,0:T(8,128)S(1)} %summed.7.refs_2_), channel_id=1, source_target_pairs={{0,2},{1,5},{2,0},{3,7},{4,6},{5,1},{6,4},{7,3},{8,10},{9,13},{10,... | collective-permute-start | bytes 405512 | tf_op jit(solution)/shard_map/ppermute | solution.py:247
  11.4 0.6 %collective-permute-done.5.refs_3_.refs_5_ = f32[32,8,128]{2,1,0:T(8,128)S(1)} collective-permute-done((f32[32,8,128]{2,1,0:T(8,128)S(1)}, f32[32,8,128]{2,1,0:T(8,128)S(1)}, u32[]{:S(2)}, u32[]{:S(2)}) %collective-permute-start.5) | collective-permute-done | bytes 131104 | tf_op jit(solution)/shard_map/ppermute | solution.py:247
  12.0 1.1 %collective-permute-start.6 = (f32[64,8,128]{2,1,0:T(8,128)S(1)}, f32[64,8,128]{2,1,0:T(8,128)S(1)}, u32[]{:S(2)}, u32[]{:S(2)}) collective-permute-start(f32[64,8,128]{2,1,0:T(8,128)S(1)} %summed.9), channel_id=1, source_target_pairs={{0,4},{1,3},{2,6},{3,1},{4,0},{5,7},{6,2},{7,5},{8,12},{9,11},{10,... | collective-permute-start | bytes 786440 | tf_op jit(solution)/shard_map/ppermute | solution.py:247
  13.1 0.0 collective-permute-done.1.refs_3_.refs_1_
  13.1 2.4 %collective-permute-done.4.refs_6_.refs_5_ = f32[33,8,128]{2,1,0:T(8,128)S(1)} collective-permute-done((f32[33,8,128]{2,1,0:T(8,128)S(1)}, f32[33,8,128]{2,1,0:T(8,128)S(1)}, u32[]{:S(2)}, u32[]{:S(2)}) %collective-permute-start.4) | collective-permute-done | bytes 135200 | tf_op jit(solution)/shard_map/ppermute | solution.py:247
  15.5 0.1 summed.10.refs_3_
  15.6 3.5 %collective-permute-start.7 = (f32[33,8,128]{2,1,0:T(8,128)S(1)}, f32[33,8,128]{2,1,0:T(8,128)S(1)}, u32[]{:S(2)}, u32[]{:S(2)}) collective-permute-start(f32[33,8,128]{2,1,0:T(8,128)S(1)} %summed.10.refs_3_), channel_id=1, source_target_pairs={{0,8},{1,9},{2,10},{3,11},{4,12},{5,13},{6,14},{7,15},{8,0},{9,1},... | collective-permute-start | bytes 405512 | tf_op jit(solution)/shard_map/ppermute | solution.py:247
  19.0 0.9 %collective-permute-done.6.refs_2_.refs_6_ = f32[64,8,128]{2,1,0:T(8,128)S(1)} collective-permute-done((f32[64,8,128]{2,1,0:T(8,128)S(1)}, f32[64,8,128]{2,1,0:T(8,128)S(1)}, u32[]{:S(2)}, u32[]{:S(2)}) %collective-permute-start.6) | collective-permute-done | bytes 262176 | tf_op jit(solution)/shard_map/ppermute | solution.py:247
  19.9 1.5 %collective-permute-start.8 = (f32[32,8,128]{2,1,0:T(8,128)S(1)}, f32[32,8,128]{2,1,0:T(8,128)S(1)}, u32[]{:S(2)}, u32[]{:S(2)}) collective-permute-start(f32[32,8,128]{2,1,0:T(8,128)S(1)} %summed.11), channel_id=1, source_target_pairs={{0,2},{1,5},{2,0},{3,7},{4,6},{5,1},{6,4},{7,3},{8,10},{9,13},{10,... | collective-permute-start | bytes 393224 | tf_op jit(solution)/shard_map/ppermute | solution.py:247
  21.4 1.4 %collective-permute-done.7.refs_7_ = f32[33,8,128]{2,1,0:T(8,128)S(1)} collective-permute-done((f32[33,8,128]{2,1,0:T(8,128)S(1)}, f32[33,8,128]{2,1,0:T(8,128)S(1)}, u32[]{:S(2)}, u32[]{:S(2)}) %collective-permute-start.7) | collective-permute-done | bytes 135200 | tf_op jit(solution)/shard_map/ppermute | solution.py:247
  22.8 2.2 %collective-permute-done.8.refs_8_ = f32[32,8,128]{2,1,0:T(8,128)S(1)} collective-permute-done((f32[32,8,128]{2,1,0:T(8,128)S(1)}, f32[32,8,128]{2,1,0:T(8,128)S(1)}, u32[]{:S(2)}, u32[]{:S(2)}) %collective-permute-start.8) | collective-permute-done | bytes 131104 | tf_op jit(solution)/shard_map/ppermute | solution.py:247
  24.9 0.8 %finish.1 = f32[32,2,512]{2,1,0:T(2,128)} custom-call(f32[33,8,128]{2,1,0:T(8,128)S(1)} %get-tuple-element.11.refs_0_, f32[33,8,128]{2,1,0:T(8,128)S(1)} %collective-permute-done.refs_2_.refs_1_, f32[96,8,128]{2,1,0:T(8,128)S(1)} %next_products.4.refs_2_.refs_0_, f32[96,8,128]{2,1,0:T(8,128)S(1)} %collective-permute-done.1.refs_3_.refs_1_, ...), custom_call_target="tpu_custom_call" | custom-call | tf_op jit(solution)/shard_map/finish/pallas_call | solution.py:206
  (5 shorter events, 0.1 us)
Async XLA Ops:
  1.8 1.5 %collective-permute-start = (f32[33,8,128]{2,1,0:T(8,128)S(1)}, f32[33,8,128]{2,1,0:T(8,128)S(1)}, u32[]{:S(2)}, u32[]{:S(2)}) collective-permute-start(f32[33,8,128]{2,1,0:T(8,128)S(1)} %get-tuple-element.11.refs_0_), channel_id=1, source_target_pairs={{0,1},{1,0},{2,3},{3,2},{4,5},{5,4},{6,7},{7,6},{8,9},{9,8},{10,11... | collective-permute-start | bytes 405512 | tf_op jit(solution)/shard_map/ppermute | solution.py:247
  2.9 3.9 %collective-permute-start.3 = (f32[128,8,128]{2,1,0:T(8,128)S(1)}, f32[128,8,128]{2,1,0:T(8,128)S(1)}, u32[]{:S(2)}, u32[]{:S(2)}) collective-permute-start(f32[128,8,128]{2,1,0:T(8,128)S(1)} %get-tuple-element.16), channel_id=1, source_target_pairs={{0,1},{1,0},{2,3},{3,2},{4,5},{5,4},{6,7},{7,6},{8,9},{9,8},{10,11... | collective-permute-start | bytes 1572872 | tf_op jit(solution)/shard_map/ppermute | solution.py:247
  3.4 6.0 %collective-permute-start.2 = (f32[33,8,128]{2,1,0:T(8,128)S(1)}, f32[33,8,128]{2,1,0:T(8,128)S(1)}, u32[]{:S(2)}, u32[]{:S(2)}) collective-permute-start(f32[33,8,128]{2,1,0:T(8,128)S(1)} %summed.6), channel_id=1, source_target_pairs={{0,4},{1,3},{2,6},{3,1},{4,0},{5,7},{6,2},{7,5},{8,12},{9,11},{10,... | collective-permute-start | bytes 405512 | tf_op jit(solution)/shard_map/ppermute | solution.py:247
  6.8 5.1 %collective-permute-start.5 = (f32[32,8,128]{2,1,0:T(8,128)S(1)}, f32[32,8,128]{2,1,0:T(8,128)S(1)}, u32[]{:S(2)}, u32[]{:S(2)}) collective-permute-start(f32[32,8,128]{2,1,0:T(8,128)S(1)} %summed.8), channel_id=1, source_target_pairs={{0,4},{1,3},{2,6},{3,1},{4,0},{5,7},{6,2},{7,5},{8,12},{9,11},{10,... | collective-permute-start | bytes 393224 | tf_op jit(solution)/shard_map/ppermute | solution.py:247
  8.1 5.0 %collective-permute-start.1 = (f32[96,8,128]{2,1,0:T(8,128)S(1)}, f32[96,8,128]{2,1,0:T(8,128)S(1)}, u32[]{:S(2)}, u32[]{:S(2)}) collective-permute-start(f32[96,8,128]{2,1,0:T(8,128)S(1)} %next_products.5), channel_id=1, source_target_pairs={{0,1},{1,0},{2,3},{3,2},{4,5},{5,4},{6,7},{7,6},{8,9},{9,8},{10,11... | collective-permute-start | bytes 1179656 | tf_op jit(solution)/shard_map/ppermute | solution.py:247
  9.4 6.1 %collective-permute-start.4 = (f32[33,8,128]{2,1,0:T(8,128)S(1)}, f32[33,8,128]{2,1,0:T(8,128)S(1)}, u32[]{:S(2)}, u32[]{:S(2)}) collective-permute-start(f32[33,8,128]{2,1,0:T(8,128)S(1)} %summed.7.refs_2_), channel_id=1, source_target_pairs={{0,2},{1,5},{2,0},{3,7},{4,6},{5,1},{6,4},{7,3},{8,10},{9,13},{10,... | collective-permute-start | bytes 405512 | tf_op jit(solution)/shard_map/ppermute | solution.py:247
  12.0 7.9 %collective-permute-start.6 = (f32[64,8,128]{2,1,0:T(8,128)S(1)}, f32[64,8,128]{2,1,0:T(8,128)S(1)}, u32[]{:S(2)}, u32[]{:S(2)}) collective-permute-start(f32[64,8,128]{2,1,0:T(8,128)S(1)} %summed.9), channel_id=1, source_target_pairs={{0,4},{1,3},{2,6},{3,1},{4,0},{5,7},{6,2},{7,5},{8,12},{9,11},{10,... | collective-permute-start | bytes 786440 | tf_op jit(solution)/shard_map/ppermute | solution.py:247
  15.6 7.2 %collective-permute-start.7 = (f32[33,8,128]{2,1,0:T(8,128)S(1)}, f32[33,8,128]{2,1,0:T(8,128)S(1)}, u32[]{:S(2)}, u32[]{:S(2)}) collective-permute-start(f32[33,8,128]{2,1,0:T(8,128)S(1)} %summed.10.refs_3_), channel_id=1, source_target_pairs={{0,8},{1,9},{2,10},{3,11},{4,12},{5,13},{6,14},{7,15},{8,0},{9,1},... | collective-permute-start | bytes 405512 | tf_op jit(solution)/shard_map/ppermute | solution.py:247
  19.9 5.0 %collective-permute-start.8 = (f32[32,8,128]{2,1,0:T(8,128)S(1)}, f32[32,8,128]{2,1,0:T(8,128)S(1)}, u32[]{:S(2)}, u32[]{:S(2)}) collective-permute-start(f32[32,8,128]{2,1,0:T(8,128)S(1)} %summed.11), channel_id=1, source_target_pairs={{0,2},{1,5},{2,0},{3,7},{4,6},{5,1},{6,4},{7,3},{8,10},{9,13},{10,... | collective-permute-start | bytes 393224 | tf_op jit(solution)/shard_map/ppermute | solution.py:247

commit v20 on v18

--- a/solution.py
+++ b/solution.py
@@ -9,6 +9,7 @@
 
 epsilon = 1e-06
 MIB = 1 << 20
+LOADS = 4
 
 
 COSTS = (8192, 64 * MIB, 65536 * MIB, 8192 * MIB) + (
@@ -35,28 +36,40 @@
     return place
 
 
+def left_side(rows):
+    antennas = rows.shape[1] // 2
+    turned = jnp.concatenate([-rows[:, antennas:], rows[:, :antennas]], axis=1)
+    return jnp.concatenate([rows, turned], axis=0)
+
+
+def put_products(value, served, users, base, out):
+    blocks, steps = value.shape[1] // 128, users // 8
+    group = value.shape[0] // users // 2
+    value = jnp.where(served, value, 0.0)
+    for half in range(2):
+        for slot in range(group):
+            top = (half * group + slot) * users
+            for block in range(blocks):
+                piece = value[top:top + users, block * 128:(block + 1) * 128]
+                start = (((base + slot) * 2 + half) * blocks + block) * steps
+                out[start:start + steps] = piece.reshape(steps, 8, 128)
+
+
 def write_products(users, rows, weights, served, out):
-    slots, antennas = rows.shape[0] // users, rows.shape[1] // 2
-    blocks, steps = weights.shape[1] // 128, users // 8
+    slots = rows.shape[0] // users
     group = max(size for size in range(1, 9) if slots % size == 0)
     for base in range(0, slots, group):
-        plain = rows[base * users:(base + group) * users, :]
-        turned = jnp.concatenate([-plain[:, antennas:], plain[:, :antennas]], axis=1)
-        both = jnp.concatenate([plain, turned], axis=0)
+        both = left_side(rows[base * users:(base + group) * users, :])
         value = jnp.dot(both, weights, preferred_element_type=jnp.float32)
-        value = jnp.where(served, value, 0.0)
-        for half in range(2):
-            for slot in range(group):
-                top = (half * group + slot) * users
-                for block in range(blocks):
-                    piece = value[top:top + users, block * 128:(block + 1) * 128]
-                    start = (((base + slot) * 2 + half) * blocks + block) * steps
-                    out[start:start + steps] = piece.reshape(steps, 8, 128)
-
-
-def power_tile(weights, served):
+        put_products(value, served, users, base, out)
+
+
+def square_sum(weights):
     wide = weights.astype(jnp.float32)
-    power = jnp.sum(wide * wide, axis=0, keepdims=True)
+    return jnp.sum(wide * wide, axis=0, keepdims=True)
+
+
+def power_tile(power, served):
     power = jnp.where(served, power, 0.0)
     blocks = power.shape[1] // 128
     pieces = [power[:, block * 128:(block + 1) * 128] for block in range(blocks)]
@@ -74,8 +87,11 @@
         pltpu.make_async_copy(visible, seen, sems.at[0]),
         pltpu.make_async_copy(channel, raw, sems.at[1]),
         pltpu.make_async_copy(cluster, names, sems.at[2]),
-        pltpu.make_async_copy(precoder, weights, sems.at[3]),
     ]
+    depth = weights.shape[0] // LOADS
+    for part in range(LOADS):
+        at = pl.ds(part * depth, depth)
+        loads.append(pltpu.make_async_copy(precoder.at[at], weights.at[at], sems.at[3 + part]))
     for load in loads:
         load.start()
     rows[...] = jnp.zeros_like(rows)
@@ -92,11 +108,19 @@
     loads[2].wait()
     here = jnp.max((names[...] == me).astype(jnp.float32), axis=0, keepdims=True)
     served[...] = here
-    loads[3].wait()
-    mask = here > 0.0
     size = (out.shape[0] // (weights.shape[1] // 128) // 2) * 8
-    write_products(users, rows.at[0, 0:size], weights[...], mask, out)
-    out[out.shape[0] - 1] = power_tile(weights[...], mask)
+    both = left_side(rows[0, 0:size, :])
+    value = power = None
+    for part in range(LOADS):
+        loads[3 + part].wait()
+        at = slice(part * depth, (part + 1) * depth)
+        block = weights[at, :]
+        term = jnp.dot(both[:, at], block, preferred_element_type=jnp.float32)
+        square = square_sum(block)
+        value = term if value is None else value + term
+        power = square if power is None else power + square
+    put_products(value, here > 0.0, users, 0, out)
+    out[out.shape[0] - 1] = power_tile(power, here > 0.0)
 
 
 def next_kernel(users, jobs, rows, weights, served, *outs):
@@ -135,7 +159,7 @@
             pltpu.SMEM(visible.shape, jnp.int32),
             pltpu.VMEM(cluster.shape, jnp.int32),
             pltpu.VMEM(channel.shape, jnp.bfloat16),
-            pltpu.SemaphoreType.DMA((4,)),
+            pltpu.SemaphoreType.DMA((3 + LOADS,)),
         ],
         compiler_params=pltpu.CompilerParams(vmem_limit_bytes=52 * MIB if slots > 8 else 24 * MIB),
         cost_estimate=estimate(),

time: 25 us -> 24.9 us (level)
  no operation moved by 1% of the time
where the time goes in v20:
time: 24.9 us; the launch traced here: 24.7 us
  starting transfers between devices  13.6 us (55%)
  waiting for transfers between devices  6.72 us (27%)
  Pallas kernels  4.35 us (17%)
    ppermute x9, starting transfers between devices, swap(): lax.ppermute(value, 'ap', [(i, i ^ 1 << bit_of[i & 1]) for i in range(dev...  13.6 us
    ppermute x9, waiting for transfers between devices, swap(): lax.ppermute(value, 'ap', [(i, i ^ 1 << bit_of[i & 1]) for i in range(dev...  6.72 us
    pallas_call x4, Pallas kernels, next_products(): pl.pallas_call(functools.partial(next_kernel, users, jobs), out_shape=[me...  1.74 us
    pallas_call x1, Pallas kernels, first_products(): pl.pallas_call(functools.partial(first_kernel, bits), out_shape=(message(...  1.69 us
    pallas_call x1, Pallas kernels, finish(): pl.pallas_call(functools.partial(final_kernel, terms, powers), out_shape=...  0.76 us
  transfers between devices with their start and end apart: 9, of which 5 were waited for; matrix products, arithmetic and copies ran while one was open for 0% of the time, Pallas kernels for 8%

profile of v20, /device:TPU:0, one launch (start us, length us, event | category | flops | bytes accessed | tf_op | source)
XLA Modules:
  0.0 24.7 jit_solution(17728306397921916888)
XLA Ops:
  0.0 1.7 %first_products.1 = (f32[33,8,128]{2,1,0:T(8,128)S(1)}, bf16[2,256,1024]{2,1,0:T(8,128)(2,1)S(1)}, bf16[1024,512]{1,0:T(8,128)(2,1)S(1)}, f32[1,512]{1,0:T(1,128)S(1)}) custom-call(s32[1,12]{1,0:T(1,128)} %visible.1, s32[4,512]{1,0:T(4,128)} %bitcast.3, bf16[1,12,2,32,512]{4,3,2,1,0:T(8,128)(2,1)} %channel.1, bf16[1024,512]{1,0:T(8,128)(2,1)} %bitcast.2), custom_call_target="tpu_custom_call" | custom-call | flops 8192 | bytes 8192 | tf_op jit(solution)/shard_map/first_products/pallas_call | solution.py:148
  1.7 0.5 %collective-permute-start = (f32[33,8,128]{2,1,0:T(8,128)S(1)}, f32[33,8,128]{2,1,0:T(8,128)S(1)}, u32[]{:S(2)}, u32[]{:S(2)}) collective-permute-start(f32[33,8,128]{2,1,0:T(8,128)S(1)} %get-tuple-element.11.refs_0_), channel_id=1, source_target_pairs={{0,1},{1,0},{2,3},{3,2},{4,5},{5,4},{6,7},{7,6},{8,9},{9,8},{10,11... | collective-permute-start | bytes 405512 | tf_op jit(solution)/shard_map/ppermute | solution.py:271
  2.2 0.6 %next_products.6 = (f32[128,8,128]{2,1,0:T(8,128)S(1)}, f32[32,8,128]{2,1,0:T(8,128)S(1)}) custom-call(bf16[2,256,1024]{2,1,0:T(8,128)(2,1)S(1)} %get-tuple-element.12.rows, bf16[1024,512]{1,0:T(8,128)(2,1)S(1)} %get-tuple-element.13.weights, f32[1,512]{1,0:T(1,128)S(1)} %get-tuple-element.14.served), custom_call_target="tpu_custom_call" | custom-call | flops 8192 | bytes 8192 | tf_op jit(solution)/shard_map/next_products/pallas_call | solution.py:174
  2.8 0.1 collective-permute-start.3
  2.9 0.3 %collective-permute-done.refs_2_.refs_1_ = f32[33,8,128]{2,1,0:T(8,128)S(1)} collective-permute-done((f32[33,8,128]{2,1,0:T(8,128)S(1)}, f32[33,8,128]{2,1,0:T(8,128)S(1)}, u32[]{:S(2)}, u32[]{:S(2)}) %collective-permute-start) | collective-permute-done | bytes 135200 | tf_op jit(solution)/shard_map/ppermute | solution.py:271
  3.2 3.0 %collective-permute-start.2 = (f32[33,8,128]{2,1,0:T(8,128)S(1)}, f32[33,8,128]{2,1,0:T(8,128)S(1)}, u32[]{:S(2)}, u32[]{:S(2)}) collective-permute-start(f32[33,8,128]{2,1,0:T(8,128)S(1)} %summed.6), channel_id=1, source_target_pairs={{0,4},{1,3},{2,6},{3,1},{4,0},{5,7},{6,2},{7,5},{8,12},{9,11},{10,... | collective-permute-start | bytes 405512 | tf_op jit(solution)/shard_map/ppermute | solution.py:271
  6.2 0.4 %next_products.5 = f32[96,8,128]{2,1,0:T(8,128)S(1)} custom-call(bf16[2,256,1024]{2,1,0:T(8,128)(2,1)S(1)} %get-tuple-element.12.rows, bf16[1024,512]{1,0:T(8,128)(2,1)S(1)} %get-tuple-element.13.weights, f32[1,512]{1,0:T(1,128)S(1)} %get-tuple-element.14.served), custom_call_target="tpu_custom_call" | custom-call | flops 68719476736 | bytes 68719476736 | tf_op jit(solution)/shard_map/next_products/pallas_call | solution.py:174
  6.6 0.1 collective-permute-start.1
  6.7 0.4 %next_products.7.refs_2_.refs_0_ = f32[128,8,128]{2,1,0:T(8,128)S(1)} custom-call(bf16[2,256,1024]{2,1,0:T(8,128)(2,1)S(1)} %get-tuple-element.12.rows, bf16[1024,512]{1,0:T(8,128)(2,1)S(1)} %get-tuple-element.13.weights, f32[1,512]{1,0:T(1,128)S(1)} %get-tuple-element.14.served), custom_call_target="tpu_custom_call" | custom-call | flops 67108864 | bytes 67108864 | tf_op jit(solution)/shard_map/next_products/pallas_call | solution.py:174
  7.1 0.0 collective-permute-done.3.refs_3_.refs_1_
  7.2 1.4 %collective-permute-start.6 = (f32[32,8,128]{2,1,0:T(8,128)S(1)}, f32[32,8,128]{2,1,0:T(8,128)S(1)}, u32[]{:S(2)}, u32[]{:S(2)}) collective-permute-start(f32[32,8,128]{2,1,0:T(8,128)S(1)} %summed.9), channel_id=1, source_target_pairs={{0,4},{1,3},{2,6},{3,1},{4,0},{5,7},{6,2},{7,5},{8,12},{9,11},{10,... | collective-permute-start | bytes 393224 | tf_op jit(solution)/shard_map/ppermute | solution.py:271
  8.6 0.7 %collective-permute-done.2.refs_4_ = f32[33,8,128]{2,1,0:T(8,128)S(1)} collective-permute-done((f32[33,8,128]{2,1,0:T(8,128)S(1)}, f32[33,8,128]{2,1,0:T(8,128)S(1)}, u32[]{:S(2)}, u32[]{:S(2)}) %collective-permute-start.2) | collective-permute-done | bytes 135200 | tf_op jit(solution)/shard_map/ppermute | solution.py:271
  9.2 2.0 %collective-permute-start.4 = (f32[33,8,128]{2,1,0:T(8,128)S(1)}, f32[33,8,128]{2,1,0:T(8,128)S(1)}, u32[]{:S(2)}, u32[]{:S(2)}) collective-permute-start(f32[33,8,128]{2,1,0:T(8,128)S(1)} %summed.7.refs_2_), channel_id=1, source_target_pairs={{0,2},{1,5},{2,0},{3,7},{4,6},{5,1},{6,4},{7,3},{8,10},{9,13},{10,... | collective-permute-start | bytes 405512 | tf_op jit(solution)/shard_map/ppermute | solution.py:271
  11.3 1.6 %collective-permute-start.5 = (f32[64,8,128]{2,1,0:T(8,128)S(1)}, f32[64,8,128]{2,1,0:T(8,128)S(1)}, u32[]{:S(2)}, u32[]{:S(2)}) collective-permute-start(f32[64,8,128]{2,1,0:T(8,128)S(1)} %summed.8), channel_id=1, source_target_pairs={{0,4},{1,3},{2,6},{3,1},{4,0},{5,7},{6,2},{7,5},{8,12},{9,11},{10,... | collective-permute-start | bytes 786440 | tf_op jit(solution)/shard_map/ppermute | solution.py:271
  12.9 0.4 %next_products.4.refs_2_.refs_0_ = f32[96,8,128]{2,1,0:T(8,128)S(1)} custom-call(bf16[2,256,1024]{2,1,0:T(8,128)(2,1)S(1)} %get-tuple-element.12.rows, bf16[1024,512]{1,0:T(8,128)(2,1)S(1)} %get-tuple-element.13.weights, f32[1,512]{1,0:T(1,128)S(1)} %get-tuple-element.14.served), custom_call_target="tpu_custom_call" | custom-call | flops 8589934592 | bytes 8589934592 | tf_op jit(solution)/shard_map/next_products/pallas_call | solution.py:174
  13.3 0.0 collective-permute-done.1.refs_3_.refs_1_
  13.3 0.0 collective-permute-done.6.refs_5_
  13.3 2.3 %collective-permute-done.4.refs_6_.refs_5_ = f32[33,8,128]{2,1,0:T(8,128)S(1)} collective-permute-done((f32[33,8,128]{2,1,0:T(8,128)S(1)}, f32[33,8,128]{2,1,0:T(8,128)S(1)}, u32[]{:S(2)}, u32[]{:S(2)}) %collective-permute-start.4) | collective-permute-done | bytes 135200 | tf_op jit(solution)/shard_map/ppermute | solution.py:271
  15.7 3.3 %collective-permute-start.7 = (f32[33,8,128]{2,1,0:T(8,128)S(1)}, f32[33,8,128]{2,1,0:T(8,128)S(1)}, u32[]{:S(2)}, u32[]{:S(2)}) collective-permute-start(f32[33,8,128]{2,1,0:T(8,128)S(1)} %summed.10.refs_3_), channel_id=1, source_target_pairs={{0,8},{1,9},{2,10},{3,11},{4,12},{5,13},{6,14},{7,15},{8,0},{9,1},... | collective-permute-start | bytes 405512 | tf_op jit(solution)/shard_map/ppermute | solution.py:271
  18.9 0.0 collective-permute-done.5.refs_2_.refs_6_
  18.9 1.6 %collective-permute-start.8 = (f32[32,8,128]{2,1,0:T(8,128)S(1)}, f32[32,8,128]{2,1,0:T(8,128)S(1)}, u32[]{:S(2)}, u32[]{:S(2)}) collective-permute-start(f32[32,8,128]{2,1,0:T(8,128)S(1)} %summed.11), channel_id=1, source_target_pairs={{0,2},{1,5},{2,0},{3,7},{4,6},{5,1},{6,4},{7,3},{8,10},{9,13},{10,... | collective-permute-start | bytes 393224 | tf_op jit(solution)/shard_map/ppermute | solution.py:271
  20.5 2.5 %collective-permute-done.7.refs_7_ = f32[33,8,128]{2,1,0:T(8,128)S(1)} collective-permute-done((f32[33,8,128]{2,1,0:T(8,128)S(1)}, f32[33,8,128]{2,1,0:T(8,128)S(1)}, u32[]{:S(2)}, u32[]{:S(2)}) %collective-permute-start.7) | collective-permute-done | bytes 135200 | tf_op jit(solution)/shard_map/ppermute | solution.py:271
  23.0 1.0 %collective-permute-done.8.refs_8_ = f32[32,8,128]{2,1,0:T(8,128)S(1)} collective-permute-done((f32[32,8,128]{2,1,0:T(8,128)S(1)}, f32[32,8,128]{2,1,0:T(8,128)S(1)}, u32[]{:S(2)}, u32[]{:S(2)}) %collective-permute-start.8) | collective-permute-done | bytes 131104 | tf_op jit(solution)/shard_map/ppermute | solution.py:271
  24.0 0.8 %finish.1 = f32[32,2,512]{2,1,0:T(2,128)} custom-call(f32[33,8,128]{2,1,0:T(8,128)S(1)} %get-tuple-element.11.refs_0_, f32[33,8,128]{2,1,0:T(8,128)S(1)} %collective-permute-done.refs_2_.refs_1_, f32[96,8,128]{2,1,0:T(8,128)S(1)} %next_products.4.refs_2_.refs_0_, f32[96,8,128]{2,1,0:T(8,128)S(1)} %collective-permute-done.1.refs_3_.refs_1_, ...), custom_call_target="tpu_custom_call" | custom-call | tf_op jit(solution)/shard_map/finish/pallas_call | solution.py:230
  (6 shorter events, 0.2 us)
Async XLA Ops:
  1.7 1.5 %collective-permute-start = (f32[33,8,128]{2,1,0:T(8,128)S(1)}, f32[33,8,128]{2,1,0:T(8,128)S(1)}, u32[]{:S(2)}, u32[]{:S(2)}) collective-permute-start(f32[33,8,128]{2,1,0:T(8,128)S(1)} %get-tuple-element.11.refs_0_), channel_id=1, source_target_pairs={{0,1},{1,0},{2,3},{3,2},{4,5},{5,4},{6,7},{7,6},{8,9},{9,8},{10,11... | collective-permute-start | bytes 405512 | tf_op jit(solution)/shard_map/ppermute | solution.py:271
  2.8 4.3 %collective-permute-start.3 = (f32[128,8,128]{2,1,0:T(8,128)S(1)}, f32[128,8,128]{2,1,0:T(8,128)S(1)}, u32[]{:S(2)}, u32[]{:S(2)}) collective-permute-start(f32[128,8,128]{2,1,0:T(8,128)S(1)} %get-tuple-element.16), channel_id=1, source_target_pairs={{0,1},{1,0},{2,3},{3,2},{4,5},{5,4},{6,7},{7,6},{8,9},{9,8},{10,11... | collective-permute-start | bytes 1572872 | tf_op jit(solution)/shard_map/ppermute | solution.py:271
  3.2 6.0 %collective-permute-start.2 = (f32[33,8,128]{2,1,0:T(8,128)S(1)}, f32[33,8,128]{2,1,0:T(8,128)S(1)}, u32[]{:S(2)}, u32[]{:S(2)}) collective-permute-start(f32[33,8,128]{2,1,0:T(8,128)S(1)} %summed.6), channel_id=1, source_target_pairs={{0,4},{1,3},{2,6},{3,1},{4,0},{5,7},{6,2},{7,5},{8,12},{9,11},{10,... | collective-permute-start | bytes 405512 | tf_op jit(solution)/shard_map/ppermute | solution.py:271
  6.6 6.7 %collective-permute-start.1 = (f32[96,8,128]{2,1,0:T(8,128)S(1)}, f32[96,8,128]{2,1,0:T(8,128)S(1)}, u32[]{:S(2)}, u32[]{:S(2)}) collective-permute-start(f32[96,8,128]{2,1,0:T(8,128)S(1)} %next_products.5), channel_id=1, source_target_pairs={{0,1},{1,0},{2,3},{3,2},{4,5},{5,4},{6,7},{7,6},{8,9},{9,8},{10,11... | collective-permute-start | bytes 1179656 | tf_op jit(solution)/shard_map/ppermute | solution.py:271
  7.2 6.1 %collective-permute-start.6 = (f32[32,8,128]{2,1,0:T(8,128)S(1)}, f32[32,8,128]{2,1,0:T(8,128)S(1)}, u32[]{:S(2)}, u32[]{:S(2)}) collective-permute-start(f32[32,8,128]{2,1,0:T(8,128)S(1)} %summed.9), channel_id=1, source_target_pairs={{0,4},{1,3},{2,6},{3,1},{4,0},{5,7},{6,2},{7,5},{8,12},{9,11},{10,... | collective-permute-start | bytes 393224 | tf_op jit(solution)/shard_map/ppermute | solution.py:271
  9.2 6.4 %collective-permute-start.4 = (f32[33,8,128]{2,1,0:T(8,128)S(1)}, f32[33,8,128]{2,1,0:T(8,128)S(1)}, u32[]{:S(2)}, u32[]{:S(2)}) collective-permute-start(f32[33,8,128]{2,1,0:T(8,128)S(1)} %summed.7.refs_2_), channel_id=1, source_target_pairs={{0,2},{1,5},{2,0},{3,7},{4,6},{5,1},{6,4},{7,3},{8,10},{9,13},{10,... | collective-permute-start | bytes 405512 | tf_op jit(solution)/shard_map/ppermute | solution.py:271
  11.3 7.6 %collective-permute-start.5 = (f32[64,8,128]{2,1,0:T(8,128)S(1)}, f32[64,8,128]{2,1,0:T(8,128)S(1)}, u32[]{:S(2)}, u32[]{:S(2)}) collective-permute-start(f32[64,8,128]{2,1,0:T(8,128)S(1)} %summed.8), channel_id=1, source_target_pairs={{0,4},{1,3},{2,6},{3,1},{4,0},{5,7},{6,2},{7,5},{8,12},{9,11},{10,... | collective-permute-start | bytes 786440 | tf_op jit(solution)/shard_map/ppermute | solution.py:271
  15.7 7.3 %collective-permute-start.7 = (f32[33,8,128]{2,1,0:T(8,128)S(1)}, f32[33,8,128]{2,1,0:T(8,128)S(1)}, u32[]{:S(2)}, u32[]{:S(2)}) collective-permute-start(f32[33,8,128]{2,1,0:T(8,128)S(1)} %summed.10.refs_3_), channel_id=1, source_target_pairs={{0,8},{1,9},{2,10},{3,11},{4,12},{5,13},{6,14},{7,15},{8,0},{9,1},... | collective-permute-start | bytes 405512 | tf_op jit(solution)/shard_map/ppermute | solution.py:271
  18.9 5.0 %collective-permute-start.8 = (f32[32,8,128]{2,1,0:T(8,128)S(1)}, f32[32,8,128]{2,1,0:T(8,128)S(1)}, u32[]{:S(2)}, u32[]{:S(2)}) collective-permute-start(f32[32,8,128]{2,1,0:T(8,128)S(1)} %summed.11), channel_id=1, source_target_pairs={{0,2},{1,5},{2,0},{3,7},{4,6},{5,1},{6,4},{7,3},{8,10},{9,13},{10,... | collective-permute-start | bytes 393224 | tf_op jit(solution)/shard_map/ppermute | solution.py:271

commit v21 on v20

--- a/solution.py
+++ b/solution.py
@@ -12,8 +12,8 @@
 LOADS = 4
 
 
-COSTS = (8192, 64 * MIB, 65536 * MIB, 8192 * MIB) + (
-    64 * MIB, 1024 * MIB, 1024 * MIB, 65536 * MIB, 1024 * MIB, 8192 * MIB
+COSTS = (64 * MIB, 8192 * MIB, 64 * MIB, 65536 * MIB) + (
+    1024 * MIB, 64 * MIB, 64 * MIB, 64 * MIB, 8192 * MIB, 1024 * MIB
 )
 
 
@@ -123,8 +123,8 @@
     out[out.shape[0] - 1] = power_tile(power, here > 0.0)
 
 
-def next_kernel(users, jobs, rows, weights, served, *outs):
-    for (keep, first, slots), out in zip(jobs, outs):
+def next_kernel(users, jobs, rows, weights, served, *refs):
+    for (keep, first, slots), out in zip(jobs, refs[-len(jobs):]):
         mine = rows.at[keep, first * users:(first + slots) * users]
         write_products(users, mine, weights[...], served[...] > 0.0, out)
 
@@ -167,19 +167,19 @@
     )(*[pltpu.with_memory_space_constraint(operand, pltpu.HBM) for operand in operands])
 
 
-def next_products(users, jobs, cost, rows, weights, served):
+def next_products(users, jobs, cost, rows, weights, served, after=()):
     vmem = pl.BlockSpec(memory_space=pltpu.VMEM)
     big = max(slots for _, _, slots in jobs) > 8
     tiles = (users // 8) * (weights.shape[1] // 128) * 2
     return pl.pallas_call(
         functools.partial(next_kernel, users, jobs),
         out_shape=[message(slots * tiles) for _, _, slots in jobs],
-        in_specs=[vmem] * 3,
+        in_specs=[vmem] * (3 + len(after)),
         out_specs=[vmem] * len(jobs),
         compiler_params=pltpu.CompilerParams(vmem_limit_bytes=48 * MIB if big else 16 * MIB),
         cost_estimate=estimate(cost),
         name="next_products",
-    )(rows, weights, served)
+    )(rows, weights, served, *after)
 
 
 def add_up(refs, terms, count):
@@ -300,16 +300,19 @@
     come = swap(send, (0, 0))
     add(products(((1, first, count),), cost=COSTS[1])[0], range(first, first + count), False)
     add(come, range(first, first + count), False)
-    first, count = 5 * quarter, 3 * quarter
-    come = swap(products(((0, first, count),), cost=COSTS[2])[0], (0, 0))
-    add(products(((1, first, count),), cost=COSTS[3])[0], range(first, first + count), False)
-    add(come, range(first, first + count), False)
     with_power = set()
     last = 2 * half - 1
     for number, (step, slots) in enumerate(message_order(bits - 1)):
+        if number == 3:
+            first, count = 5 * quarter, 3 * quarter
+            send = products(((0, first, count),), cost=COSTS[2], after=[now])[0]
+            come = swap(send, (0, 0))
+            mine = products(((1, first, count),), cost=COSTS[3], after=[send])[0]
+            add(mine, range(first, first + count), False)
+            add(come, range(first, first + count), False)
         power = step not in with_power
         with_power.add(step)
-        after = [now] if number in (3, 5) else []
+        after = [mine] if number == 3 else [now] if number in (2, 5) else []
         now = total(slots, power, COSTS[4 + number] if number < 6 else 8192, after)
         came = swap(now, (orders[0][step], orders[1][step]))
         slots = [slot + (1 << (bits - 2 - step)) for slot in slots]

time: 24.9 us -> 26.8 us (1.076)
  waiting for transfers between devices: 6.72 us -> 11 us
  starting transfers between devices: 13.6 us -> 11.2 us
    ppermute x9, waiting for transfers between devices: 6.72 us -> 11 us  [swap(): lax.ppermute(value, 'ap', [(i, i ^ 1 << bit_of[i & 1]) for i in range(dev...]
    ppermute x9, starting transfers between devices: 13.6 us -> 11.2 us  [swap(): lax.ppermute(value, 'ap', [(i, i ^ 1 << bit_of[i & 1]) for i in range(dev...]
  transfers between devices with their start and end apart: 9 -> 9, of which waited for: 5 -> 5; matrix products, arithmetic and copies ran while one was open for 0% -> 0% of each run, Pallas kernels for 8% -> 7%
where the time goes in v21:
time: 26.8 us; the launch traced here: 26.6 us
  starting transfers between devices  11.2 us (42%)
  waiting for transfers between devices  11 us (41%)
  Pallas kernels  4.36 us (16%)
    ppermute x9, starting transfers between devices, swap(): lax.ppermute(value, 'ap', [(i, i ^ 1 << bit_of[i & 1]) for i in range(dev...  11.2 us
    ppermute x9, waiting for transfers between devices, swap(): lax.ppermute(value, 'ap', [(i, i ^ 1 << bit_of[i & 1]) for i in range(dev...  11 us
    pallas_call x4, Pallas kernels, next_products(): pl.pallas_call(functools.partial(next_kernel, users, jobs), out_shape=[me...  1.74 us
    pallas_call x1, Pallas kernels, first_products(): pl.pallas_call(functools.partial(first_kernel, bits), out_shape=(message(...  1.69 us
    pallas_call x1, Pallas kernels, finish(): pl.pallas_call(functools.partial(final_kernel, terms, powers), out_shape=...  0.77 us
  transfers between devices with their start and end apart: 9, of which 5 were waited for; matrix products, arithmetic and copies ran while one was open for 0% of the time, Pallas kernels for 7%

profile of v21, /device:TPU:0, one launch (start us, length us, event | category | flops | bytes accessed | tf_op | source)
XLA Modules:
  0.0 26.6 jit_solution(6113393073757545144)
XLA Ops:
  0.0 1.7 %first_products.1 = (f32[33,8,128]{2,1,0:T(8,128)S(1)}, bf16[2,256,1024]{2,1,0:T(8,128)(2,1)S(1)}, bf16[1024,512]{1,0:T(8,128)(2,1)S(1)}, f32[1,512]{1,0:T(1,128)S(1)}) custom-call(s32[1,12]{1,0:T(1,128)} %visible.1, s32[4,512]{1,0:T(4,128)} %bitcast.3, bf16[1,12,2,32,512]{4,3,2,1,0:T(8,128)(2,1)} %channel.1, bf16[1024,512]{1,0:T(8,128)(2,1)} %bitcast.2), custom_call_target="tpu_custom_call" | custom-call | flops 8192 | bytes 8192 | tf_op jit(solution)/shard_map/first_products/pallas_call | solution.py:148
  1.7 0.5 %collective-permute-start = (f32[33,8,128]{2,1,0:T(8,128)S(1)}, f32[33,8,128]{2,1,0:T(8,128)S(1)}, u32[]{:S(2)}, u32[]{:S(2)}) collective-permute-start(f32[33,8,128]{2,1,0:T(8,128)S(1)} %get-tuple-element.11.refs_0_), channel_id=1, source_target_pairs={{0,1},{1,0},{2,3},{3,2},{4,5},{5,4},{6,7},{7,6},{8,9},{9,8},{10,11... | collective-permute-start | bytes 405512 | tf_op jit(solution)/shard_map/ppermute | solution.py:271
  2.2 0.6 %next_products.4 = (f32[128,8,128]{2,1,0:T(8,128)S(1)}, f32[32,8,128]{2,1,0:T(8,128)S(1)}) custom-call(bf16[2,256,1024]{2,1,0:T(8,128)(2,1)S(1)} %get-tuple-element.12.rows, bf16[1024,512]{1,0:T(8,128)(2,1)S(1)} %get-tuple-element.13.weights, f32[1,512]{1,0:T(1,128)S(1)} %get-tuple-element.14.served), custom_call_target="tpu_custom_call" | custom-call | flops 67108864 | bytes 67108864 | tf_op jit(solution)/shard_map/next_products/pallas_call | solution.py:174
  2.8 0.1 collective-permute-start.2
  2.9 0.3 %collective-permute-done.refs_2_.refs_1_ = f32[33,8,128]{2,1,0:T(8,128)S(1)} collective-permute-done((f32[33,8,128]{2,1,0:T(8,128)S(1)}, f32[33,8,128]{2,1,0:T(8,128)S(1)}, u32[]{:S(2)}, u32[]{:S(2)}) %collective-permute-start) | collective-permute-done | bytes 135200 | tf_op jit(solution)/shard_map/ppermute | solution.py:271
  3.2 3.0 %collective-permute-start.1 = (f32[33,8,128]{2,1,0:T(8,128)S(1)}, f32[33,8,128]{2,1,0:T(8,128)S(1)}, u32[]{:S(2)}, u32[]{:S(2)}) collective-permute-start(f32[33,8,128]{2,1,0:T(8,128)S(1)} %summed.6), channel_id=1, source_target_pairs={{0,4},{1,3},{2,6},{3,1},{4,0},{5,7},{6,2},{7,5},{8,12},{9,11},{10,... | collective-permute-start | bytes 405512 | tf_op jit(solution)/shard_map/ppermute | solution.py:271
  6.2 0.4 %next_products.5.refs_0_.refs_2_ = f32[128,8,128]{2,1,0:T(8,128)S(1)} custom-call(bf16[2,256,1024]{2,1,0:T(8,128)(2,1)S(1)} %get-tuple-element.12.rows, bf16[1024,512]{1,0:T(8,128)(2,1)S(1)} %get-tuple-element.13.weights, f32[1,512]{1,0:T(1,128)S(1)} %get-tuple-element.14.served), custom_call_target="tpu_custom_call" | custom-call | flops 8589934592 | bytes 8589934592 | tf_op jit(solution)/shard_map/next_products/pallas_call | solution.py:174
  6.7 0.0 collective-permute-done.2.refs_1_.refs_3_
  6.7 0.9 %collective-permute-start.6 = (f32[32,8,128]{2,1,0:T(8,128)S(1)}, f32[32,8,128]{2,1,0:T(8,128)S(1)}, u32[]{:S(2)}, u32[]{:S(2)}) collective-permute-start(f32[32,8,128]{2,1,0:T(8,128)S(1)} %summed.7.refs_5_), channel_id=1, source_target_pairs={{0,4},{1,3},{2,6},{3,1},{4,0},{5,7},{6,2},{7,5},{8,12},{9,11},{10,... | collective-permute-start | bytes 393224 | tf_op jit(solution)/shard_map/ppermute | solution.py:271
  7.6 1.7 %collective-permute-done.1.refs_4_.refs_2_ = f32[33,8,128]{2,1,0:T(8,128)S(1)} collective-permute-done((f32[33,8,128]{2,1,0:T(8,128)S(1)}, f32[33,8,128]{2,1,0:T(8,128)S(1)}, u32[]{:S(2)}, u32[]{:S(2)}) %collective-permute-start.1) | collective-permute-done | bytes 135200 | tf_op jit(solution)/shard_map/ppermute | solution.py:271
  9.2 2.0 %collective-permute-start.3 = (f32[33,8,128]{2,1,0:T(8,128)S(1)}, f32[33,8,128]{2,1,0:T(8,128)S(1)}, u32[]{:S(2)}, u32[]{:S(2)}) collective-permute-start(f32[33,8,128]{2,1,0:T(8,128)S(1)} %summed.8.refs_0_), channel_id=1, source_target_pairs={{0,2},{1,5},{2,0},{3,7},{4,6},{5,1},{6,4},{7,3},{8,10},{9,13},{10,... | collective-permute-start | bytes 405512 | tf_op jit(solution)/shard_map/ppermute | solution.py:271
  11.2 0.4 %next_products.6.refs_0_ = f32[96,8,128]{2,1,0:T(8,128)S(1)} custom-call(bf16[2,256,1024]{2,1,0:T(8,128)(2,1)S(1)} %get-tuple-element.12.rows, bf16[1024,512]{1,0:T(8,128)(2,1)S(1)} %get-tuple-element.13.weights, f32[1,512]{1,0:T(1,128)S(1)} %get-tuple-element.14.served, f32[33,8,128]{2,1,0:T(8,128)S(1)} %summed.8.refs_0_), custom_call_target="tpu_custom_call" | custom-call | flops 67108864 | bytes 67108864 | tf_op jit(solution)/shard_map/next_products/pallas_call | solution.py:174
  11.6 0.1 collective-permute-start.4
  11.7 0.4 %next_products.7.refs_2_.refs_5_.refs_0_.refs_4_ = f32[96,8,128]{2,1,0:T(8,128)S(1)} custom-call(bf16[2,256,1024]{2,1,0:T(8,128)(2,1)S(1)} %get-tuple-element.12.rows, bf16[1024,512]{1,0:T(8,128)(2,1)S(1)} %get-tuple-element.13.weights, f32[1,512]{1,0:T(1,128)S(1)} %get-tuple-element.14.served, f32[96,8,128]{2,1,0:T(8,128)S(1)} %next_products.6.refs_0_), custom_call_target="tpu_custom_call" | custom-call | flops 68719476736 | bytes 68719476736 | tf_op jit(solution)/shard_map/next_products/pallas_call | solution.py:174
  12.1 1.6 %collective-permute-start.5 = (f32[64,8,128]{2,1,0:T(8,128)S(1)}, f32[64,8,128]{2,1,0:T(8,128)S(1)}, u32[]{:S(2)}, u32[]{:S(2)}) collective-permute-start(f32[64,8,128]{2,1,0:T(8,128)S(1)} %summed.9), channel_id=1, source_target_pairs={{0,4},{1,3},{2,6},{3,1},{4,0},{5,7},{6,2},{7,5},{8,12},{9,11},{10,... | collective-permute-start | bytes 786440 | tf_op jit(solution)/shard_map/ppermute | solution.py:271
  13.8 0.0 collective-permute-done.6.refs_3_
  13.8 0.7 %collective-permute-done.3.refs_4_.refs_3_ = f32[33,8,128]{2,1,0:T(8,128)S(1)} collective-permute-done((f32[33,8,128]{2,1,0:T(8,128)S(1)}, f32[33,8,128]{2,1,0:T(8,128)S(1)}, u32[]{:S(2)}, u32[]{:S(2)}) %collective-permute-start.3) | collective-permute-done | bytes 135200 | tf_op jit(solution)/shard_map/ppermute | solution.py:271
  14.5 0.0 collective-permute-done.4.refs_6_.refs_1_.refs_5_
  14.6 2.9 %collective-permute-start.7 = (f32[33,8,128]{2,1,0:T(8,128)S(1)}, f32[33,8,128]{2,1,0:T(8,128)S(1)}, u32[]{:S(2)}, u32[]{:S(2)}) collective-permute-start(f32[33,8,128]{2,1,0:T(8,128)S(1)} %summed.10.refs_3_), channel_id=1, source_target_pairs={{0,8},{1,9},{2,10},{3,11},{4,12},{5,13},{6,14},{7,15},{8,0},{9,1},... | collective-permute-start | bytes 405512 | tf_op jit(solution)/shard_map/ppermute | solution.py:271
  17.5 3.3 %collective-permute-done.5.refs_2_.refs_6_ = f32[64,8,128]{2,1,0:T(8,128)S(1)} collective-permute-done((f32[64,8,128]{2,1,0:T(8,128)S(1)}, f32[64,8,128]{2,1,0:T(8,128)S(1)}, u32[]{:S(2)}, u32[]{:S(2)}) %collective-permute-start.5) | collective-permute-done | bytes 262176 | tf_op jit(solution)/shard_map/ppermute | solution.py:271
  20.8 0.1 collective-permute-start.8
  20.9 5.0 %collective-permute-done.8.refs_8_ = f32[32,8,128]{2,1,0:T(8,128)S(1)} collective-permute-done((f32[32,8,128]{2,1,0:T(8,128)S(1)}, f32[32,8,128]{2,1,0:T(8,128)S(1)}, u32[]{:S(2)}, u32[]{:S(2)}) %collective-permute-start.8) | collective-permute-done | bytes 131104 | tf_op jit(solution)/shard_map/ppermute | solution.py:271
  25.9 0.0 collective-permute-done.7.refs_7_
  25.9 0.8 %finish.1 = f32[32,2,512]{2,1,0:T(2,128)} custom-call(f32[33,8,128]{2,1,0:T(8,128)S(1)} %get-tuple-element.11.refs_0_, f32[33,8,128]{2,1,0:T(8,128)S(1)} %collective-permute-done.refs_2_.refs_1_, f32[33,8,128]{2,1,0:T(8,128)S(1)} %collective-permute-done.1.refs_4_.refs_2_, f32[33,8,128]{2,1,0:T(8,128)S(1)} %collective-permute-done.3.refs_4_.refs_3_, ...), custom_call_target="tpu_custom_call" | custom-call | tf_op jit(solution)/shard_map/finish/pallas_call | solution.py:230
  (6 shorter events, 0.2 us)
Async XLA Ops:
  1.7 1.5 %collective-permute-start = (f32[33,8,128]{2,1,0:T(8,128)S(1)}, f32[33,8,128]{2,1,0:T(8,128)S(1)}, u32[]{:S(2)}, u32[]{:S(2)}) collective-permute-start(f32[33,8,128]{2,1,0:T(8,128)S(1)} %get-tuple-element.11.refs_0_), channel_id=1, source_target_pairs={{0,1},{1,0},{2,3},{3,2},{4,5},{5,4},{6,7},{7,6},{8,9},{9,8},{10,11... | collective-permute-start | bytes 405512 | tf_op jit(solution)/shard_map/ppermute | solution.py:271
  2.8 3.9 %collective-permute-start.2 = (f32[128,8,128]{2,1,0:T(8,128)S(1)}, f32[128,8,128]{2,1,0:T(8,128)S(1)}, u32[]{:S(2)}, u32[]{:S(2)}) collective-permute-start(f32[128,8,128]{2,1,0:T(8,128)S(1)} %get-tuple-element.16), channel_id=1, source_target_pairs={{0,1},{1,0},{2,3},{3,2},{4,5},{5,4},{6,7},{7,6},{8,9},{9,8},{10,11... | collective-permute-start | bytes 1572872 | tf_op jit(solution)/shard_map/ppermute | solution.py:271
  3.2 6.0 %collective-permute-start.1 = (f32[33,8,128]{2,1,0:T(8,128)S(1)}, f32[33,8,128]{2,1,0:T(8,128)S(1)}, u32[]{:S(2)}, u32[]{:S(2)}) collective-permute-start(f32[33,8,128]{2,1,0:T(8,128)S(1)} %summed.6), channel_id=1, source_target_pairs={{0,4},{1,3},{2,6},{3,1},{4,0},{5,7},{6,2},{7,5},{8,12},{9,11},{10,... | collective-permute-start | bytes 405512 | tf_op jit(solution)/shard_map/ppermute | solution.py:271
  6.7 7.1 %collective-permute-start.6 = (f32[32,8,128]{2,1,0:T(8,128)S(1)}, f32[32,8,128]{2,1,0:T(8,128)S(1)}, u32[]{:S(2)}, u32[]{:S(2)}) collective-permute-start(f32[32,8,128]{2,1,0:T(8,128)S(1)} %summed.7.refs_5_), channel_id=1, source_target_pairs={{0,4},{1,3},{2,6},{3,1},{4,0},{5,7},{6,2},{7,5},{8,12},{9,11},{10,... | collective-permute-start | bytes 393224 | tf_op jit(solution)/shard_map/ppermute | solution.py:271
  9.2 5.3 %collective-permute-start.3 = (f32[33,8,128]{2,1,0:T(8,128)S(1)}, f32[33,8,128]{2,1,0:T(8,128)S(1)}, u32[]{:S(2)}, u32[]{:S(2)}) collective-permute-start(f32[33,8,128]{2,1,0:T(8,128)S(1)} %summed.8.refs_0_), channel_id=1, source_target_pairs={{0,2},{1,5},{2,0},{3,7},{4,6},{5,1},{6,4},{7,3},{8,10},{9,13},{10,... | collective-permute-start | bytes 405512 | tf_op jit(solution)/shard_map/ppermute | solution.py:271
  11.6 2.9 %collective-permute-start.4 = (f32[96,8,128]{2,1,0:T(8,128)S(1)}, f32[96,8,128]{2,1,0:T(8,128)S(1)}, u32[]{:S(2)}, u32[]{:S(2)}) collective-permute-start(f32[96,8,128]{2,1,0:T(8,128)S(1)} %next_products.6.refs_0_), channel_id=1, source_target_pairs={{0,1},{1,0},{2,3},{3,2},{4,5},{5,4},{6,7},{7,6},{8,9},{9,8},{10,11... | collective-permute-start | bytes 1179656 | tf_op jit(solution)/shard_map/ppermute | solution.py:271
  12.1 8.7 %collective-permute-start.5 = (f32[64,8,128]{2,1,0:T(8,128)S(1)}, f32[64,8,128]{2,1,0:T(8,128)S(1)}, u32[]{:S(2)}, u32[]{:S(2)}) collective-permute-start(f32[64,8,128]{2,1,0:T(8,128)S(1)} %summed.9), channel_id=1, source_target_pairs={{0,4},{1,3},{2,6},{3,1},{4,0},{5,7},{6,2},{7,5},{8,12},{9,11},{10,... | collective-permute-start | bytes 786440 | tf_op jit(solution)/shard_map/ppermute | solution.py:271
  14.6 11.3 %collective-permute-start.7 = (f32[33,8,128]{2,1,0:T(8,128)S(1)}, f32[33,8,128]{2,1,0:T(8,128)S(1)}, u32[]{:S(2)}, u32[]{:S(2)}) collective-permute-start(f32[33,8,128]{2,1,0:T(8,128)S(1)} %summed.10.refs_3_), channel_id=1, source_target_pairs={{0,8},{1,9},{2,10},{3,11},{4,12},{5,13},{6,14},{7,15},{8,0},{9,1},... | collective-permute-start | bytes 405512 | tf_op jit(solution)/shard_map/ppermute | solution.py:271
  20.8 5.0 %collective-permute-start.8 = (f32[32,8,128]{2,1,0:T(8,128)S(1)}, f32[32,8,128]{2,1,0:T(8,128)S(1)}, u32[]{:S(2)}, u32[]{:S(2)}) collective-permute-start(f32[32,8,128]{2,1,0:T(8,128)S(1)} %summed.11), channel_id=1, source_target_pairs={{0,2},{1,5},{2,0},{3,7},{4,6},{5,1},{6,4},{7,3},{8,10},{9,13},{10,... | collective-permute-start | bytes 393224 | tf_op jit(solution)/shard_map/ppermute | solution.py:271

commit v22 on v21

--- a/solution.py
+++ b/solution.py
@@ -13,7 +13,7 @@
 
 
 COSTS = (64 * MIB, 8192 * MIB, 64 * MIB, 65536 * MIB) + (
-    1024 * MIB, 64 * MIB, 64 * MIB, 64 * MIB, 8192 * MIB, 1024 * MIB
+    1024 * MIB, 64 * MIB, 64 * MIB, 64 * MIB, 64 * MIB, 8192 * MIB, 1024 * MIB
 )
 
 
@@ -251,7 +251,8 @@
         (0, parts[0]),
         (0, parts[2]),
         (1, steps[1][:half]),
-        (0, parts[1] + parts[3]),
+        (0, parts[1]),
+        (0, parts[3]),
         (2, steps[2]),
         (1, steps[1][half:]),
     ]
@@ -312,8 +313,8 @@
             add(come, range(first, first + count), False)
         power = step not in with_power
         with_power.add(step)
-        after = [mine] if number == 3 else [now] if number in (2, 5) else []
-        now = total(slots, power, COSTS[4 + number] if number < 6 else 8192, after)
+        after = [mine] if number == 3 else [now] if number in (2, 4, 6) else []
+        now = total(slots, power, COSTS[4 + number] if number < 7 else 8192, after)
         came = swap(now, (orders[0][step], orders[1][step]))
         slots = [slot + (1 << (bits - 2 - step)) for slot in slots]
         add(came, slots, power)

time: 26.8 us -> 23.5 us (0.88)
  waiting for transfers between devices: 11 us -> 5.21 us
  starting transfers between devices: 11.2 us -> 13.6 us
    ppermute x9 -> x10, waiting for transfers between devices: 11 us -> 5.21 us  [swap(): lax.ppermute(value, 'ap', [(i, i ^ 1 << bit_of[i & 1]) for i in range(dev...]
    ppermute x9 -> x10, starting transfers between devices: 11.2 us -> 13.6 us  [swap(): lax.ppermute(value, 'ap', [(i, i ^ 1 << bit_of[i & 1]) for i in range(dev...]
  transfers between devices with their start and end apart: 9 -> 10, of which waited for: 5 -> 5; matrix products, arithmetic and copies ran while one was open for 0% -> 0% of each run, Pallas kernels for 7% -> 8%
where the time goes in v22:
time: 23.5 us; the launch traced here: 23.3 us
  starting transfers between devices  13.6 us (58%)
  waiting for transfers between devices  5.21 us (22%)
  Pallas kernels  4.36 us (19%)
    ppermute x10, starting transfers between devices, swap(): lax.ppermute(value, 'ap', [(i, i ^ 1 << bit_of[i & 1]) for i in range(dev...  13.6 us
    ppermute x10, waiting for transfers between devices, swap(): lax.ppermute(value, 'ap', [(i, i ^ 1 << bit_of[i & 1]) for i in range(dev...  5.21 us
    pallas_call x4, Pallas kernels, next_products(): pl.pallas_call(functools.partial(next_kernel, users, jobs), out_shape=[me...  1.74 us
    pallas_call x1, Pallas kernels, first_products(): pl.pallas_call(functools.partial(first_kernel, bits), out_shape=(message(...  1.69 us
    pallas_call x1, Pallas kernels, finish(): pl.pallas_call(functools.partial(final_kernel, terms, powers), out_shape=...  0.78 us
  transfers between devices with their start and end apart: 10, of which 5 were waited for; matrix products, arithmetic and copies ran while one was open for 0% of the time, Pallas kernels for 8%

profile of v22, /device:TPU:0, one launch (start us, length us, event | category | flops | bytes accessed | tf_op | source)
XLA Modules:
  0.0 23.3 jit_solution(9699040392491611154)
XLA Ops:
  0.0 1.7 %first_products.1 = (f32[33,8,128]{2,1,0:T(8,128)S(1)}, bf16[2,256,1024]{2,1,0:T(8,128)(2,1)S(1)}, bf16[1024,512]{1,0:T(8,128)(2,1)S(1)}, f32[1,512]{1,0:T(1,128)S(1)}) custom-call(s32[1,12]{1,0:T(1,128)} %visible.1, s32[4,512]{1,0:T(4,128)} %bitcast.3, bf16[1,12,2,32,512]{4,3,2,1,0:T(8,128)(2,1)} %channel.1, bf16[1024,512]{1,0:T(8,128)(2,1)} %bitcast.2), custom_call_target="tpu_custom_call" | custom-call | flops 8192 | bytes 8192 | tf_op jit(solution)/shard_map/first_products/pallas_call | solution.py:148
  1.7 0.5 %collective-permute-start = (f32[33,8,128]{2,1,0:T(8,128)S(1)}, f32[33,8,128]{2,1,0:T(8,128)S(1)}, u32[]{:S(2)}, u32[]{:S(2)}) collective-permute-start(f32[33,8,128]{2,1,0:T(8,128)S(1)} %get-tuple-element.11.refs_0_), channel_id=1, source_target_pairs={{0,1},{1,0},{2,3},{3,2},{4,5},{5,4},{6,7},{7,6},{8,9},{9,8},{10,11... | collective-permute-start | bytes 405512 | tf_op jit(solution)/shard_map/ppermute | solution.py:272
  2.2 0.6 %next_products.4 = (f32[128,8,128]{2,1,0:T(8,128)S(1)}, f32[32,8,128]{2,1,0:T(8,128)S(1)}) custom-call(bf16[2,256,1024]{2,1,0:T(8,128)(2,1)S(1)} %get-tuple-element.12.rows, bf16[1024,512]{1,0:T(8,128)(2,1)S(1)} %get-tuple-element.13.weights, f32[1,512]{1,0:T(1,128)S(1)} %get-tuple-element.14.served), custom_call_target="tpu_custom_call" | custom-call | flops 67108864 | bytes 67108864 | tf_op jit(solution)/shard_map/next_products/pallas_call | solution.py:174
  2.8 0.1 collective-permute-start.2
  2.9 0.3 %collective-permute-done.refs_2_.refs_1_ = f32[33,8,128]{2,1,0:T(8,128)S(1)} collective-permute-done((f32[33,8,128]{2,1,0:T(8,128)S(1)}, f32[33,8,128]{2,1,0:T(8,128)S(1)}, u32[]{:S(2)}, u32[]{:S(2)}) %collective-permute-start) | collective-permute-done | bytes 135200 | tf_op jit(solution)/shard_map/ppermute | solution.py:272
  3.2 3.0 %collective-permute-start.1 = (f32[33,8,128]{2,1,0:T(8,128)S(1)}, f32[33,8,128]{2,1,0:T(8,128)S(1)}, u32[]{:S(2)}, u32[]{:S(2)}) collective-permute-start(f32[33,8,128]{2,1,0:T(8,128)S(1)} %summed.7), channel_id=1, source_target_pairs={{0,4},{1,3},{2,6},{3,1},{4,0},{5,7},{6,2},{7,5},{8,12},{9,11},{10,... | collective-permute-start | bytes 405512 | tf_op jit(solution)/shard_map/ppermute | solution.py:272
  6.2 0.4 %next_products.5.refs_0_.refs_2_ = f32[128,8,128]{2,1,0:T(8,128)S(1)} custom-call(bf16[2,256,1024]{2,1,0:T(8,128)(2,1)S(1)} %get-tuple-element.12.rows, bf16[1024,512]{1,0:T(8,128)(2,1)S(1)} %get-tuple-element.13.weights, f32[1,512]{1,0:T(1,128)S(1)} %get-tuple-element.14.served), custom_call_target="tpu_custom_call" | custom-call | flops 8589934592 | bytes 8589934592 | tf_op jit(solution)/shard_map/next_products/pallas_call | solution.py:174
  6.7 0.0 collective-permute-done.2.refs_1_.refs_3_
  6.7 0.9 %collective-permute-start.6 = (f32[32,8,128]{2,1,0:T(8,128)S(1)}, f32[32,8,128]{2,1,0:T(8,128)S(1)}, u32[]{:S(2)}, u32[]{:S(2)}) collective-permute-start(f32[32,8,128]{2,1,0:T(8,128)S(1)} %summed.8.refs_5_), channel_id=1, source_target_pairs={{0,4},{1,3},{2,6},{3,1},{4,0},{5,7},{6,2},{7,5},{8,12},{9,11},{10,... | collective-permute-start | bytes 393224 | tf_op jit(solution)/shard_map/ppermute | solution.py:272
  7.6 1.7 %collective-permute-done.1.refs_4_.refs_2_ = f32[33,8,128]{2,1,0:T(8,128)S(1)} collective-permute-done((f32[33,8,128]{2,1,0:T(8,128)S(1)}, f32[33,8,128]{2,1,0:T(8,128)S(1)}, u32[]{:S(2)}, u32[]{:S(2)}) %collective-permute-start.1) | collective-permute-done | bytes 135200 | tf_op jit(solution)/shard_map/ppermute | solution.py:272
  9.2 2.0 %collective-permute-start.3 = (f32[33,8,128]{2,1,0:T(8,128)S(1)}, f32[33,8,128]{2,1,0:T(8,128)S(1)}, u32[]{:S(2)}, u32[]{:S(2)}) collective-permute-start(f32[33,8,128]{2,1,0:T(8,128)S(1)} %summed.9.refs_0_), channel_id=1, source_target_pairs={{0,2},{1,5},{2,0},{3,7},{4,6},{5,1},{6,4},{7,3},{8,10},{9,13},{10,... | collective-permute-start | bytes 405512 | tf_op jit(solution)/shard_map/ppermute | solution.py:272
  11.2 0.4 %next_products.6.refs_0_ = f32[96,8,128]{2,1,0:T(8,128)S(1)} custom-call(bf16[2,256,1024]{2,1,0:T(8,128)(2,1)S(1)} %get-tuple-element.12.rows, bf16[1024,512]{1,0:T(8,128)(2,1)S(1)} %get-tuple-element.13.weights, f32[1,512]{1,0:T(1,128)S(1)} %get-tuple-element.14.served, f32[33,8,128]{2,1,0:T(8,128)S(1)} %summed.9.refs_0_), custom_call_target="tpu_custom_call" | custom-call | flops 67108864 | bytes 67108864 | tf_op jit(solution)/shard_map/next_products/pallas_call | solution.py:174
  11.6 0.1 collective-permute-start.4
  11.7 0.4 %next_products.7.refs_2_.refs_5_.refs_0_.refs_4_ = f32[96,8,128]{2,1,0:T(8,128)S(1)} custom-call(bf16[2,256,1024]{2,1,0:T(8,128)(2,1)S(1)} %get-tuple-element.12.rows, bf16[1024,512]{1,0:T(8,128)(2,1)S(1)} %get-tuple-element.13.weights, f32[1,512]{1,0:T(1,128)S(1)} %get-tuple-element.14.served, f32[96,8,128]{2,1,0:T(8,128)S(1)} %next_products.6.refs_0_), custom_call_target="tpu_custom_call" | custom-call | flops 68719476736 | bytes 68719476736 | tf_op jit(solution)/shard_map/next_products/pallas_call | solution.py:174
  12.1 1.6 %collective-permute-start.8 = (f32[32,8,128]{2,1,0:T(8,128)S(1)}, f32[32,8,128]{2,1,0:T(8,128)S(1)}, u32[]{:S(2)}, u32[]{:S(2)}) collective-permute-start(f32[32,8,128]{2,1,0:T(8,128)S(1)} %summed.10.refs_2_), channel_id=1, source_target_pairs={{0,4},{1,3},{2,6},{3,1},{4,0},{5,7},{6,2},{7,5},{8,12},{9,11},{10,... | collective-permute-start | bytes 393224 | tf_op jit(solution)/shard_map/ppermute | solution.py:272
  13.8 0.5 %collective-permute-start.5 = (f32[32,8,128]{2,1,0:T(8,128)S(1)}, f32[32,8,128]{2,1,0:T(8,128)S(1)}, u32[]{:S(2)}, u32[]{:S(2)}) collective-permute-start(f32[32,8,128]{2,1,0:T(8,128)S(1)} %summed.11), channel_id=1, source_target_pairs={{0,4},{1,3},{2,6},{3,1},{4,0},{5,7},{6,2},{7,5},{8,12},{9,11},{10,... | collective-permute-start | bytes 393224 | tf_op jit(solution)/shard_map/ppermute | solution.py:272
  14.3 0.0 collective-permute-done.6.refs_3_
  14.3 0.2 %collective-permute-done.3.refs_4_.refs_3_ = f32[33,8,128]{2,1,0:T(8,128)S(1)} collective-permute-done((f32[33,8,128]{2,1,0:T(8,128)S(1)}, f32[33,8,128]{2,1,0:T(8,128)S(1)}, u32[]{:S(2)}, u32[]{:S(2)}) %collective-permute-start.3) | collective-permute-done | bytes 135200 | tf_op jit(solution)/shard_map/ppermute | solution.py:272
  14.5 0.0 collective-permute-done.4.refs_6_.refs_1_.refs_5_
  14.6 2.9 %collective-permute-start.7 = (f32[33,8,128]{2,1,0:T(8,128)S(1)}, f32[33,8,128]{2,1,0:T(8,128)S(1)}, u32[]{:S(2)}, u32[]{:S(2)}) collective-permute-start(f32[33,8,128]{2,1,0:T(8,128)S(1)} %summed.12.refs_3_), channel_id=1, source_target_pairs={{0,8},{1,9},{2,10},{3,11},{4,12},{5,13},{6,14},{7,15},{8,0},{9,1},... | collective-permute-start | bytes 405512 | tf_op jit(solution)/shard_map/ppermute | solution.py:272
  17.5 0.0 collective-permute-done.8.refs_2_
  17.5 2.0 %collective-permute-start.9 = (f32[32,8,128]{2,1,0:T(8,128)S(1)}, f32[32,8,128]{2,1,0:T(8,128)S(1)}, u32[]{:S(2)}, u32[]{:S(2)}) collective-permute-start(f32[32,8,128]{2,1,0:T(8,128)S(1)} %summed.13), channel_id=1, source_target_pairs={{0,2},{1,5},{2,0},{3,7},{4,6},{5,1},{6,4},{7,3},{8,10},{9,13},{10,... | collective-permute-start | bytes 393224 | tf_op jit(solution)/shard_map/ppermute | solution.py:272
  19.5 2.6 %collective-permute-done.5.refs_6_ = f32[32,8,128]{2,1,0:T(8,128)S(1)} collective-permute-done((f32[32,8,128]{2,1,0:T(8,128)S(1)}, f32[32,8,128]{2,1,0:T(8,128)S(1)}, u32[]{:S(2)}, u32[]{:S(2)}) %collective-permute-start.5) | collective-permute-done | bytes 131104 | tf_op jit(solution)/shard_map/ppermute | solution.py:272
  22.1 0.5 %collective-permute-done.9.refs_8_ = f32[32,8,128]{2,1,0:T(8,128)S(1)} collective-permute-done((f32[32,8,128]{2,1,0:T(8,128)S(1)}, f32[32,8,128]{2,1,0:T(8,128)S(1)}, u32[]{:S(2)}, u32[]{:S(2)}) %collective-permute-start.9) | collective-permute-done | bytes 131104 | tf_op jit(solution)/shard_map/ppermute | solution.py:272
  22.5 0.0 collective-permute-done.7.refs_7_
  22.5 0.8 %finish.1 = f32[32,2,512]{2,1,0:T(2,128)} custom-call(f32[33,8,128]{2,1,0:T(8,128)S(1)} %get-tuple-element.11.refs_0_, f32[33,8,128]{2,1,0:T(8,128)S(1)} %collective-permute-done.refs_2_.refs_1_, f32[33,8,128]{2,1,0:T(8,128)S(1)} %collective-permute-done.1.refs_4_.refs_2_, f32[33,8,128]{2,1,0:T(8,128)S(1)} %collective-permute-done.3.refs_4_.refs_3_, ...), custom_call_target="tpu_custom_call" | custom-call | tf_op jit(solution)/shard_map/finish/pallas_call | solution.py:230
  (7 shorter events, 0.2 us)
Async XLA Ops:
  1.7 1.5 %collective-permute-start = (f32[33,8,128]{2,1,0:T(8,128)S(1)}, f32[33,8,128]{2,1,0:T(8,128)S(1)}, u32[]{:S(2)}, u32[]{:S(2)}) collective-permute-start(f32[33,8,128]{2,1,0:T(8,128)S(1)} %get-tuple-element.11.refs_0_), channel_id=1, source_target_pairs={{0,1},{1,0},{2,3},{3,2},{4,5},{5,4},{6,7},{7,6},{8,9},{9,8},{10,11... | collective-permute-start | bytes 405512 | tf_op jit(solution)/shard_map/ppermute | solution.py:272
  2.8 3.9 %collective-permute-start.2 = (f32[128,8,128]{2,1,0:T(8,128)S(1)}, f32[128,8,128]{2,1,0:T(8,128)S(1)}, u32[]{:S(2)}, u32[]{:S(2)}) collective-permute-start(f32[128,8,128]{2,1,0:T(8,128)S(1)} %get-tuple-element.16), channel_id=1, source_target_pairs={{0,1},{1,0},{2,3},{3,2},{4,5},{5,4},{6,7},{7,6},{8,9},{9,8},{10,11... | collective-permute-start | bytes 1572872 | tf_op jit(solution)/shard_map/ppermute | solution.py:272
  3.2 6.0 %collective-permute-start.1 = (f32[33,8,128]{2,1,0:T(8,128)S(1)}, f32[33,8,128]{2,1,0:T(8,128)S(1)}, u32[]{:S(2)}, u32[]{:S(2)}) collective-permute-start(f32[33,8,128]{2,1,0:T(8,128)S(1)} %summed.7), channel_id=1, source_target_pairs={{0,4},{1,3},{2,6},{3,1},{4,0},{5,7},{6,2},{7,5},{8,12},{9,11},{10,... | collective-permute-start | bytes 405512 | tf_op jit(solution)/shard_map/ppermute | solution.py:272
  6.7 7.6 %collective-permute-start.6 = (f32[32,8,128]{2,1,0:T(8,128)S(1)}, f32[32,8,128]{2,1,0:T(8,128)S(1)}, u32[]{:S(2)}, u32[]{:S(2)}) collective-permute-start(f32[32,8,128]{2,1,0:T(8,128)S(1)} %summed.8.refs_5_), channel_id=1, source_target_pairs={{0,4},{1,3},{2,6},{3,1},{4,0},{5,7},{6,2},{7,5},{8,12},{9,11},{10,... | collective-permute-start | bytes 393224 | tf_op jit(solution)/shard_map/ppermute | solution.py:272
  9.2 5.3 %collective-permute-start.3 = (f32[33,8,128]{2,1,0:T(8,128)S(1)}, f32[33,8,128]{2,1,0:T(8,128)S(1)}, u32[]{:S(2)}, u32[]{:S(2)}) collective-permute-start(f32[33,8,128]{2,1,0:T(8,128)S(1)} %summed.9.refs_0_), channel_id=1, source_target_pairs={{0,2},{1,5},{2,0},{3,7},{4,6},{5,1},{6,4},{7,3},{8,10},{9,13},{10,... | collective-permute-start | bytes 405512 | tf_op jit(solution)/shard_map/ppermute | solution.py:272
  11.6 2.9 %collective-permute-start.4 = (f32[96,8,128]{2,1,0:T(8,128)S(1)}, f32[96,8,128]{2,1,0:T(8,128)S(1)}, u32[]{:S(2)}, u32[]{:S(2)}) collective-permute-start(f32[96,8,128]{2,1,0:T(8,128)S(1)} %next_products.6.refs_0_), channel_id=1, source_target_pairs={{0,1},{1,0},{2,3},{3,2},{4,5},{5,4},{6,7},{7,6},{8,9},{9,8},{10,11... | collective-permute-start | bytes 1179656 | tf_op jit(solution)/shard_map/ppermute | solution.py:272
  12.1 5.4 %collective-permute-start.8 = (f32[32,8,128]{2,1,0:T(8,128)S(1)}, f32[32,8,128]{2,1,0:T(8,128)S(1)}, u32[]{:S(2)}, u32[]{:S(2)}) collective-permute-start(f32[32,8,128]{2,1,0:T(8,128)S(1)} %summed.10.refs_2_), channel_id=1, source_target_pairs={{0,4},{1,3},{2,6},{3,1},{4,0},{5,7},{6,2},{7,5},{8,12},{9,11},{10,... | collective-permute-start | bytes 393224 | tf_op jit(solution)/shard_map/ppermute | solution.py:272
  13.8 8.3 %collective-permute-start.5 = (f32[32,8,128]{2,1,0:T(8,128)S(1)}, f32[32,8,128]{2,1,0:T(8,128)S(1)}, u32[]{:S(2)}, u32[]{:S(2)}) collective-permute-start(f32[32,8,128]{2,1,0:T(8,128)S(1)} %summed.11), channel_id=1, source_target_pairs={{0,4},{1,3},{2,6},{3,1},{4,0},{5,7},{6,2},{7,5},{8,12},{9,11},{10,... | collective-permute-start | bytes 393224 | tf_op jit(solution)/shard_map/ppermute | solution.py:272
  14.6 8.0 %collective-permute-start.7 = (f32[33,8,128]{2,1,0:T(8,128)S(1)}, f32[33,8,128]{2,1,0:T(8,128)S(1)}, u32[]{:S(2)}, u32[]{:S(2)}) collective-permute-start(f32[33,8,128]{2,1,0:T(8,128)S(1)} %summed.12.refs_3_), channel_id=1, source_target_pairs={{0,8},{1,9},{2,10},{3,11},{4,12},{5,13},{6,14},{7,15},{8,0},{9,1},... | collective-permute-start | bytes 405512 | tf_op jit(solution)/shard_map/ppermute | solution.py:272
  17.5 5.0 %collective-permute-start.9 = (f32[32,8,128]{2,1,0:T(8,128)S(1)}, f32[32,8,128]{2,1,0:T(8,128)S(1)}, u32[]{:S(2)}, u32[]{:S(2)}) collective-permute-start(f32[32,8,128]{2,1,0:T(8,128)S(1)} %summed.13), channel_id=1, source_target_pairs={{0,2},{1,5},{2,0},{3,7},{4,6},{5,1},{6,4},{7,3},{8,10},{9,13},{10,... | collective-permute-start | bytes 393224 | tf_op jit(solution)/shard_map/ppermute | solution.py:272

commit v23 on v22

--- a/solution.py
+++ b/solution.py
@@ -22,13 +22,13 @@
     second = list(first)
     if bits > 2:
         second[0], second[1] = second[1], second[0]
-    return second, first
+    return first, second
 
 
 def place_of(group, me, core, bits):
     away = [1 - (((group ^ me) >> bit) & 1) for bit in range(1, bits)]
     if bits > 2:
-        swapped = core == 0
+        swapped = core == 1
         away[:2] = [jnp.where(swapped, away[1], away[0]), jnp.where(swapped, away[0], away[1])]
     place = 0
     for value in away:

time: 23.5 us -> 24.7 us (1.051)
  waiting for transfers between devices: 5.21 us -> 6.24 us
    ppermute x10, waiting for transfers between devices: 5.21 us -> 6.24 us  [swap(): lax.ppermute(value, 'ap', [(i, i ^ 1 << bit_of[i & 1]) for i in range(dev...]
where the time goes in v23:
time: 24.7 us; the launch traced here: 24.5 us
  starting transfers between devices  13.8 us (56%)
  waiting for transfers between devices  6.24 us (25%)
  Pallas kernels  4.36 us (18%)
    ppermute x10, starting transfers between devices, swap(): lax.ppermute(value, 'ap', [(i, i ^ 1 << bit_of[i & 1]) for i in range(dev...  13.8 us
    ppermute x10, waiting for transfers between devices, swap(): lax.ppermute(value, 'ap', [(i, i ^ 1 << bit_of[i & 1]) for i in range(dev...  6.24 us
    pallas_call x4, Pallas kernels, next_products(): pl.pallas_call(functools.partial(next_kernel, users, jobs), out_shape=[me...  1.74 us
    pallas_call x1, Pallas kernels, first_products(): pl.pallas_call(functools.partial(first_kernel, bits), out_shape=(message(...  1.69 us
    pallas_call x1, Pallas kernels, finish(): pl.pallas_call(functools.partial(final_kernel, terms, powers), out_shape=...  0.78 us
  transfers between devices with their start and end apart: 10, of which 5 were waited for; matrix products, arithmetic and copies ran while one was open for 0% of the time, Pallas kernels for 8%

profile of v23, /device:TPU:0, one launch (start us, length us, event | category | flops | bytes accessed | tf_op | source)
XLA Modules:
  0.0 24.5 jit_solution(7096832169966573672)
XLA Ops:
  0.0 1.7 %first_products.1 = (f32[33,8,128]{2,1,0:T(8,128)S(1)}, bf16[2,256,1024]{2,1,0:T(8,128)(2,1)S(1)}, bf16[1024,512]{1,0:T(8,128)(2,1)S(1)}, f32[1,512]{1,0:T(1,128)S(1)}) custom-call(s32[1,12]{1,0:T(1,128)} %visible.1, s32[4,512]{1,0:T(4,128)} %bitcast.3, bf16[1,12,2,32,512]{4,3,2,1,0:T(8,128)(2,1)} %channel.1, bf16[1024,512]{1,0:T(8,128)(2,1)} %bitcast.2), custom_call_target="tpu_custom_call" | custom-call | flops 8192 | bytes 8192 | tf_op jit(solution)/shard_map/first_products/pallas_call | solution.py:148
  1.7 0.5 %collective-permute-start = (f32[33,8,128]{2,1,0:T(8,128)S(1)}, f32[33,8,128]{2,1,0:T(8,128)S(1)}, u32[]{:S(2)}, u32[]{:S(2)}) collective-permute-start(f32[33,8,128]{2,1,0:T(8,128)S(1)} %get-tuple-element.11.refs_0_), channel_id=1, source_target_pairs={{0,1},{1,0},{2,3},{3,2},{4,5},{5,4},{6,7},{7,6},{8,9},{9,8},{10,11... | collective-permute-start | bytes 405512 | tf_op jit(solution)/shard_map/ppermute | solution.py:272
  2.2 0.6 %next_products.4 = (f32[128,8,128]{2,1,0:T(8,128)S(1)}, f32[32,8,128]{2,1,0:T(8,128)S(1)}) custom-call(bf16[2,256,1024]{2,1,0:T(8,128)(2,1)S(1)} %get-tuple-element.12.rows, bf16[1024,512]{1,0:T(8,128)(2,1)S(1)} %get-tuple-element.13.weights, f32[1,512]{1,0:T(1,128)S(1)} %get-tuple-element.14.served), custom_call_target="tpu_custom_call" | custom-call | flops 67108864 | bytes 67108864 | tf_op jit(solution)/shard_map/next_products/pallas_call | solution.py:174
  2.8 0.1 collective-permute-start.2
  2.9 0.3 %collective-permute-done.refs_2_.refs_1_ = f32[33,8,128]{2,1,0:T(8,128)S(1)} collective-permute-done((f32[33,8,128]{2,1,0:T(8,128)S(1)}, f32[33,8,128]{2,1,0:T(8,128)S(1)}, u32[]{:S(2)}, u32[]{:S(2)}) %collective-permute-start) | collective-permute-done | bytes 135200 | tf_op jit(solution)/shard_map/ppermute | solution.py:272
  3.2 2.9 %collective-permute-start.1 = (f32[33,8,128]{2,1,0:T(8,128)S(1)}, f32[33,8,128]{2,1,0:T(8,128)S(1)}, u32[]{:S(2)}, u32[]{:S(2)}) collective-permute-start(f32[33,8,128]{2,1,0:T(8,128)S(1)} %summed.7), channel_id=1, source_target_pairs={{0,2},{1,5},{2,0},{3,7},{4,6},{5,1},{6,4},{7,3},{8,10},{9,13},{10,... | collective-permute-start | bytes 405512 | tf_op jit(solution)/shard_map/ppermute | solution.py:272
  6.1 0.4 %next_products.5.refs_0_.refs_2_ = f32[128,8,128]{2,1,0:T(8,128)S(1)} custom-call(bf16[2,256,1024]{2,1,0:T(8,128)(2,1)S(1)} %get-tuple-element.12.rows, bf16[1024,512]{1,0:T(8,128)(2,1)S(1)} %get-tuple-element.13.weights, f32[1,512]{1,0:T(1,128)S(1)} %get-tuple-element.14.served), custom_call_target="tpu_custom_call" | custom-call | flops 8589934592 | bytes 8589934592 | tf_op jit(solution)/shard_map/next_products/pallas_call | solution.py:174
  6.6 0.0 collective-permute-done.2.refs_1_.refs_3_
  6.6 0.9 %collective-permute-start.6 = (f32[32,8,128]{2,1,0:T(8,128)S(1)}, f32[32,8,128]{2,1,0:T(8,128)S(1)}, u32[]{:S(2)}, u32[]{:S(2)}) collective-permute-start(f32[32,8,128]{2,1,0:T(8,128)S(1)} %summed.8.refs_5_), channel_id=1, source_target_pairs={{0,2},{1,5},{2,0},{3,7},{4,6},{5,1},{6,4},{7,3},{8,10},{9,13},{10,... | collective-permute-start | bytes 393224 | tf_op jit(solution)/shard_map/ppermute | solution.py:272
  7.5 1.7 %collective-permute-done.1.refs_4_.refs_2_ = f32[33,8,128]{2,1,0:T(8,128)S(1)} collective-permute-done((f32[33,8,128]{2,1,0:T(8,128)S(1)}, f32[33,8,128]{2,1,0:T(8,128)S(1)}, u32[]{:S(2)}, u32[]{:S(2)}) %collective-permute-start.1) | collective-permute-done | bytes 135200 | tf_op jit(solution)/shard_map/ppermute | solution.py:272
  9.2 2.2 %collective-permute-start.3 = (f32[33,8,128]{2,1,0:T(8,128)S(1)}, f32[33,8,128]{2,1,0:T(8,128)S(1)}, u32[]{:S(2)}, u32[]{:S(2)}) collective-permute-start(f32[33,8,128]{2,1,0:T(8,128)S(1)} %summed.9.refs_0_), channel_id=1, source_target_pairs={{0,4},{1,3},{2,6},{3,1},{4,0},{5,7},{6,2},{7,5},{8,12},{9,11},{10,... | collective-permute-start | bytes 405512 | tf_op jit(solution)/shard_map/ppermute | solution.py:272
  11.3 0.4 %next_products.6.refs_0_ = f32[96,8,128]{2,1,0:T(8,128)S(1)} custom-call(bf16[2,256,1024]{2,1,0:T(8,128)(2,1)S(1)} %get-tuple-element.12.rows, bf16[1024,512]{1,0:T(8,128)(2,1)S(1)} %get-tuple-element.13.weights, f32[1,512]{1,0:T(1,128)S(1)} %get-tuple-element.14.served, f32[33,8,128]{2,1,0:T(8,128)S(1)} %summed.9.refs_0_), custom_call_target="tpu_custom_call" | custom-call | flops 67108864 | bytes 67108864 | tf_op jit(solution)/shard_map/next_products/pallas_call | solution.py:174
  11.7 0.1 collective-permute-start.4
  11.8 0.4 %next_products.7.refs_2_.refs_5_.refs_0_.refs_4_ = f32[96,8,128]{2,1,0:T(8,128)S(1)} custom-call(bf16[2,256,1024]{2,1,0:T(8,128)(2,1)S(1)} %get-tuple-element.12.rows, bf16[1024,512]{1,0:T(8,128)(2,1)S(1)} %get-tuple-element.13.weights, f32[1,512]{1,0:T(1,128)S(1)} %get-tuple-element.14.served, f32[96,8,128]{2,1,0:T(8,128)S(1)} %next_products.6.refs_0_), custom_call_target="tpu_custom_call" | custom-call | flops 68719476736 | bytes 68719476736 | tf_op jit(solution)/shard_map/next_products/pallas_call | solution.py:174
  12.2 1.6 %collective-permute-start.8 = (f32[32,8,128]{2,1,0:T(8,128)S(1)}, f32[32,8,128]{2,1,0:T(8,128)S(1)}, u32[]{:S(2)}, u32[]{:S(2)}) collective-permute-start(f32[32,8,128]{2,1,0:T(8,128)S(1)} %summed.10.refs_2_), channel_id=1, source_target_pairs={{0,2},{1,5},{2,0},{3,7},{4,6},{5,1},{6,4},{7,3},{8,10},{9,13},{10,... | collective-permute-start | bytes 393224 | tf_op jit(solution)/shard_map/ppermute | solution.py:272
  13.8 0.6 %collective-permute-start.5 = (f32[32,8,128]{2,1,0:T(8,128)S(1)}, f32[32,8,128]{2,1,0:T(8,128)S(1)}, u32[]{:S(2)}, u32[]{:S(2)}) collective-permute-start(f32[32,8,128]{2,1,0:T(8,128)S(1)} %summed.11), channel_id=1, source_target_pairs={{0,2},{1,5},{2,0},{3,7},{4,6},{5,1},{6,4},{7,3},{8,10},{9,13},{10,... | collective-permute-start | bytes 393224 | tf_op jit(solution)/shard_map/ppermute | solution.py:272
  14.4 0.0 collective-permute-done.6.refs_3_
  14.4 0.2 collective-permute-done.3.refs_4_.refs_3_
  14.6 0.0 collective-permute-done.4.refs_6_.refs_1_.refs_5_
  14.6 2.8 %collective-permute-start.7 = (f32[33,8,128]{2,1,0:T(8,128)S(1)}, f32[33,8,128]{2,1,0:T(8,128)S(1)}, u32[]{:S(2)}, u32[]{:S(2)}) collective-permute-start(f32[33,8,128]{2,1,0:T(8,128)S(1)} %summed.12.refs_3_), channel_id=1, source_target_pairs={{0,8},{1,9},{2,10},{3,11},{4,12},{5,13},{6,14},{7,15},{8,0},{9,1},... | collective-permute-start | bytes 405512 | tf_op jit(solution)/shard_map/ppermute | solution.py:272
  17.5 0.0 collective-permute-done.8.refs_2_
  17.5 2.2 %collective-permute-start.9 = (f32[32,8,128]{2,1,0:T(8,128)S(1)}, f32[32,8,128]{2,1,0:T(8,128)S(1)}, u32[]{:S(2)}, u32[]{:S(2)}) collective-permute-start(f32[32,8,128]{2,1,0:T(8,128)S(1)} %summed.13), channel_id=1, source_target_pairs={{0,4},{1,3},{2,6},{3,1},{4,0},{5,7},{6,2},{7,5},{8,12},{9,11},{10,... | collective-permute-start | bytes 393224 | tf_op jit(solution)/shard_map/ppermute | solution.py:272
  19.7 0.0 collective-permute-done.5.refs_6_
  19.7 2.9 %collective-permute-done.9.refs_8_ = f32[32,8,128]{2,1,0:T(8,128)S(1)} collective-permute-done((f32[32,8,128]{2,1,0:T(8,128)S(1)}, f32[32,8,128]{2,1,0:T(8,128)S(1)}, u32[]{:S(2)}, u32[]{:S(2)}) %collective-permute-start.9) | collective-permute-done | bytes 131104 | tf_op jit(solution)/shard_map/ppermute | solution.py:272
  22.6 1.1 %collective-permute-done.7.refs_7_ = f32[33,8,128]{2,1,0:T(8,128)S(1)} collective-permute-done((f32[33,8,128]{2,1,0:T(8,128)S(1)}, f32[33,8,128]{2,1,0:T(8,128)S(1)}, u32[]{:S(2)}, u32[]{:S(2)}) %collective-permute-start.7) | collective-permute-done | bytes 135200 | tf_op jit(solution)/shard_map/ppermute | solution.py:272
  23.8 0.8 %finish.1 = f32[32,2,512]{2,1,0:T(2,128)} custom-call(f32[33,8,128]{2,1,0:T(8,128)S(1)} %get-tuple-element.11.refs_0_, f32[33,8,128]{2,1,0:T(8,128)S(1)} %collective-permute-done.refs_2_.refs_1_, f32[33,8,128]{2,1,0:T(8,128)S(1)} %collective-permute-done.1.refs_4_.refs_2_, f32[33,8,128]{2,1,0:T(8,128)S(1)} %collective-permute-done.3.refs_4_.refs_3_, ...), custom_call_target="tpu_custom_call" | custom-call | tf_op jit(solution)/shard_map/finish/pallas_call | solution.py:230
  (7 shorter events, 0.2 us)
Async XLA Ops:
  1.7 1.5 %collective-permute-start = (f32[33,8,128]{2,1,0:T(8,128)S(1)}, f32[33,8,128]{2,1,0:T(8,128)S(1)}, u32[]{:S(2)}, u32[]{:S(2)}) collective-permute-start(f32[33,8,128]{2,1,0:T(8,128)S(1)} %get-tuple-element.11.refs_0_), channel_id=1, source_target_pairs={{0,1},{1,0},{2,3},{3,2},{4,5},{5,4},{6,7},{7,6},{8,9},{9,8},{10,11... | collective-permute-start | bytes 405512 | tf_op jit(solution)/shard_map/ppermute | solution.py:272
  2.8 3.8 %collective-permute-start.2 = (f32[128,8,128]{2,1,0:T(8,128)S(1)}, f32[128,8,128]{2,1,0:T(8,128)S(1)}, u32[]{:S(2)}, u32[]{:S(2)}) collective-permute-start(f32[128,8,128]{2,1,0:T(8,128)S(1)} %get-tuple-element.16), channel_id=1, source_target_pairs={{0,1},{1,0},{2,3},{3,2},{4,5},{5,4},{6,7},{7,6},{8,9},{9,8},{10,11... | collective-permute-start | bytes 1572872 | tf_op jit(solution)/shard_map/ppermute | solution.py:272
  3.2 5.9 %collective-permute-start.1 = (f32[33,8,128]{2,1,0:T(8,128)S(1)}, f32[33,8,128]{2,1,0:T(8,128)S(1)}, u32[]{:S(2)}, u32[]{:S(2)}) collective-permute-start(f32[33,8,128]{2,1,0:T(8,128)S(1)} %summed.7), channel_id=1, source_target_pairs={{0,2},{1,5},{2,0},{3,7},{4,6},{5,1},{6,4},{7,3},{8,10},{9,13},{10,... | collective-permute-start | bytes 405512 | tf_op jit(solution)/shard_map/ppermute | solution.py:272
  6.6 7.8 %collective-permute-start.6 = (f32[32,8,128]{2,1,0:T(8,128)S(1)}, f32[32,8,128]{2,1,0:T(8,128)S(1)}, u32[]{:S(2)}, u32[]{:S(2)}) collective-permute-start(f32[32,8,128]{2,1,0:T(8,128)S(1)} %summed.8.refs_5_), channel_id=1, source_target_pairs={{0,2},{1,5},{2,0},{3,7},{4,6},{5,1},{6,4},{7,3},{8,10},{9,13},{10,... | collective-permute-start | bytes 393224 | tf_op jit(solution)/shard_map/ppermute | solution.py:272
  9.2 5.5 %collective-permute-start.3 = (f32[33,8,128]{2,1,0:T(8,128)S(1)}, f32[33,8,128]{2,1,0:T(8,128)S(1)}, u32[]{:S(2)}, u32[]{:S(2)}) collective-permute-start(f32[33,8,128]{2,1,0:T(8,128)S(1)} %summed.9.refs_0_), channel_id=1, source_target_pairs={{0,4},{1,3},{2,6},{3,1},{4,0},{5,7},{6,2},{7,5},{8,12},{9,11},{10,... | collective-permute-start | bytes 405512 | tf_op jit(solution)/shard_map/ppermute | solution.py:272
  11.7 2.9 %collective-permute-start.4 = (f32[96,8,128]{2,1,0:T(8,128)S(1)}, f32[96,8,128]{2,1,0:T(8,128)S(1)}, u32[]{:S(2)}, u32[]{:S(2)}) collective-permute-start(f32[96,8,128]{2,1,0:T(8,128)S(1)} %next_products.6.refs_0_), channel_id=1, source_target_pairs={{0,1},{1,0},{2,3},{3,2},{4,5},{5,4},{6,7},{7,6},{8,9},{9,8},{10,11... | collective-permute-start | bytes 1179656 | tf_op jit(solution)/shard_map/ppermute | solution.py:272
  12.2 5.3 %collective-permute-start.8 = (f32[32,8,128]{2,1,0:T(8,128)S(1)}, f32[32,8,128]{2,1,0:T(8,128)S(1)}, u32[]{:S(2)}, u32[]{:S(2)}) collective-permute-start(f32[32,8,128]{2,1,0:T(8,128)S(1)} %summed.10.refs_2_), channel_id=1, source_target_pairs={{0,2},{1,5},{2,0},{3,7},{4,6},{5,1},{6,4},{7,3},{8,10},{9,13},{10,... | collective-permute-start | bytes 393224 | tf_op jit(solution)/shard_map/ppermute | solution.py:272
  13.8 5.9 %collective-permute-start.5 = (f32[32,8,128]{2,1,0:T(8,128)S(1)}, f32[32,8,128]{2,1,0:T(8,128)S(1)}, u32[]{:S(2)}, u32[]{:S(2)}) collective-permute-start(f32[32,8,128]{2,1,0:T(8,128)S(1)} %summed.11), channel_id=1, source_target_pairs={{0,2},{1,5},{2,0},{3,7},{4,6},{5,1},{6,4},{7,3},{8,10},{9,13},{10,... | collective-permute-start | bytes 393224 | tf_op jit(solution)/shard_map/ppermute | solution.py:272
  14.6 9.1 %collective-permute-start.7 = (f32[33,8,128]{2,1,0:T(8,128)S(1)}, f32[33,8,128]{2,1,0:T(8,128)S(1)}, u32[]{:S(2)}, u32[]{:S(2)}) collective-permute-start(f32[33,8,128]{2,1,0:T(8,128)S(1)} %summed.12.refs_3_), channel_id=1, source_target_pairs={{0,8},{1,9},{2,10},{3,11},{4,12},{5,13},{6,14},{7,15},{8,0},{9,1},... | collective-permute-start | bytes 405512 | tf_op jit(solution)/shard_map/ppermute | solution.py:272
  17.5 5.2 %collective-permute-start.9 = (f32[32,8,128]{2,1,0:T(8,128)S(1)}, f32[32,8,128]{2,1,0:T(8,128)S(1)}, u32[]{:S(2)}, u32[]{:S(2)}) collective-permute-start(f32[32,8,128]{2,1,0:T(8,128)S(1)} %summed.13), channel_id=1, source_target_pairs={{0,4},{1,3},{2,6},{3,1},{4,0},{5,7},{6,2},{7,5},{8,12},{9,11},{10,... | collective-permute-start | bytes 393224 | tf_op jit(solution)/shard_map/ppermute | solution.py:272

commit v24 on v22

--- a/solution.py
+++ b/solution.py
@@ -215,10 +215,10 @@
     users, blocks = out.shape[0], out.shape[2] // 128
     steps = users // 8
     scale = lax.rsqrt(add_up(refs, powers, 1)[0] + epsilon)
-    total = add_up(refs, terms, 2 * blocks * steps)
     for half in range(2):
+        total = add_up(refs, terms[half], blocks * steps)
         for block in range(blocks):
-            start = (half * blocks + block) * steps
+            start = block * steps
             value = total[start:start + steps].reshape(users, 128)
             factor = scale[block:block + 1, :]
             value = jnp.where(factor > 0.0, value * factor, 0.0)
@@ -242,16 +242,16 @@
     for step in range(chips):
         size = 1 << (chips - 1 - step)
         first = (1 << chips) - 2 * size
-        steps.append(list(range(first, first + size)))
+        steps.append([(slot, part) for slot in range(first, first + size) for part in range(2)])
     if chips < 3:
-        return [(step, slots) for step, slots in enumerate(steps)]
+        return [(step, pieces) for step, pieces in enumerate(steps)]
     quarter, half = len(steps[0]) // 4, len(steps[1]) // 2
     parts = [steps[0][at * quarter:(at + 1) * quarter] for at in range(4)]
     order = [
         (0, parts[0]),
-        (0, parts[2]),
+        (0, parts[2] + parts[1][::2]),
         (1, steps[1][:half]),
-        (0, parts[1]),
+        (0, parts[1][1::2]),
         (0, parts[3]),
         (2, steps[2]),
         (1, steps[1][half:]),
@@ -263,7 +263,7 @@
     devices = lax.axis_size("ap")
     bits = devices.bit_length() - 1
     users, columns = channel.shape[3], precoder.shape[2]
-    tiles = (users // 8) * (columns // 128) * 2
+    tiles = (users // 8) * (columns // 128)
     orders = chip_orders(bits)
     flat = precoder.reshape(-1, columns)
     half = devices // 4
@@ -272,18 +272,22 @@
         return lax.ppermute(value, "ap", [(i, i ^ (1 << bit_of[i & 1])) for i in range(devices)])
 
     arrays = []
-    terms = [[] for _ in range(2 * half)]
+    terms = {(slot, part): [] for slot in range(2 * half) for part in range(2)}
     powers = []
 
-    def add(array, slots, power):
-        for at, slot in enumerate(slots):
-            terms[slot].append((len(arrays), at * tiles))
+    def add(array, pieces, power):
+        for at, piece in enumerate(pieces):
+            terms[piece].append((len(arrays), at * tiles))
         if power:
-            powers.append((len(arrays), len(slots) * tiles))
+            powers.append((len(arrays), len(pieces) * tiles))
         arrays.append(array)
 
-    def total(slots, power, cost=8192, after=()):
-        jobs = [(list(terms[slot]), tiles) for slot in slots] + ([(list(powers), 1)] if power else [])
+    def pieces_of(first, count):
+        return [(slot, part) for slot in range(first, first + count) for part in range(2)]
+
+    def total(pieces, power, cost=8192, after=()):
+        jobs = [(list(terms[piece]), tiles) for piece in pieces]
+        jobs += [(list(powers), 1)] * int(power)
         used = sorted({array for parts, _ in jobs for array, _ in parts})
         jobs = [([(used.index(array), start) for array, start in parts], count) for parts, count in jobs]
         return summed([arrays[array] for array in used], jobs, cost, after)
@@ -292,36 +296,36 @@
     sent, rows, weights, served = first_products(bits, quarter, visible, cluster.T, channel, flat)
     came = swap(sent, (0, 0))
     add(sent, [], False)
-    powers.append((0, quarter * tiles))
+    powers.append((0, 2 * quarter * tiles))
     products = functools.partial(next_products, users, rows=rows, weights=weights, served=served)
     first, count = quarter, 4 * quarter
     send, kept = products(((0, first, count), (1, 0, quarter)), cost=COSTS[0])
-    add(kept, range(quarter), False)
-    add(came, range(quarter), True)
+    add(kept, pieces_of(0, quarter), False)
+    add(came, pieces_of(0, quarter), True)
     come = swap(send, (0, 0))
-    add(products(((1, first, count),), cost=COSTS[1])[0], range(first, first + count), False)
-    add(come, range(first, first + count), False)
+    add(products(((1, first, count),), cost=COSTS[1])[0], pieces_of(first, count), False)
+    add(come, pieces_of(first, count), False)
     with_power = set()
-    last = 2 * half - 1
-    for number, (step, slots) in enumerate(message_order(bits - 1)):
+    last = [(2 * half - 1, part) for part in range(2)]
+    for number, (step, pieces) in enumerate(message_order(bits - 1)):
         if number == 3:
             first, count = 5 * quarter, 3 * quarter
             send = products(((0, first, count),), cost=COSTS[2], after=[now])[0]
             come = swap(send, (0, 0))
             mine = products(((1, first, count),), cost=COSTS[3], after=[send])[0]
-            add(mine, range(first, first + count), False)
-            add(come, range(first, first + count), False)
+            add(mine, pieces_of(first, count), False)
+            add(come, pieces_of(first, count), False)
         power = step not in with_power
         with_power.add(step)
         after = [mine] if number == 3 else [now] if number in (2, 4, 6) else []
-        now = total(slots, power, COSTS[4 + number] if number < 7 else 8192, after)
+        now = total(pieces, power, COSTS[4 + number] if number < 7 else 8192, after)
         came = swap(now, (orders[0][step], orders[1][step]))
-        slots = [slot + (1 << (bits - 2 - step)) for slot in slots]
-        add(came, slots, power)
-    used = sorted({array for array, _ in terms[last] + powers})
+        pieces = [(slot + (1 << (bits - 2 - step)), part) for slot, part in pieces]
+        add(came, pieces, power)
+    used = sorted({array for parts in [terms[piece] for piece in last] + [powers] for array, _ in parts})
     return finish(
         [arrays[array] for array in used],
-        [(used.index(array), start) for array, start in terms[last]],
+        [[(used.index(array), start) for array, start in terms[piece]] for piece in last],
         [(used.index(array), start) for array, start in powers],
         users, columns,
     )

time: 23.5 us -> 23.5 us (level)
  no operation moved by 1% of the time
where the time goes in v24:
time: 23.5 us; the launch traced here: 23.3 us
  starting transfers between devices  13.7 us (58%)
  waiting for transfers between devices  5.18 us (22%)
  Pallas kernels  4.36 us (19%)
    ppermute x10, starting transfers between devices, swap(): lax.ppermute(value, 'ap', [(i, i ^ 1 << bit_of[i & 1]) for i in range(dev...  13.7 us
    ppermute x10, waiting for transfers between devices, swap(): lax.ppermute(value, 'ap', [(i, i ^ 1 << bit_of[i & 1]) for i in range(dev...  5.18 us
    pallas_call x4, Pallas kernels, next_products(): pl.pallas_call(functools.partial(next_kernel, users, jobs), out_shape=[me...  1.74 us
    pallas_call x1, Pallas kernels, first_products(): pl.pallas_call(functools.partial(first_kernel, bits), out_shape=(message(...  1.69 us
    pallas_call x1, Pallas kernels, finish(): pl.pallas_call(functools.partial(final_kernel, terms, powers), out_shape=...  0.78 us
  transfers between devices with their start and end apart: 10, of which 5 were waited for; matrix products, arithmetic and copies ran while one was open for 0% of the time, Pallas kernels for 8%

profile of v24, /device:TPU:0, one launch (start us, length us, event | category | flops | bytes accessed | tf_op | source)
XLA Modules:
  0.0 23.3 jit_solution(4598662592988058996)
XLA Ops:
  0.0 1.7 %first_products.1 = (f32[33,8,128]{2,1,0:T(8,128)S(1)}, bf16[2,256,1024]{2,1,0:T(8,128)(2,1)S(1)}, bf16[1024,512]{1,0:T(8,128)(2,1)S(1)}, f32[1,512]{1,0:T(1,128)S(1)}) custom-call(s32[1,12]{1,0:T(1,128)} %visible.1, s32[4,512]{1,0:T(4,128)} %bitcast.3, bf16[1,12,2,32,512]{4,3,2,1,0:T(8,128)(2,1)} %channel.1, bf16[1024,512]{1,0:T(8,128)(2,1)} %bitcast.2), custom_call_target="tpu_custom_call" | custom-call | flops 8192 | bytes 8192 | tf_op jit(solution)/shard_map/first_products/pallas_call | solution.py:148
  1.7 0.5 %collective-permute-start = (f32[33,8,128]{2,1,0:T(8,128)S(1)}, f32[33,8,128]{2,1,0:T(8,128)S(1)}, u32[]{:S(2)}, u32[]{:S(2)}) collective-permute-start(f32[33,8,128]{2,1,0:T(8,128)S(1)} %get-tuple-element.11.refs_0_), channel_id=1, source_target_pairs={{0,1},{1,0},{2,3},{3,2},{4,5},{5,4},{6,7},{7,6},{8,9},{9,8},{10,11... | collective-permute-start | bytes 405512 | tf_op jit(solution)/shard_map/ppermute | solution.py:272
  2.2 0.6 %next_products.4 = (f32[128,8,128]{2,1,0:T(8,128)S(1)}, f32[32,8,128]{2,1,0:T(8,128)S(1)}) custom-call(bf16[2,256,1024]{2,1,0:T(8,128)(2,1)S(1)} %get-tuple-element.12.rows, bf16[1024,512]{1,0:T(8,128)(2,1)S(1)} %get-tuple-element.13.weights, f32[1,512]{1,0:T(1,128)S(1)} %get-tuple-element.14.served), custom_call_target="tpu_custom_call" | custom-call | flops 67108864 | bytes 67108864 | tf_op jit(solution)/shard_map/next_products/pallas_call | solution.py:174
  2.8 0.1 collective-permute-start.2
  2.9 0.3 %collective-permute-done.refs_2_.refs_1_ = f32[33,8,128]{2,1,0:T(8,128)S(1)} collective-permute-done((f32[33,8,128]{2,1,0:T(8,128)S(1)}, f32[33,8,128]{2,1,0:T(8,128)S(1)}, u32[]{:S(2)}, u32[]{:S(2)}) %collective-permute-start) | collective-permute-done | bytes 135200 | tf_op jit(solution)/shard_map/ppermute | solution.py:272
  3.2 3.0 %collective-permute-start.1 = (f32[33,8,128]{2,1,0:T(8,128)S(1)}, f32[33,8,128]{2,1,0:T(8,128)S(1)}, u32[]{:S(2)}, u32[]{:S(2)}) collective-permute-start(f32[33,8,128]{2,1,0:T(8,128)S(1)} %summed.7), channel_id=1, source_target_pairs={{0,4},{1,3},{2,6},{3,1},{4,0},{5,7},{6,2},{7,5},{8,12},{9,11},{10,... | collective-permute-start | bytes 405512 | tf_op jit(solution)/shard_map/ppermute | solution.py:272
  6.2 0.4 %next_products.5.refs_0_.refs_2_ = f32[128,8,128]{2,1,0:T(8,128)S(1)} custom-call(bf16[2,256,1024]{2,1,0:T(8,128)(2,1)S(1)} %get-tuple-element.12.rows, bf16[1024,512]{1,0:T(8,128)(2,1)S(1)} %get-tuple-element.13.weights, f32[1,512]{1,0:T(1,128)S(1)} %get-tuple-element.14.served), custom_call_target="tpu_custom_call" | custom-call | flops 8589934592 | bytes 8589934592 | tf_op jit(solution)/shard_map/next_products/pallas_call | solution.py:174
  6.7 0.0 collective-permute-done.2.refs_1_.refs_3_
  6.7 0.9 %collective-permute-start.6 = (f32[48,8,128]{2,1,0:T(8,128)S(1)}, f32[48,8,128]{2,1,0:T(8,128)S(1)}, u32[]{:S(2)}, u32[]{:S(2)}) collective-permute-start(f32[48,8,128]{2,1,0:T(8,128)S(1)} %summed.8.refs_5_), channel_id=1, source_target_pairs={{0,4},{1,3},{2,6},{3,1},{4,0},{5,7},{6,2},{7,5},{8,12},{9,11},{10,... | collective-permute-start | bytes 589832 | tf_op jit(solution)/shard_map/ppermute | solution.py:272
  7.6 1.6 %collective-permute-done.1.refs_4_.refs_2_ = f32[33,8,128]{2,1,0:T(8,128)S(1)} collective-permute-done((f32[33,8,128]{2,1,0:T(8,128)S(1)}, f32[33,8,128]{2,1,0:T(8,128)S(1)}, u32[]{:S(2)}, u32[]{:S(2)}) %collective-permute-start.1) | collective-permute-done | bytes 135200 | tf_op jit(solution)/shard_map/ppermute | solution.py:272
  9.2 2.0 %collective-permute-start.3 = (f32[33,8,128]{2,1,0:T(8,128)S(1)}, f32[33,8,128]{2,1,0:T(8,128)S(1)}, u32[]{:S(2)}, u32[]{:S(2)}) collective-permute-start(f32[33,8,128]{2,1,0:T(8,128)S(1)} %summed.9.refs_0_), channel_id=1, source_target_pairs={{0,2},{1,5},{2,0},{3,7},{4,6},{5,1},{6,4},{7,3},{8,10},{9,13},{10,... | collective-permute-start | bytes 405512 | tf_op jit(solution)/shard_map/ppermute | solution.py:272
  11.2 0.4 %next_products.6.refs_0_ = f32[96,8,128]{2,1,0:T(8,128)S(1)} custom-call(bf16[2,256,1024]{2,1,0:T(8,128)(2,1)S(1)} %get-tuple-element.12.rows, bf16[1024,512]{1,0:T(8,128)(2,1)S(1)} %get-tuple-element.13.weights, f32[1,512]{1,0:T(1,128)S(1)} %get-tuple-element.14.served, f32[33,8,128]{2,1,0:T(8,128)S(1)} %summed.9.refs_0_), custom_call_target="tpu_custom_call" | custom-call | flops 67108864 | bytes 67108864 | tf_op jit(solution)/shard_map/next_products/pallas_call | solution.py:174
  11.6 0.1 collective-permute-start.4
  11.7 0.4 %next_products.7.refs_2_.refs_5_.refs_1_.refs_4_ = f32[96,8,128]{2,1,0:T(8,128)S(1)} custom-call(bf16[2,256,1024]{2,1,0:T(8,128)(2,1)S(1)} %get-tuple-element.12.rows, bf16[1024,512]{1,0:T(8,128)(2,1)S(1)} %get-tuple-element.13.weights, f32[1,512]{1,0:T(1,128)S(1)} %get-tuple-element.14.served, f32[96,8,128]{2,1,0:T(8,128)S(1)} %next_products.6.refs_0_), custom_call_target="tpu_custom_call" | custom-call | flops 68719476736 | bytes 68719476736 | tf_op jit(solution)/shard_map/next_products/pallas_call | solution.py:174
  12.1 1.6 %collective-permute-start.8 = (f32[16,8,128]{2,1,0:T(8,128)S(1)}, f32[16,8,128]{2,1,0:T(8,128)S(1)}, u32[]{:S(2)}, u32[]{:S(2)}) collective-permute-start(f32[16,8,128]{2,1,0:T(8,128)S(1)} %summed.10.refs_2_), channel_id=1, source_target_pairs={{0,4},{1,3},{2,6},{3,1},{4,0},{5,7},{6,2},{7,5},{8,12},{9,11},{10,... | collective-permute-start | bytes 196616 | tf_op jit(solution)/shard_map/ppermute | solution.py:272
  13.8 0.5 %collective-permute-start.5 = (f32[32,8,128]{2,1,0:T(8,128)S(1)}, f32[32,8,128]{2,1,0:T(8,128)S(1)}, u32[]{:S(2)}, u32[]{:S(2)}) collective-permute-start(f32[32,8,128]{2,1,0:T(8,128)S(1)} %summed.11), channel_id=1, source_target_pairs={{0,4},{1,3},{2,6},{3,1},{4,0},{5,7},{6,2},{7,5},{8,12},{9,11},{10,... | collective-permute-start | bytes 393224 | tf_op jit(solution)/shard_map/ppermute | solution.py:272
  14.3 0.2 collective-permute-done.3.refs_4_.refs_3_
  14.5 0.0 collective-permute-done.6.refs_3_.refs_0_
  14.5 0.0 collective-permute-done.4.refs_6_.refs_2_.refs_5_
  14.5 2.9 %collective-permute-start.7 = (f32[33,8,128]{2,1,0:T(8,128)S(1)}, f32[33,8,128]{2,1,0:T(8,128)S(1)}, u32[]{:S(2)}, u32[]{:S(2)}) collective-permute-start(f32[33,8,128]{2,1,0:T(8,128)S(1)} %summed.12.refs_4_), channel_id=1, source_target_pairs={{0,8},{1,9},{2,10},{3,11},{4,12},{5,13},{6,14},{7,15},{8,0},{9,1},... | collective-permute-start | bytes 405512 | tf_op jit(solution)/shard_map/ppermute | solution.py:272
  17.5 0.0 collective-permute-done.8.refs_3_
  17.5 2.0 %collective-permute-start.9 = (f32[32,8,128]{2,1,0:T(8,128)S(1)}, f32[32,8,128]{2,1,0:T(8,128)S(1)}, u32[]{:S(2)}, u32[]{:S(2)}) collective-permute-start(f32[32,8,128]{2,1,0:T(8,128)S(1)} %summed.13), channel_id=1, source_target_pairs={{0,2},{1,5},{2,0},{3,7},{4,6},{5,1},{6,4},{7,3},{8,10},{9,13},{10,... | collective-permute-start | bytes 393224 | tf_op jit(solution)/shard_map/ppermute | solution.py:272
  19.5 1.6 %collective-permute-done.5.refs_6_ = f32[32,8,128]{2,1,0:T(8,128)S(1)} collective-permute-done((f32[32,8,128]{2,1,0:T(8,128)S(1)}, f32[32,8,128]{2,1,0:T(8,128)S(1)}, u32[]{:S(2)}, u32[]{:S(2)}) %collective-permute-start.5) | collective-permute-done | bytes 131104 | tf_op jit(solution)/shard_map/ppermute | solution.py:272
  21.1 1.4 %collective-permute-done.9.refs_8_ = f32[32,8,128]{2,1,0:T(8,128)S(1)} collective-permute-done((f32[32,8,128]{2,1,0:T(8,128)S(1)}, f32[32,8,128]{2,1,0:T(8,128)S(1)}, u32[]{:S(2)}, u32[]{:S(2)}) %collective-permute-start.9) | collective-permute-done | bytes 131104 | tf_op jit(solution)/shard_map/ppermute | solution.py:272
  22.5 0.0 collective-permute-done.7.refs_7_
  22.5 0.8 %finish.1 = f32[32,2,512]{2,1,0:T(2,128)} custom-call(f32[33,8,128]{2,1,0:T(8,128)S(1)} %get-tuple-element.11.refs_0_, f32[33,8,128]{2,1,0:T(8,128)S(1)} %collective-permute-done.refs_2_.refs_1_, f32[33,8,128]{2,1,0:T(8,128)S(1)} %collective-permute-done.1.refs_4_.refs_2_, f32[33,8,128]{2,1,0:T(8,128)S(1)} %collective-permute-done.3.refs_4_.refs_3_, ...), custom_call_target="tpu_custom_call" | custom-call | tf_op jit(solution)/shard_map/finish/pallas_call | solution.py:230
  (7 shorter events, 0.1 us)
Async XLA Ops:
  1.7 1.5 %collective-permute-start = (f32[33,8,128]{2,1,0:T(8,128)S(1)}, f32[33,8,128]{2,1,0:T(8,128)S(1)}, u32[]{:S(2)}, u32[]{:S(2)}) collective-permute-start(f32[33,8,128]{2,1,0:T(8,128)S(1)} %get-tuple-element.11.refs_0_), channel_id=1, source_target_pairs={{0,1},{1,0},{2,3},{3,2},{4,5},{5,4},{6,7},{7,6},{8,9},{9,8},{10,11... | collective-permute-start | bytes 405512 | tf_op jit(solution)/shard_map/ppermute | solution.py:272
  2.8 3.9 %collective-permute-start.2 = (f32[128,8,128]{2,1,0:T(8,128)S(1)}, f32[128,8,128]{2,1,0:T(8,128)S(1)}, u32[]{:S(2)}, u32[]{:S(2)}) collective-permute-start(f32[128,8,128]{2,1,0:T(8,128)S(1)} %get-tuple-element.16), channel_id=1, source_target_pairs={{0,1},{1,0},{2,3},{3,2},{4,5},{5,4},{6,7},{7,6},{8,9},{9,8},{10,11... | collective-permute-start | bytes 1572872 | tf_op jit(solution)/shard_map/ppermute | solution.py:272
  3.2 6.0 %collective-permute-start.1 = (f32[33,8,128]{2,1,0:T(8,128)S(1)}, f32[33,8,128]{2,1,0:T(8,128)S(1)}, u32[]{:S(2)}, u32[]{:S(2)}) collective-permute-start(f32[33,8,128]{2,1,0:T(8,128)S(1)} %summed.7), channel_id=1, source_target_pairs={{0,4},{1,3},{2,6},{3,1},{4,0},{5,7},{6,2},{7,5},{8,12},{9,11},{10,... | collective-permute-start | bytes 405512 | tf_op jit(solution)/shard_map/ppermute | solution.py:272
  6.7 7.8 %collective-permute-start.6 = (f32[48,8,128]{2,1,0:T(8,128)S(1)}, f32[48,8,128]{2,1,0:T(8,128)S(1)}, u32[]{:S(2)}, u32[]{:S(2)}) collective-permute-start(f32[48,8,128]{2,1,0:T(8,128)S(1)} %summed.8.refs_5_), channel_id=1, source_target_pairs={{0,4},{1,3},{2,6},{3,1},{4,0},{5,7},{6,2},{7,5},{8,12},{9,11},{10,... | collective-permute-start | bytes 589832 | tf_op jit(solution)/shard_map/ppermute | solution.py:272
  9.2 5.3 %collective-permute-start.3 = (f32[33,8,128]{2,1,0:T(8,128)S(1)}, f32[33,8,128]{2,1,0:T(8,128)S(1)}, u32[]{:S(2)}, u32[]{:S(2)}) collective-permute-start(f32[33,8,128]{2,1,0:T(8,128)S(1)} %summed.9.refs_0_), channel_id=1, source_target_pairs={{0,2},{1,5},{2,0},{3,7},{4,6},{5,1},{6,4},{7,3},{8,10},{9,13},{10,... | collective-permute-start | bytes 405512 | tf_op jit(solution)/shard_map/ppermute | solution.py:272
  11.6 2.9 %collective-permute-start.4 = (f32[96,8,128]{2,1,0:T(8,128)S(1)}, f32[96,8,128]{2,1,0:T(8,128)S(1)}, u32[]{:S(2)}, u32[]{:S(2)}) collective-permute-start(f32[96,8,128]{2,1,0:T(8,128)S(1)} %next_products.6.refs_0_), channel_id=1, source_target_pairs={{0,1},{1,0},{2,3},{3,2},{4,5},{5,4},{6,7},{7,6},{8,9},{9,8},{10,11... | collective-permute-start | bytes 1179656 | tf_op jit(solution)/shard_map/ppermute | solution.py:272
  12.1 5.4 %collective-permute-start.8 = (f32[16,8,128]{2,1,0:T(8,128)S(1)}, f32[16,8,128]{2,1,0:T(8,128)S(1)}, u32[]{:S(2)}, u32[]{:S(2)}) collective-permute-start(f32[16,8,128]{2,1,0:T(8,128)S(1)} %summed.10.refs_2_), channel_id=1, source_target_pairs={{0,4},{1,3},{2,6},{3,1},{4,0},{5,7},{6,2},{7,5},{8,12},{9,11},{10,... | collective-permute-start | bytes 196616 | tf_op jit(solution)/shard_map/ppermute | solution.py:272
  13.8 7.3 %collective-permute-start.5 = (f32[32,8,128]{2,1,0:T(8,128)S(1)}, f32[32,8,128]{2,1,0:T(8,128)S(1)}, u32[]{:S(2)}, u32[]{:S(2)}) collective-permute-start(f32[32,8,128]{2,1,0:T(8,128)S(1)} %summed.11), channel_id=1, source_target_pairs={{0,4},{1,3},{2,6},{3,1},{4,0},{5,7},{6,2},{7,5},{8,12},{9,11},{10,... | collective-permute-start | bytes 393224 | tf_op jit(solution)/shard_map/ppermute | solution.py:272
  14.5 8.0 %collective-permute-start.7 = (f32[33,8,128]{2,1,0:T(8,128)S(1)}, f32[33,8,128]{2,1,0:T(8,128)S(1)}, u32[]{:S(2)}, u32[]{:S(2)}) collective-permute-start(f32[33,8,128]{2,1,0:T(8,128)S(1)} %summed.12.refs_4_), channel_id=1, source_target_pairs={{0,8},{1,9},{2,10},{3,11},{4,12},{5,13},{6,14},{7,15},{8,0},{9,1},... | collective-permute-start | bytes 405512 | tf_op jit(solution)/shard_map/ppermute | solution.py:272
  17.5 5.0 %collective-permute-start.9 = (f32[32,8,128]{2,1,0:T(8,128)S(1)}, f32[32,8,128]{2,1,0:T(8,128)S(1)}, u32[]{:S(2)}, u32[]{:S(2)}) collective-permute-start(f32[32,8,128]{2,1,0:T(8,128)S(1)} %summed.13), channel_id=1, source_target_pairs={{0,2},{1,5},{2,0},{3,7},{4,6},{5,1},{6,4},{7,3},{8,10},{9,13},{10,... | collective-permute-start | bytes 393224 | tf_op jit(solution)/shard_map/ppermute | solution.py:272

commit v25 on v21

--- a/solution.py
+++ b/solution.py
@@ -249,9 +249,9 @@
     parts = [steps[0][at * quarter:(at + 1) * quarter] for at in range(4)]
     order = [
         (0, parts[0]),
-        (0, parts[2]),
+        (0, parts[1] + parts[2]),
         (1, steps[1][:half]),
-        (0, parts[1] + parts[3]),
+        (0, parts[3]),
         (2, steps[2]),
         (1, steps[1][half:]),
     ]

time: 26.8 us -> 25 us (0.933)
  waiting for transfers between devices: 11 us -> 7.31 us
  starting transfers between devices: 11.2 us -> 13.1 us
    ppermute x9, waiting for transfers between devices: 11 us -> 7.31 us  [swap(): lax.ppermute(value, 'ap', [(i, i ^ 1 << bit_of[i & 1]) for i in range(dev...]
    ppermute x9, starting transfers between devices: 11.2 us -> 13.1 us  [swap(): lax.ppermute(value, 'ap', [(i, i ^ 1 << bit_of[i & 1]) for i in range(dev...]
  transfers between devices with their start and end apart: 9 -> 9, of which waited for: 5 -> 6; matrix products, arithmetic and copies ran while one was open for 0% -> 0% of each run, Pallas kernels for 7% -> 8%
where the time goes in v25:
time: 25 us; the launch traced here: 24.8 us
  starting transfers between devices  13.1 us (52%)
  waiting for transfers between devices  7.31 us (29%)
  Pallas kernels  4.36 us (17%)
    ppermute x9, starting transfers between devices, swap(): lax.ppermute(value, 'ap', [(i, i ^ 1 << bit_of[i & 1]) for i in range(dev...  13.1 us
    ppermute x9, waiting for transfers between devices, swap(): lax.ppermute(value, 'ap', [(i, i ^ 1 << bit_of[i & 1]) for i in range(dev...  7.31 us
    pallas_call x4, Pallas kernels, next_products(): pl.pallas_call(functools.partial(next_kernel, users, jobs), out_shape=[me...  1.74 us
    pallas_call x1, Pallas kernels, first_products(): pl.pallas_call(functools.partial(first_kernel, bits), out_shape=(message(...  1.69 us
    pallas_call x1, Pallas kernels, finish(): pl.pallas_call(functools.partial(final_kernel, terms, powers), out_shape=...  0.77 us
  transfers between devices with their start and end apart: 9, of which 6 were waited for; matrix products, arithmetic and copies ran while one was open for 0% of the time, Pallas kernels for 8%

profile of v25, /device:TPU:0, one launch (start us, length us, event | category | flops | bytes accessed | tf_op | source)
XLA Modules:
  0.0 24.8 jit_solution(9865032570921498135)
XLA Ops:
  0.0 1.7 %first_products.1 = (f32[33,8,128]{2,1,0:T(8,128)S(1)}, bf16[2,256,1024]{2,1,0:T(8,128)(2,1)S(1)}, bf16[1024,512]{1,0:T(8,128)(2,1)S(1)}, f32[1,512]{1,0:T(1,128)S(1)}) custom-call(s32[1,12]{1,0:T(1,128)} %visible.1, s32[4,512]{1,0:T(4,128)} %bitcast.3, bf16[1,12,2,32,512]{4,3,2,1,0:T(8,128)(2,1)} %channel.1, bf16[1024,512]{1,0:T(8,128)(2,1)} %bitcast.2), custom_call_target="tpu_custom_call" | custom-call | flops 8192 | bytes 8192 | tf_op jit(solution)/shard_map/first_products/pallas_call | solution.py:148
  1.7 0.5 %collective-permute-start = (f32[33,8,128]{2,1,0:T(8,128)S(1)}, f32[33,8,128]{2,1,0:T(8,128)S(1)}, u32[]{:S(2)}, u32[]{:S(2)}) collective-permute-start(f32[33,8,128]{2,1,0:T(8,128)S(1)} %get-tuple-element.11.refs_0_), channel_id=1, source_target_pairs={{0,1},{1,0},{2,3},{3,2},{4,5},{5,4},{6,7},{7,6},{8,9},{9,8},{10,11... | collective-permute-start | bytes 405512 | tf_op jit(solution)/shard_map/ppermute | solution.py:271
  2.2 0.6 %next_products.4 = (f32[128,8,128]{2,1,0:T(8,128)S(1)}, f32[32,8,128]{2,1,0:T(8,128)S(1)}) custom-call(bf16[2,256,1024]{2,1,0:T(8,128)(2,1)S(1)} %get-tuple-element.12.rows, bf16[1024,512]{1,0:T(8,128)(2,1)S(1)} %get-tuple-element.13.weights, f32[1,512]{1,0:T(1,128)S(1)} %get-tuple-element.14.served), custom_call_target="tpu_custom_call" | custom-call | flops 67108864 | bytes 67108864 | tf_op jit(solution)/shard_map/next_products/pallas_call | solution.py:174
  2.8 0.1 collective-permute-start.2
  2.9 0.3 %collective-permute-done.refs_2_.refs_1_ = f32[33,8,128]{2,1,0:T(8,128)S(1)} collective-permute-done((f32[33,8,128]{2,1,0:T(8,128)S(1)}, f32[33,8,128]{2,1,0:T(8,128)S(1)}, u32[]{:S(2)}, u32[]{:S(2)}) %collective-permute-start) | collective-permute-done | bytes 135200 | tf_op jit(solution)/shard_map/ppermute | solution.py:271
  3.2 3.0 %collective-permute-start.1 = (f32[33,8,128]{2,1,0:T(8,128)S(1)}, f32[33,8,128]{2,1,0:T(8,128)S(1)}, u32[]{:S(2)}, u32[]{:S(2)}) collective-permute-start(f32[33,8,128]{2,1,0:T(8,128)S(1)} %summed.6), channel_id=1, source_target_pairs={{0,4},{1,3},{2,6},{3,1},{4,0},{5,7},{6,2},{7,5},{8,12},{9,11},{10,... | collective-permute-start | bytes 405512 | tf_op jit(solution)/shard_map/ppermute | solution.py:271
  6.2 0.4 %next_products.5.refs_0_.refs_2_ = f32[128,8,128]{2,1,0:T(8,128)S(1)} custom-call(bf16[2,256,1024]{2,1,0:T(8,128)(2,1)S(1)} %get-tuple-element.12.rows, bf16[1024,512]{1,0:T(8,128)(2,1)S(1)} %get-tuple-element.13.weights, f32[1,512]{1,0:T(1,128)S(1)} %get-tuple-element.14.served), custom_call_target="tpu_custom_call" | custom-call | flops 8589934592 | bytes 8589934592 | tf_op jit(solution)/shard_map/next_products/pallas_call | solution.py:174
  6.7 0.0 collective-permute-done.2.refs_1_.refs_3_
  6.7 0.9 %collective-permute-start.6 = (f32[64,8,128]{2,1,0:T(8,128)S(1)}, f32[64,8,128]{2,1,0:T(8,128)S(1)}, u32[]{:S(2)}, u32[]{:S(2)}) collective-permute-start(f32[64,8,128]{2,1,0:T(8,128)S(1)} %summed.7.refs_5_), channel_id=1, source_target_pairs={{0,4},{1,3},{2,6},{3,1},{4,0},{5,7},{6,2},{7,5},{8,12},{9,11},{10,... | collective-permute-start | bytes 786440 | tf_op jit(solution)/shard_map/ppermute | solution.py:271
  7.6 1.6 %collective-permute-done.1.refs_4_.refs_2_ = f32[33,8,128]{2,1,0:T(8,128)S(1)} collective-permute-done((f32[33,8,128]{2,1,0:T(8,128)S(1)}, f32[33,8,128]{2,1,0:T(8,128)S(1)}, u32[]{:S(2)}, u32[]{:S(2)}) %collective-permute-start.1) | collective-permute-done | bytes 135200 | tf_op jit(solution)/shard_map/ppermute | solution.py:271
  9.2 2.0 %collective-permute-start.3 = (f32[33,8,128]{2,1,0:T(8,128)S(1)}, f32[33,8,128]{2,1,0:T(8,128)S(1)}, u32[]{:S(2)}, u32[]{:S(2)}) collective-permute-start(f32[33,8,128]{2,1,0:T(8,128)S(1)} %summed.8.refs_0_), channel_id=1, source_target_pairs={{0,2},{1,5},{2,0},{3,7},{4,6},{5,1},{6,4},{7,3},{8,10},{9,13},{10,... | collective-permute-start | bytes 405512 | tf_op jit(solution)/shard_map/ppermute | solution.py:271
  11.2 0.4 %next_products.6.refs_0_ = f32[96,8,128]{2,1,0:T(8,128)S(1)} custom-call(bf16[2,256,1024]{2,1,0:T(8,128)(2,1)S(1)} %get-tuple-element.12.rows, bf16[1024,512]{1,0:T(8,128)(2,1)S(1)} %get-tuple-element.13.weights, f32[1,512]{1,0:T(1,128)S(1)} %get-tuple-element.14.served, f32[33,8,128]{2,1,0:T(8,128)S(1)} %summed.8.refs_0_), custom_call_target="tpu_custom_call" | custom-call | flops 67108864 | bytes 67108864 | tf_op jit(solution)/shard_map/next_products/pallas_call | solution.py:174
  11.6 0.1 collective-permute-start.4
  11.7 0.4 %next_products.7.refs_2_.refs_5_.refs_1_.refs_4_ = f32[96,8,128]{2,1,0:T(8,128)S(1)} custom-call(bf16[2,256,1024]{2,1,0:T(8,128)(2,1)S(1)} %get-tuple-element.12.rows, bf16[1024,512]{1,0:T(8,128)(2,1)S(1)} %get-tuple-element.13.weights, f32[1,512]{1,0:T(1,128)S(1)} %get-tuple-element.14.served, f32[96,8,128]{2,1,0:T(8,128)S(1)} %next_products.6.refs_0_), custom_call_target="tpu_custom_call" | custom-call | flops 68719476736 | bytes 68719476736 | tf_op jit(solution)/shard_map/next_products/pallas_call | solution.py:174
  12.1 1.6 %collective-permute-start.5 = (f32[32,8,128]{2,1,0:T(8,128)S(1)}, f32[32,8,128]{2,1,0:T(8,128)S(1)}, u32[]{:S(2)}, u32[]{:S(2)}) collective-permute-start(f32[32,8,128]{2,1,0:T(8,128)S(1)} %summed.9), channel_id=1, source_target_pairs={{0,4},{1,3},{2,6},{3,1},{4,0},{5,7},{6,2},{7,5},{8,12},{9,11},{10,... | collective-permute-start | bytes 393224 | tf_op jit(solution)/shard_map/ppermute | solution.py:271
  13.7 0.8 %collective-permute-done.3.refs_4_.refs_3_ = f32[33,8,128]{2,1,0:T(8,128)S(1)} collective-permute-done((f32[33,8,128]{2,1,0:T(8,128)S(1)}, f32[33,8,128]{2,1,0:T(8,128)S(1)}, u32[]{:S(2)}, u32[]{:S(2)}) %collective-permute-start.3) | collective-permute-done | bytes 135200 | tf_op jit(solution)/shard_map/ppermute | solution.py:271
  14.5 0.1 collective-permute-done.6.refs_3_.refs_0_
  14.6 0.0 collective-permute-done.4.refs_6_.refs_2_.refs_5_
  14.6 2.8 %collective-permute-start.7 = (f32[33,8,128]{2,1,0:T(8,128)S(1)}, f32[33,8,128]{2,1,0:T(8,128)S(1)}, u32[]{:S(2)}, u32[]{:S(2)}) collective-permute-start(f32[33,8,128]{2,1,0:T(8,128)S(1)} %summed.10.refs_3_), channel_id=1, source_target_pairs={{0,8},{1,9},{2,10},{3,11},{4,12},{5,13},{6,14},{7,15},{8,0},{9,1},... | collective-permute-start | bytes 405512 | tf_op jit(solution)/shard_map/ppermute | solution.py:271
  17.5 2.0 %collective-permute-start.8 = (f32[32,8,128]{2,1,0:T(8,128)S(1)}, f32[32,8,128]{2,1,0:T(8,128)S(1)}, u32[]{:S(2)}, u32[]{:S(2)}) collective-permute-start(f32[32,8,128]{2,1,0:T(8,128)S(1)} %summed.11), channel_id=1, source_target_pairs={{0,2},{1,5},{2,0},{3,7},{4,6},{5,1},{6,4},{7,3},{8,10},{9,13},{10,... | collective-permute-start | bytes 393224 | tf_op jit(solution)/shard_map/ppermute | solution.py:271
  19.5 0.0 collective-permute-done.5.refs_6_
  19.5 3.0 %collective-permute-done.8.refs_8_ = f32[32,8,128]{2,1,0:T(8,128)S(1)} collective-permute-done((f32[32,8,128]{2,1,0:T(8,128)S(1)}, f32[32,8,128]{2,1,0:T(8,128)S(1)}, u32[]{:S(2)}, u32[]{:S(2)}) %collective-permute-start.8) | collective-permute-done | bytes 131104 | tf_op jit(solution)/shard_map/ppermute | solution.py:271
  22.5 1.5 %collective-permute-done.7.refs_7_ = f32[33,8,128]{2,1,0:T(8,128)S(1)} collective-permute-done((f32[33,8,128]{2,1,0:T(8,128)S(1)}, f32[33,8,128]{2,1,0:T(8,128)S(1)}, u32[]{:S(2)}, u32[]{:S(2)}) %collective-permute-start.7) | collective-permute-done | bytes 135200 | tf_op jit(solution)/shard_map/ppermute | solution.py:271
  24.0 0.8 %finish.1 = f32[32,2,512]{2,1,0:T(2,128)} custom-call(f32[33,8,128]{2,1,0:T(8,128)S(1)} %get-tuple-element.11.refs_0_, f32[33,8,128]{2,1,0:T(8,128)S(1)} %collective-permute-done.refs_2_.refs_1_, f32[33,8,128]{2,1,0:T(8,128)S(1)} %collective-permute-done.1.refs_4_.refs_2_, f32[33,8,128]{2,1,0:T(8,128)S(1)} %collective-permute-done.3.refs_4_.refs_3_, ...), custom_call_target="tpu_custom_call" | custom-call | tf_op jit(solution)/shard_map/finish/pallas_call | solution.py:230
  (6 shorter events, 0.2 us)
Async XLA Ops:
  1.7 1.5 %collective-permute-start = (f32[33,8,128]{2,1,0:T(8,128)S(1)}, f32[33,8,128]{2,1,0:T(8,128)S(1)}, u32[]{:S(2)}, u32[]{:S(2)}) collective-permute-start(f32[33,8,128]{2,1,0:T(8,128)S(1)} %get-tuple-element.11.refs_0_), channel_id=1, source_target_pairs={{0,1},{1,0},{2,3},{3,2},{4,5},{5,4},{6,7},{7,6},{8,9},{9,8},{10,11... | collective-permute-start | bytes 405512 | tf_op jit(solution)/shard_map/ppermute | solution.py:271
  2.8 3.9 %collective-permute-start.2 = (f32[128,8,128]{2,1,0:T(8,128)S(1)}, f32[128,8,128]{2,1,0:T(8,128)S(1)}, u32[]{:S(2)}, u32[]{:S(2)}) collective-permute-start(f32[128,8,128]{2,1,0:T(8,128)S(1)} %get-tuple-element.16), channel_id=1, source_target_pairs={{0,1},{1,0},{2,3},{3,2},{4,5},{5,4},{6,7},{7,6},{8,9},{9,8},{10,11... | collective-permute-start | bytes 1572872 | tf_op jit(solution)/shard_map/ppermute | solution.py:271
  3.2 6.0 %collective-permute-start.1 = (f32[33,8,128]{2,1,0:T(8,128)S(1)}, f32[33,8,128]{2,1,0:T(8,128)S(1)}, u32[]{:S(2)}, u32[]{:S(2)}) collective-permute-start(f32[33,8,128]{2,1,0:T(8,128)S(1)} %summed.6), channel_id=1, source_target_pairs={{0,4},{1,3},{2,6},{3,1},{4,0},{5,7},{6,2},{7,5},{8,12},{9,11},{10,... | collective-permute-start | bytes 405512 | tf_op jit(solution)/shard_map/ppermute | solution.py:271
  6.7 7.9 %collective-permute-start.6 = (f32[64,8,128]{2,1,0:T(8,128)S(1)}, f32[64,8,128]{2,1,0:T(8,128)S(1)}, u32[]{:S(2)}, u32[]{:S(2)}) collective-permute-start(f32[64,8,128]{2,1,0:T(8,128)S(1)} %summed.7.refs_5_), channel_id=1, source_target_pairs={{0,4},{1,3},{2,6},{3,1},{4,0},{5,7},{6,2},{7,5},{8,12},{9,11},{10,... | collective-permute-start | bytes 786440 | tf_op jit(solution)/shard_map/ppermute | solution.py:271
  9.2 5.3 %collective-permute-start.3 = (f32[33,8,128]{2,1,0:T(8,128)S(1)}, f32[33,8,128]{2,1,0:T(8,128)S(1)}, u32[]{:S(2)}, u32[]{:S(2)}) collective-permute-start(f32[33,8,128]{2,1,0:T(8,128)S(1)} %summed.8.refs_0_), channel_id=1, source_target_pairs={{0,2},{1,5},{2,0},{3,7},{4,6},{5,1},{6,4},{7,3},{8,10},{9,13},{10,... | collective-permute-start | bytes 405512 | tf_op jit(solution)/shard_map/ppermute | solution.py:271
  11.6 3.0 %collective-permute-start.4 = (f32[96,8,128]{2,1,0:T(8,128)S(1)}, f32[96,8,128]{2,1,0:T(8,128)S(1)}, u32[]{:S(2)}, u32[]{:S(2)}) collective-permute-start(f32[96,8,128]{2,1,0:T(8,128)S(1)} %next_products.6.refs_0_), channel_id=1, source_target_pairs={{0,1},{1,0},{2,3},{3,2},{4,5},{5,4},{6,7},{7,6},{8,9},{9,8},{10,11... | collective-permute-start | bytes 1179656 | tf_op jit(solution)/shard_map/ppermute | solution.py:271
  12.1 7.4 %collective-permute-start.5 = (f32[32,8,128]{2,1,0:T(8,128)S(1)}, f32[32,8,128]{2,1,0:T(8,128)S(1)}, u32[]{:S(2)}, u32[]{:S(2)}) collective-permute-start(f32[32,8,128]{2,1,0:T(8,128)S(1)} %summed.9), channel_id=1, source_target_pairs={{0,4},{1,3},{2,6},{3,1},{4,0},{5,7},{6,2},{7,5},{8,12},{9,11},{10,... | collective-permute-start | bytes 393224 | tf_op jit(solution)/shard_map/ppermute | solution.py:271
  14.6 9.4 %collective-permute-start.7 = (f32[33,8,128]{2,1,0:T(8,128)S(1)}, f32[33,8,128]{2,1,0:T(8,128)S(1)}, u32[]{:S(2)}, u32[]{:S(2)}) collective-permute-start(f32[33,8,128]{2,1,0:T(8,128)S(1)} %summed.10.refs_3_), channel_id=1, source_target_pairs={{0,8},{1,9},{2,10},{3,11},{4,12},{5,13},{6,14},{7,15},{8,0},{9,1},... | collective-permute-start | bytes 405512 | tf_op jit(solution)/shard_map/ppermute | solution.py:271
  17.5 5.0 %collective-permute-start.8 = (f32[32,8,128]{2,1,0:T(8,128)S(1)}, f32[32,8,128]{2,1,0:T(8,128)S(1)}, u32[]{:S(2)}, u32[]{:S(2)}) collective-permute-start(f32[32,8,128]{2,1,0:T(8,128)S(1)} %summed.11), channel_id=1, source_target_pairs={{0,2},{1,5},{2,0},{3,7},{4,6},{5,1},{6,4},{7,3},{8,10},{9,13},{10,... | collective-permute-start | bytes 393224 | tf_op jit(solution)/shard_map/ppermute | solution.py:271

commit v26 on v25

--- a/solution.py
+++ b/solution.py
@@ -312,9 +312,11 @@
             add(come, range(first, first + count), False)
         power = step not in with_power
         with_power.add(step)
-        after = [mine] if number == 3 else [now] if number in (2, 5) else []
+        after = [mine] if number == 3 else [now, came_late] if number == 5 else [now] if number == 2 else []
         now = total(slots, power, COSTS[4 + number] if number < 6 else 8192, after)
         came = swap(now, (orders[0][step], orders[1][step]))
+        if number == 3:
+            came_late = came
         slots = [slot + (1 << (bits - 2 - step)) for slot in slots]
         add(came, slots, power)
     used = sorted({array for array, _ in terms[last] + powers})

time: 25 us -> 25 us (level)
  no operation moved by 1% of the time
where the time goes in v26:
time: 25 us; the launch traced here: 24.8 us
  starting transfers between devices  13.1 us (52%)
  waiting for transfers between devices  7.31 us (29%)
  Pallas kernels  4.36 us (17%)
    ppermute x9, starting transfers between devices, swap(): lax.ppermute(value, 'ap', [(i, i ^ 1 << bit_of[i & 1]) for i in range(dev...  13.1 us
    ppermute x9, waiting for transfers between devices, swap(): lax.ppermute(value, 'ap', [(i, i ^ 1 << bit_of[i & 1]) for i in range(dev...  7.31 us
    pallas_call x4, Pallas kernels, next_products(): pl.pallas_call(functools.partial(next_kernel, users, jobs), out_shape=[me...  1.74 us
    pallas_call x1, Pallas kernels, first_products(): pl.pallas_call(functools.partial(first_kernel, bits), out_shape=(message(...  1.69 us
    pallas_call x1, Pallas kernels, finish(): pl.pallas_call(functools.partial(final_kernel, terms, powers), out_shape=...  0.77 us
  transfers between devices with their start and end apart: 9, of which 6 were waited for; matrix products, arithmetic and copies ran while one was open for 0% of the time, Pallas kernels for 8%

profile of v26, /device:TPU:0, one launch (start us, length us, event | category | flops | bytes accessed | tf_op | source)
XLA Modules:
  0.0 24.8 jit_solution(7531272629869744912)
XLA Ops:
  0.0 1.7 %first_products.1 = (f32[33,8,128]{2,1,0:T(8,128)S(1)}, bf16[2,256,1024]{2,1,0:T(8,128)(2,1)S(1)}, bf16[1024,512]{1,0:T(8,128)(2,1)S(1)}, f32[1,512]{1,0:T(1,128)S(1)}) custom-call(s32[1,12]{1,0:T(1,128)} %visible.1, s32[4,512]{1,0:T(4,128)} %bitcast.3, bf16[1,12,2,32,512]{4,3,2,1,0:T(8,128)(2,1)} %channel.1, bf16[1024,512]{1,0:T(8,128)(2,1)} %bitcast.2), custom_call_target="tpu_custom_call" | custom-call | flops 8192 | bytes 8192 | tf_op jit(solution)/shard_map/first_products/pallas_call | solution.py:148
  1.7 0.5 %collective-permute-start = (f32[33,8,128]{2,1,0:T(8,128)S(1)}, f32[33,8,128]{2,1,0:T(8,128)S(1)}, u32[]{:S(2)}, u32[]{:S(2)}) collective-permute-start(f32[33,8,128]{2,1,0:T(8,128)S(1)} %get-tuple-element.11.refs_0_), channel_id=1, source_target_pairs={{0,1},{1,0},{2,3},{3,2},{4,5},{5,4},{6,7},{7,6},{8,9},{9,8},{10,11... | collective-permute-start | bytes 405512 | tf_op jit(solution)/shard_map/ppermute | solution.py:271
  2.2 0.6 %next_products.4 = (f32[128,8,128]{2,1,0:T(8,128)S(1)}, f32[32,8,128]{2,1,0:T(8,128)S(1)}) custom-call(bf16[2,256,1024]{2,1,0:T(8,128)(2,1)S(1)} %get-tuple-element.12.rows, bf16[1024,512]{1,0:T(8,128)(2,1)S(1)} %get-tuple-element.13.weights, f32[1,512]{1,0:T(1,128)S(1)} %get-tuple-element.14.served), custom_call_target="tpu_custom_call" | custom-call | flops 67108864 | bytes 67108864 | tf_op jit(solution)/shard_map/next_products/pallas_call | solution.py:174
  2.8 0.1 collective-permute-start.2
  2.9 0.3 %collective-permute-done.refs_2_.refs_1_ = f32[33,8,128]{2,1,0:T(8,128)S(1)} collective-permute-done((f32[33,8,128]{2,1,0:T(8,128)S(1)}, f32[33,8,128]{2,1,0:T(8,128)S(1)}, u32[]{:S(2)}, u32[]{:S(2)}) %collective-permute-start) | collective-permute-done | bytes 135200 | tf_op jit(solution)/shard_map/ppermute | solution.py:271
  3.2 3.0 %collective-permute-start.1 = (f32[33,8,128]{2,1,0:T(8,128)S(1)}, f32[33,8,128]{2,1,0:T(8,128)S(1)}, u32[]{:S(2)}, u32[]{:S(2)}) collective-permute-start(f32[33,8,128]{2,1,0:T(8,128)S(1)} %summed.6), channel_id=1, source_target_pairs={{0,4},{1,3},{2,6},{3,1},{4,0},{5,7},{6,2},{7,5},{8,12},{9,11},{10,... | collective-permute-start | bytes 405512 | tf_op jit(solution)/shard_map/ppermute | solution.py:271
  6.2 0.4 %next_products.5.refs_0_.refs_2_ = f32[128,8,128]{2,1,0:T(8,128)S(1)} custom-call(bf16[2,256,1024]{2,1,0:T(8,128)(2,1)S(1)} %get-tuple-element.12.rows, bf16[1024,512]{1,0:T(8,128)(2,1)S(1)} %get-tuple-element.13.weights, f32[1,512]{1,0:T(1,128)S(1)} %get-tuple-element.14.served), custom_call_target="tpu_custom_call" | custom-call | flops 8589934592 | bytes 8589934592 | tf_op jit(solution)/shard_map/next_products/pallas_call | solution.py:174
  6.7 0.0 collective-permute-done.2.refs_1_.refs_3_
  6.7 0.9 %collective-permute-start.6 = (f32[64,8,128]{2,1,0:T(8,128)S(1)}, f32[64,8,128]{2,1,0:T(8,128)S(1)}, u32[]{:S(2)}, u32[]{:S(2)}) collective-permute-start(f32[64,8,128]{2,1,0:T(8,128)S(1)} %summed.7.refs_5_), channel_id=1, source_target_pairs={{0,4},{1,3},{2,6},{3,1},{4,0},{5,7},{6,2},{7,5},{8,12},{9,11},{10,... | collective-permute-start | bytes 786440 | tf_op jit(solution)/shard_map/ppermute | solution.py:271
  7.6 1.6 %collective-permute-done.1.refs_4_.refs_2_ = f32[33,8,128]{2,1,0:T(8,128)S(1)} collective-permute-done((f32[33,8,128]{2,1,0:T(8,128)S(1)}, f32[33,8,128]{2,1,0:T(8,128)S(1)}, u32[]{:S(2)}, u32[]{:S(2)}) %collective-permute-start.1) | collective-permute-done | bytes 135200 | tf_op jit(solution)/shard_map/ppermute | solution.py:271
  9.2 2.0 %collective-permute-start.3 = (f32[33,8,128]{2,1,0:T(8,128)S(1)}, f32[33,8,128]{2,1,0:T(8,128)S(1)}, u32[]{:S(2)}, u32[]{:S(2)}) collective-permute-start(f32[33,8,128]{2,1,0:T(8,128)S(1)} %summed.8.refs_0_), channel_id=1, source_target_pairs={{0,2},{1,5},{2,0},{3,7},{4,6},{5,1},{6,4},{7,3},{8,10},{9,13},{10,... | collective-permute-start | bytes 405512 | tf_op jit(solution)/shard_map/ppermute | solution.py:271
  11.2 0.4 %next_products.6.refs_0_ = f32[96,8,128]{2,1,0:T(8,128)S(1)} custom-call(bf16[2,256,1024]{2,1,0:T(8,128)(2,1)S(1)} %get-tuple-element.12.rows, bf16[1024,512]{1,0:T(8,128)(2,1)S(1)} %get-tuple-element.13.weights, f32[1,512]{1,0:T(1,128)S(1)} %get-tuple-element.14.served, f32[33,8,128]{2,1,0:T(8,128)S(1)} %summed.8.refs_0_), custom_call_target="tpu_custom_call" | custom-call | flops 67108864 | bytes 67108864 | tf_op jit(solution)/shard_map/next_products/pallas_call | solution.py:174
  11.6 0.1 collective-permute-start.4
  11.7 0.4 %next_products.7.refs_2_.refs_5_.refs_1_.refs_4_ = f32[96,8,128]{2,1,0:T(8,128)S(1)} custom-call(bf16[2,256,1024]{2,1,0:T(8,128)(2,1)S(1)} %get-tuple-element.12.rows, bf16[1024,512]{1,0:T(8,128)(2,1)S(1)} %get-tuple-element.13.weights, f32[1,512]{1,0:T(1,128)S(1)} %get-tuple-element.14.served, f32[96,8,128]{2,1,0:T(8,128)S(1)} %next_products.6.refs_0_), custom_call_target="tpu_custom_call" | custom-call | flops 68719476736 | bytes 68719476736 | tf_op jit(solution)/shard_map/next_products/pallas_call | solution.py:174
  12.1 1.6 %collective-permute-start.5 = (f32[32,8,128]{2,1,0:T(8,128)S(1)}, f32[32,8,128]{2,1,0:T(8,128)S(1)}, u32[]{:S(2)}, u32[]{:S(2)}) collective-permute-start(f32[32,8,128]{2,1,0:T(8,128)S(1)} %summed.9), channel_id=1, source_target_pairs={{0,4},{1,3},{2,6},{3,1},{4,0},{5,7},{6,2},{7,5},{8,12},{9,11},{10,... | collective-permute-start | bytes 393224 | tf_op jit(solution)/shard_map/ppermute | solution.py:271
  13.7 0.8 %collective-permute-done.3.refs_4_.refs_3_ = f32[33,8,128]{2,1,0:T(8,128)S(1)} collective-permute-done((f32[33,8,128]{2,1,0:T(8,128)S(1)}, f32[33,8,128]{2,1,0:T(8,128)S(1)}, u32[]{:S(2)}, u32[]{:S(2)}) %collective-permute-start.3) | collective-permute-done | bytes 135200 | tf_op jit(solution)/shard_map/ppermute | solution.py:271
  14.5 0.1 collective-permute-done.6.refs_3_.refs_0_
  14.6 0.0 collective-permute-done.4.refs_6_.refs_2_.refs_5_
  14.6 2.8 %collective-permute-start.7 = (f32[33,8,128]{2,1,0:T(8,128)S(1)}, f32[33,8,128]{2,1,0:T(8,128)S(1)}, u32[]{:S(2)}, u32[]{:S(2)}) collective-permute-start(f32[33,8,128]{2,1,0:T(8,128)S(1)} %summed.10.refs_3_), channel_id=1, source_target_pairs={{0,8},{1,9},{2,10},{3,11},{4,12},{5,13},{6,14},{7,15},{8,0},{9,1},... | collective-permute-start | bytes 405512 | tf_op jit(solution)/shard_map/ppermute | solution.py:271
  17.5 0.0 collective-permute-done.5.refs_4_.refs_6_
  17.5 2.0 %collective-permute-start.8 = (f32[32,8,128]{2,1,0:T(8,128)S(1)}, f32[32,8,128]{2,1,0:T(8,128)S(1)}, u32[]{:S(2)}, u32[]{:S(2)}) collective-permute-start(f32[32,8,128]{2,1,0:T(8,128)S(1)} %summed.11), channel_id=1, source_target_pairs={{0,2},{1,5},{2,0},{3,7},{4,6},{5,1},{6,4},{7,3},{8,10},{9,13},{10,... | collective-permute-start | bytes 393224 | tf_op jit(solution)/shard_map/ppermute | solution.py:271
  19.5 3.0 %collective-permute-done.8.refs_8_ = f32[32,8,128]{2,1,0:T(8,128)S(1)} collective-permute-done((f32[32,8,128]{2,1,0:T(8,128)S(1)}, f32[32,8,128]{2,1,0:T(8,128)S(1)}, u32[]{:S(2)}, u32[]{:S(2)}) %collective-permute-start.8) | collective-permute-done | bytes 131104 | tf_op jit(solution)/shard_map/ppermute | solution.py:271
  22.5 1.5 %collective-permute-done.7.refs_7_ = f32[33,8,128]{2,1,0:T(8,128)S(1)} collective-permute-done((f32[33,8,128]{2,1,0:T(8,128)S(1)}, f32[33,8,128]{2,1,0:T(8,128)S(1)}, u32[]{:S(2)}, u32[]{:S(2)}) %collective-permute-start.7) | collective-permute-done | bytes 135200 | tf_op jit(solution)/shard_map/ppermute | solution.py:271
  24.0 0.8 %finish.1 = f32[32,2,512]{2,1,0:T(2,128)} custom-call(f32[33,8,128]{2,1,0:T(8,128)S(1)} %get-tuple-element.11.refs_0_, f32[33,8,128]{2,1,0:T(8,128)S(1)} %collective-permute-done.refs_2_.refs_1_, f32[33,8,128]{2,1,0:T(8,128)S(1)} %collective-permute-done.1.refs_4_.refs_2_, f32[33,8,128]{2,1,0:T(8,128)S(1)} %collective-permute-done.3.refs_4_.refs_3_, ...), custom_call_target="tpu_custom_call" | custom-call | tf_op jit(solution)/shard_map/finish/pallas_call | solution.py:230
  (6 shorter events, 0.2 us)
Async XLA Ops:
  1.7 1.5 %collective-permute-start = (f32[33,8,128]{2,1,0:T(8,128)S(1)}, f32[33,8,128]{2,1,0:T(8,128)S(1)}, u32[]{:S(2)}, u32[]{:S(2)}) collective-permute-start(f32[33,8,128]{2,1,0:T(8,128)S(1)} %get-tuple-element.11.refs_0_), channel_id=1, source_target_pairs={{0,1},{1,0},{2,3},{3,2},{4,5},{5,4},{6,7},{7,6},{8,9},{9,8},{10,11... | collective-permute-start | bytes 405512 | tf_op jit(solution)/shard_map/ppermute | solution.py:271
  2.8 3.9 %collective-permute-start.2 = (f32[128,8,128]{2,1,0:T(8,128)S(1)}, f32[128,8,128]{2,1,0:T(8,128)S(1)}, u32[]{:S(2)}, u32[]{:S(2)}) collective-permute-start(f32[128,8,128]{2,1,0:T(8,128)S(1)} %get-tuple-element.16), channel_id=1, source_target_pairs={{0,1},{1,0},{2,3},{3,2},{4,5},{5,4},{6,7},{7,6},{8,9},{9,8},{10,11... | collective-permute-start | bytes 1572872 | tf_op jit(solution)/shard_map/ppermute | solution.py:271
  3.2 6.0 %collective-permute-start.1 = (f32[33,8,128]{2,1,0:T(8,128)S(1)}, f32[33,8,128]{2,1,0:T(8,128)S(1)}, u32[]{:S(2)}, u32[]{:S(2)}) collective-permute-start(f32[33,8,128]{2,1,0:T(8,128)S(1)} %summed.6), channel_id=1, source_target_pairs={{0,4},{1,3},{2,6},{3,1},{4,0},{5,7},{6,2},{7,5},{8,12},{9,11},{10,... | collective-permute-start | bytes 405512 | tf_op jit(solution)/shard_map/ppermute | solution.py:271
  6.7 7.9 %collective-permute-start.6 = (f32[64,8,128]{2,1,0:T(8,128)S(1)}, f32[64,8,128]{2,1,0:T(8,128)S(1)}, u32[]{:S(2)}, u32[]{:S(2)}) collective-permute-start(f32[64,8,128]{2,1,0:T(8,128)S(1)} %summed.7.refs_5_), channel_id=1, source_target_pairs={{0,4},{1,3},{2,6},{3,1},{4,0},{5,7},{6,2},{7,5},{8,12},{9,11},{10,... | collective-permute-start | bytes 786440 | tf_op jit(solution)/shard_map/ppermute | solution.py:271
  9.2 5.3 %collective-permute-start.3 = (f32[33,8,128]{2,1,0:T(8,128)S(1)}, f32[33,8,128]{2,1,0:T(8,128)S(1)}, u32[]{:S(2)}, u32[]{:S(2)}) collective-permute-start(f32[33,8,128]{2,1,0:T(8,128)S(1)} %summed.8.refs_0_), channel_id=1, source_target_pairs={{0,2},{1,5},{2,0},{3,7},{4,6},{5,1},{6,4},{7,3},{8,10},{9,13},{10,... | collective-permute-start | bytes 405512 | tf_op jit(solution)/shard_map/ppermute | solution.py:271
  11.6 3.0 %collective-permute-start.4 = (f32[96,8,128]{2,1,0:T(8,128)S(1)}, f32[96,8,128]{2,1,0:T(8,128)S(1)}, u32[]{:S(2)}, u32[]{:S(2)}) collective-permute-start(f32[96,8,128]{2,1,0:T(8,128)S(1)} %next_products.6.refs_0_), channel_id=1, source_target_pairs={{0,1},{1,0},{2,3},{3,2},{4,5},{5,4},{6,7},{7,6},{8,9},{9,8},{10,11... | collective-permute-start | bytes 1179656 | tf_op jit(solution)/shard_map/ppermute | solution.py:271
  12.1 5.4 %collective-permute-start.5 = (f32[32,8,128]{2,1,0:T(8,128)S(1)}, f32[32,8,128]{2,1,0:T(8,128)S(1)}, u32[]{:S(2)}, u32[]{:S(2)}) collective-permute-start(f32[32,8,128]{2,1,0:T(8,128)S(1)} %summed.9), channel_id=1, source_target_pairs={{0,4},{1,3},{2,6},{3,1},{4,0},{5,7},{6,2},{7,5},{8,12},{9,11},{10,... | collective-permute-start | bytes 393224 | tf_op jit(solution)/shard_map/ppermute | solution.py:271
  14.6 9.4 %collective-permute-start.7 = (f32[33,8,128]{2,1,0:T(8,128)S(1)}, f32[33,8,128]{2,1,0:T(8,128)S(1)}, u32[]{:S(2)}, u32[]{:S(2)}) collective-permute-start(f32[33,8,128]{2,1,0:T(8,128)S(1)} %summed.10.refs_3_), channel_id=1, source_target_pairs={{0,8},{1,9},{2,10},{3,11},{4,12},{5,13},{6,14},{7,15},{8,0},{9,1},... | collective-permute-start | bytes 405512 | tf_op jit(solution)/shard_map/ppermute | solution.py:271
  17.5 5.0 %collective-permute-start.8 = (f32[32,8,128]{2,1,0:T(8,128)S(1)}, f32[32,8,128]{2,1,0:T(8,128)S(1)}, u32[]{:S(2)}, u32[]{:S(2)}) collective-permute-start(f32[32,8,128]{2,1,0:T(8,128)S(1)} %summed.11), channel_id=1, source_target_pairs={{0,2},{1,5},{2,0},{3,7},{4,6},{5,1},{6,4},{7,3},{8,10},{9,13},{10,... | collective-permute-start | bytes 393224 | tf_op jit(solution)/shard_map/ppermute | solution.py:271

commit v27 on v24

--- a/solution.py
+++ b/solution.py
@@ -249,10 +249,10 @@
     parts = [steps[0][at * quarter:(at + 1) * quarter] for at in range(4)]
     order = [
         (0, parts[0]),
-        (0, parts[2] + parts[1][::2]),
+        (0, parts[2] + parts[3][::2]),
         (1, steps[1][:half]),
-        (0, parts[1][1::2]),
-        (0, parts[3]),
+        (0, parts[1]),
+        (0, parts[3][1::2]),
         (2, steps[2]),
         (1, steps[1][half:]),
     ]

time: 23.5 us -> 25 us (1.064)
  starting transfers between devices: 13.7 us -> 14.8 us
  waiting for transfers between devices: 5.18 us -> 5.65 us
    ppermute x10, starting transfers between devices: 13.7 us -> 14.8 us  [swap(): lax.ppermute(value, 'ap', [(i, i ^ 1 << bit_of[i & 1]) for i in range(dev...]
    ppermute x10, waiting for transfers between devices: 5.18 us -> 5.65 us  [swap(): lax.ppermute(value, 'ap', [(i, i ^ 1 << bit_of[i & 1]) for i in range(dev...]
  transfers between devices with their start and end apart: 10 -> 10, of which waited for: 5 -> 4; matrix products, arithmetic and copies ran while one was open for 0% -> 0% of each run, Pallas kernels for 8% -> 8%
where the time goes in v27:
time: 25 us; the launch traced here: 24.9 us
  starting transfers between devices  14.8 us (59%)
  waiting for transfers between devices  5.65 us (23%)
  Pallas kernels  4.37 us (17%)
    ppermute x10, starting transfers between devices, swap(): lax.ppermute(value, 'ap', [(i, i ^ 1 << bit_of[i & 1]) for i in range(dev...  14.8 us
    ppermute x10, waiting for transfers between devices, swap(): lax.ppermute(value, 'ap', [(i, i ^ 1 << bit_of[i & 1]) for i in range(dev...  5.65 us
    pallas_call x4, Pallas kernels, next_products(): pl.pallas_call(functools.partial(next_kernel, users, jobs), out_shape=[me...  1.74 us
    pallas_call x1, Pallas kernels, first_products(): pl.pallas_call(functools.partial(first_kernel, bits), out_shape=(message(...  1.69 us
    pallas_call x1, Pallas kernels, finish(): pl.pallas_call(functools.partial(final_kernel, terms, powers), out_shape=...  0.78 us
  transfers between devices with their start and end apart: 10, of which 4 were waited for; matrix products, arithmetic and copies ran while one was open for 0% of the time, Pallas kernels for 8%

profile of v27, /device:TPU:0, one launch (start us, length us, event | category | flops | bytes accessed | tf_op | source)
XLA Modules:
  0.0 24.9 jit_solution(18248870466768733780)
XLA Ops:
  0.0 1.7 %first_products.1 = (f32[33,8,128]{2,1,0:T(8,128)S(1)}, bf16[2,256,1024]{2,1,0:T(8,128)(2,1)S(1)}, bf16[1024,512]{1,0:T(8,128)(2,1)S(1)}, f32[1,512]{1,0:T(1,128)S(1)}) custom-call(s32[1,12]{1,0:T(1,128)} %visible.1, s32[4,512]{1,0:T(4,128)} %bitcast.3, bf16[1,12,2,32,512]{4,3,2,1,0:T(8,128)(2,1)} %channel.1, bf16[1024,512]{1,0:T(8,128)(2,1)} %bitcast.2), custom_call_target="tpu_custom_call" | custom-call | flops 8192 | bytes 8192 | tf_op jit(solution)/shard_map/first_products/pallas_call | solution.py:148
  1.7 0.5 %collective-permute-start = (f32[33,8,128]{2,1,0:T(8,128)S(1)}, f32[33,8,128]{2,1,0:T(8,128)S(1)}, u32[]{:S(2)}, u32[]{:S(2)}) collective-permute-start(f32[33,8,128]{2,1,0:T(8,128)S(1)} %get-tuple-element.11.refs_0_), channel_id=1, source_target_pairs={{0,1},{1,0},{2,3},{3,2},{4,5},{5,4},{6,7},{7,6},{8,9},{9,8},{10,11... | collective-permute-start | bytes 405512 | tf_op jit(solution)/shard_map/ppermute | solution.py:272
  2.2 0.6 %next_products.4 = (f32[128,8,128]{2,1,0:T(8,128)S(1)}, f32[32,8,128]{2,1,0:T(8,128)S(1)}) custom-call(bf16[2,256,1024]{2,1,0:T(8,128)(2,1)S(1)} %get-tuple-element.12.rows, bf16[1024,512]{1,0:T(8,128)(2,1)S(1)} %get-tuple-element.13.weights, f32[1,512]{1,0:T(1,128)S(1)} %get-tuple-element.14.served), custom_call_target="tpu_custom_call" | custom-call | flops 67108864 | bytes 67108864 | tf_op jit(solution)/shard_map/next_products/pallas_call | solution.py:174
  2.8 0.1 collective-permute-start.2
  2.9 0.3 %collective-permute-done.refs_2_.refs_1_ = f32[33,8,128]{2,1,0:T(8,128)S(1)} collective-permute-done((f32[33,8,128]{2,1,0:T(8,128)S(1)}, f32[33,8,128]{2,1,0:T(8,128)S(1)}, u32[]{:S(2)}, u32[]{:S(2)}) %collective-permute-start) | collective-permute-done | bytes 135200 | tf_op jit(solution)/shard_map/ppermute | solution.py:272
  3.2 3.0 %collective-permute-start.1 = (f32[33,8,128]{2,1,0:T(8,128)S(1)}, f32[33,8,128]{2,1,0:T(8,128)S(1)}, u32[]{:S(2)}, u32[]{:S(2)}) collective-permute-start(f32[33,8,128]{2,1,0:T(8,128)S(1)} %summed.7), channel_id=1, source_target_pairs={{0,4},{1,3},{2,6},{3,1},{4,0},{5,7},{6,2},{7,5},{8,12},{9,11},{10,... | collective-permute-start | bytes 405512 | tf_op jit(solution)/shard_map/ppermute | solution.py:272
  6.2 0.4 %next_products.5.refs_0_.refs_2_ = f32[128,8,128]{2,1,0:T(8,128)S(1)} custom-call(bf16[2,256,1024]{2,1,0:T(8,128)(2,1)S(1)} %get-tuple-element.12.rows, bf16[1024,512]{1,0:T(8,128)(2,1)S(1)} %get-tuple-element.13.weights, f32[1,512]{1,0:T(1,128)S(1)} %get-tuple-element.14.served), custom_call_target="tpu_custom_call" | custom-call | flops 8589934592 | bytes 8589934592 | tf_op jit(solution)/shard_map/next_products/pallas_call | solution.py:174
  6.7 0.0 collective-permute-done.2.refs_1_.refs_3_
  6.7 0.9 %collective-permute-start.3 = (f32[48,8,128]{2,1,0:T(8,128)S(1)}, f32[48,8,128]{2,1,0:T(8,128)S(1)}, u32[]{:S(2)}, u32[]{:S(2)}) collective-permute-start(f32[48,8,128]{2,1,0:T(8,128)S(1)} %summed.8.refs_5_), channel_id=1, source_target_pairs={{0,4},{1,3},{2,6},{3,1},{4,0},{5,7},{6,2},{7,5},{8,12},{9,11},{10,... | collective-permute-start | bytes 589832 | tf_op jit(solution)/shard_map/ppermute | solution.py:272
  7.6 1.6 %collective-permute-done.1.refs_4_.refs_2_ = f32[33,8,128]{2,1,0:T(8,128)S(1)} collective-permute-done((f32[33,8,128]{2,1,0:T(8,128)S(1)}, f32[33,8,128]{2,1,0:T(8,128)S(1)}, u32[]{:S(2)}, u32[]{:S(2)}) %collective-permute-start.1) | collective-permute-done | bytes 135200 | tf_op jit(solution)/shard_map/ppermute | solution.py:272
  9.2 2.0 %collective-permute-start.4 = (f32[33,8,128]{2,1,0:T(8,128)S(1)}, f32[33,8,128]{2,1,0:T(8,128)S(1)}, u32[]{:S(2)}, u32[]{:S(2)}) collective-permute-start(f32[33,8,128]{2,1,0:T(8,128)S(1)} %summed.9.refs_0_), channel_id=1, source_target_pairs={{0,2},{1,5},{2,0},{3,7},{4,6},{5,1},{6,4},{7,3},{8,10},{9,13},{10,... | collective-permute-start | bytes 405512 | tf_op jit(solution)/shard_map/ppermute | solution.py:272
  11.2 0.4 %next_products.6.refs_0_ = f32[96,8,128]{2,1,0:T(8,128)S(1)} custom-call(bf16[2,256,1024]{2,1,0:T(8,128)(2,1)S(1)} %get-tuple-element.12.rows, bf16[1024,512]{1,0:T(8,128)(2,1)S(1)} %get-tuple-element.13.weights, f32[1,512]{1,0:T(1,128)S(1)} %get-tuple-element.14.served, f32[33,8,128]{2,1,0:T(8,128)S(1)} %summed.9.refs_0_), custom_call_target="tpu_custom_call" | custom-call | flops 67108864 | bytes 67108864 | tf_op jit(solution)/shard_map/next_products/pallas_call | solution.py:174
  11.6 0.1 collective-permute-start.5
  11.7 0.4 %next_products.7.refs_2_.refs_5_.refs_0_ = f32[96,8,128]{2,1,0:T(8,128)S(1)} custom-call(bf16[2,256,1024]{2,1,0:T(8,128)(2,1)S(1)} %get-tuple-element.12.rows, bf16[1024,512]{1,0:T(8,128)(2,1)S(1)} %get-tuple-element.13.weights, f32[1,512]{1,0:T(1,128)S(1)} %get-tuple-element.14.served, f32[96,8,128]{2,1,0:T(8,128)S(1)} %next_products.6.refs_0_), custom_call_target="tpu_custom_call" | custom-call | flops 68719476736 | bytes 68719476736 | tf_op jit(solution)/shard_map/next_products/pallas_call | solution.py:174
  12.1 1.6 %collective-permute-start.8 = (f32[32,8,128]{2,1,0:T(8,128)S(1)}, f32[32,8,128]{2,1,0:T(8,128)S(1)}, u32[]{:S(2)}, u32[]{:S(2)}) collective-permute-start(f32[32,8,128]{2,1,0:T(8,128)S(1)} %summed.10.refs_2_), channel_id=1, source_target_pairs={{0,4},{1,3},{2,6},{3,1},{4,0},{5,7},{6,2},{7,5},{8,12},{9,11},{10,... | collective-permute-start | bytes 393224 | tf_op jit(solution)/shard_map/ppermute | solution.py:272
  13.7 0.8 %collective-permute-done.4.refs_4_ = f32[33,8,128]{2,1,0:T(8,128)S(1)} collective-permute-done((f32[33,8,128]{2,1,0:T(8,128)S(1)}, f32[33,8,128]{2,1,0:T(8,128)S(1)}, u32[]{:S(2)}, u32[]{:S(2)}) %collective-permute-start.4) | collective-permute-done | bytes 135200 | tf_op jit(solution)/shard_map/ppermute | solution.py:272
  14.5 0.0 collective-permute-done.3.refs_3_
  14.5 0.0 collective-permute-done.5.refs_6_.refs_1_
  14.6 2.9 %collective-permute-start.7 = (f32[33,8,128]{2,1,0:T(8,128)S(1)}, f32[33,8,128]{2,1,0:T(8,128)S(1)}, u32[]{:S(2)}, u32[]{:S(2)}) collective-permute-start(f32[33,8,128]{2,1,0:T(8,128)S(1)} %summed.12.refs_3_), channel_id=1, source_target_pairs={{0,8},{1,9},{2,10},{3,11},{4,12},{5,13},{6,14},{7,15},{8,0},{9,1},... | collective-permute-start | bytes 405512 | tf_op jit(solution)/shard_map/ppermute | solution.py:272
  17.5 0.0 collective-permute-done.8.refs_2_
  17.5 2.0 %collective-permute-start.9 = (f32[32,8,128]{2,1,0:T(8,128)S(1)}, f32[32,8,128]{2,1,0:T(8,128)S(1)}, u32[]{:S(2)}, u32[]{:S(2)}) collective-permute-start(f32[32,8,128]{2,1,0:T(8,128)S(1)} %summed.13), channel_id=1, source_target_pairs={{0,2},{1,5},{2,0},{3,7},{4,6},{5,1},{6,4},{7,3},{8,10},{9,13},{10,... | collective-permute-start | bytes 393224 | tf_op jit(solution)/shard_map/ppermute | solution.py:272
  19.5 1.6 %collective-permute-start.6 = (f32[16,8,128]{2,1,0:T(8,128)S(1)}, f32[16,8,128]{2,1,0:T(8,128)S(1)}, u32[]{:S(2)}, u32[]{:S(2)}) collective-permute-start(f32[16,8,128]{2,1,0:T(8,128)S(1)} %summed.11), channel_id=1, source_target_pairs={{0,4},{1,3},{2,6},{3,1},{4,0},{5,7},{6,2},{7,5},{8,12},{9,11},{10,... | collective-permute-start | bytes 196616 | tf_op jit(solution)/shard_map/ppermute | solution.py:272
  21.2 2.9 %collective-permute-done.6.refs_7_ = f32[16,8,128]{2,1,0:T(8,128)S(1)} collective-permute-done((f32[16,8,128]{2,1,0:T(8,128)S(1)}, f32[16,8,128]{2,1,0:T(8,128)S(1)}, u32[]{:S(2)}, u32[]{:S(2)}) %collective-permute-start.6) | collective-permute-done | bytes 65568 | tf_op jit(solution)/shard_map/ppermute | solution.py:272
  24.1 0.0 collective-permute-done.9.refs_9_
  24.1 0.0 collective-permute-done.7.refs_8_
  24.1 0.8 %finish.1 = f32[32,2,512]{2,1,0:T(2,128)} custom-call(f32[33,8,128]{2,1,0:T(8,128)S(1)} %get-tuple-element.11.refs_0_, f32[33,8,128]{2,1,0:T(8,128)S(1)} %collective-permute-done.refs_2_.refs_1_, f32[33,8,128]{2,1,0:T(8,128)S(1)} %collective-permute-done.1.refs_4_.refs_2_, f32[48,8,128]{2,1,0:T(8,128)S(1)} %collective-permute-done.3.refs_3_, ...), custom_call_target="tpu_custom_call" | custom-call | tf_op jit(solution)/shard_map/finish/pallas_call | solution.py:230
  (7 shorter events, 0.2 us)
Async XLA Ops:
  1.7 1.5 %collective-permute-start = (f32[33,8,128]{2,1,0:T(8,128)S(1)}, f32[33,8,128]{2,1,0:T(8,128)S(1)}, u32[]{:S(2)}, u32[]{:S(2)}) collective-permute-start(f32[33,8,128]{2,1,0:T(8,128)S(1)} %get-tuple-element.11.refs_0_), channel_id=1, source_target_pairs={{0,1},{1,0},{2,3},{3,2},{4,5},{5,4},{6,7},{7,6},{8,9},{9,8},{10,11... | collective-permute-start | bytes 405512 | tf_op jit(solution)/shard_map/ppermute | solution.py:272
  2.8 3.9 %collective-permute-start.2 = (f32[128,8,128]{2,1,0:T(8,128)S(1)}, f32[128,8,128]{2,1,0:T(8,128)S(1)}, u32[]{:S(2)}, u32[]{:S(2)}) collective-permute-start(f32[128,8,128]{2,1,0:T(8,128)S(1)} %get-tuple-element.16), channel_id=1, source_target_pairs={{0,1},{1,0},{2,3},{3,2},{4,5},{5,4},{6,7},{7,6},{8,9},{9,8},{10,11... | collective-permute-start | bytes 1572872 | tf_op jit(solution)/shard_map/ppermute | solution.py:272
  3.2 6.0 %collective-permute-start.1 = (f32[33,8,128]{2,1,0:T(8,128)S(1)}, f32[33,8,128]{2,1,0:T(8,128)S(1)}, u32[]{:S(2)}, u32[]{:S(2)}) collective-permute-start(f32[33,8,128]{2,1,0:T(8,128)S(1)} %summed.7), channel_id=1, source_target_pairs={{0,4},{1,3},{2,6},{3,1},{4,0},{5,7},{6,2},{7,5},{8,12},{9,11},{10,... | collective-permute-start | bytes 405512 | tf_op jit(solution)/shard_map/ppermute | solution.py:272
  6.7 7.8 %collective-permute-start.3 = (f32[48,8,128]{2,1,0:T(8,128)S(1)}, f32[48,8,128]{2,1,0:T(8,128)S(1)}, u32[]{:S(2)}, u32[]{:S(2)}) collective-permute-start(f32[48,8,128]{2,1,0:T(8,128)S(1)} %summed.8.refs_5_), channel_id=1, source_target_pairs={{0,4},{1,3},{2,6},{3,1},{4,0},{5,7},{6,2},{7,5},{8,12},{9,11},{10,... | collective-permute-start | bytes 589832 | tf_op jit(solution)/shard_map/ppermute | solution.py:272
  9.2 5.3 %collective-permute-start.4 = (f32[33,8,128]{2,1,0:T(8,128)S(1)}, f32[33,8,128]{2,1,0:T(8,128)S(1)}, u32[]{:S(2)}, u32[]{:S(2)}) collective-permute-start(f32[33,8,128]{2,1,0:T(8,128)S(1)} %summed.9.refs_0_), channel_id=1, source_target_pairs={{0,2},{1,5},{2,0},{3,7},{4,6},{5,1},{6,4},{7,3},{8,10},{9,13},{10,... | collective-permute-start | bytes 405512 | tf_op jit(solution)/shard_map/ppermute | solution.py:272
  11.6 2.9 %collective-permute-start.5 = (f32[96,8,128]{2,1,0:T(8,128)S(1)}, f32[96,8,128]{2,1,0:T(8,128)S(1)}, u32[]{:S(2)}, u32[]{:S(2)}) collective-permute-start(f32[96,8,128]{2,1,0:T(8,128)S(1)} %next_products.6.refs_0_), channel_id=1, source_target_pairs={{0,1},{1,0},{2,3},{3,2},{4,5},{5,4},{6,7},{7,6},{8,9},{9,8},{10,11... | collective-permute-start | bytes 1179656 | tf_op jit(solution)/shard_map/ppermute | solution.py:272
  12.1 5.4 %collective-permute-start.8 = (f32[32,8,128]{2,1,0:T(8,128)S(1)}, f32[32,8,128]{2,1,0:T(8,128)S(1)}, u32[]{:S(2)}, u32[]{:S(2)}) collective-permute-start(f32[32,8,128]{2,1,0:T(8,128)S(1)} %summed.10.refs_2_), channel_id=1, source_target_pairs={{0,4},{1,3},{2,6},{3,1},{4,0},{5,7},{6,2},{7,5},{8,12},{9,11},{10,... | collective-permute-start | bytes 393224 | tf_op jit(solution)/shard_map/ppermute | solution.py:272
  14.6 9.5 %collective-permute-start.7 = (f32[33,8,128]{2,1,0:T(8,128)S(1)}, f32[33,8,128]{2,1,0:T(8,128)S(1)}, u32[]{:S(2)}, u32[]{:S(2)}) collective-permute-start(f32[33,8,128]{2,1,0:T(8,128)S(1)} %summed.12.refs_3_), channel_id=1, source_target_pairs={{0,8},{1,9},{2,10},{3,11},{4,12},{5,13},{6,14},{7,15},{8,0},{9,1},... | collective-permute-start | bytes 405512 | tf_op jit(solution)/shard_map/ppermute | solution.py:272
  17.5 6.6 %collective-permute-start.9 = (f32[32,8,128]{2,1,0:T(8,128)S(1)}, f32[32,8,128]{2,1,0:T(8,128)S(1)}, u32[]{:S(2)}, u32[]{:S(2)}) collective-permute-start(f32[32,8,128]{2,1,0:T(8,128)S(1)} %summed.13), channel_id=1, source_target_pairs={{0,2},{1,5},{2,0},{3,7},{4,6},{5,1},{6,4},{7,3},{8,10},{9,13},{10,... | collective-permute-start | bytes 393224 | tf_op jit(solution)/shard_map/ppermute | solution.py:272
  19.5 4.6 %collective-permute-start.6 = (f32[16,8,128]{2,1,0:T(8,128)S(1)}, f32[16,8,128]{2,1,0:T(8,128)S(1)}, u32[]{:S(2)}, u32[]{:S(2)}) collective-permute-start(f32[16,8,128]{2,1,0:T(8,128)S(1)} %summed.11), channel_id=1, source_target_pairs={{0,4},{1,3},{2,6},{3,1},{4,0},{5,7},{6,2},{7,5},{8,12},{9,11},{10,... | collective-permute-start | bytes 196616 | tf_op jit(solution)/shard_map/ppermute | solution.py:272

commit v28 on v22

--- a/solution.py
+++ b/solution.py
@@ -9,7 +9,7 @@
 
 epsilon = 1e-06
 MIB = 1 << 20
-LOADS = 4
+LOADS = 8
 
 
 COSTS = (64 * MIB, 8192 * MIB, 64 * MIB, 65536 * MIB) + (

time: 23.5 us -> 23.6 us (level)
  no operation moved by 1% of the time
where the time goes in v28:
time: 23.6 us; the launch traced here: 23.4 us
  starting transfers between devices  13.7 us (58%)
  waiting for transfers between devices  5.19 us (22%)
  Pallas kernels  4.45 us (19%)
    ppermute x10, starting transfers between devices, swap(): lax.ppermute(value, 'ap', [(i, i ^ 1 << bit_of[i & 1]) for i in range(dev...  13.7 us
    ppermute x10, waiting for transfers between devices, swap(): lax.ppermute(value, 'ap', [(i, i ^ 1 << bit_of[i & 1]) for i in range(dev...  5.19 us
    pallas_call x1, Pallas kernels, first_products(): pl.pallas_call(functools.partial(first_kernel, bits), out_shape=(message(...  1.78 us
    pallas_call x4, Pallas kernels, next_products(): pl.pallas_call(functools.partial(next_kernel, users, jobs), out_shape=[me...  1.74 us
    pallas_call x1, Pallas kernels, finish(): pl.pallas_call(functools.partial(final_kernel, terms, powers), out_shape=...  0.78 us
  transfers between devices with their start and end apart: 10, of which 5 were waited for; matrix products, arithmetic and copies ran while one was open for 0% of the time, Pallas kernels for 8%

profile of v28, /device:TPU:0, one launch (start us, length us, event | category | flops | bytes accessed | tf_op | source)
XLA Modules:
  0.0 23.4 jit_solution(16359285097645508929)
XLA Ops:
  0.0 1.8 %first_products.1 = (f32[33,8,128]{2,1,0:T(8,128)S(1)}, bf16[2,256,1024]{2,1,0:T(8,128)(2,1)S(1)}, bf16[1024,512]{1,0:T(8,128)(2,1)S(1)}, f32[1,512]{1,0:T(1,128)S(1)}) custom-call(s32[1,12]{1,0:T(1,128)} %visible.1, s32[4,512]{1,0:T(4,128)} %bitcast.3, bf16[1,12,2,32,512]{4,3,2,1,0:T(8,128)(2,1)} %channel.1, bf16[1024,512]{1,0:T(8,128)(2,1)} %bitcast.2), custom_call_target="tpu_custom_call" | custom-call | flops 8192 | bytes 8192 | tf_op jit(solution)/shard_map/first_products/pallas_call | solution.py:148
  1.8 0.5 %collective-permute-start = (f32[33,8,128]{2,1,0:T(8,128)S(1)}, f32[33,8,128]{2,1,0:T(8,128)S(1)}, u32[]{:S(2)}, u32[]{:S(2)}) collective-permute-start(f32[33,8,128]{2,1,0:T(8,128)S(1)} %get-tuple-element.11.refs_0_), channel_id=1, source_target_pairs={{0,1},{1,0},{2,3},{3,2},{4,5},{5,4},{6,7},{7,6},{8,9},{9,8},{10,11... | collective-permute-start | bytes 405512 | tf_op jit(solution)/shard_map/ppermute | solution.py:272
  2.3 0.6 %next_products.4 = (f32[128,8,128]{2,1,0:T(8,128)S(1)}, f32[32,8,128]{2,1,0:T(8,128)S(1)}) custom-call(bf16[2,256,1024]{2,1,0:T(8,128)(2,1)S(1)} %get-tuple-element.12.rows, bf16[1024,512]{1,0:T(8,128)(2,1)S(1)} %get-tuple-element.13.weights, f32[1,512]{1,0:T(1,128)S(1)} %get-tuple-element.14.served), custom_call_target="tpu_custom_call" | custom-call | flops 67108864 | bytes 67108864 | tf_op jit(solution)/shard_map/next_products/pallas_call | solution.py:174
  2.9 0.1 collective-permute-start.2
  3.0 0.3 %collective-permute-done.refs_2_.refs_1_ = f32[33,8,128]{2,1,0:T(8,128)S(1)} collective-permute-done((f32[33,8,128]{2,1,0:T(8,128)S(1)}, f32[33,8,128]{2,1,0:T(8,128)S(1)}, u32[]{:S(2)}, u32[]{:S(2)}) %collective-permute-start) | collective-permute-done | bytes 135200 | tf_op jit(solution)/shard_map/ppermute | solution.py:272
  3.3 3.0 %collective-permute-start.1 = (f32[33,8,128]{2,1,0:T(8,128)S(1)}, f32[33,8,128]{2,1,0:T(8,128)S(1)}, u32[]{:S(2)}, u32[]{:S(2)}) collective-permute-start(f32[33,8,128]{2,1,0:T(8,128)S(1)} %summed.7), channel_id=1, source_target_pairs={{0,4},{1,3},{2,6},{3,1},{4,0},{5,7},{6,2},{7,5},{8,12},{9,11},{10,... | collective-permute-start | bytes 405512 | tf_op jit(solution)/shard_map/ppermute | solution.py:272
  6.3 0.4 %next_products.5.refs_0_.refs_2_ = f32[128,8,128]{2,1,0:T(8,128)S(1)} custom-call(bf16[2,256,1024]{2,1,0:T(8,128)(2,1)S(1)} %get-tuple-element.12.rows, bf16[1024,512]{1,0:T(8,128)(2,1)S(1)} %get-tuple-element.13.weights, f32[1,512]{1,0:T(1,128)S(1)} %get-tuple-element.14.served), custom_call_target="tpu_custom_call" | custom-call | flops 8589934592 | bytes 8589934592 | tf_op jit(solution)/shard_map/next_products/pallas_call | solution.py:174
  6.8 0.0 collective-permute-done.2.refs_1_.refs_3_
  6.8 0.9 %collective-permute-start.6 = (f32[32,8,128]{2,1,0:T(8,128)S(1)}, f32[32,8,128]{2,1,0:T(8,128)S(1)}, u32[]{:S(2)}, u32[]{:S(2)}) collective-permute-start(f32[32,8,128]{2,1,0:T(8,128)S(1)} %summed.8.refs_5_), channel_id=1, source_target_pairs={{0,4},{1,3},{2,6},{3,1},{4,0},{5,7},{6,2},{7,5},{8,12},{9,11},{10,... | collective-permute-start | bytes 393224 | tf_op jit(solution)/shard_map/ppermute | solution.py:272
  7.7 1.7 %collective-permute-done.1.refs_4_.refs_2_ = f32[33,8,128]{2,1,0:T(8,128)S(1)} collective-permute-done((f32[33,8,128]{2,1,0:T(8,128)S(1)}, f32[33,8,128]{2,1,0:T(8,128)S(1)}, u32[]{:S(2)}, u32[]{:S(2)}) %collective-permute-start.1) | collective-permute-done | bytes 135200 | tf_op jit(solution)/shard_map/ppermute | solution.py:272
  9.3 2.0 %collective-permute-start.3 = (f32[33,8,128]{2,1,0:T(8,128)S(1)}, f32[33,8,128]{2,1,0:T(8,128)S(1)}, u32[]{:S(2)}, u32[]{:S(2)}) collective-permute-start(f32[33,8,128]{2,1,0:T(8,128)S(1)} %summed.9.refs_0_), channel_id=1, source_target_pairs={{0,2},{1,5},{2,0},{3,7},{4,6},{5,1},{6,4},{7,3},{8,10},{9,13},{10,... | collective-permute-start | bytes 405512 | tf_op jit(solution)/shard_map/ppermute | solution.py:272
  11.3 0.4 %next_products.6.refs_0_ = f32[96,8,128]{2,1,0:T(8,128)S(1)} custom-call(bf16[2,256,1024]{2,1,0:T(8,128)(2,1)S(1)} %get-tuple-element.12.rows, bf16[1024,512]{1,0:T(8,128)(2,1)S(1)} %get-tuple-element.13.weights, f32[1,512]{1,0:T(1,128)S(1)} %get-tuple-element.14.served, f32[33,8,128]{2,1,0:T(8,128)S(1)} %summed.9.refs_0_), custom_call_target="tpu_custom_call" | custom-call | flops 67108864 | bytes 67108864 | tf_op jit(solution)/shard_map/next_products/pallas_call | solution.py:174
  11.7 0.1 collective-permute-start.4
  11.8 0.4 %next_products.7.refs_2_.refs_5_.refs_0_.refs_4_ = f32[96,8,128]{2,1,0:T(8,128)S(1)} custom-call(bf16[2,256,1024]{2,1,0:T(8,128)(2,1)S(1)} %get-tuple-element.12.rows, bf16[1024,512]{1,0:T(8,128)(2,1)S(1)} %get-tuple-element.13.weights, f32[1,512]{1,0:T(1,128)S(1)} %get-tuple-element.14.served, f32[96,8,128]{2,1,0:T(8,128)S(1)} %next_products.6.refs_0_), custom_call_target="tpu_custom_call" | custom-call | flops 68719476736 | bytes 68719476736 | tf_op jit(solution)/shard_map/next_products/pallas_call | solution.py:174
  12.2 1.6 %collective-permute-start.8 = (f32[32,8,128]{2,1,0:T(8,128)S(1)}, f32[32,8,128]{2,1,0:T(8,128)S(1)}, u32[]{:S(2)}, u32[]{:S(2)}) collective-permute-start(f32[32,8,128]{2,1,0:T(8,128)S(1)} %summed.10.refs_2_), channel_id=1, source_target_pairs={{0,4},{1,3},{2,6},{3,1},{4,0},{5,7},{6,2},{7,5},{8,12},{9,11},{10,... | collective-permute-start | bytes 393224 | tf_op jit(solution)/shard_map/ppermute | solution.py:272
  13.9 0.5 %collective-permute-start.5 = (f32[32,8,128]{2,1,0:T(8,128)S(1)}, f32[32,8,128]{2,1,0:T(8,128)S(1)}, u32[]{:S(2)}, u32[]{:S(2)}) collective-permute-start(f32[32,8,128]{2,1,0:T(8,128)S(1)} %summed.11), channel_id=1, source_target_pairs={{0,4},{1,3},{2,6},{3,1},{4,0},{5,7},{6,2},{7,5},{8,12},{9,11},{10,... | collective-permute-start | bytes 393224 | tf_op jit(solution)/shard_map/ppermute | solution.py:272
  14.4 0.0 collective-permute-done.6.refs_3_
  14.4 0.2 %collective-permute-done.3.refs_4_.refs_3_ = f32[33,8,128]{2,1,0:T(8,128)S(1)} collective-permute-done((f32[33,8,128]{2,1,0:T(8,128)S(1)}, f32[33,8,128]{2,1,0:T(8,128)S(1)}, u32[]{:S(2)}, u32[]{:S(2)}) %collective-permute-start.3) | collective-permute-done | bytes 135200 | tf_op jit(solution)/shard_map/ppermute | solution.py:272
  14.6 0.0 collective-permute-done.4.refs_6_.refs_1_.refs_5_
  14.7 2.9 %collective-permute-start.7 = (f32[33,8,128]{2,1,0:T(8,128)S(1)}, f32[33,8,128]{2,1,0:T(8,128)S(1)}, u32[]{:S(2)}, u32[]{:S(2)}) collective-permute-start(f32[33,8,128]{2,1,0:T(8,128)S(1)} %summed.12.refs_3_), channel_id=1, source_target_pairs={{0,8},{1,9},{2,10},{3,11},{4,12},{5,13},{6,14},{7,15},{8,0},{9,1},... | collective-permute-start | bytes 405512 | tf_op jit(solution)/shard_map/ppermute | solution.py:272
  17.6 0.0 collective-permute-done.8.refs_2_
  17.6 2.0 %collective-permute-start.9 = (f32[32,8,128]{2,1,0:T(8,128)S(1)}, f32[32,8,128]{2,1,0:T(8,128)S(1)}, u32[]{:S(2)}, u32[]{:S(2)}) collective-permute-start(f32[32,8,128]{2,1,0:T(8,128)S(1)} %summed.13), channel_id=1, source_target_pairs={{0,2},{1,5},{2,0},{3,7},{4,6},{5,1},{6,4},{7,3},{8,10},{9,13},{10,... | collective-permute-start | bytes 393224 | tf_op jit(solution)/shard_map/ppermute | solution.py:272
  19.6 2.6 %collective-permute-done.5.refs_6_ = f32[32,8,128]{2,1,0:T(8,128)S(1)} collective-permute-done((f32[32,8,128]{2,1,0:T(8,128)S(1)}, f32[32,8,128]{2,1,0:T(8,128)S(1)}, u32[]{:S(2)}, u32[]{:S(2)}) %collective-permute-start.5) | collective-permute-done | bytes 131104 | tf_op jit(solution)/shard_map/ppermute | solution.py:272
  22.2 0.4 %collective-permute-done.9.refs_8_ = f32[32,8,128]{2,1,0:T(8,128)S(1)} collective-permute-done((f32[32,8,128]{2,1,0:T(8,128)S(1)}, f32[32,8,128]{2,1,0:T(8,128)S(1)}, u32[]{:S(2)}, u32[]{:S(2)}) %collective-permute-start.9) | collective-permute-done | bytes 131104 | tf_op jit(solution)/shard_map/ppermute | solution.py:272
  22.6 0.0 collective-permute-done.7.refs_7_
  22.6 0.8 %finish.1 = f32[32,2,512]{2,1,0:T(2,128)} custom-call(f32[33,8,128]{2,1,0:T(8,128)S(1)} %get-tuple-element.11.refs_0_, f32[33,8,128]{2,1,0:T(8,128)S(1)} %collective-permute-done.refs_2_.refs_1_, f32[33,8,128]{2,1,0:T(8,128)S(1)} %collective-permute-done.1.refs_4_.refs_2_, f32[33,8,128]{2,1,0:T(8,128)S(1)} %collective-permute-done.3.refs_4_.refs_3_, ...), custom_call_target="tpu_custom_call" | custom-call | tf_op jit(solution)/shard_map/finish/pallas_call | solution.py:230
  (7 shorter events, 0.2 us)
Async XLA Ops:
  1.8 1.5 %collective-permute-start = (f32[33,8,128]{2,1,0:T(8,128)S(1)}, f32[33,8,128]{2,1,0:T(8,128)S(1)}, u32[]{:S(2)}, u32[]{:S(2)}) collective-permute-start(f32[33,8,128]{2,1,0:T(8,128)S(1)} %get-tuple-element.11.refs_0_), channel_id=1, source_target_pairs={{0,1},{1,0},{2,3},{3,2},{4,5},{5,4},{6,7},{7,6},{8,9},{9,8},{10,11... | collective-permute-start | bytes 405512 | tf_op jit(solution)/shard_map/ppermute | solution.py:272
  2.9 3.9 %collective-permute-start.2 = (f32[128,8,128]{2,1,0:T(8,128)S(1)}, f32[128,8,128]{2,1,0:T(8,128)S(1)}, u32[]{:S(2)}, u32[]{:S(2)}) collective-permute-start(f32[128,8,128]{2,1,0:T(8,128)S(1)} %get-tuple-element.16), channel_id=1, source_target_pairs={{0,1},{1,0},{2,3},{3,2},{4,5},{5,4},{6,7},{7,6},{8,9},{9,8},{10,11... | collective-permute-start | bytes 1572872 | tf_op jit(solution)/shard_map/ppermute | solution.py:272
  3.3 6.0 %collective-permute-start.1 = (f32[33,8,128]{2,1,0:T(8,128)S(1)}, f32[33,8,128]{2,1,0:T(8,128)S(1)}, u32[]{:S(2)}, u32[]{:S(2)}) collective-permute-start(f32[33,8,128]{2,1,0:T(8,128)S(1)} %summed.7), channel_id=1, source_target_pairs={{0,4},{1,3},{2,6},{3,1},{4,0},{5,7},{6,2},{7,5},{8,12},{9,11},{10,... | collective-permute-start | bytes 405512 | tf_op jit(solution)/shard_map/ppermute | solution.py:272
  6.8 7.6 %collective-permute-start.6 = (f32[32,8,128]{2,1,0:T(8,128)S(1)}, f32[32,8,128]{2,1,0:T(8,128)S(1)}, u32[]{:S(2)}, u32[]{:S(2)}) collective-permute-start(f32[32,8,128]{2,1,0:T(8,128)S(1)} %summed.8.refs_5_), channel_id=1, source_target_pairs={{0,4},{1,3},{2,6},{3,1},{4,0},{5,7},{6,2},{7,5},{8,12},{9,11},{10,... | collective-permute-start | bytes 393224 | tf_op jit(solution)/shard_map/ppermute | solution.py:272
  9.3 5.3 %collective-permute-start.3 = (f32[33,8,128]{2,1,0:T(8,128)S(1)}, f32[33,8,128]{2,1,0:T(8,128)S(1)}, u32[]{:S(2)}, u32[]{:S(2)}) collective-permute-start(f32[33,8,128]{2,1,0:T(8,128)S(1)} %summed.9.refs_0_), channel_id=1, source_target_pairs={{0,2},{1,5},{2,0},{3,7},{4,6},{5,1},{6,4},{7,3},{8,10},{9,13},{10,... | collective-permute-start | bytes 405512 | tf_op jit(solution)/shard_map/ppermute | solution.py:272
  11.7 2.9 %collective-permute-start.4 = (f32[96,8,128]{2,1,0:T(8,128)S(1)}, f32[96,8,128]{2,1,0:T(8,128)S(1)}, u32[]{:S(2)}, u32[]{:S(2)}) collective-permute-start(f32[96,8,128]{2,1,0:T(8,128)S(1)} %next_products.6.refs_0_), channel_id=1, source_target_pairs={{0,1},{1,0},{2,3},{3,2},{4,5},{5,4},{6,7},{7,6},{8,9},{9,8},{10,11... | collective-permute-start | bytes 1179656 | tf_op jit(solution)/shard_map/ppermute | solution.py:272
  12.2 5.4 %collective-permute-start.8 = (f32[32,8,128]{2,1,0:T(8,128)S(1)}, f32[32,8,128]{2,1,0:T(8,128)S(1)}, u32[]{:S(2)}, u32[]{:S(2)}) collective-permute-start(f32[32,8,128]{2,1,0:T(8,128)S(1)} %summed.10.refs_2_), channel_id=1, source_target_pairs={{0,4},{1,3},{2,6},{3,1},{4,0},{5,7},{6,2},{7,5},{8,12},{9,11},{10,... | collective-permute-start | bytes 393224 | tf_op jit(solution)/shard_map/ppermute | solution.py:272
  13.9 8.4 %collective-permute-start.5 = (f32[32,8,128]{2,1,0:T(8,128)S(1)}, f32[32,8,128]{2,1,0:T(8,128)S(1)}, u32[]{:S(2)}, u32[]{:S(2)}) collective-permute-start(f32[32,8,128]{2,1,0:T(8,128)S(1)} %summed.11), channel_id=1, source_target_pairs={{0,4},{1,3},{2,6},{3,1},{4,0},{5,7},{6,2},{7,5},{8,12},{9,11},{10,... | collective-permute-start | bytes 393224 | tf_op jit(solution)/shard_map/ppermute | solution.py:272
  14.7 8.0 %collective-permute-start.7 = (f32[33,8,128]{2,1,0:T(8,128)S(1)}, f32[33,8,128]{2,1,0:T(8,128)S(1)}, u32[]{:S(2)}, u32[]{:S(2)}) collective-permute-start(f32[33,8,128]{2,1,0:T(8,128)S(1)} %summed.12.refs_3_), channel_id=1, source_target_pairs={{0,8},{1,9},{2,10},{3,11},{4,12},{5,13},{6,14},{7,15},{8,0},{9,1},... | collective-permute-start | bytes 405512 | tf_op jit(solution)/shard_map/ppermute | solution.py:272
  17.6 5.0 %collective-permute-start.9 = (f32[32,8,128]{2,1,0:T(8,128)S(1)}, f32[32,8,128]{2,1,0:T(8,128)S(1)}, u32[]{:S(2)}, u32[]{:S(2)}) collective-permute-start(f32[32,8,128]{2,1,0:T(8,128)S(1)} %summed.13), channel_id=1, source_target_pairs={{0,2},{1,5},{2,0},{3,7},{4,6},{5,1},{6,4},{7,3},{8,10},{9,13},{10,... | collective-permute-start | bytes 393224 | tf_op jit(solution)/shard_map/ppermute | solution.py:272
